TPU v7x, 32 devices: a whole 2x2x4 slice. The times are simulated.
32 devices in a mesh: gx: 8 (over y, x, core), gy: 4 (over z).
Axes of the slice: x: 2, y: 2, z: 4, core: 2. Of those that a mesh axis runs over, the one named last changes fastest.
Arguments:
- right_side: float32 [128, 64, 256], P('gx', 'gy'), may hold values from -24 to 24
- solution: float32 [128, 64, 256], P('gx', 'gy'), may hold values from -6 to 6
- phase: int32 [128, 64, 256], P('gx', 'gy'), may hold values from 0 to 2
- permeability: float32 [3], replicated, may hold values from 1 to 30
Outputs:
- solution_next: float32 [128, 64, 256], P('gx', 'gy')
Inputs may be any that keep to these rules, and one draw needn't show every extreme that they name: `phase`: material id of each cell.
All inputs are finite; a program needn't handle non-finite values.
Results may differ from a plain program's by a relative error of at most 0.0003.
Values sent between devices are 32-bit elements; how exact they have to be, the bound alone decides.
No kernel may reach another device: no remote copies, remote signals or barrier semaphores. Data moves between devices by JAX's collectives and lax.ppermute only.
A program may use at most 128 MiB of HBM per device.

v0:
```python
import jax
import jax.numpy as jnp
from jax import lax
from jax.sharding import PartitionSpec as P

DEG = 4
LEVELS = 4
COARSE_SWEEPS = 4


THETA = 1.15
DELTA = 0.85
SIGMA = 1.15 / 0.85
DAMPING = 0.6


def extended(block, sides, width):
    for axis, dim in sides:
        count = lax.axis_size(axis)
        forward = [(i, i + 1) for i in range(count - 1)]
        backward = [(target, source) for source, target in forward]
        low = lax.ppermute(
            lax.slice_in_dim(block, block.shape[dim] - width, None, axis=dim), axis, forward
        )
        high = lax.ppermute(lax.slice_in_dim(block, 0, width, axis=dim), axis, backward)
        block = jnp.concatenate([low, block, high], axis=dim)
    return block


def shift_lower(field):
    return jnp.concatenate([jnp.zeros_like(field[:, :, :1]), field[:, :, :-1]], axis=2)


def shift_upper(field):
    return jnp.concatenate([field[:, :, 1:], jnp.zeros_like(field[:, :, :1])], axis=2)


def face_weights(padded):
    centre = padded[1:-1, 1:-1]
    inside = (centre > 0).astype(jnp.float32)

    def weight(other):
        other = jnp.where(other > 0, other, centre)
        return 2.0 * centre * other / (centre + other + 1.0 - inside)

    return (
        weight(padded[:-2, 1:-1]),
        weight(padded[2:, 1:-1]),
        weight(padded[1:-1, :-2]),
        weight(padded[1:-1, 2:]),
        weight(shift_lower(centre)),
        weight(shift_upper(centre)),
    )


def inverse_diagonal(weights, scale):
    diagonal = scale * (weights[0] + weights[1] + weights[2] + weights[3] + weights[4] + weights[5])
    inside = (diagonal > 0).astype(jnp.float32)
    return inside / (diagonal + 1.0 - inside)


def apply_operator(padded, weights, scale):
    field = padded[1:-1, 1:-1]
    total = weights[0] * (field - padded[:-2, 1:-1])
    total = total + weights[1] * (field - padded[2:, 1:-1])
    total = total + weights[2] * (field - padded[1:-1, :-2])
    total = total + weights[3] * (field - padded[1:-1, 2:])
    total = total + weights[4] * (field - shift_lower(field))
    total = total + weights[5] * (field - shift_upper(field))
    return scale * total


def restrict(field):
    shape = field.shape
    blocks = field.reshape(shape[0] // 2, 2, shape[1] // 2, 2, shape[2] // 2, 2)
    return jnp.mean(blocks, axis=(1, 3, 5))


def prolong(field):
    return jnp.repeat(jnp.repeat(jnp.repeat(field, 2, axis=0), 2, axis=1), 2, axis=2)


def jacobi(source, operate, inverse, sweeps):
    correction = DAMPING * inverse * source
    for sweep in range(sweeps - 1):
        correction = correction + DAMPING * inverse * (source - operate(correction))
    return correction


def coarse_rim(field):
    return extended(field, (("gx", 0), ("gy", 1)), 1)


def local(right_side, solution, phase, permeability):
    material = jnp.where(
        phase == 0, permeability[0], jnp.where(phase == 1, permeability[1], permeability[2])
    )
    width = 1
    padded_material = extended(material, (("gx", 0), ("gy", 1)), width)
    weights = face_weights(padded_material)
    inverse = inverse_diagonal(weights, 1.0)

    def fine_op(field):
        return apply_operator(extended(field, (("gx", 0), ("gy", 1)), 1), weights, 1.0)

    residual = right_side - fine_op(solution)
    rho = 1.0 / SIGMA
    direction = inverse * residual / THETA
    smoothed = direction
    for step in range(DEG - 1):
        rho_next = 1.0 / (2.0 * SIGMA - rho)
        image = fine_op(smoothed)
        direction = rho_next * rho * direction + 2.0 * rho_next / DELTA * inverse * (
            residual - image
        )
        smoothed = smoothed + direction
        rho = rho_next
    tables = []
    materials = []
    material_level = material
    for level in range(1, LEVELS + 1):
        material_level = restrict(material_level)
        materials.append(material_level)
        scale = 0.25**level
        level_weights = face_weights(coarse_rim(material_level))
        tables.append((level_weights, inverse_diagonal(level_weights, scale), scale))

    def level_op(level, field):
        level_weights, level_inverse, scale = tables[level - 1]
        return apply_operator(coarse_rim(field), level_weights, scale)

    def coarsest(source):
        return jacobi(source, lambda f: level_op(LEVELS, f), tables[LEVELS - 1][1], COARSE_SWEEPS)

    def vcycle(level, source):
        if level == LEVELS:
            return coarsest(source)
        level_inverse = tables[level - 1][1]
        correction = DAMPING * level_inverse * source
        remainder = source - level_op(level, correction)
        correction = correction + prolong(vcycle(level + 1, restrict(remainder)))
        correction = correction + DAMPING * level_inverse * (source - level_op(level, correction))
        return correction

    coarse_source = restrict(residual)
    coarse = vcycle(1, coarse_source)
    coarse = coarse + vcycle(1, coarse_source - level_op(1, coarse))
    return solution + smoothed + prolong(coarse)


def solution(mesh):
    placed = (P("gx", "gy", None), P("gx", "gy", None), P("gx", "gy", None), P())
    return jax.shard_map(
        local, mesh=mesh, in_specs=placed, out_specs=P("gx", "gy", None), check_vma=False
    )
```

profile of v0, /device:TPU:28, one launch (start us, length us, event | category | flops | bytes accessed | tf_op | source)
XLA Modules:
  0.0 482.9 jit_solution(810258849572995632)
XLA Ops:
  12.5 18.1 %reshape.300 = f32[8,2,8,2,128,2]{5,4,3,2,1,0:T(8,128)} reshape(f32[16,16,256]{2,1,0:T(8,128)S(1)} %select_select_fusion) | data formatting | bytes 524288 | tf_op jit(solution)/shard_map/reshape | solution.py:75
  30.6 7.0 %reduce_sum.120 = f32[8,8,128]{2,1,0:T(8,128)S(1)} reduce(f32[8,2,8,2,128,2]{5,4,3,2,1,0:T(8,128)} %reshape.300, f32[]{:T(128)} %constant.22.clone.1), dimensions={1,3,5}, to_apply=%region_0.1 | reduce | flops 57344 | bytes 294916 | tf_op jit(solution)/shard_map/reduce_sum | solution.py:76
  48.3 4.5 collective-permute-start.5
  65.7 4.5 collective-permute-start.7
  74.9 5.2 %collective-permute-start.23 = (f32[10,1,128]{2,1,0:T(1,128)S(1)}, f32[10,1,128]{2,1,0:T(1,128)S(1)}, u32[]{:S(2)}, u32[]{:S(2)}) collective-permute-start(f32[10,1,128]{2,1,0:T(1,128)S(1)} %get-tuple-element.86), channel_id=1, source_target_pairs={{1,0},{2,1},{3,2},{5,4},{6,5},{7,6},{9,8},{10,9},{11,10},{13,12},{... | collective-permute-start | bytes 15368 | tf_op jit(solution)/shard_map/ppermute | solution.py:25
  81.7 18.1 %reshape.301 = f32[8,2,8,2,128,2]{5,4,3,2,1,0:T(8,128)} reshape(f32[16,16,256]{2,1,0:T(8,128)S(1)} %get-tuple-element.11) | data formatting | bytes 524288 | tf_op jit(solution)/shard_map/reshape | solution.py:75
  99.8 7.0 %reduce_sum.121 = f32[8,8,128]{2,1,0:T(8,128)S(1)} reduce(f32[8,2,8,2,128,2]{5,4,3,2,1,0:T(8,128)} %reshape.301, f32[]{:T(128)} %constant.22.clone.1), dimensions={1,3,5}, to_apply=%region_1.2 | reduce | flops 57344 | bytes 294916 | tf_op jit(solution)/shard_map/reduce_sum | solution.py:76
  107.5 4.3 collective-permute-start.29
  115.7 5.1 %collective-permute-start.27 = (f32[6,1,64]{2,1,0:T(1,128)}, f32[6,1,64]{2,1,0:T(1,128)}, u32[]{:S(2)}, u32[]{:S(2)}) collective-permute-start(f32[6,1,64]{2,1,0:T(1,128)} %get-tuple-element.120), channel_id=1, source_target_pairs={{1,0},{2,1},{3,2},{5,4},{6,5},{7,6},{9,8},{10,9},{11,10},{13,12},{... | collective-permute-start | bytes 4616 | tf_op jit(solution)/shard_map/ppermute | solution.py:25
  125.3 4.1 collective-permute-done.30
  141.5 4.5 collective-permute-start.35
  161.5 4.5 collective-permute-start.45
  176.7 5.2 %collective-permute-start.43 = (f32[3,1,16]{2,1,0:T(1,128)S(1)}, f32[3,1,16]{2,1,0:T(1,128)S(1)}, u32[]{:S(2)}, u32[]{:S(2)}) collective-permute-start(f32[3,1,16]{2,1,0:T(1,128)S(1)} %pad_maximum_fusion.214), channel_id=1, source_target_pairs={{1,0},{2,1},{3,2},{5,4},{6,5},{7,6},{9,8},{10,9},{11,10},{13,12},{... | collective-permute-start | bytes 584 | tf_op jit(solution)/shard_map/ppermute | solution.py:25
  191.0 4.2 collective-permute-start.51
  196.6 4.1 collective-permute-done.50
  213.7 4.1 collective-permute-done.54
  229.2 4.1 collective-permute-done.58
  244.6 4.1 collective-permute-done.62
  260.9 4.1 collective-permute-done.66
  279.4 4.1 collective-permute-done.70
  292.6 4.2 collective-permute-start.75
  298.3 4.1 collective-permute-done.74
  314.5 4.1 collective-permute-done.78
  332.7 4.1 collective-permute-done.82
  349.0 4.1 collective-permute-done.86
  365.7 4.1 collective-permute-done.90
  381.6 4.1 collective-permute-done.94
  416.2 4.1 collective-permute-done.102
  434.6 5.1 %collective-permute-start.15 = (f32[18,1,256]{2,1,0:T(1,128)}, f32[18,1,256]{2,1,0:T(1,128)}, u32[]{:S(2)}, u32[]{:S(2)}) collective-permute-start(f32[18,1,256]{2,1,0:T(1,128)} %get-tuple-element.49), channel_id=1, source_target_pairs={{1,0},{2,1},{3,2},{5,4},{6,5},{7,6},{9,8},{10,9},{11,10},{13,12},{... | collective-permute-start | bytes 55304 | tf_op jit(solution)/shard_map/ppermute | solution.py:25
  450.2 4.5 collective-permute-start.111
  470.0 4.5 collective-permute-start.19
  476.0 4.2 collective-permute-done.18
  (540 shorter events, 307.5 us)
Async XLA Ops:
  4.4 51.0 %collective-permute-start.1 = (f32[1,16,256]{2,1,0:T(8,128)S(1)}, f32[1,16,256]{2,1,0:T(8,128)S(1)}, u32[]{:S(2)}, u32[]{:S(2)}) collective-permute-start(f32[1,16,256]{2,1,0:T(8,128)S(1)} %get-tuple-element.75), channel_id=1, source_target_pairs={{4,0},{8,4},{12,8},{16,12},{20,16},{24,20},{28,24},{5,1},{9,5},{13... | collective-permute-start | bytes 49160 | tf_op jit(solution)/shard_map/ppermute | solution.py:25
  7.2 50.6 %collective-permute-start = (f32[1,16,256]{2,1,0:T(8,128)S(1)}, f32[1,16,256]{2,1,0:T(8,128)S(1)}, u32[]{:S(2)}, u32[]{:S(2)}) collective-permute-start(f32[1,16,256]{2,1,0:T(8,128)S(1)} %get-tuple-element.74), channel_id=1, source_target_pairs={{0,4},{4,8},{8,12},{12,16},{16,20},{20,24},{24,28},{1,5},{5,9},{9,... | collective-permute-start | bytes 49160 | tf_op jit(solution)/shard_map/ppermute | solution.py:22
  9.8 52.1 %collective-permute-start.4 = (f32[1,16,256]{2,1,0:T(8,128)S(1)}, f32[1,16,256]{2,1,0:T(8,128)S(1)}, u32[]{:S(2)}, u32[]{:S(2)}) collective-permute-start(f32[1,16,256]{2,1,0:T(8,128)S(1)} %get-tuple-element.71), channel_id=1, source_target_pairs={{0,4},{4,8},{8,12},{12,16},{16,20},{20,24},{24,28},{1,5},{5,9},{9,... | collective-permute-start | bytes 49160 | tf_op jit(solution)/shard_map/ppermute | solution.py:22
  48.3 16.0 %collective-permute-start.5 = (f32[1,16,256]{2,1,0:T(8,128)S(1)}, f32[1,16,256]{2,1,0:T(8,128)S(1)}, u32[]{:S(2)}, u32[]{:S(2)}) collective-permute-start(f32[1,16,256]{2,1,0:T(8,128)S(1)} %get-tuple-element.70), channel_id=1, source_target_pairs={{4,0},{8,4},{12,8},{16,12},{20,16},{24,20},{28,24},{5,1},{9,5},{13... | collective-permute-start | bytes 49160 | tf_op jit(solution)/shard_map/ppermute | solution.py:25
  52.9 12.8 %collective-permute-start.21 = (f32[1,8,128]{2,1,0:T(8,128)S(1)}, f32[1,8,128]{2,1,0:T(8,128)S(1)}, u32[]{:S(2)}, u32[]{:S(2)}) collective-permute-start(f32[1,8,128]{2,1,0:T(8,128)S(1)} %get-tuple-element.111), channel_id=1, source_target_pairs={{4,0},{8,4},{12,8},{16,12},{20,16},{24,20},{28,24},{5,1},{9,5},{13... | collective-permute-start | bytes 12296 | tf_op jit(solution)/shard_map/ppermute | solution.py:25
  55.4 14.9 %collective-permute-start.20 = (f32[1,8,128]{2,1,0:T(8,128)S(1)}, f32[1,8,128]{2,1,0:T(8,128)S(1)}, u32[]{:S(2)}, u32[]{:S(2)}) collective-permute-start(f32[1,8,128]{2,1,0:T(8,128)S(1)} %get-tuple-element.110), channel_id=1, source_target_pairs={{0,4},{4,8},{8,12},{12,16},{16,20},{20,24},{24,28},{1,5},{5,9},{9,... | collective-permute-start | bytes 12296 | tf_op jit(solution)/shard_map/ppermute | solution.py:22
  57.8 55.9 %collective-permute-start.25 = (f32[1,4,64]{2,1,0:T(4,128)S(1)}, f32[1,4,64]{2,1,0:T(4,128)S(1)}, u32[]{:S(2)}, u32[]{:S(2)}) collective-permute-start(f32[1,4,64]{2,1,0:T(4,128)S(1)} %get-tuple-element.141), channel_id=1, source_target_pairs={{4,0},{8,4},{12,8},{16,12},{20,16},{24,20},{28,24},{5,1},{9,5},{13... | collective-permute-start | bytes 3080 | tf_op jit(solution)/shard_map/ppermute | solution.py:25
  71.6 42.1 %collective-permute-start.24 = (f32[1,4,64]{2,1,0:T(4,128)S(1)}, f32[1,4,64]{2,1,0:T(4,128)S(1)}, u32[]{:S(2)}, u32[]{:S(2)}) collective-permute-start(f32[1,4,64]{2,1,0:T(4,128)S(1)} %get-tuple-element.140), channel_id=1, source_target_pairs={{0,4},{4,8},{8,12},{12,16},{16,20},{20,24},{24,28},{1,5},{5,9},{9,... | collective-permute-start | bytes 3080 | tf_op jit(solution)/shard_map/ppermute | solution.py:22
  73.6 33.2 %collective-permute-start.22 = (f32[10,1,128]{2,1,0:T(1,128)S(1)}, f32[10,1,128]{2,1,0:T(1,128)S(1)}, u32[]{:S(2)}, u32[]{:S(2)}) collective-permute-start(f32[10,1,128]{2,1,0:T(1,128)S(1)} %get-tuple-element.87), channel_id=1, source_target_pairs={{0,1},{1,2},{2,3},{4,5},{5,6},{6,7},{8,9},{9,10},{10,11},{12,13},{... | collective-permute-start | bytes 15368 | tf_op jit(solution)/shard_map/ppermute | solution.py:22
  74.9 31.9 %collective-permute-start.23 = (f32[10,1,128]{2,1,0:T(1,128)S(1)}, f32[10,1,128]{2,1,0:T(1,128)S(1)}, u32[]{:S(2)}, u32[]{:S(2)}) collective-permute-start(f32[10,1,128]{2,1,0:T(1,128)S(1)} %get-tuple-element.86), channel_id=1, source_target_pairs={{1,0},{2,1},{3,2},{5,4},{6,5},{7,6},{9,8},{10,9},{11,10},{13,12},{... | collective-permute-start | bytes 15368 | tf_op jit(solution)/shard_map/ppermute | solution.py:25
  107.5 13.3 %collective-permute-start.29 = (f32[1,8,128]{2,1,0:T(8,128)S(1)}, f32[1,8,128]{2,1,0:T(8,128)S(1)}, u32[]{:S(2)}, u32[]{:S(2)}) collective-permute-start(f32[1,8,128]{2,1,0:T(8,128)S(1)} %get-tuple-element.107), channel_id=1, source_target_pairs={{4,0},{8,4},{12,8},{16,12},{20,16},{24,20},{28,24},{5,1},{9,5},{13... | collective-permute-start | bytes 12296 | tf_op jit(solution)/shard_map/ppermute | solution.py:25
  114.4 19.5 %collective-permute-start.26 = (f32[6,1,64]{2,1,0:T(1,128)}, f32[6,1,64]{2,1,0:T(1,128)}, u32[]{:S(2)}, u32[]{:S(2)}) collective-permute-start(f32[6,1,64]{2,1,0:T(1,128)} %get-tuple-element.121), channel_id=1, source_target_pairs={{0,1},{1,2},{2,3},{4,5},{5,6},{6,7},{8,9},{9,10},{10,11},{12,13},{... | collective-permute-start | bytes 4616 | tf_op jit(solution)/shard_map/ppermute | solution.py:22
  115.7 18.2 %collective-permute-start.27 = (f32[6,1,64]{2,1,0:T(1,128)}, f32[6,1,64]{2,1,0:T(1,128)}, u32[]{:S(2)}, u32[]{:S(2)}) collective-permute-start(f32[6,1,64]{2,1,0:T(1,128)} %get-tuple-element.120), channel_id=1, source_target_pairs={{1,0},{2,1},{3,2},{5,4},{6,5},{7,6},{9,8},{10,9},{11,10},{13,12},{... | collective-permute-start | bytes 4616 | tf_op jit(solution)/shard_map/ppermute | solution.py:25
  135.0 11.1 %collective-permute-start.37 = (f32[1,4,64]{2,1,0:T(4,128)S(1)}, f32[1,4,64]{2,1,0:T(4,128)S(1)}, u32[]{:S(2)}, u32[]{:S(2)}) collective-permute-start(f32[1,4,64]{2,1,0:T(4,128)S(1)} %get-tuple-element.137), channel_id=1, source_target_pairs={{4,0},{8,4},{12,8},{16,12},{20,16},{24,20},{28,24},{5,1},{9,5},{13... | collective-permute-start | bytes 3080 | tf_op jit(solution)/shard_map/ppermute | solution.py:25
  140.2 15.5 %collective-permute-start.34 = (f32[4,1,32]{2,1,0:T(1,128)S(1)}, f32[4,1,32]{2,1,0:T(1,128)S(1)}, u32[]{:S(2)}, u32[]{:S(2)}) collective-permute-start(f32[4,1,32]{2,1,0:T(1,128)S(1)} %get-tuple-element.151), channel_id=1, source_target_pairs={{0,1},{1,2},{2,3},{4,5},{5,6},{6,7},{8,9},{9,10},{10,11},{12,13},{... | collective-permute-start | bytes 1544 | tf_op jit(solution)/shard_map/ppermute | solution.py:22
  141.5 14.2 %collective-permute-start.35 = (f32[4,1,32]{2,1,0:T(1,128)S(1)}, f32[4,1,32]{2,1,0:T(1,128)S(1)}, u32[]{:S(2)}, u32[]{:S(2)}) collective-permute-start(f32[4,1,32]{2,1,0:T(1,128)S(1)} %get-tuple-element.150), channel_id=1, source_target_pairs={{1,0},{2,1},{3,2},{5,4},{6,5},{7,6},{9,8},{10,9},{11,10},{13,12},{... | collective-permute-start | bytes 1544 | tf_op jit(solution)/shard_map/ppermute | solution.py:25
  157.0 18.3 %collective-permute-start.41 = (f32[1,1,16]{2,1,0:T(1,128)S(1)}, f32[1,1,16]{2,1,0:T(1,128)S(1)}, u32[]{:S(2)}, u32[]{:S(2)}) collective-permute-start(f32[1,1,16]{2,1,0:T(1,128)S(1)} %multiply_bitcast_fusion), channel_id=1, source_target_pairs={{4,0},{8,4},{12,8},{16,12},{20,16},{24,20},{28,24},{5,1},{9,5},{13... | collective-permute-start | bytes 200 | tf_op jit(solution)/shard_map/ppermute | solution.py:25
  159.6 15.8 %collective-permute-start.40 = (f32[1,1,16]{2,1,0:T(1,128)S(1)}, f32[1,1,16]{2,1,0:T(1,128)S(1)}, u32[]{:S(2)}, u32[]{:S(2)}) collective-permute-start(f32[1,1,16]{2,1,0:T(1,128)S(1)} %multiply_bitcast_fusion), channel_id=1, source_target_pairs={{0,4},{4,8},{8,12},{12,16},{16,20},{20,24},{24,28},{1,5},{5,9},{9,... | collective-permute-start | bytes 200 | tf_op jit(solution)/shard_map/ppermute | solution.py:22
  171.9 10.0 %collective-permute-start.47 = (f32[4,1,32]{2,1,0:T(1,128)S(1)}, f32[4,1,32]{2,1,0:T(1,128)S(1)}, u32[]{:S(2)}, u32[]{:S(2)}) collective-permute-start(f32[4,1,32]{2,1,0:T(1,128)S(1)} %get-tuple-element.149), channel_id=1, source_target_pairs={{1,0},{2,1},{3,2},{5,4},{6,5},{7,6},{9,8},{10,9},{11,10},{13,12},{... | collective-permute-start | bytes 1544 | tf_op jit(solution)/shard_map/ppermute | solution.py:25
  265.7 10.3 %collective-permute-start.69 = (f32[1,8,128]{2,1,0:T(8,128)S(1)}, f32[1,8,128]{2,1,0:T(8,128)S(1)}, u32[]{:S(2)}, u32[]{:S(2)}) collective-permute-start(f32[1,8,128]{2,1,0:T(8,128)S(1)} %get-tuple-element.103), channel_id=1, source_target_pairs={{4,0},{8,4},{12,8},{16,12},{20,16},{24,20},{28,24},{5,1},{9,5},{13... | collective-permute-start | bytes 12296 | tf_op jit(solution)/shard_map/ppermute | solution.py:25
  270.0 18.7 %collective-permute-start.9 = (f32[1,16,256]{2,1,0:T(8,128)S(1)}, f32[1,16,256]{2,1,0:T(8,128)S(1)}, u32[]{:S(2)}, u32[]{:S(2)}) collective-permute-start(f32[1,16,256]{2,1,0:T(8,128)S(1)} %get-tuple-element.65), channel_id=1, source_target_pairs={{4,0},{8,4},{12,8},{16,12},{20,16},{24,20},{28,24},{5,1},{9,5},{13... | collective-permute-start | bytes 49160 | tf_op jit(solution)/shard_map/ppermute | solution.py:25
  274.1 14.6 %collective-permute-start.8 = (f32[1,16,256]{2,1,0:T(8,128)S(1)}, f32[1,16,256]{2,1,0:T(8,128)S(1)}, u32[]{:S(2)}, u32[]{:S(2)}) collective-permute-start(f32[1,16,256]{2,1,0:T(8,128)S(1)} %get-tuple-element.64), channel_id=1, source_target_pairs={{0,4},{4,8},{8,12},{12,16},{16,20},{20,24},{24,28},{1,5},{5,9},{9,... | collective-permute-start | bytes 49160 | tf_op jit(solution)/shard_map/ppermute | solution.py:22
  288.7 18.3 %collective-permute-start.11 = (f32[18,1,256]{2,1,0:T(1,128)S(1)}, f32[18,1,256]{2,1,0:T(1,128)S(1)}, u32[]{:S(2)}, u32[]{:S(2)}) collective-permute-start(f32[18,1,256]{2,1,0:T(1,128)S(1)} %get-tuple-element.51), channel_id=1, source_target_pairs={{1,0},{2,1},{3,2},{5,4},{6,5},{7,6},{9,8},{10,9},{11,10},{13,12},{... | collective-permute-start | bytes 55304 | tf_op jit(solution)/shard_map/ppermute | solution.py:25
  290.9 16.1 %collective-permute-start.10 = (f32[18,1,256]{2,1,0:T(1,128)S(1)}, f32[18,1,256]{2,1,0:T(1,128)S(1)}, u32[]{:S(2)}, u32[]{:S(2)}) collective-permute-start(f32[18,1,256]{2,1,0:T(1,128)S(1)} %get-tuple-element.50), channel_id=1, source_target_pairs={{0,1},{1,2},{2,3},{4,5},{5,6},{6,7},{8,9},{9,10},{10,11},{12,13},{... | collective-permute-start | bytes 55304 | tf_op jit(solution)/shard_map/ppermute | solution.py:22
  402.5 10.3 %collective-permute-start.101 = (f32[1,2,32]{2,1,0:T(2,128)S(1)}, f32[1,2,32]{2,1,0:T(2,128)S(1)}, u32[]{:S(2)}, u32[]{:S(2)}) collective-permute-start(f32[1,2,32]{2,1,0:T(2,128)S(1)} %get-tuple-element.155), channel_id=1, source_target_pairs={{4,0},{8,4},{12,8},{16,12},{20,16},{24,20},{28,24},{5,1},{9,5},{13... | collective-permute-start | bytes 776 | tf_op jit(solution)/shard_map/ppermute | solution.py:25
  406.9 27.0 %collective-permute-start.13 = (f32[1,16,256]{2,1,0:T(8,128)S(1)}, f32[1,16,256]{2,1,0:T(8,128)S(1)}, u32[]{:S(2)}, u32[]{:S(2)}) collective-permute-start(f32[1,16,256]{2,1,0:T(8,128)S(1)} %get-tuple-element.61), channel_id=1, source_target_pairs={{4,0},{8,4},{12,8},{16,12},{20,16},{24,20},{28,24},{5,1},{9,5},{13... | collective-permute-start | bytes 49160 | tf_op jit(solution)/shard_map/ppermute | solution.py:25
  411.0 22.9 %collective-permute-start.12 = (f32[1,16,256]{2,1,0:T(8,128)S(1)}, f32[1,16,256]{2,1,0:T(8,128)S(1)}, u32[]{:S(2)}, u32[]{:S(2)}) collective-permute-start(f32[1,16,256]{2,1,0:T(8,128)S(1)} %get-tuple-element.60), channel_id=1, source_target_pairs={{0,4},{4,8},{8,12},{12,16},{16,20},{20,24},{24,28},{1,5},{5,9},{9,... | collective-permute-start | bytes 49160 | tf_op jit(solution)/shard_map/ppermute | solution.py:22
  430.4 10.6 %collective-permute-start.107 = (f32[6,1,64]{2,1,0:T(1,128)S(1)}, f32[6,1,64]{2,1,0:T(1,128)S(1)}, u32[]{:S(2)}, u32[]{:S(2)}) collective-permute-start(f32[6,1,64]{2,1,0:T(1,128)S(1)} %get-tuple-element.113), channel_id=1, source_target_pairs={{1,0},{2,1},{3,2},{5,4},{6,5},{7,6},{9,8},{10,9},{11,10},{13,12},{... | collective-permute-start | bytes 4616 | tf_op jit(solution)/shard_map/ppermute | solution.py:25
  434.6 21.5 %collective-permute-start.15 = (f32[18,1,256]{2,1,0:T(1,128)}, f32[18,1,256]{2,1,0:T(1,128)}, u32[]{:S(2)}, u32[]{:S(2)}) collective-permute-start(f32[18,1,256]{2,1,0:T(1,128)} %get-tuple-element.49), channel_id=1, source_target_pairs={{1,0},{2,1},{3,2},{5,4},{6,5},{7,6},{9,8},{10,9},{11,10},{13,12},{... | collective-permute-start | bytes 55304 | tf_op jit(solution)/shard_map/ppermute | solution.py:25
  439.7 16.3 %collective-permute-start.14 = (f32[18,1,256]{2,1,0:T(1,128)}, f32[18,1,256]{2,1,0:T(1,128)}, u32[]{:S(2)}, u32[]{:S(2)}) collective-permute-start(f32[18,1,256]{2,1,0:T(1,128)} %get-tuple-element.48), channel_id=1, source_target_pairs={{0,1},{1,2},{2,3},{4,5},{5,6},{6,7},{8,9},{9,10},{10,11},{12,13},{... | collective-permute-start | bytes 55304 | tf_op jit(solution)/shard_map/ppermute | solution.py:22
  450.2 13.5 %collective-permute-start.111 = (f32[10,1,128]{2,1,0:T(1,128)S(1)}, f32[10,1,128]{2,1,0:T(1,128)S(1)}, u32[]{:S(2)}, u32[]{:S(2)}) collective-permute-start(f32[10,1,128]{2,1,0:T(1,128)S(1)} %get-tuple-element.77), channel_id=1, source_target_pairs={{1,0},{2,1},{3,2},{5,4},{6,5},{7,6},{9,8},{10,9},{11,10},{13,12},{... | collective-permute-start | bytes 15368 | tf_op jit(solution)/shard_map/ppermute | solution.py:25
  459.1 10.1 %collective-permute-start.17 = (f32[1,16,256]{2,1,0:T(8,128)}, f32[1,16,256]{2,1,0:T(8,128)}, u32[]{:S(2)}, u32[]{:S(2)}) collective-permute-start(f32[1,16,256]{2,1,0:T(8,128)} %get-tuple-element.59), channel_id=1, source_target_pairs={{4,0},{8,4},{12,8},{16,12},{20,16},{24,20},{28,24},{5,1},{9,5},{13... | collective-permute-start | bytes 49160 | tf_op jit(solution)/shard_map/ppermute | solution.py:25
  (164 other events, 5842.2 us)
where the time goes:
time: 487 us; the launch traced here: 483 us
  starting transfers between devices  261 us (54%)
  waiting for transfers between devices  116 us (24%)
  local copies, waits for them, and re-layouts  59.2 us (12%)
  other arithmetic  44 us (9%)
    ppermute x56, starting transfers between devices, extended(): lax.ppermute(lax.slice_in_dim(block, 0, width, axis=dim), axis, backward)  163 us
    ppermute x56, waiting for transfers between devices, extended(): lax.ppermute(lax.slice_in_dim(block, block.shape[dim] - width, None, axis...  115 us
    ppermute x56, starting transfers between devices, extended(): lax.ppermute(lax.slice_in_dim(block, block.shape[dim] - width, None, axis...  98.3 us
    reshape x6, local copies, waits for them, and re-layouts, restrict(): blocks = field.reshape(shape[0] // 2, 2, shape[1] // 2, 2, shape[2] // 2, 2)  41.6 us
    reduce_sum x13, other arithmetic, restrict(): return jnp.mean(blocks, axis=(1, 3, 5))  17.5 us
  transfers between devices with their start and end apart: 112, of which 33 were waited for; matrix products, arithmetic and copies ran while one was open for 17% of the time, Pallas kernels for 0%

commit v1 on v0

v1 whole, which is shorter than its diff:
```python
import functools
import math

import jax
import jax.numpy as jnp
from jax import lax
from jax.experimental import pallas as pl
from jax.experimental.pallas import tpu as pltpu
from jax.sharding import PartitionSpec as P

DEG = 4
COARSE_SWEEPS = 4
THETA = 1.15
DELTA = 0.85
SIGMA = 1.15 / 0.85
DAMPING = 0.6
KEPT = 1.0 - DAMPING
F32 = jnp.float32
LANES = 128
MIB = 1024 * 1024
HELD = 4 * MIB


def iota(shape, axis):
    return lax.broadcasted_iota(jnp.int32, shape, axis)


def invert(x):
    guess = pl.reciprocal(x, approx=True)
    return guess * (2.0 - x * guess)


def harmonic(a, b, scale):
    return (2.0 * scale) * a * b * invert(jnp.maximum(a + b, 1e-3))


def pair_matrix(size, offset=0):
    column = iota((size, LANES), 1)
    return ((column >= offset) & (iota((size, LANES), 0) // 2 == column - offset)).astype(jnp.bfloat16)


def spread_matrix(width):
    return (iota((LANES, width), 1) // 2 == iota((LANES, width), 0)).astype(jnp.bfloat16)


def select(values, matrix):
    high = values.astype(jnp.bfloat16)
    rest = values - high.astype(F32)
    middle = rest.astype(jnp.bfloat16)
    low = (rest - middle.astype(F32)).astype(jnp.bfloat16)
    out = jnp.dot(high, matrix, preferred_element_type=F32)
    out = out + jnp.dot(middle, matrix, preferred_element_type=F32)
    return out + jnp.dot(low, matrix, preferred_element_type=F32)


def roll(x, shift, axis):
    return pltpu.roll(x, shift % x.shape[axis], axis)


def lower(x, axis):
    return roll(x, 1, axis)


def upper(x, axis):
    return roll(x, x.shape[axis] - 1, axis)


def faces_kernel(place, permeability, potential, phase, material, inner, outer, even, odd):
    low_x, low_y = place[0] == 1, place[1] == 1
    count, rows = potential.shape[:2]
    ids = phase[...]
    p0, p1, p2 = permeability[0], permeability[1], permeability[2]
    material[...] = jnp.where(ids == 0, p0, jnp.where(ids == 1, p1, p2))
    last = count - 1
    first = jnp.where(low_x, 0, last)
    second = jnp.where(low_x, 1, last - 1)
    inner[0] = potential[first]
    inner[1] = material[first]
    inner[2] = material[second]
    outer[0] = potential[last - first]
    outer[1] = material[last - first]
    outer[2] = material[last - second]
    for i in range(count):
        for slot, (ref, a, b) in enumerate(((potential, 0, rows - 1), (material, 0, rows - 1), (material, 1, rows - 2))):
            low, high = ref[i, a : a + 1, :], ref[i, b : b + 1, :]
            even[slot, i : i + 1, :] = jnp.where(low_y, low, high)
            odd[slot, i : i + 1, :] = jnp.where(low_y, high, low)


def residual_kernel(
    place, source, potential, material, inner, outer, even, odd,
    residual, payload, source1, material1, strip_even, strip_odd,
    mat, pot, wide, narrow, coarse, wide2, narrow2,
):
    low_x, low_y = place[0] == 1, place[1] == 1
    count, rows, depth = source.shape
    c1, r1, d1 = count // 2, rows // 2, depth // 2
    c2, r2 = c1 // 2, r1 // 2

    def ordered(flag, a, b):
        return jnp.where(flag, a, b), jnp.where(flag, b, a)

    x_low, x_high = ordered(low_x, inner[...], outer[...])
    y_low, y_high = ordered(low_y, even[...], odd[...])
    mat[0], mat[count + 1] = x_low[1], x_high[1]
    pot[0], pot[count + 1] = x_low[0], x_high[0]
    mat[pl.ds(1, count)] = material[...]
    pot[pl.ds(1, count)] = potential[...]
    row, lane = iota((rows, depth), 0), iota((rows, depth), 1)

    def neighbours(a, low, high):
        below = jnp.where(row == 0, low, lower(a, 0))
        above = jnp.where(row == rows - 1, high, upper(a, 0))
        return below, above

    face = harmonic(mat[0], mat[1], 1.0)
    for i in range(count):
        a, v = mat[i + 1], pot[i + 1]
        m_down, m_up = neighbours(a, y_low[1, i : i + 1], y_high[1, i : i + 1])
        v_down, v_up = neighbours(v, y_low[0, i : i + 1], y_high[0, i : i + 1])
        m_back = jnp.where(lane == 0, 0.0, lower(a, 1))
        m_front = jnp.where(lane == depth - 1, 0.0, upper(a, 1))
        next_face = harmonic(a, mat[i + 2], 1.0)
        weights = [face, next_face] + [harmonic(a, b, 1.0) for b in (m_down, m_up, m_back, m_front)]
        others = (mat[i], mat[i + 2], m_down, m_up, m_back, m_front)
        fields = (pot[i], pot[i + 2], v_down, v_up, lower(v, 1), upper(v, 1))
        diagonal = sum(jnp.where(b > 0.0, w, a) for w, b in zip(weights, others))
        off = sum(w * f for w, f in zip(weights, fields))
        left = source[i] - (diagonal * v - off)
        residual[i] = left
        face = next_face
        at = (i // 2) * rows
        if i % 2 == 0:
            kept_left, kept_a = left, a
        else:
            wide[at : at + rows] = kept_left + left
            wide[count // 2 * rows + at : count // 2 * rows + at + rows] = kept_a + a
        low = jnp.concatenate([left[:4], a[:4]], axis=0)
        high = jnp.concatenate([left[rows - 4 :], a[rows - 4 :]], axis=0)
        for ref, strip in ((strip_even, jnp.where(low_y, low, high)), (strip_odd, jnp.where(low_y, high, low))):
            for piece in range(depth // LANES):
                ref[i * (depth // LANES) + piece] = strip[:, piece * LANES : (piece + 1) * LANES]
    base = 2 * c1 * rows
    for n, both in enumerate((x_low[1] + x_low[2], x_high[1] + x_high[2], y_low[1] + y_low[2], y_high[1] + y_high[2])):
        wide[base + n * rows : base + (n + 1) * rows] = both
    narrow[...] = select(wide[...], pair_matrix(depth)) * 0.125
    half = narrow.shape[0] // 2
    coarse[...] = narrow[pl.ds(0, half, 2)] + narrow[pl.ds(1, half, 2)]

    s = [coarse[k * r1 : (k + 1) * r1] for k in range(c1)]
    m = [coarse[c1 * r1 + k * r1 : c1 * r1 + (k + 1) * r1] for k in range(c1)]
    base = 2 * c1 * r1
    m_xlow, m_xhigh, m_ylow, m_yhigh = (coarse[base + n * r1 : base + (n + 1) * r1] for n in range(4))
    row, lane = iota((r1, d1), 0), iota((r1, d1), 1)
    around = [m_xlow] + m + [m_xhigh]
    errors, tables = [], []
    face = harmonic(around[0], around[1], 0.25)
    for k in range(c1):
        a = m[k]
        down = jnp.where(row == 0, m_ylow[k : k + 1], lower(a, 0))
        up = jnp.where(row == r1 - 1, m_yhigh[k : k + 1], upper(a, 0))
        back = jnp.where(lane == 0, 0.0, lower(a, 1))
        front = jnp.where(lane == d1 - 1, 0.0, upper(a, 1))
        next_face = harmonic(a, around[k + 2], 0.25)
        weights = [face, next_face] + [harmonic(a, b, 0.25) for b in (down, up, back, front)]
        others = (around[k], around[k + 2], down, up, back, front)
        diagonal = sum(jnp.where(b > 0.0, w, 0.25 * a) for w, b in zip(weights, others))
        errors.append(DAMPING * s[k] * invert(diagonal))
        tables.append(weights)
        face = next_face
        source1[k] = s[k]
        material1[k] = a
        low = jnp.concatenate([s[k][:4], a[:4]], axis=0)
        high = jnp.concatenate([s[k][r1 - 4 :], a[r1 - 4 :]], axis=0)
        at = count * (depth // LANES) + k
        strip_even[at] = jnp.where(low_y, low, high)
        strip_odd[at] = jnp.where(low_y, high, low)
    for k in range(c1):
        e, w = errors[k], tables[k]
        t = KEPT * s[k] + w[4] * lower(e, 1) + w[5] * upper(e, 1)
        t = t + w[2] * jnp.where(row == 0, 0.0, lower(e, 0)) + w[3] * jnp.where(row == r1 - 1, 0.0, upper(e, 0))
        if k > 0:
            t = t + w[0] * errors[k - 1]
        if k < c1 - 1:
            t = t + w[1] * errors[k + 1]
        at = (k // 2) * r1
        if k % 2 == 0:
            kept = t
        else:
            wide2[0, at : at + r1] = kept + t
            wide2[1, at : at + r1] = m[k - 1] + m[k]
        base = c2 * r1
        wide2[1, base + k : base + k + 1] = (w[2] * e)[:1]
        wide2[1, base + r1 + k : base + r1 + k + 1] = (w[3] * e)[r1 - 1 :]
    wide2[0, base : base + r1] = tables[0][0] * errors[0]
    wide2[0, base + r1 : base + 2 * r1] = tables[c1 - 1][1] * errors[c1 - 1]
    narrow2[...] = (select(wide2[0], pair_matrix(d1)) + select(wide2[1], pair_matrix(d1, LANES // 2))) * 0.125
    half = narrow2.shape[0] // 2
    block = narrow2[pl.ds(0, half, 2)] + narrow2[pl.ds(1, half, 2)]
    payload[...] = jnp.broadcast_to(block[None], payload.shape)


def strips_kernel(
    place, residual, material, source1, material1, even, odd,
    inner, outer, long_r, long_m, long_s1, long_m1,
):
    low_x, low_y = place[0] == 1, place[1] == 1
    count, rows, depth = residual.shape
    pieces = depth // LANES
    c1 = source1.shape[0]

    def sides(at):
        a, b = even[at], odd[at]
        return jnp.where(low_y, a, b), jnp.where(low_y, b, a)

    for i in range(count):
        for piece in range(pieces):
            low, high = sides(i * pieces + piece)
            z = slice(piece * LANES, (piece + 1) * LANES)
            long_r[i, :, z] = jnp.concatenate([low[:4], residual[i, :, z], high[:4]], axis=0)
            long_m[i, :, z] = jnp.concatenate([low[4:], material[i, :, z], high[4:]], axis=0)
    for k in range(c1):
        low, high = sides(count * pieces + k)
        long_s1[k] = jnp.concatenate([low[:4], source1[k], high[:4]], axis=0)
        long_m1[k] = jnp.concatenate([low[4:], material1[k], high[4:]], axis=0)

    def pack(out, flag):
        at = 0
        for ref, planes in ((long_r, 3), (long_m, 4), (long_s1, 3), (long_m1, 4)):
            start = jnp.where(flag, 0, ref.shape[0] - planes)
            for n in range(planes):
                for tile in range(ref.shape[1] // 8):
                    for piece in range(ref.shape[2] // LANES):
                        out[at] = ref[start + n, tile * 8 : tile * 8 + 8, piece * LANES : (piece + 1) * LANES]
                        at += 1

    pack(inner, low_x)
    pack(outer, jnp.logical_not(low_x))


def unpack(source, flag, out, start, planes, tiles, pieces, at):
    for n in range(planes):
        for tile in range(tiles):
            for piece in range(pieces):
                value = jnp.where(flag, source[0][at], source[1][at])
                out[start + n, tile * 8 : tile * 8 + 8, piece * LANES : (piece + 1) * LANES] = value
                at += 1
    return at


def smooth_kernel(place, potential, long_r, long_m, inner, outer, out, mat, res, x, d, fx, fy, fz, inv):
    low_x = place[0] == 1
    count, rows, depth = potential.shape
    pieces, tiles = depth // LANES, long_r.shape[1] // 8
    both = (inner, outer)
    flags = (low_x, jnp.logical_not(low_x))
    n_r = 3 * tiles * pieces
    for flag, start_r, start_m in ((flags[0], 1, 0), (flags[1], count + 4, count + 4)):
        at = unpack(both, flag, res, start_r, 3, tiles, pieces, 0)
        unpack(both, flag, mat, start_m, 4, tiles, pieces, at)
    res[pl.ds(4, count)] = long_r[...]
    mat[pl.ds(4, count)] = long_m[...]
    total = count + 8
    length = rows + 8
    lane = iota((length, depth), 1)

    def weigh(i, previous):
        a, ahead = mat[i], mat[i + 1]
        f = harmonic(a, ahead, 1.0)
        fx[i + 1] = f
        down = lower(a, 0)
        back = jnp.where(lane == 0, 0.0, lower(a, 1))
        w_down, w_back = harmonic(a, down, 1.0), harmonic(a, back, 1.0)
        fy[i], fz[i] = w_down, w_back
        w_up, w_front = upper(w_down, 0), upper(w_back, 1)
        pairs = (
            (previous, mat[i - 1]), (f, ahead), (w_down, down), (w_up, upper(a, 0)), (w_back, back),
            (w_front, jnp.where(lane == depth - 1, 0.0, upper(a, 1))),
        )
        diagonal = sum(jnp.where(b > 0.0, w, a) for w, b in pairs)
        inverse = jnp.where(a > 0.0, invert(jnp.maximum(diagonal, 1e-3)), 0.0)
        inv[i] = inverse
        res[i] = inverse * res[i]
        start = res[i] * (1.0 / THETA)
        x[0, i] = start
        d[i] = start
        return f

    first = harmonic(mat[0], mat[1], 1.0)
    fx[1] = first
    lax.fori_loop(1, total - 1, weigh, first)
    rho = 1.0 / SIGMA
    for step in range(DEG - 1):
        ahead = 1.0 / (2.0 * SIGMA - rho)
        old, new = step % 2, (step + 1) % 2
        final = step == DEG - 2

        def sweep(i, _):
            v = x[old, i]
            w_down, w_back = fy[i], fz[i]
            off = fx[i] * x[old, i - 1] + fx[i + 1] * x[old, i + 1]
            off = off + w_down * lower(v, 0) + upper(w_down * v, 0)
            off = off + w_back * lower(v, 1) + upper(w_back * v, 1)
            change = ahead * rho * d[i] + (2.0 * ahead / DELTA) * (res[i] - v + inv[i] * off)
            if final:
                out[i - 4] = potential[i - 4] + (v + change)[4 : 4 + rows]
            else:
                d[i] = change
                x[new, i] = v + change
            return 0

        lax.fori_loop(2 + step, total - 2 - step, sweep, 0)
        rho = ahead


def chunk_of(count):
    return min(count, 8)


def tables_of(mat, table, scale, valid_rows, valid_lanes):
    count, rows = mat.shape[0] - 2, mat.shape[1]
    step = chunk_of(count)
    shape = (step, rows, LANES)
    row, lane = iota(shape, 1), iota(shape, 2)

    def body(n, _):
        at = n * step
        a, before, ahead = mat[pl.ds(at + 1, step)], mat[pl.ds(at, step)], mat[pl.ds(at + 2, step)]
        down = jnp.where(row == 0, 0.0, lower(a, 1))
        back = jnp.where(lane == 0, 0.0, lower(a, 2))
        up = jnp.where(row == rows - 1, 0.0, upper(a, 1))
        front = jnp.where(lane == LANES - 1, 0.0, upper(a, 2))
        w = [harmonic(a, b, scale) for b in (before, ahead, down, back)]
        w += [upper(w[2], 1), upper(w[3], 2)]
        diagonal = sum(jnp.where(b > 0.0, f, scale * a) for f, b in zip(w, (before, ahead, down, back, up, front)))
        table[0, pl.ds(at, step)] = w[0]
        table[1, pl.ds(at, step)] = w[2]
        table[2, pl.ds(at, step)] = w[3]
        table[3, pl.ds(at, step)] = jnp.where(a > 0.0, invert(jnp.maximum(diagonal, 1e-4)), 0.0)
        return 0

    lax.fori_loop(0, count // step, body, 0)
    table[0, count] = jnp.zeros((rows, LANES), F32)


def off_diagonal(e, table, at, step):
    v = e[pl.ds(at + 1, step)]
    total = table[0, pl.ds(at, step)] * e[pl.ds(at, step)] + table[0, pl.ds(at + 1, step)] * e[pl.ds(at + 2, step)]
    fy, fz = table[1, pl.ds(at, step)], table[2, pl.ds(at, step)]
    total = total + fy * lower(v, 1) + upper(fy * v, 1)
    return v, total + fz * lower(v, 2) + upper(fz * v, 2)


def each(count, body):
    step = chunk_of(count)

    def run(n, _):
        body(n * step, step)
        return 0

    lax.fori_loop(0, count // step, run, 0)


def halve(fine, out, first, temp, count, rows, rows_out):
    step = chunk_of(count // 2)
    padded = fine.shape[1]

    def add(at, step):
        a = fine[pl.ds(first + 2 * at, 2 * step)].reshape(step, 2, padded, LANES)
        sums = (a[:, 0] + a[:, 1]).reshape(step * padded, LANES)
        temp[pl.ds(pl.multiple_of(at * padded, 8), step * padded)] = select(sums, pair_matrix(LANES)) * 0.125

    each(count // 2, add)
    keep = rows // 2

    def fold(k, _):
        base = pl.multiple_of(k * padded, 8)
        value = temp[pl.ds(base, padded // 2, 2)] + temp[pl.ds(base + 1, padded // 2, 2)]
        out[k + 1, 0 : padded // 2, :] = value
        return 0

    lax.fori_loop(0, count // 2, fold, 0)


def widen(coarse, temp, out, count, rows):
    padded = coarse.shape[1]
    step = chunk_of(count)

    def lanes(at, step):
        values = coarse[pl.ds(at + 1, step)].reshape(step * padded, LANES)
        temp[pl.ds(pl.multiple_of(at * padded, 8), step * padded)] = select(values, spread_matrix(LANES))

    each(count, lanes)
    keep = out.shape[0] // count // 2

    def fold(k, _):
        value = temp[pl.ds(pl.multiple_of(k * padded, 8), keep)]
        base = pl.multiple_of(k * 2 * keep, 8)
        out[pl.ds(base, keep, 2)] = value
        out[pl.ds(base + 1, keep, 2)] = value
        return 0

    lax.fori_loop(0, count, fold, 0)


def cycle(s, e, tables, work, dims):
    for ref in e:
        zero = jnp.zeros(ref.shape[1:], F32)
        ref[0] = zero
        ref[ref.shape[0] - 1] = zero
    temp, spread, rest = work
    for level in range(2):
        count, rows, padded = dims[level]
        s_l, e_l, table, t = s[level], e[level], tables[level], rest[level]

        def start(at, step):
            e_l[pl.ds(at + 1, step)] = DAMPING * s_l[pl.ds(at + 1, step)] * table[3, pl.ds(at, step)]

        each(count, start)

        def remainder(at, step):
            _, off = off_diagonal(e_l, table, at, step)
            t[pl.ds(at, step)] = KEPT * s_l[pl.ds(at + 1, step)] + off

        each(count, remainder)
        halve(t, s[level + 1], 0, temp, count, rows, dims[level + 1][2])
    count, rows, padded = dims[2]
    s_l, e_l, table = s[2], e[2], tables[2]

    def start(at, step):
        e_l[pl.ds(at + 1, step)] = DAMPING * s_l[pl.ds(at + 1, step)] * table[3, pl.ds(at, step)]

    def relax(s_l, e_l, table, t, count):
        def sweep(at, step):
            v, off = off_diagonal(e_l, table, at, step)
            t[pl.ds(at, step)] = KEPT * v + DAMPING * table[3, pl.ds(at, step)] * (s_l[pl.ds(at + 1, step)] + off)

        def back(at, step):
            e_l[pl.ds(at + 1, step)] = t[pl.ds(at, step)]

        each(count, sweep)
        each(count, back)

    each(count, start)
    for _ in range(COARSE_SWEEPS - 1):
        relax(s_l, e_l, table, rest[2], count)
    for level in (1, 0):
        count, rows, padded = dims[level]
        s_l, e_l, table, t = s[level], e[level], tables[level], rest[level]
        up = spread[level]
        widen(e[level + 1], temp, up, dims[level + 1][0], dims[level + 1][1])

        def correct(at, step):
            more = up[pl.ds(pl.multiple_of(at * padded, 8), step * padded)].reshape(step, 1, padded, LANES)
            now = e_l[pl.ds(2 * at + 1, 2 * step)].reshape(step, 2, padded, LANES)
            e_l[pl.ds(2 * at + 1, 2 * step)] = (now + more).reshape(2 * step, padded, LANES)

        each(count // 2, correct)
        relax(s_l, e_l, table, t, count)


def window(e, place, out, c2, r2, pad):
    count, rows = e.shape[0] - 2, e.shape[1]
    pad[...] = jnp.zeros(pad.shape, F32)
    planes = c2 + 4
    for n in range(planes):
        at = place[2] * c2 + n - 2
        inside = (at >= 0) & (at < count)
        value = e[jnp.clip(at, 0, count - 1) + 1]
        pad[n, 8 : 8 + rows, :] = jnp.where(inside, value, 0.0)
    for n in range(planes):
        out[n] = pad[n, pl.ds(place[3] * r2 + 6, r2 + 4), :]


def level_shapes(count, rows, depth):
    return [(count // k, rows // k, max(rows // k, 8)) for k in (1, 2, 4)]


def work_shapes(dims):
    out = []
    for count, _, padded in dims:
        out.append(pltpu.VMEM((count + 2, padded, LANES), F32))
    for count, _, padded in dims:
        out.append(pltpu.VMEM((count + 2, padded, LANES), F32))
    for count, _, padded in dims:
        out.append(pltpu.VMEM((count + 2, padded, LANES), F32))
    out.append(pltpu.VMEM((dims[0][0] // 2 * dims[0][2], LANES), F32))
    for count, _, padded in dims[:2]:
        out.append(pltpu.VMEM((count // 2 * padded, LANES), F32))
    return out


def first_cycle_kernel(dims, grid, c2, r2, place, blocks, out, table2, table3, table4, *scratch):
    s, e, rest = scratch[0:3], scratch[3:6], scratch[6:9]
    temp, spread = scratch[9], scratch[10:12]
    mats, pad = scratch[12:15], scratch[15]
    face_y, face_x = e[0], rest[0]
    tables = (table2, table3, table4)
    gx, gy = grid
    count, rows, _ = dims[0]
    for ref in (*s, *mats, face_y, face_x):
        ref[...] = jnp.zeros(ref.shape, F32)
    lane = iota((c2 * r2, LANES), 1)
    half = LANES // 2

    def place_column(i, _):
        for j in range(gy):
            block = blocks[i * gy + j]
            turned = roll(block, half, 1)
            own = jnp.where(lane < half, block[: c2 * r2], 0.0)
            own_m = jnp.where(lane < half, turned[: c2 * r2], 0.0)
            x_faces = jnp.where(lane[: 2 * r2] < half, block[c2 * r2 :], 0.0)
            y_faces = jnp.where(lane[: 2 * c2] < half, turned[c2 * r2 :], 0.0)
            for k in range(c2):
                at = i * c2 + k + 1
                s[0][at, j * r2 : (j + 1) * r2, :] = own[k * r2 : (k + 1) * r2]
                mats[0][at, j * r2 : (j + 1) * r2, :] = own_m[k * r2 : (k + 1) * r2]
                if j > 0:
                    face_y[at, j * r2 - 1 : j * r2, :] = y_faces[k : k + 1]
                if j < gy - 1:
                    face_y[at, (j + 1) * r2 : (j + 1) * r2 + 1, :] = y_faces[c2 + k : c2 + k + 1]
            face_x[i * c2, j * r2 : (j + 1) * r2, :] = x_faces[:r2]
            face_x[(i + 1) * c2 + 1, j * r2 : (j + 1) * r2, :] = x_faces[r2:]
        return 0

    lax.fori_loop(0, gx, place_column, 0)

    def join(at, step):
        now = pl.ds(at + 1, step)
        s[0][now] = s[0][now] + face_x[now] + face_y[now]

    each(count, join)
    scale = 0.0625
    for level in range(3):
        if level:
            count, rows, padded = dims[level - 1]
            halve(mats[level - 1], mats[level], 1, temp, count, rows, dims[level][2])
        tables_of(mats[level], tables[level], scale, None, None)
        scale *= 0.25
    cycle(s, e, tables, (temp, spread, rest), dims)
    window(e[0], place, out, c2, r2, pad)


def shifted(a):
    zero = jnp.zeros_like(a[:1])
    return jnp.concatenate([zero, a[:-1]], axis=0), jnp.concatenate([a[1:], zero], axis=0)


def apply_off(e, fx, fy, fz):
    before, ahead = shifted(e)
    out = fx[:-1] * before + fx[1:] * ahead
    out = out + fy * lower(e, 1) + upper(fy * e, 1)
    return out + fz * lower(e, 2) + upper(fz * e, 2)


def raise_window(window_ref, flat, out):
    planes, rows, _ = window_ref.shape
    values = select(window_ref[...].reshape(planes * rows, LANES), spread_matrix(LANES))
    flat[pl.ds(0, planes * rows, 2)] = values
    flat[pl.ds(1, planes * rows, 2)] = values
    v = flat[...].reshape(planes, 1, 2 * rows, LANES)
    out[...] = jnp.broadcast_to(v, (planes, 2, 2 * rows, LANES)).reshape(2 * planes, 2 * rows, LANES)


def level1_kernel(
    offset, place, long_s1, long_m1, inner, outer, window1,
    payload, first, error2, source2, faces,
    src, mat, flat, prolonged, wide, narrow,
):
    low_x = place[0] == 1
    count, length, depth = long_s1.shape
    rows = length - 8
    both = (inner, outer)
    zero = jnp.zeros((length, depth), F32)
    src[0] = zero
    src[count + 7] = zero
    for flag, start_s, start_m in ((low_x, 1, 0), (jnp.logical_not(low_x), count + 4, count + 4)):
        at = unpack(both, flag, src, start_s, 3, length // 8, 1, offset)
        unpack(both, flag, mat, start_m, 4, length // 8, 1, at)
    src[pl.ds(4, count)] = long_s1[...]
    mat[pl.ds(4, count)] = long_m1[...]
    raise_window(window1, flat, prolonged)
    a = mat[...]
    lane = iota(a.shape, 2)
    before, ahead = shifted(a)
    down, up = lower(a, 1), upper(a, 1)
    back = jnp.where(lane == 0, 0.0, lower(a, 2))
    front = jnp.where(lane == depth - 1, 0.0, upper(a, 2))
    w_x, w_y, w_z = (harmonic(a, b, 0.25) for b in (before, down, back))
    _, w_ahead = shifted(w_x)
    pairs = ((w_x, before), (w_ahead, ahead), (w_y, down), (upper(w_y, 1), up), (w_z, back), (upper(w_z, 2), front))
    diagonal = sum(jnp.where(b > 0.0, w, 0.25 * a) for w, b in pairs)
    inverse = jnp.where(a > 0.0, invert(jnp.maximum(diagonal, 1e-4)), 0.0)
    w_x = jnp.concatenate([w_x, zero[None]], axis=0)
    faces[0] = w_x[:-1]
    faces[1] = w_y
    faces[2] = w_z
    faces[3] = inverse
    s = src[...]
    e = DAMPING * inverse * s + prolonged[...]
    c = KEPT * e + DAMPING * inverse * (s + apply_off(e, w_x, w_y, w_z))
    s2 = s - diagonal * c + apply_off(c, w_x, w_y, w_z)
    e2 = DAMPING * inverse * s2
    t = KEPT * s2 + apply_off(e2, w_x, w_y, w_z)
    first[...] = c
    error2[...] = e2
    source2[...] = s2
    wide[...] = t[4 : 4 + count, 4 : 4 + rows].reshape(count // 2, 2, rows, depth).sum(axis=1).reshape(count // 2 * rows, depth)
    part = count // 4 * rows
    narrow[...] = (select(wide[:part], pair_matrix(depth)) + select(wide[part:], pair_matrix(depth, LANES // 2))) * 0.125
    block = narrow[pl.ds(0, part // 2, 2)] + narrow[pl.ds(1, part // 2, 2)]
    payload[...] = jnp.broadcast_to(block[None], payload.shape)


def last_cycle_kernel(
    dims, grid, c2, r2, place, blocks, table2, table3, table4, first, error2, source2, faces, partial,
    out, *scratch,
):
    s, e, rest = scratch[0:3], scratch[3:6], scratch[6:9]
    temp, spread = scratch[9], scratch[10:12]
    pad, view, flat, prolonged, tall = scratch[12:17]
    gx, gy = grid
    for ref in s:
        ref[...] = jnp.zeros(ref.shape, F32)
    half = LANES // 2
    lane = iota((c2 // 2 * r2, LANES), 1)

    def place_column(i, _):
        for j in range(gy):
            block = blocks[i * gy + j]
            turned = roll(block, half, 1)
            parts = (jnp.where(lane < half, block, 0.0), jnp.where(lane < half, turned, 0.0))
            for k in range(c2):
                n = k % (c2 // 2)
                s[0][i * c2 + k + 1, j * r2 : (j + 1) * r2, :] = parts[k // (c2 // 2)][n * r2 : (n + 1) * r2]
        return 0

    lax.fori_loop(0, gx, place_column, 0)
    cycle(s, e, (table2, table3, table4), (temp, spread, rest), dims)
    window(e[0], place, view, c2, r2, pad)
    raise_window(view, flat, prolonged)
    count, rows, depth = partial.shape
    c1, r1 = count // 2, rows // 2
    ext = first.shape[0]
    w_x = jnp.concatenate([faces[0], jnp.zeros_like(faces[0, :1])], axis=0)
    v = error2[...] + prolonged[...]
    v = KEPT * v + DAMPING * faces[3] * (source2[...] + apply_off(v, w_x, faces[1], faces[2]))
    coarse = (first[...] + v)[4 : 4 + c1, 4 : 4 + r1].reshape(c1 * r1, LANES)
    values = select(coarse, spread_matrix(depth))
    for piece in range(depth // LANES):
        z = slice(piece * LANES, (piece + 1) * LANES)
        tall[piece, pl.ds(0, c1 * r1, 2)] = values[:, z]
        tall[piece, pl.ds(1, c1 * r1, 2)] = values[:, z]
        v = tall[piece].reshape(c1, 1, rows, LANES)
        v = jnp.broadcast_to(v, (c1, 2, rows, LANES)).reshape(count, rows, LANES)
        out[:, :, z] = partial[:, :, z] + v


def size_of(shape):
    lead = math.prod(shape[:-2])
    return 4 * lead * (-(-shape[-2] // 8) * 8) * (-(-shape[-1] // LANES) * LANES)


def call(kernel, name, inputs, outputs, scratch=()):
    streamed = 0

    def held(x):
        nonlocal streamed
        if x.ndim == 1:
            return x
        if size_of(x.shape) <= HELD:
            return pltpu.with_memory_space_constraint(x, pltpu.VMEM)
        streamed += size_of(x.shape)
        return x

    def result(shape):
        nonlocal streamed
        if size_of(shape) <= HELD:
            return pltpu.VMEM(shape, F32)
        streamed += size_of(shape)
        return jax.ShapeDtypeStruct(shape, F32)

    inputs = [held(x) for x in inputs]
    results = [result(shape) for shape in outputs]
    need = streamed + sum(size_of(x.shape) for x in scratch) + 6 * MIB
    return pl.pallas_call(
        kernel,
        out_shape=results,
        in_specs=[pl.BlockSpec(memory_space=pltpu.SMEM if x.ndim == 1 else pltpu.VMEM) for x in inputs],
        out_specs=[pl.BlockSpec(memory_space=pltpu.VMEM) for _ in outputs],
        scratch_shapes=list(scratch),
        compiler_params=pltpu.CompilerParams(vmem_limit_bytes=max(need, 16 * MIB)),
        name=name,
    )(*inputs)


def swaps(count):
    inner = [(i, i + 1) for i in range(0, count - 1, 2)]
    outer = [(i, i + 1) for i in range(1, count - 1, 2)]
    return [pairs + [(b, a) for a, b in pairs] for pairs in (inner, outer)]


def local(right_side, potential, phase, permeability):
    gx, gy = lax.axis_size("gx"), lax.axis_size("gy")
    devices = gx * gy
    here_x, here_y = lax.axis_index("gx"), lax.axis_index("gy")
    place = jnp.stack([here_x % 2, here_y % 2, here_x, here_y]).astype(jnp.int32)
    count, rows, depth = right_side.shape
    c1, r1, d1 = count // 2, rows // 2, depth // 2
    c2, r2 = c1 // 2, r1 // 2
    pieces = depth // LANES
    swap_x, swap_y = swaps(gx), swaps(gy)
    VM = lambda *shape: pltpu.VMEM(shape, F32)

    brick = (count, rows, depth)
    face = (3, rows, depth)
    material, inner, outer, even, odd = call(
        faces_kernel, "faces", (place, permeability, potential, phase), (brick, face, face, (3, count, depth), (3, count, depth))
    )
    even = lax.ppermute(even, "gy", swap_y[0])
    odd = lax.ppermute(odd, "gy", swap_y[1])
    outer = lax.ppermute(outer, "gx", swap_x[1])
    inner = lax.ppermute(inner, "gx", swap_x[0])

    strip = (count * pieces + c1, 8, LANES)
    block = (devices, c2 * r2 + 2 * r2, LANES)
    total = 2 * c1 * rows + 4 * rows
    small = c2 * r1 + 2 * r1
    residual, payload, source1, material1, even, odd = call(
        residual_kernel, "residual",
        (place, right_side, potential, material, inner, outer, even, odd),
        (brick, block, (c1, r1, d1), (c1, r1, d1), strip, strip),
        (
            VM(count + 2, rows, depth), VM(count + 2, rows, depth), VM(total, depth), VM(total, LANES), VM(total // 2, LANES),
            VM(2, small, d1), VM(small, LANES),
        ),
    )
    blocks = lax.all_to_all(payload, ("gx", "gy"), 0, 0)
    even = lax.ppermute(even, "gy", swap_y[0])
    odd = lax.ppermute(odd, "gy", swap_y[1])
    tiles, tiles1 = (rows + 8) // 8, (r1 + 8) // 8
    strip = (7 * tiles * pieces + 7 * tiles1, 8, LANES)
    long, long1 = (count, rows + 8, depth), (c1, r1 + 8, d1)
    inner, outer, long_r, long_m, long_s1, long_m1 = call(
        strips_kernel, "strips",
        (place, residual, material, source1, material1, even, odd),
        (strip, strip, long, long, long1, long1),
    )
    outer = lax.ppermute(outer, "gx", swap_x[1])
    inner = lax.ppermute(inner, "gx", swap_x[0])

    dims = level_shapes(gx * c2, gy * r2, d1 // 2)
    work = work_shapes(dims)
    view = (c2 + 4, r2 + 4, LANES)
    pad = VM(c2 + 4, dims[0][2] + 16, LANES)
    mats = [VM(n + 2, padded, LANES) for n, _, padded in dims]
    table_shapes = [(4, n + 1, padded, LANES) for n, _, padded in dims]
    window1, table2, table3, table4 = call(
        functools.partial(first_cycle_kernel, dims, (gx, gy), c2, r2), "cycle1",
        (place, blocks), (view, *table_shapes), (*work, *mats, pad),
    )
    frame = (c1 + 8, r1 + 8, d1)
    flat = VM((c2 + 4) * (r2 + 4) * 2, LANES)
    payload, first, error2, source2, faces = call(
        functools.partial(level1_kernel, 7 * tiles * pieces), "level1",
        (place, long_s1, long_m1, inner, outer, window1),
        ((devices, c2 // 2 * r2, LANES), frame, frame, frame, (4, *frame)),
        (VM(*frame), VM(*frame), flat, VM(*frame), VM(c1 // 2 * r1, d1), VM(c1 // 4 * r1, LANES)),
    )
    blocks = lax.all_to_all(payload, ("gx", "gy"), 0, 0)
    wide = (count + 8, rows + 8, depth)
    (partial,) = call(
        smooth_kernel, "smooth", (place, potential, long_r, long_m, inner, outer), (brick,),
        (
            VM(*wide), VM(*wide), VM(2, *wide), VM(*wide), VM(count + 9, rows + 8, depth), VM(*wide), VM(*wide), VM(*wide),
        ),
    )
    (out,) = call(
        functools.partial(last_cycle_kernel, dims, (gx, gy), c2, r2), "cycle2",
        (place, blocks, table2, table3, table4, first, error2, source2, faces, partial), (brick,),
        (*work, pad, VM(*view), flat, VM(*frame), VM(pieces, count // 2 * rows, LANES)),
    )
    return out


def solution(mesh):
    placed = (P("gx", "gy", None), P("gx", "gy", None), P("gx", "gy", None), P())
    return jax.shard_map(local, mesh=mesh, in_specs=placed, out_specs=P("gx", "gy", None), check_vma=False)
```

time: 487 us -> 80.5 us (0.17)
  the two profiles are of different devices: /device:TPU:28 before, /device:TPU:0 now
where the time goes in v1:
time: 80.5 us; the launch traced here: 79.9 us
  Pallas kernels  26.8 us (33%)
  starting transfers between devices  25.9 us (32%)
  local copies, waits for them, and re-layouts  15.3 us (19%)
  waiting for transfers between devices  11.6 us (14%)
    pallas_call x7, Pallas kernels, call(): pl.pallas_call(kernel, out_shape=results, in_specs=[pl.BlockSpec(memory_s...  26.8 us
    all_to_all x2, starting transfers between devices, local(): blocks = lax.all_to_all(payload, ('gx', 'gy'), 0, 0)  18.3 us
    unnamed x41, local copies, waits for them, and re-layouts  15.3 us
    ppermute x2, waiting for transfers between devices, local(): even = lax.ppermute(even, 'gy', swap_y[0])  11.6 us
    ppermute x2, starting transfers between devices, local(): even = lax.ppermute(even, 'gy', swap_y[0])  4.5 us
  transfers between devices with their start and end apart: 10, of which 2 were waited for; matrix products, arithmetic and copies ran while one was open for 0% of the time, Pallas kernels for 21%

profile of v1, /device:TPU:0, one launch (start us, length us, event | category | flops | bytes accessed | tf_op | source)
XLA Modules:
  0.0 79.9 jit_solution(8401226922229781780)
XLA Ops:
  0.1 0.9 %copy-done = f32[16,16,256]{2,1,0:T(8,128)S(1)} copy-done((f32[16,16,256]{2,1,0:T(8,128)S(1)}, f32[16,16,256]{2,1,0:T(8,128)}, u32[]{:S(2)}) %copy-start) | copy-done | bytes 262168
  1.0 0.9 %copy-done.6 = s32[16,16,256]{2,1,0:T(8,128)S(1)} copy-done((s32[16,16,256]{2,1,0:T(8,128)S(1)}, s32[16,16,256]{2,1,0:T(8,128)}, u32[]{:S(2)}) %copy-start.6) | copy-done | bytes 262168
  2.0 0.7 copy-done.19
  3.8 0.7 collective-permute-start.1
  4.5 2.7 %collective-permute-start.2 = (f32[3,16,256]{2,1,0:T(8,128)S(1)}, f32[3,16,256]{2,1,0:T(8,128)S(1)}, u32[]{:S(2)}, u32[]{:S(2)}) collective-permute-start(f32[3,16,256]{2,1,0:T(8,128)S(1)} %get-tuple-element.34), channel_id=1, source_target_pairs={{0,1},{2,3},{1,0},{3,2},{4,5},{6,7},{5,4},{7,6},{8,9},{10,11},{9,8... | collective-permute-start | bytes 147464 | tf_op jit(solution)/shard_map/ppermute | solution.py:720
  7.1 0.7 collective-permute-start.3
  7.8 1.4 %collective-permute-done.2.even = f32[3,16,256]{2,1,0:T(8,128)S(1)} collective-permute-done((f32[3,16,256]{2,1,0:T(8,128)S(1)}, f32[3,16,256]{2,1,0:T(8,128)S(1)}, u32[]{:S(2)}, u32[]{:S(2)}) %collective-permute-start.2) | collective-permute-done | bytes 49184 | tf_op jit(solution)/shard_map/ppermute | solution.py:720
  9.2 0.9 %copy-done.1 = f32[16,16,256]{2,1,0:T(8,128)S(1)} copy-done((f32[16,16,256]{2,1,0:T(8,128)S(1)}, f32[16,16,256]{2,1,0:T(8,128)}, u32[]{:S(2)}) %copy-start.1) | copy-done | bytes 262168
  10.2 0.9 %copy-done.5 = f32[16,16,256]{2,1,0:T(8,128)S(1)} copy-done((f32[16,16,256]{2,1,0:T(8,128)S(1)}, f32[16,16,256]{2,1,0:T(8,128)}, u32[]{:S(2)}) %copy-start.5) | copy-done | bytes 262168
  11.1 3.1 %residual.1 = (f32[16,16,256]{2,1,0:T(8,128)S(1)}, f32[32,24,128]{2,1,0:T(8,128)}, f32[8,8,128]{2,1,0:T(8,128)S(1)}, f32[8,8,128]{2,1,0:T(8,128)S(1)}, f32[40,8,...) custom-call(s32[4]{0:T(128)S(1)} %pad_add_fusion.place, f32[16,16,256]{2,1,0:T(8,128)S(1)} %copy-done.5, ...), custom_call_target="tpu_custom_call" | custom-call | tf_op jit(solution)/shard_map/residual/pallas_call | solution.py:686
  14.2 10.6 %all-to-all-start = ((f32[32,24,128]{2,1,0:T(8,128)}), f32[32,24,128]{2,1,0:T(8,128)S(1)}, u32[]{:S(2)}, u32[]{:S(2)}) async-start(f32[32,24,128]{2,1,0:T(8,128)} %get-tuple-element.45), calls=%async_computation | async-start | bytes 786432 | tf_op jit(solution)/shard_map/all_to_all | solution.py:738
  24.8 1.8 %collective-permute-start.4 = (f32[40,8,128]{2,1,0:T(8,128)S(1)}, f32[40,8,128]{2,1,0:T(8,128)S(1)}, u32[]{:S(2)}, u32[]{:S(2)}) collective-permute-start(f32[40,8,128]{2,1,0:T(8,128)S(1)} %get-tuple-element.39), channel_id=1, source_target_pairs={{0,1},{2,3},{1,0},{3,2},{4,5},{6,7},{5,4},{7,6},{8,9},{10,11},{9,8... | collective-permute-start | bytes 491528 | tf_op jit(solution)/shard_map/ppermute | solution.py:739
  26.6 0.7 collective-permute-start.5
  27.3 10.2 %collective-permute-done.4.even = f32[40,8,128]{2,1,0:T(8,128)S(1)} collective-permute-done((f32[40,8,128]{2,1,0:T(8,128)S(1)}, f32[40,8,128]{2,1,0:T(8,128)S(1)}, u32[]{:S(2)}, u32[]{:S(2)}) %collective-permute-start.4) | collective-permute-done | bytes 163872 | tf_op jit(solution)/shard_map/ppermute | solution.py:739
  37.5 1.4 %strips.1 = (f32[56,8,128]{2,1,0:T(8,128)}, f32[56,8,128]{2,1,0:T(8,128)S(1)}, f32[16,24,256]{2,1,0:T(8,128)S(1)}, f32[16,24,256]{2,1,0:T(8,128)S(1)}, f32[8,16,...) custom-call(s32[4]{0:T(128)S(1)} %pad_add_fusion.place, f32[16,16,256]{2,1,0:T(8,128)S(1)} %get-tuple-element.36.residual, ...), custom_call_target="tpu_custom_call" | custom-call | tf_op jit(solution)/shard_map/strips/pallas_call | solution.py:686
  40.1 0.7 collective-permute-start.7
  40.8 6.0 %cycle1.1 = (f32[8,8,128]{2,1,0:T(8,128)S(1)}, f32[4,33,16,128]{3,2,1,0:T(8,128)S(1)}, f32[4,17,8,128]{3,2,1,0:T(8,128)S(1)}, f32[4,9,8,128]{3,2,1,0:T(8,128)S(1)}) custom-call(s32[4]{0:T(128)S(1)} %pad_add_fusion.place, f32[32,24,128]{2,1,0:T(8,128)S(1)} %all-to-all-done.blocks), custom_call_target="tpu_custom_call" | custom-call | tf_op jit(solution)/shard_map/cycle1/pallas_call | solution.py:686
  46.8 0.7 copy-done.3
  47.5 0.7 copy-done.7
  48.2 0.8 %copy-done.16 = f32[8,16,128]{2,1,0:T(8,128)S(1)} copy-done((f32[8,16,128]{2,1,0:T(8,128)S(1)}, f32[8,16,128]{2,1,0:T(8,128)}, u32[]{:S(2)}) %copy-start.16) | copy-done | bytes 65560
  49.0 0.8 %copy-done.18 = f32[8,16,128]{2,1,0:T(8,128)S(1)} copy-done((f32[8,16,128]{2,1,0:T(8,128)S(1)}, f32[8,16,128]{2,1,0:T(8,128)}, u32[]{:S(2)}) %copy-start.18) | copy-done | bytes 65560
  49.9 1.9 %level1.1 = (f32[32,8,128]{2,1,0:T(8,128)}, f32[16,16,128]{2,1,0:T(8,128)S(1)}, f32[16,16,128]{2,1,0:T(8,128)S(1)}, f32[16,16,128]{2,1,0:T(8,128)S(1)}, f32[4,16,16,128]{3,2,1,0:T(8,128)S(1)}) custom-call(s32[4]{0:T(128)S(1)} %pad_add_fusion.place, f32[8,16,128]{2,1,0:T(8,128)S(1)} %copy-done.16, f32[8,16,128]{2,1,0:T(8,128)S(1)} %copy-done.18, ...), custom_call_target="tpu_custom_call" | custom-call | tf_op jit(solution)/shard_map/level1/pallas_call | solution.py:686
  52.4 0.7 copy-done.11
  53.1 7.7 %all-to-all-start.1 = ((f32[32,8,128]{2,1,0:T(8,128)}), f32[32,8,128]{2,1,0:T(8,128)S(1)}, u32[]{:S(2)}, u32[]{:S(2)}) async-start(f32[32,8,128]{2,1,0:T(8,128)} %get-tuple-element.47), calls=%async_computation.1 | async-start | bytes 262144 | tf_op jit(solution)/shard_map/all_to_all | solution.py:770
  60.8 9.4 %smooth.1.partial = f32[16,16,256]{2,1,0:T(8,128)S(1)} custom-call(s32[4]{0:T(128)S(1)} %pad_add_fusion.place, f32[16,16,256]{2,1,0:T(8,128)S(1)} %copy-done.2, f32[16,24,256]{2,1,0:T(8,128)S(1)} %get-tuple-element.55.long_r, f32[16,24,256]{2,1,0:T(8,128)S(1)} %get-tuple-element.56.long_m, f32[56,8,128]{2,1,0:T(8,128)S(1)} %collective-permute-done.6.inner, ...), custom_call_target="tpu_custom_call" | custom-call | tf_op jit(solution)/shard_map/smooth/pallas_call | solution.py:686
  70.2 0.9 %copy-done.4 = f32[4,17,8,128]{3,2,1,0:T(8,128)S(1)} copy-done((f32[4,17,8,128]{3,2,1,0:T(8,128)S(1)}, f32[4,17,8,128]{3,2,1,0:T(8,128)}, u32[]{:S(2)}) %copy-start.4) | copy-done | bytes 278552
  71.2 0.9 %copy-done.8 = f32[4,9,8,128]{3,2,1,0:T(8,128)S(1)} copy-done((f32[4,9,8,128]{3,2,1,0:T(8,128)S(1)}, f32[4,9,8,128]{3,2,1,0:T(8,128)}, u32[]{:S(2)}) %copy-start.8) | copy-done | bytes 147480
  72.1 0.9 %copy-done.10 = f32[16,16,128]{2,1,0:T(8,128)S(1)} copy-done((f32[16,16,128]{2,1,0:T(8,128)S(1)}, f32[16,16,128]{2,1,0:T(8,128)}, u32[]{:S(2)}) %copy-start.10) | copy-done | bytes 131096
  73.0 0.9 %copy-done.12 = f32[16,16,128]{2,1,0:T(8,128)S(1)} copy-done((f32[16,16,128]{2,1,0:T(8,128)S(1)}, f32[16,16,128]{2,1,0:T(8,128)}, u32[]{:S(2)}) %copy-start.12) | copy-done | bytes 131096
  73.9 0.9 %copy-done.14 = f32[16,16,128]{2,1,0:T(8,128)S(1)} copy-done((f32[16,16,128]{2,1,0:T(8,128)S(1)}, f32[16,16,128]{2,1,0:T(8,128)}, u32[]{:S(2)}) %copy-start.14) | copy-done | bytes 131096
  74.8 4.4 %cycle2.1 = f32[16,16,256]{2,1,0:T(8,128)S(1)} custom-call(s32[4]{0:T(128)S(1)} %pad_add_fusion.place, f32[32,8,128]{2,1,0:T(8,128)S(1)} %all-to-all-done.1.blocks, f32[4,33,16,128]{3,2,1,0:T(8,128)S(1)} %get-tuple-element.48.table2, f32[4,17,8,128]{3,2,1,0:T(8,128)S(1)} %copy-done.4, f32[4,9,8,128]{3,2,1,0:T(8,128)S(1)} %copy-done.8, ...), custom_call_target="tpu_custom_call" | custom-call | tf_op jit(solution)/shard_map/cycle2/pallas_call | solution.py:686
  79.2 0.7 copy.5
  (37 shorter events, 3.2 us)
Async XLA Ops:
  0.1 1.0 %copy-start = (f32[16,16,256]{2,1,0:T(8,128)S(1)}, f32[16,16,256]{2,1,0:T(8,128)}, u32[]{:S(2)}) copy-start(f32[16,16,256]{2,1,0:T(8,128)} %potential.5) | copy-start | bytes 786436
  1.0 0.9 %copy-start.6 = (s32[16,16,256]{2,1,0:T(8,128)S(1)}, s32[16,16,256]{2,1,0:T(8,128)}, u32[]{:S(2)}) copy-start(s32[16,16,256]{2,1,0:T(8,128)} %phase.1) | copy-start | bytes 786436
  2.0 0.7 copy-start.19
  3.3 4.5 %collective-permute-start = (f32[3,16,256]{2,1,0:T(8,128)S(1)}, f32[3,16,256]{2,1,0:T(8,128)S(1)}, u32[]{:S(2)}, u32[]{:S(2)}) collective-permute-start(f32[3,16,256]{2,1,0:T(8,128)S(1)} %get-tuple-element.32), channel_id=1, source_target_pairs={{0,4},{8,12},{16,20},{24,28},{4,0},{12,8},{20,16},{28,24},{1,5},{9... | collective-permute-start | bytes 147464 | tf_op jit(solution)/shard_map/ppermute | solution.py:723
  3.8 4.0 %collective-permute-start.1 = (f32[3,16,256]{2,1,0:T(8,128)S(1)}, f32[3,16,256]{2,1,0:T(8,128)S(1)}, u32[]{:S(2)}, u32[]{:S(2)}) collective-permute-start(f32[3,16,256]{2,1,0:T(8,128)S(1)} %get-tuple-element.33), channel_id=1, source_target_pairs={{4,8},{12,16},{20,24},{8,4},{16,12},{24,20},{5,9},{13,17},{21,25},... | collective-permute-start | bytes 147464 | tf_op jit(solution)/shard_map/ppermute | solution.py:722
  4.5 4.7 %collective-permute-start.2 = (f32[3,16,256]{2,1,0:T(8,128)S(1)}, f32[3,16,256]{2,1,0:T(8,128)S(1)}, u32[]{:S(2)}, u32[]{:S(2)}) collective-permute-start(f32[3,16,256]{2,1,0:T(8,128)S(1)} %get-tuple-element.34), channel_id=1, source_target_pairs={{0,1},{2,3},{1,0},{3,2},{4,5},{6,7},{5,4},{7,6},{8,9},{10,11},{9,8... | collective-permute-start | bytes 147464 | tf_op jit(solution)/shard_map/ppermute | solution.py:720
  7.1 2.1 %collective-permute-start.3 = (f32[3,16,256]{2,1,0:T(8,128)S(1)}, f32[3,16,256]{2,1,0:T(8,128)S(1)}, u32[]{:S(2)}, u32[]{:S(2)}) collective-permute-start(f32[3,16,256]{2,1,0:T(8,128)S(1)} %get-tuple-element.35), channel_id=1, source_target_pairs={{1,2},{2,1},{5,6},{6,5},{9,10},{10,9},{13,14},{14,13},{17,18},{18,... | collective-permute-start | bytes 147464 | tf_op jit(solution)/shard_map/ppermute | solution.py:721
  9.2 1.0 %copy-start.1 = (f32[16,16,256]{2,1,0:T(8,128)S(1)}, f32[16,16,256]{2,1,0:T(8,128)}, u32[]{:S(2)}) copy-start(f32[16,16,256]{2,1,0:T(8,128)} %potential.5) | copy-start | bytes 786436
  10.2 0.9 %copy-start.5 = (f32[16,16,256]{2,1,0:T(8,128)S(1)}, f32[16,16,256]{2,1,0:T(8,128)}, u32[]{:S(2)}) copy-start(f32[16,16,256]{2,1,0:T(8,128)} %source.1) | copy-start | bytes 786436
  14.2 26.6 %all-to-all-start = ((f32[32,24,128]{2,1,0:T(8,128)}), f32[32,24,128]{2,1,0:T(8,128)S(1)}, u32[]{:S(2)}, u32[]{:S(2)}) async-start(f32[32,24,128]{2,1,0:T(8,128)} %get-tuple-element.45), calls=%async_computation | async-start | bytes 786432 | tf_op jit(solution)/shard_map/all_to_all | solution.py:738
  24.8 12.7 %collective-permute-start.4 = (f32[40,8,128]{2,1,0:T(8,128)S(1)}, f32[40,8,128]{2,1,0:T(8,128)S(1)}, u32[]{:S(2)}, u32[]{:S(2)}) collective-permute-start(f32[40,8,128]{2,1,0:T(8,128)S(1)} %get-tuple-element.39), channel_id=1, source_target_pairs={{0,1},{2,3},{1,0},{3,2},{4,5},{6,7},{5,4},{7,6},{8,9},{10,11},{9,8... | collective-permute-start | bytes 491528 | tf_op jit(solution)/shard_map/ppermute | solution.py:739
  26.6 10.9 %collective-permute-start.5 = (f32[40,8,128]{2,1,0:T(8,128)S(1)}, f32[40,8,128]{2,1,0:T(8,128)S(1)}, u32[]{:S(2)}, u32[]{:S(2)}) collective-permute-start(f32[40,8,128]{2,1,0:T(8,128)S(1)} %get-tuple-element.40), channel_id=1, source_target_pairs={{1,2},{2,1},{5,6},{6,5},{9,10},{10,9},{13,14},{14,13},{17,18},{18,... | collective-permute-start | bytes 491528 | tf_op jit(solution)/shard_map/ppermute | solution.py:740
  37.5 23.3 %copy-start.2 = (f32[16,16,256]{2,1,0:T(8,128)S(1)}, f32[16,16,256]{2,1,0:T(8,128)}, u32[]{:S(2)}) copy-start(f32[16,16,256]{2,1,0:T(8,128)} %potential.5) | copy-start | bytes 786436
  38.8 0.6 copy-start.15
  39.5 0.6 copy-start.17
  40.1 8.1 %collective-permute-start.6 = (f32[56,8,128]{2,1,0:T(8,128)}, f32[56,8,128]{2,1,0:T(8,128)S(1)}, u32[]{:S(2)}, u32[]{:S(2)}) collective-permute-start(f32[56,8,128]{2,1,0:T(8,128)} %get-tuple-element.43), channel_id=1, source_target_pairs={{0,4},{8,12},{16,20},{24,28},{4,0},{12,8},{20,16},{28,24},{1,5},{9... | collective-permute-start | bytes 688136 | tf_op jit(solution)/shard_map/ppermute | solution.py:750
  40.1 8.1 %collective-permute-start.7 = (f32[56,8,128]{2,1,0:T(8,128)S(1)}, f32[56,8,128]{2,1,0:T(8,128)S(1)}, u32[]{:S(2)}, u32[]{:S(2)}) collective-permute-start(f32[56,8,128]{2,1,0:T(8,128)S(1)} %get-tuple-element.44), channel_id=1, source_target_pairs={{4,8},{12,16},{20,24},{8,4},{16,12},{24,20},{5,9},{13,17},{21,25},... | collective-permute-start | bytes 688136 | tf_op jit(solution)/shard_map/ppermute | solution.py:749
  46.8 0.7 copy-start.3
  47.5 0.7 copy-start.7
  48.2 0.8 %copy-start.16 = (f32[8,16,128]{2,1,0:T(8,128)S(1)}, f32[8,16,128]{2,1,0:T(8,128)}, u32[]{:S(2)}) copy-start(f32[8,16,128]{2,1,0:T(8,128)} %copy-done.15) | copy-start | bytes 196612
  49.0 0.8 %copy-start.18 = (f32[8,16,128]{2,1,0:T(8,128)S(1)}, f32[8,16,128]{2,1,0:T(8,128)}, u32[]{:S(2)}) copy-start(f32[8,16,128]{2,1,0:T(8,128)} %copy-done.17) | copy-start | bytes 196612
  51.8 0.6 copy-start.9
  52.4 0.7 copy-start.11
  53.1 7.7 %copy-start.13 = (f32[16,16,128]{2,1,0:T(8,128)}, f32[16,16,128]{2,1,0:T(8,128)S(1)}, u32[]{:S(2)}) copy-start(f32[16,16,128]{2,1,0:T(8,128)S(1)} %get-tuple-element.53.source2) | copy-start | bytes 393220
  53.1 17.1 %all-to-all-start.1 = ((f32[32,8,128]{2,1,0:T(8,128)}), f32[32,8,128]{2,1,0:T(8,128)S(1)}, u32[]{:S(2)}, u32[]{:S(2)}) async-start(f32[32,8,128]{2,1,0:T(8,128)} %get-tuple-element.47), calls=%async_computation.1 | async-start | bytes 262144 | tf_op jit(solution)/shard_map/all_to_all | solution.py:770
  70.2 1.0 %copy-start.4 = (f32[4,17,8,128]{3,2,1,0:T(8,128)S(1)}, f32[4,17,8,128]{3,2,1,0:T(8,128)}, u32[]{:S(2)}) copy-start(f32[4,17,8,128]{3,2,1,0:T(8,128)} %copy-done.3) | copy-start | bytes 835588
  71.1 0.9 %copy-start.8 = (f32[4,9,8,128]{3,2,1,0:T(8,128)S(1)}, f32[4,9,8,128]{3,2,1,0:T(8,128)}, u32[]{:S(2)}) copy-start(f32[4,9,8,128]{3,2,1,0:T(8,128)} %copy-done.7) | copy-start | bytes 442372
  72.1 0.9 %copy-start.10 = (f32[16,16,128]{2,1,0:T(8,128)S(1)}, f32[16,16,128]{2,1,0:T(8,128)}, u32[]{:S(2)}) copy-start(f32[16,16,128]{2,1,0:T(8,128)} %copy-done.9) | copy-start | bytes 393220
  73.0 0.9 %copy-start.12 = (f32[16,16,128]{2,1,0:T(8,128)S(1)}, f32[16,16,128]{2,1,0:T(8,128)}, u32[]{:S(2)}) copy-start(f32[16,16,128]{2,1,0:T(8,128)} %copy-done.11) | copy-start | bytes 393220
  73.9 0.9 %copy-start.14 = (f32[16,16,128]{2,1,0:T(8,128)S(1)}, f32[16,16,128]{2,1,0:T(8,128)}, u32[]{:S(2)}) copy-start(f32[16,16,128]{2,1,0:T(8,128)} %copy-done.13) | copy-start | bytes 393220

commit v2 on v0

v2 whole, which is shorter than its diff:
```python
import functools
import math

import jax
import jax.numpy as jnp
from jax import lax
from jax.experimental import pallas as pl
from jax.experimental.pallas import tpu as pltpu
from jax.sharding import PartitionSpec as P

DEG = 4
COARSE_SWEEPS = 4
THETA = 1.15
DELTA = 0.85
SIGMA = 1.15 / 0.85
DAMPING = 0.6
KEPT = 1.0 - DAMPING
F32 = jnp.float32
LANES = 128
MIB = 1024 * 1024
HELD = 4 * MIB


def iota(shape, axis):
    return lax.broadcasted_iota(jnp.int32, shape, axis)


def invert(x):
    guess = pl.reciprocal(x, approx=True)
    return guess * (2.0 - x * guess)


def harmonic(a, b, scale):
    return (2.0 * scale) * a * b * invert(jnp.maximum(a + b, 1e-3))


def pair_matrix(size, offset=0):
    column = iota((size, LANES), 1)
    return ((column >= offset) & (iota((size, LANES), 0) // 2 == column - offset)).astype(jnp.bfloat16)


def spread_matrix(width):
    return (iota((LANES, width), 1) // 2 == iota((LANES, width), 0)).astype(jnp.bfloat16)


def select(values, matrix):
    high = values.astype(jnp.bfloat16)
    rest = (values - high.astype(F32)).astype(jnp.bfloat16)
    return jnp.dot(high, matrix, preferred_element_type=F32) + jnp.dot(rest, matrix, preferred_element_type=F32)


def lower(x, axis, stride=1):
    return pltpu.roll(x, stride, axis)


def upper(x, axis, stride=1):
    return pltpu.roll(x, x.shape[axis] - stride, axis)


def as_float(condition):
    return jnp.where(condition, 1.0, 0.0)


def faces_kernel(
    place, permeability, potential, phase, source,
    material, pot, src, inner, outer, even, odd,
    ids, values, semaphores,
):
    arriving = [
        pltpu.make_async_copy(a, b, semaphores.at[n])
        for n, (a, b) in enumerate(((permeability, values), (phase, ids), (potential, pot), (source, src)))
    ]
    for copy in arriving:
        copy.start()
    low_x, low_y = place[0] == 1, place[1] == 1
    count, rows = pot.shape[:2]
    arriving[0].wait()
    arriving[1].wait()
    p0, p1, p2 = values[0], values[1], values[2]
    for i in range(count):
        here = ids[i]
        material[i] = jnp.where(here == 0, p0, jnp.where(here == 1, p1, p2))
    last = count - 1
    first = jnp.where(low_x, 0, last)
    second = jnp.where(low_x, 1, last - 1)
    inner[1] = material[first]
    inner[2] = material[second]
    outer[1] = material[last - first]
    outer[2] = material[last - second]

    def edge(slot, ref, a, b):
        for i in range(count):
            low, high = ref[i, a : a + 1, :], ref[i, b : b + 1, :]
            even[slot, i : i + 1, :] = jnp.where(low_y, low, high)
            odd[slot, i : i + 1, :] = jnp.where(low_y, high, low)

    edge(1, material, 0, rows - 1)
    edge(2, material, 1, rows - 2)
    arriving[2].wait()
    inner[0] = pot[first]
    outer[0] = pot[last - first]
    edge(0, pot, 0, rows - 1)
    arriving[3].wait()


def residual_kernel(
    place, source, potential, material, inner, outer, even, odd,
    residual, coarse, strip_even, strip_odd,
    wide, narrow, y_faces,
):
    low_x, low_y = place[0] == 1, place[1] == 1
    count, rows, depth = source.shape
    c1, r1 = count // 2, rows // 2
    pieces = depth // LANES

    def ordered(flag, a, b):
        return jnp.where(flag, a, b), jnp.where(flag, b, a)

    x_low, x_high = ordered(low_x, inner[...], outer[...])
    y_low, y_high = ordered(low_y, even[...], odd[...])
    row, lane = iota((rows, depth), 0), iota((rows, depth), 1)
    first, last = row == 0, row == rows - 1
    y_faces[0], y_faces[1] = y_low[0], y_high[0]
    y_faces[2], y_faces[3] = y_low[1], y_high[1]
    outside = as_float(lane == 0) + as_float(lane == depth - 1)

    def edge_count(faces):
        return as_float(faces[:1, :1] <= 0.0)

    outside_y = outside + jnp.where(first, edge_count(y_low[1]), 0.0) + jnp.where(last, edge_count(y_high[1]), 0.0)
    face = harmonic(x_low[1], material[0], 1.0)
    for i in range(count):
        a, v = material[i], potential[i]
        v_before = potential[i - 1] if i else x_low[0]
        v_ahead = potential[i + 1] if i < count - 1 else x_high[0]
        next_face = harmonic(a, material[i + 1] if i < count - 1 else x_high[1], 1.0)
        down = jnp.where(first, y_faces[2, i : i + 1], lower(a, 0))
        w_down = harmonic(a, down, 1.0)
        w_top = harmonic(a[rows - 1 :], y_faces[3, i : i + 1], 1.0)
        w_up = jnp.where(last, w_top, upper(w_down, 0))
        w_back = jnp.where(lane == 0, 0.0, harmonic(a, lower(a, 1), 1.0))
        w_front = upper(w_back, 1)
        v_down = jnp.where(first, y_faces[0, i : i + 1], lower(v, 0))
        v_up = jnp.where(last, y_faces[1, i : i + 1], upper(v, 0))
        outer_faces = outside_y
        if i == 0:
            outer_faces = outer_faces + edge_count(x_low[1])
        if i == count - 1:
            outer_faces = outer_faces + edge_count(x_high[1])
        diagonal = face + next_face + w_down + w_up + w_back + w_front + a * outer_faces
        off = face * v_before + next_face * v_ahead + w_down * v_down + w_up * v_up
        off = off + w_back * lower(v, 1) + w_front * upper(v, 1)
        left = source[i] - diagonal * v + off
        residual[i] = left
        face = next_face
        at = (i // 2) * rows
        if i % 2 == 0:
            kept_left, kept_a = left, a
        else:
            wide[at : at + rows] = kept_left + left
            wide[c1 * rows + at : c1 * rows + at + rows] = kept_a + a
        low = jnp.concatenate([left[:4], a[:4]], axis=0)
        high = jnp.concatenate([left[rows - 4 :], a[rows - 4 :]], axis=0)
        for ref, strip in ((strip_even, jnp.where(low_y, low, high)), (strip_odd, jnp.where(low_y, high, low))):
            for piece in range(pieces):
                ref[i * pieces + piece] = strip[:, piece * LANES : (piece + 1) * LANES]
    base = 2 * c1 * rows
    for n, both in enumerate((x_low[1] + x_low[2], x_high[1] + x_high[2], y_low[1] + y_low[2], y_high[1] + y_high[2])):
        wide[base + n * rows : base + (n + 1) * rows] = both
    narrow[...] = select(wide[...], pair_matrix(depth)) * 0.125
    half = narrow.shape[0] // 2
    coarse[...] = narrow[pl.ds(0, half, 2)] + narrow[pl.ds(1, half, 2)]
    for k in range(c1):
        s, m = coarse[k * r1 : (k + 1) * r1], coarse[(c1 + k) * r1 : (c1 + k + 1) * r1]
        low = jnp.concatenate([s[:4], m[:4]], axis=0)
        high = jnp.concatenate([s[r1 - 4 :], m[r1 - 4 :]], axis=0)
        strip_even[count * pieces + k] = jnp.where(low_y, low, high)
        strip_odd[count * pieces + k] = jnp.where(low_y, high, low)


def payload_kernel(c1, r1, coarse, payload, wide, narrow):
    c2 = c1 // 2
    depth = coarse.shape[1]
    s = [coarse[k * r1 : (k + 1) * r1] for k in range(c1)]
    m = [coarse[(c1 + k) * r1 : (c1 + k + 1) * r1] for k in range(c1)]
    base = 2 * c1 * r1
    m_xlow, m_xhigh, m_ylow, m_yhigh = (coarse[base + n * r1 : base + (n + 1) * r1] for n in range(4))
    row, lane = iota((r1, depth), 0), iota((r1, depth), 1)
    first, last = row == 0, row == r1 - 1
    around = [m_xlow] + m + [m_xhigh]
    errors, tables = [], []
    face = harmonic(around[0], around[1], 0.25)
    for k in range(c1):
        a = m[k]
        down = jnp.where(first, m_ylow[k : k + 1], lower(a, 0))
        up = jnp.where(last, m_yhigh[k : k + 1], upper(a, 0))
        next_face = harmonic(a, around[k + 2], 0.25)
        w_down = harmonic(a, down, 0.25)
        w_up = jnp.where(last, harmonic(a, up, 0.25), upper(w_down, 0))
        w_back = jnp.where(lane == 0, 0.0, harmonic(a, lower(a, 1), 0.25))
        w_front = upper(w_back, 1)
        outside = as_float(lane == 0) + as_float(lane == depth - 1)
        outside = outside + as_float(down <= 0.0) + as_float(up <= 0.0)
        outside = outside + as_float(around[k] <= 0.0) + as_float(around[k + 2] <= 0.0)
        diagonal = face + next_face + w_down + w_up + w_back + w_front + 0.25 * a * outside
        errors.append(DAMPING * s[k] * invert(diagonal))
        tables.append((face, next_face, w_down, w_up, w_back, w_front))
        face = next_face
    base = c2 * r1
    for k in range(c1):
        e, w = errors[k], tables[k]
        t = KEPT * s[k] + w[4] * lower(e, 1) + w[5] * upper(e, 1)
        t = t + jnp.where(first, 0.0, w[2] * lower(e, 0)) + jnp.where(last, 0.0, w[3] * upper(e, 0))
        if k > 0:
            t = t + w[0] * errors[k - 1]
        if k < c1 - 1:
            t = t + w[1] * errors[k + 1]
        at = (k // 2) * r1
        if k % 2 == 0:
            kept = t
        else:
            wide[0, at : at + r1] = kept + t
            wide[1, at : at + r1] = m[k - 1] + m[k]
        wide[1, base + k : base + k + 1] = (w[2] * e)[:1]
        wide[1, base + r1 + k : base + r1 + k + 1] = (w[3] * e)[r1 - 1 :]
    wide[0, base : base + r1] = tables[0][0] * errors[0]
    wide[0, base + r1 : base + 2 * r1] = tables[c1 - 1][1] * errors[c1 - 1]
    narrow[...] = (select(wide[0], pair_matrix(depth)) + select(wide[1], pair_matrix(depth, LANES // 2))) * 0.125
    half = narrow.shape[0] // 2
    block = narrow[pl.ds(0, half, 2)] + narrow[pl.ds(1, half, 2)]
    payload[...] = jnp.broadcast_to(block[None], payload.shape)


def strips_kernel(place, residual, material, coarse, even, odd, inner, outer, long):
    low_x, low_y = place[0] == 1, place[1] == 1
    count, rows, depth = residual.shape
    pieces = depth // LANES
    c1, r1 = count // 2, rows // 2
    base = count * pieces

    def sides(at):
        a, b = even[at], odd[at]
        return jnp.where(low_y, a, b), jnp.where(low_y, b, a)

    for i in range(count):
        for piece in range(pieces):
            low, high = sides(i * pieces + piece)
            z = slice(piece * LANES, (piece + 1) * LANES)
            long[0, i, :, z] = jnp.concatenate([low[:4], residual[i, :, z], high[:4]], axis=0)
            long[1, i, :, z] = jnp.concatenate([low[4:], material[i, :, z], high[4:]], axis=0)
    for k in range(c1):
        low, high = sides(base + k)
        s, m = coarse[k * r1 : (k + 1) * r1], coarse[(c1 + k) * r1 : (c1 + k + 1) * r1]
        i, z = count + k // 2, slice(k % 2 * LANES, (k % 2 + 1) * LANES)
        long[0, i, : r1 + 8, z] = jnp.concatenate([low[:4], s, high[:4]], axis=0)
        long[1, i, : r1 + 8, z] = jnp.concatenate([low[4:], m, high[4:]], axis=0)

    def pack(out, flag):
        at = 0
        for n, planes in ((0, 3), (1, 4)):
            start = jnp.where(flag, 0, count - planes)
            for k in range(planes):
                for tile in range((rows + 8) // 8):
                    for piece in range(pieces):
                        out[at] = long[n, start + k, tile * 8 : tile * 8 + 8, piece * LANES : (piece + 1) * LANES]
                        at += 1
        for n, planes in ((0, 3), (1, 4)):
            for k in range(planes):
                low, high = k, c1 - planes + k
                for tile in range((r1 + 8) // 8):
                    y = slice(tile * 8, tile * 8 + 8)
                    a = long[n, count + low // 2, y, low % 2 * LANES : (low % 2 + 1) * LANES]
                    b = long[n, count + high // 2, y, high % 2 * LANES : (high % 2 + 1) * LANES]
                    out[at] = jnp.where(flag, a, b)
                    at += 1

    pack(inner, low_x)
    pack(outer, jnp.logical_not(low_x))


def unpack(source, flag, out, start, planes, tiles, pieces, at):
    for n in range(planes):
        for tile in range(tiles):
            for piece in range(pieces):
                value = jnp.where(flag, source[0][at], source[1][at])
                out[start + n, tile * 8 : tile * 8 + 8, piece * LANES : (piece + 1) * LANES] = value
                at += 1
    return at


def smooth_kernel(ends, place, potential, long, inner, outer, out, mat, res, x, d, fx, fy, fz, inv):
    low_x = place[0] == 1
    count, rows, depth = potential.shape
    pieces, tiles = depth // LANES, (rows + 8) // 8
    both = (inner, outer)
    for flag, start_r, start_m in ((low_x, 1, 0), (jnp.logical_not(low_x), count + 4, count + 4)):
        at = unpack(both, flag, res, start_r, 3, tiles, pieces, 0)
        unpack(both, flag, mat, start_m, 4, tiles, pieces, at)
    res[pl.ds(4, count)] = long[0, :count]
    mat[pl.ds(4, count)] = long[1, :count]
    total, length = count + 8, rows + 8
    row, lane = iota((length, depth), 0), iota((length, depth), 1)
    outside = as_float(lane == 0) + as_float(lane == depth - 1)
    outside = outside + as_float((row == 4) & (place[3] == 0)) + as_float((row == rows + 3) & (place[3] == ends[1] - 1))
    low_end, high_end = place[2] == 0, place[2] == ends[0] - 1

    def weigh(at, step, previous):
        for n in range(step):
            i = at + n
            a, ahead = mat[i], mat[i + 1]
            f = harmonic(a, ahead, 1.0)
            w_down = harmonic(a, lower(a, 0), 1.0)
            w_back = jnp.where(lane == 0, 0.0, harmonic(a, lower(a, 1), 1.0))
            edges = as_float((i == 4) & low_end) + as_float((i == count + 3) & high_end)
            diagonal = previous + f + w_down + upper(w_down, 0) + w_back + upper(w_back, 1) + a * (outside + edges)
            inverse = jnp.where(a > 0.0, invert(jnp.maximum(diagonal, 1e-3)), 0.0)
            fx[i + 1], fy[i], fz[i], inv[i] = f, w_down, w_back, inverse
            scaled = inverse * res[i]
            res[i] = scaled
            x[0, i] = scaled * (1.0 / THETA)
            previous = f
        return previous

    first = harmonic(mat[0], mat[1], 1.0)
    fx[1] = first
    step = 2
    lax.fori_loop(0, (total - 2) // step, lambda n, f: weigh(1 + n * step, step, f), first)
    rho = 1.0 / SIGMA
    for turn in range(DEG - 1):
        following = 1.0 / (2.0 * SIGMA - rho)
        old, new = turn % 2, (turn + 1) % 2
        keep, gain = following * rho, 2.0 * following / DELTA

        def sweep(n, _):
            for k in range(step):
                i = 2 + turn + n * step + k
                v = x[old, i]
                w_down, w_back = fy[i], fz[i]
                off = fx[i] * x[old, i - 1] + fx[i + 1] * x[old, i + 1]
                off = off + w_down * lower(v, 0) + upper(w_down * v, 0)
                off = off + w_back * lower(v, 1) + upper(w_back * v, 1)
                before = v * keep if turn == 0 else d[i] * keep
                change = before + gain * (res[i] - v + inv[i] * off)
                if turn == DEG - 2:
                    out[i - 4] = potential[i - 4] + (v + change)[4 : 4 + rows]
                else:
                    d[i] = change
                    x[new, i] = v + change
            return 0

        lax.fori_loop(0, (total - 4 - 2 * turn) // step, sweep, 0)
        rho = following


def each(count, body, most=8):
    step = min(count, most)
    if count // step <= 4:
        for n in range(count // step):
            body(n * step, step)
        return

    def run(n, _):
        body(n * step, step)
        return 0

    lax.fori_loop(0, count // step, run, 0)


def fill_table(mat, table, level, count, base, width):
    stride, scale = 2**level, 0.25 ** (level + 2)
    rows = mat.shape[1]

    def body(at, step):
        shape = (step, rows, LANES)
        plane, row, lane = (iota(shape, axis) for axis in range(3))
        a, before, ahead = mat[pl.ds(at + 1, step)], mat[pl.ds(at, step)], mat[pl.ds(at + 2, step)]
        w_before, w_ahead = harmonic(a, before, scale), harmonic(a, ahead, scale)
        w_down = jnp.where(row < stride, 0.0, harmonic(a, lower(a, 1, stride), scale))
        w_back = jnp.where(lane < stride, 0.0, harmonic(a, lower(a, 2, stride), scale))
        outside = as_float(row == 0) + as_float(row == rows - stride) + as_float(lane == 0) + as_float(lane == width - stride)
        outside = outside + as_float(plane == -at) + as_float(plane == count - 1 - at)
        diagonal = w_before + w_ahead + w_down + upper(w_down, 1, stride) + w_back + upper(w_back, 2, stride)
        diagonal = diagonal + scale * a * outside
        table[0, pl.ds(base + at, step)] = w_before
        table[1, pl.ds(base + at, step)] = w_down
        table[2, pl.ds(base + at, step)] = w_back
        table[3, pl.ds(base + at, step)] = jnp.where(a > 0.0, invert(jnp.maximum(diagonal, 1e-4)), 0.0)

    each(count, body, 4)
    table[0, base + count] = jnp.zeros((rows, LANES), F32)


def fold(t, stride):
    a = t.reshape(t.shape[0] // 2, 2, *t.shape[1:])
    a = a[:, 0] + a[:, 1]
    a = a + upper(a, 1, stride)
    return a + upper(a, 2, stride)


def unfold(e, stride):
    e = e + lower(e, 1, stride)
    e = e + lower(e, 2, stride)
    return jnp.broadcast_to(e[:, None], (e.shape[0], 2, *e.shape[1:])).reshape(2 * e.shape[0], *e.shape[1:])


def off_diagonal(e, table, base, at, step, stride):
    v = e[pl.ds(at + 1, step)]
    total = table[0, pl.ds(base + at, step)] * e[pl.ds(at, step)]
    total = total + table[0, pl.ds(base + at + 1, step)] * e[pl.ds(at + 2, step)]
    fy, fz = table[1, pl.ds(base + at, step)], table[2, pl.ds(base + at, step)]
    total = total + fy * lower(v, 1, stride) + upper(fy * v, 1, stride)
    return v, total + fz * lower(v, 2, stride) + upper(fz * v, 2, stride)


def cycle(s, e, t, table, counts, bases, place, out, c2, r2, pad):
    zero = jnp.zeros(t.shape[1:], F32)
    for ref, count in zip(e, counts):
        ref[0] = zero
        ref[count + 1] = zero
    for level, (count, base) in enumerate(zip(counts, bases)):
        s_l, e_l, stride = s[level], e[level], 2**level

        def start(at, step):
            e_l[pl.ds(at + 1, step)] = DAMPING * s_l[pl.ds(at + 1, step)] * table[3, pl.ds(base + at, step)]

        each(count, start)
        if level == len(counts) - 1:
            break

        def remainder(at, step):
            _, off = off_diagonal(e_l, table, base, at, step, stride)
            left = KEPT * s_l[pl.ds(at + 1, step)] + off
            s[level + 1][pl.ds(at // 2 + 1, step // 2)] = 0.125 * fold(left, stride)

        each(count, remainder)

    def relax(s_l, source, target, base, count, stride):
        def sweep(at, step):
            v, off = off_diagonal(source, table, base, at, step, stride)
            inverse = table[3, pl.ds(base + at, step)]
            target[pl.ds(at + 1, step)] = KEPT * v + DAMPING * inverse * (s_l[pl.ds(at + 1, step)] + off)

        each(count, sweep)

    t[0] = zero
    t[counts[2] + 1] = zero
    now, other = e[2], t
    for _ in range(COARSE_SWEEPS - 1):
        relax(s[2], now, other, bases[2], counts[2], 4)
        now, other = other, now

    def add(at, step):
        e[1][pl.ds(2 * at + 1, 2 * step)] = e[1][pl.ds(2 * at + 1, 2 * step)] + unfold(now[pl.ds(at + 1, step)], 2)

    each(counts[2], add, 4)
    if now is t:
        now = e[2] = s[1]
    relax(s[1], e[1], t, bases[1], counts[1], 2)

    planes = c2 + 4
    begin = place[2] * c2 - 2
    inside = jnp.clip(begin, 0, counts[0] - planes)
    coarse = jnp.clip(place[2] * c2 // 2 - 2, 0, counts[1] - planes // 2 - 2)
    number = planes // 2 + 2
    at = pl.ds(2 * coarse + 1, 2 * number)
    e[0][at] = e[0][at] + unfold(t[pl.ds(coarse + 1, number)], 1)
    v, off = off_diagonal(e[0], table, bases[0], inside, planes, 1)
    inverse = table[3, pl.ds(bases[0] + inside, planes)]
    pad[...] = jnp.zeros(pad.shape, F32)
    rows = t.shape[1]
    value = KEPT * v + DAMPING * inverse * (s[0][pl.ds(inside + 1, planes)] + off)
    pad[pl.ds(2 + inside - begin, planes), 8 : 8 + rows, :] = value
    for n in range(planes):
        out[n] = pad[n + 2, pl.ds(place[3] * r2 + 6, r2 + 4), :]


def cycle_shapes(counts, rows, c2):
    out = [pltpu.VMEM((count + 2, rows, LANES), F32) for count in (*counts, *counts, counts[0])]
    return out + [pltpu.VMEM((c2 + 8, rows + 16, LANES), F32)]


def first_cycle_kernel(counts, bases, grid, c2, r2, width, place, blocks, out, table, *scratch):
    s, e, t, pad = scratch[0:3], list(scratch[3:6]), scratch[6], scratch[7]
    gx, gy = grid
    zero = jnp.zeros(t.shape[1:], F32)
    for ref, count in zip((t, *s), (counts[0], *counts)):
        ref[0] = zero
        ref[count + 1] = zero
    half = LANES // 2
    rows = gy * r2
    own = c2 * r2
    face_y = e[0]
    edge = iota((rows, LANES), 0) % r2
    edge = (edge == 0) | (edge == r2 - 1)
    valid = iota((own, LANES), 1) < half
    for n in range(counts[0] + 2):
        face_y[n, 0:8] = jnp.zeros((8, LANES), F32)
        face_y[n, rows - 8 : rows] = jnp.zeros((8, LANES), F32)

    def column(i, _):
        for j in range(gy):
            block = blocks[i * gy + j]
            turned = pltpu.roll(block, half, 1)
            values = jnp.where(valid, block[:own], 0.0)
            materials = jnp.where(valid, turned[:own], 0.0)
            y_faces = jnp.where(valid[: 2 * c2], turned[own:], 0.0)
            for k in range(c2):
                at = i * c2 + k + 1
                s[0][at, j * r2 : (j + 1) * r2, :] = values[k * r2 : (k + 1) * r2]
                t[at, j * r2 : (j + 1) * r2, :] = materials[k * r2 : (k + 1) * r2]
                if j > 0:
                    face_y[at, j * r2 - 1 : j * r2, :] = y_faces[k : k + 1]
                if j < gy - 1:
                    face_y[at, (j + 1) * r2 : (j + 1) * r2 + 1, :] = y_faces[c2 + k : c2 + k + 1]
        return 0

    lax.fori_loop(0, gx, column, 0)

    def sides(i, _):
        low = [blocks[i * gy + j, own : own + r2] for j in range(gy)]
        high = [blocks[i * gy + j, own + r2 :] for j in range(gy)]
        keep = iota((rows, LANES), 1) < half
        for parts, at in ((low, i * c2), (high, (i + 1) * c2 + 1)):
            s[0][at] = s[0][at] + jnp.where(keep, jnp.concatenate(parts, axis=0), 0.0)
        return 0

    lax.fori_loop(0, gx, sides, 0)

    def join(at, step):
        now = pl.ds(at + 1, step)
        s[0][now] = s[0][now] + jnp.where(edge, face_y[now], 0.0)

    each(counts[0], join)
    s[0][0] = zero
    s[0][counts[0] + 1] = zero
    mats = (t, s[1], s[2])
    for level, (count, base) in enumerate(zip(counts, bases)):
        if level:

            def coarsen(at, step):
                shape = (step // 2, rows, LANES)
                whole = (iota(shape, 1) % 2**level == 0) & (iota(shape, 2) % 2**level == 0)
                mean = 0.125 * fold(mats[level - 1][pl.ds(at + 1, step)], 2 ** (level - 1))
                mats[level][pl.ds(at // 2 + 1, step // 2)] = jnp.where(whole, mean, 0.0)

            each(counts[level - 1], coarsen)
        fill_table(mats[level], table, level, count, base, width)
    cycle(s, e, t, table, counts, bases, place, out, c2, r2, pad)


def shifted(a):
    zero = jnp.zeros_like(a[:1])
    return jnp.concatenate([zero, a[:-1]], axis=0), jnp.concatenate([a[1:], zero], axis=0)


def apply_off(e, fx, fy, fz):
    before, ahead = shifted(e)
    out = fx[:-1] * before + fx[1:] * ahead
    out = out + fy * lower(e, 1) + upper(fy * e, 1)
    return out + fz * lower(e, 2) + upper(fz * e, 2)


def raise_window(window_ref, flat, out):
    planes, rows, _ = window_ref.shape
    values = select(window_ref[...].reshape(planes * rows, LANES), spread_matrix(LANES))
    flat[pl.ds(0, planes * rows, 2)] = values
    flat[pl.ds(1, planes * rows, 2)] = values
    v = flat[...].reshape(planes, 1, 2 * rows, LANES)
    out[...] = jnp.broadcast_to(v, (planes, 2, 2 * rows, LANES)).reshape(2 * planes, 2 * rows, LANES)


def level1_kernel(offset, place, long, inner, outer, window1, payload, state, src, mat, flat, prolonged, wide, narrow):
    low_x = place[0] == 1
    total, length, depth = src.shape
    count, rows = total - 8, length - 8
    both = (inner, outer)
    zero = jnp.zeros((length, depth), F32)
    src[0] = zero
    src[total - 1] = zero
    for flag, start_s, start_m in ((low_x, 1, 0), (jnp.logical_not(low_x), count + 4, count + 4)):
        at = unpack(both, flag, src, start_s, 3, length // 8, 1, offset)
        unpack(both, flag, mat, start_m, 4, length // 8, 1, at)
    for n, ref in enumerate((src, mat)):
        for k in range(count):
            ref[4 + k] = long[n, 2 * count + k // 2, :length, k % 2 * LANES : (k % 2 + 1) * LANES]
    raise_window(window1, flat, prolonged)
    a = mat[...]
    lane = iota(a.shape, 2)
    before, ahead = shifted(a)
    down, up = lower(a, 1), upper(a, 1)
    w_x, w_y = harmonic(a, before, 0.25), harmonic(a, down, 0.25)
    w_z = jnp.where(lane == 0, 0.0, harmonic(a, lower(a, 2), 0.25))
    _, w_ahead = shifted(w_x)
    outside = as_float(lane == 0) + as_float(lane == depth - 1)
    for b in (before, ahead, down, up):
        outside = outside + as_float(b <= 0.0)
    diagonal = w_x + w_ahead + w_y + upper(w_y, 1) + w_z + upper(w_z, 2) + 0.25 * a * outside
    inverse = jnp.where(a > 0.0, invert(jnp.maximum(diagonal, 1e-4)), 0.0)
    state[0], state[1], state[2], state[3] = w_x, w_y, w_z, inverse
    w_x = jnp.concatenate([w_x, zero[None]], axis=0)
    s = src[...]
    e = DAMPING * inverse * s + prolonged[...]
    c = KEPT * e + DAMPING * inverse * (s + apply_off(e, w_x, w_y, w_z))
    s2 = s - diagonal * c + apply_off(c, w_x, w_y, w_z)
    e2 = DAMPING * inverse * s2
    t = KEPT * s2 + apply_off(e2, w_x, w_y, w_z)
    state[4], state[5], state[6] = c, s2, e2
    own = t[4 : 4 + count, 4 : 4 + rows].reshape(count // 2, 2, rows, depth)
    wide[...] = (own[:, 0] + own[:, 1]).reshape(count // 2 * rows, depth)
    part = count // 4 * rows
    narrow[...] = (select(wide[:part], pair_matrix(depth)) + select(wide[part:], pair_matrix(depth, LANES // 2))) * 0.125
    block = narrow[pl.ds(0, part // 2, 2)] + narrow[pl.ds(1, part // 2, 2)]
    payload[...] = jnp.broadcast_to(block[None], payload.shape)


def last_cycle_kernel(counts, bases, grid, c2, r2, place, blocks, table, state, partial, out, *scratch):
    s, e, t, pad = scratch[0:3], list(scratch[3:6]), scratch[6], scratch[7]
    view, flat, prolonged, tall = scratch[8:12]
    gx, gy = grid
    half = LANES // 2
    valid = iota((c2 // 2 * r2, LANES), 1) < half

    def column(i, _):
        for j in range(gy):
            block = blocks[i * gy + j]
            parts = (jnp.where(valid, block, 0.0), jnp.where(valid, pltpu.roll(block, half, 1), 0.0))
            for k in range(c2):
                n = k % (c2 // 2)
                s[0][i * c2 + k + 1, j * r2 : (j + 1) * r2, :] = parts[k // (c2 // 2)][n * r2 : (n + 1) * r2]
        return 0

    lax.fori_loop(0, gx, column, 0)
    cycle(s, e, t, table, counts, bases, place, view, c2, r2, pad)
    raise_window(view, flat, prolonged)
    count, rows, depth = partial.shape
    c1, r1 = count // 2, rows // 2
    near = slice(3, c1 + 5)
    own = slice(4, 4 + c1)
    v = state[6, near] + prolonged[near]
    w_x, w_y, w_z = state[0, 4 : c1 + 5], state[1, own], state[2, own]
    here = v[1:-1]
    off = w_x[:-1] * v[:-2] + w_x[1:] * v[2:]
    off = off + w_y * lower(here, 1) + upper(w_y * here, 1) + w_z * lower(here, 2) + upper(w_z * here, 2)
    here = KEPT * here + DAMPING * state[3, own] * (state[5, own] + off)
    coarse = (state[4, own] + here)[:, 4 : 4 + r1].reshape(c1 * r1, LANES)
    values = select(coarse, spread_matrix(depth))
    for piece in range(depth // LANES):
        z = slice(piece * LANES, (piece + 1) * LANES)
        tall[piece, pl.ds(0, c1 * r1, 2)] = values[:, z]
        tall[piece, pl.ds(1, c1 * r1, 2)] = values[:, z]
        for k in range(c1):
            more = tall[piece, k * rows : (k + 1) * rows]
            out[2 * k, :, z] = partial[2 * k, :, z] + more
            out[2 * k + 1, :, z] = partial[2 * k + 1, :, z] + more


def size_of(shape):
    lead = math.prod(shape[:-2])
    return 4 * lead * (-(-shape[-2] // 8) * 8) * (-(-shape[-1] // LANES) * LANES)


def call(kernel, name, inputs, outputs, scratch=(), apart=()):
    streamed = 0

    def held(n, x):
        nonlocal streamed
        if x.ndim == 1 or n in apart:
            return x
        if size_of(x.shape) <= HELD:
            return pltpu.with_memory_space_constraint(x, pltpu.VMEM)
        streamed += size_of(x.shape)
        return x

    def result(shape):
        nonlocal streamed
        if isinstance(shape, jax.ShapeDtypeStruct):
            streamed += size_of(shape.shape)
            return shape
        if size_of(shape) <= HELD:
            return pltpu.VMEM(shape, F32)
        streamed += size_of(shape)
        return jax.ShapeDtypeStruct(shape, F32)

    def space(n, x):
        return pl.ANY if n in apart else pltpu.SMEM if x.ndim == 1 else pltpu.VMEM

    specs = [pl.BlockSpec(memory_space=space(n, x)) for n, x in enumerate(inputs)]
    inputs = [held(n, x) for n, x in enumerate(inputs)]
    results = [result(shape) for shape in outputs]
    need = streamed + sum(size_of(x.shape) for x in scratch if len(x.shape) > 1) + 3 * MIB
    return pl.pallas_call(
        kernel,
        out_shape=results,
        in_specs=specs,
        out_specs=[pl.BlockSpec(memory_space=pltpu.VMEM) for _ in outputs],
        scratch_shapes=list(scratch),
        compiler_params=pltpu.CompilerParams(vmem_limit_bytes=max(need, 8 * MIB)),
        name=name,
    )(*inputs)


def swaps(count):
    inner = [(i, i + 1) for i in range(0, count - 1, 2)]
    outer = [(i, i + 1) for i in range(1, count - 1, 2)]
    return [pairs + [(b, a) for a, b in pairs] for pairs in (inner, outer)]


def local(right_side, potential, phase, permeability):
    gx, gy = lax.axis_size("gx"), lax.axis_size("gy")
    devices = gx * gy
    here_x, here_y = lax.axis_index("gx"), lax.axis_index("gy")
    place = jnp.stack([here_x % 2, here_y % 2, here_x, here_y]).astype(jnp.int32)
    count, rows, depth = right_side.shape
    c1, r1, d1 = count // 2, rows // 2, depth // 2
    c2, r2 = c1 // 2, r1 // 2
    pieces = depth // LANES
    swap_x, swap_y = swaps(gx), swaps(gy)
    VM = lambda *shape: pltpu.VMEM(shape, F32)

    brick = (count, rows, depth)
    face = (3, rows, depth)
    material, potential_here, source_here, inner, outer, even, odd = call(
        faces_kernel, "faces", (place, permeability, potential, phase, right_side),
        (brick, brick, brick, face, face, (3, count, depth), (3, count, depth)),
        (pltpu.VMEM(brick, jnp.int32), pltpu.SMEM(permeability.shape, F32), pltpu.SemaphoreType.DMA((4,))),
        apart=(1, 2, 3, 4),
    )
    even = lax.ppermute(even, "gy", swap_y[0])
    odd = lax.ppermute(odd, "gy", swap_y[1])
    outer = lax.ppermute(outer, "gx", swap_x[1])
    inner = lax.ppermute(inner, "gx", swap_x[0])

    strip = (count * pieces + c1, 8, LANES)
    total = 2 * c1 * rows + 4 * rows
    residual, coarse, even, odd = call(
        residual_kernel, "residual", (place, source_here, potential_here, material, inner, outer, even, odd),
        (brick, (total // 2, LANES), strip, strip),
        (VM(total, depth), VM(total, LANES), VM(4, count, depth)),
    )
    even = lax.ppermute(even, "gy", swap_y[0])
    odd = lax.ppermute(odd, "gy", swap_y[1])
    small = c2 * r1 + 2 * r1
    (payload,) = call(
        functools.partial(payload_kernel, c1, r1), "payload", (coarse,), ((devices, c2 * r2 + 2 * r2, LANES),),
        (VM(2, small, d1), VM(small, LANES)),
    )
    blocks = lax.all_to_all(payload, ("gx", "gy"), 0, 0)
    tiles, tiles1 = (rows + 8) // 8, (r1 + 8) // 8
    strip = (7 * tiles * pieces + 7 * tiles1, 8, LANES)
    inner, outer, long = call(
        strips_kernel, "strips", (place, residual, material, coarse, even, odd),
        (strip, strip, (2, count + c1 // 2, rows + 8, depth)),
    )
    outer = lax.ppermute(outer, "gx", swap_x[1])
    inner = lax.ppermute(inner, "gx", swap_x[0])

    counts = tuple(gx * c2 // k for k in (1, 2, 4))
    bases = (0, counts[0] + 1, counts[0] + counts[1] + 2)
    work = cycle_shapes(counts, gy * r2, c2)
    view = (c2 + 4, r2 + 4, LANES)
    window1, table = call(
        functools.partial(first_cycle_kernel, counts, bases, (gx, gy), c2, r2, d1 // 2), "cycle1", (place, blocks),
        (view, (4, sum(counts) + 3, gy * r2, LANES)), work,
    )
    frame = (c1 + 8, r1 + 8, d1)
    flat = VM((c2 + 4) * (r2 + 4) * 2, LANES)
    payload, state = call(
        functools.partial(level1_kernel, 7 * tiles * pieces), "level1", (place, long, inner, outer, window1),
        ((devices, c2 // 2 * r2, LANES), (7, *frame)),
        (VM(*frame), VM(*frame), flat, VM(*frame), VM(c1 // 2 * r1, d1), VM(c1 // 4 * r1, LANES)),
    )
    blocks = lax.all_to_all(payload, ("gx", "gy"), 0, 0)
    wide = (count + 8, rows + 8, depth)
    (partial,) = call(
        functools.partial(smooth_kernel, (gx, gy)), "smooth", (place, potential, long, inner, outer), (brick,),
        (VM(*wide), VM(*wide), VM(2, *wide), VM(*wide), VM(count + 9, rows + 8, depth), VM(*wide), VM(*wide), VM(*wide)),
    )
    (out,) = call(
        functools.partial(last_cycle_kernel, counts, bases, (gx, gy), c2, r2), "cycle2",
        (place, blocks, table, state, partial), (jax.ShapeDtypeStruct(brick, F32),),
        (*work, VM(*view), flat, VM(*frame), VM(pieces, count // 2 * rows, LANES)),
    )
    return out


def solution(mesh):
    placed = (P("gx", "gy", None), P("gx", "gy", None), P("gx", "gy", None), P())
    return jax.shard_map(local, mesh=mesh, in_specs=placed, out_specs=P("gx", "gy", None), check_vma=False)
```

time: 487 us -> 70.5 us (0.14)
  the two profiles are of different devices: /device:TPU:28 before, /device:TPU:0 now
where the time goes in v2:
time: 70.5 us; the launch traced here: 70 us
  starting transfers between devices  28.9 us (41%)
  Pallas kernels  21.2 us (30%)
  waiting for transfers between devices  13.1 us (19%)
  local copies, waits for them, and re-layouts  6.57 us (9%)
    pallas_call x8, Pallas kernels, call(): pl.pallas_call(kernel, out_shape=results, in_specs=specs, out_specs=[pl.B...  21.2 us
    all_to_all x2, starting transfers between devices, local(): blocks = lax.all_to_all(payload, ('gx', 'gy'), 0, 0)  20.6 us
    ppermute x2, waiting for transfers between devices, local(): even = lax.ppermute(even, 'gy', swap_y[0])  11.6 us
    unnamed x14, local copies, waits for them, and re-layouts  6.57 us
    ppermute x2, starting transfers between devices, local(): even = lax.ppermute(even, 'gy', swap_y[0])  4.5 us
    ppermute x2, starting transfers between devices, local(): outer = lax.ppermute(outer, 'gx', swap_x[1])  2.01 us
    all_to_all x2, waiting for transfers between devices, local(): blocks = lax.all_to_all(payload, ('gx', 'gy'), 0, 0)  1.53 us
  transfers between devices with their start and end apart: 10, of which 3 were waited for; matrix products, arithmetic and copies ran while one was open for 0% of the time, Pallas kernels for 17%

profile of v2, /device:TPU:0, one launch (start us, length us, event | category | flops | bytes accessed | tf_op | source)
XLA Modules:
  0.0 70.0 jit_solution(15608079926774037933)
XLA Ops:
  0.0 0.1 pad_add_fusion.place
  0.1 0.9 %copy-done = f32[16,16,256]{2,1,0:T(8,128)S(1)} copy-done((f32[16,16,256]{2,1,0:T(8,128)S(1)}, f32[16,16,256]{2,1,0:T(8,128)}, u32[]{:S(2)}) %copy-start) | copy-done | bytes 262168
  1.0 0.9 %copy-done.4 = s32[16,16,256]{2,1,0:T(8,128)S(1)} copy-done((s32[16,16,256]{2,1,0:T(8,128)S(1)}, s32[16,16,256]{2,1,0:T(8,128)}, u32[]{:S(2)}) %copy-start.4) | copy-done | bytes 262168
  2.0 0.9 %copy-done.5 = f32[16,16,256]{2,1,0:T(8,128)S(1)} copy-done((f32[16,16,256]{2,1,0:T(8,128)S(1)}, f32[16,16,256]{2,1,0:T(8,128)}, u32[]{:S(2)}) %copy-start.5) | copy-done | bytes 262168
  2.9 0.7 copy-done.6
  3.6 1.2 %faces.1 = (f32[16,16,256]{2,1,0:T(8,128)S(1)}, f32[16,16,256]{2,1,0:T(8,128)S(1)}, f32[16,16,256]{2,1,0:T(8,128)S(1)}, f32[3,16,256]{2,1,0:T(8,128)S(1)}, f32[3...) custom-call(s32[4]{0:T(128)S(1)} %pad_add_fusion.place, f32[3]{0:T(128)S(1)} %copy-done.6, ...), custom_call_target="tpu_custom_call" | custom-call | tf_op jit(solution)/shard_map/faces/pallas_call | solution.py:691
  4.8 0.5 collective-permute-start
  5.3 0.7 collective-permute-start.1
  6.0 2.7 %collective-permute-start.2 = (f32[3,16,256]{2,1,0:T(8,128)S(1)}, f32[3,16,256]{2,1,0:T(8,128)S(1)}, u32[]{:S(2)}, u32[]{:S(2)}) collective-permute-start(f32[3,16,256]{2,1,0:T(8,128)S(1)} %get-tuple-element.28), channel_id=1, source_target_pairs={{0,1},{2,3},{1,0},{3,2},{4,5},{6,7},{5,4},{7,6},{8,9},{10,11},{9,8... | collective-permute-start | bytes 147464 | tf_op jit(solution)/shard_map/ppermute | solution.py:728
  8.6 0.7 collective-permute-start.3
  9.3 0.0 collective-permute-done.inner
  9.3 1.4 %collective-permute-done.2.even = f32[3,16,256]{2,1,0:T(8,128)S(1)} collective-permute-done((f32[3,16,256]{2,1,0:T(8,128)S(1)}, f32[3,16,256]{2,1,0:T(8,128)S(1)}, u32[]{:S(2)}, u32[]{:S(2)}) %collective-permute-start.2) | collective-permute-done | bytes 49184 | tf_op jit(solution)/shard_map/ppermute | solution.py:728
  10.7 1.5 %residual.1 = (f32[16,16,256]{2,1,0:T(8,128)S(1)}, f32[160,128]{1,0:T(8,128)S(1)}, f32[40,8,128]{2,1,0:T(8,128)S(1)}, f32[40,8,128]{2,1,0:T(8,128)S(1)}) custom-call(s32[4]{0:T(128)S(1)} %pad_add_fusion.place, f32[16,16,256]{2,1,0:T(8,128)S(1)} %get-tuple-element.23.source, f32[16,16,256]{2,1,0:T(8,128)S(1)} %get-tuple-element.24.potential, ...), custom_call_target="tpu_custom_call" | custom-call | tf_op jit(solution)/shard_map/residual/pallas_call | solution.py:691
  12.2 1.2 %payload.1 = f32[32,24,128]{2,1,0:T(8,128)} custom-call(f32[160,128]{1,0:T(8,128)S(1)} %get-tuple-element.31.coarse), custom_call_target="tpu_custom_call" | custom-call | tf_op jit(solution)/shard_map/payload/pallas_call | solution.py:691
  13.4 10.6 %all-to-all-start = ((f32[32,24,128]{2,1,0:T(8,128)}), f32[32,24,128]{2,1,0:T(8,128)S(1)}, u32[]{:S(2)}, u32[]{:S(2)}) async-start(f32[32,24,128]{2,1,0:T(8,128)} %payload.1), calls=%async_computation | async-start | bytes 786432 | tf_op jit(solution)/shard_map/all_to_all | solution.py:747
  24.0 1.8 %collective-permute-start.4 = (f32[40,8,128]{2,1,0:T(8,128)S(1)}, f32[40,8,128]{2,1,0:T(8,128)S(1)}, u32[]{:S(2)}, u32[]{:S(2)}) collective-permute-start(f32[40,8,128]{2,1,0:T(8,128)S(1)} %get-tuple-element.32), channel_id=1, source_target_pairs={{0,1},{2,3},{1,0},{3,2},{4,5},{6,7},{5,4},{7,6},{8,9},{10,11},{9,8... | collective-permute-start | bytes 491528 | tf_op jit(solution)/shard_map/ppermute | solution.py:740
  25.9 0.7 collective-permute-start.5
  26.5 10.2 %collective-permute-done.4.even = f32[40,8,128]{2,1,0:T(8,128)S(1)} collective-permute-done((f32[40,8,128]{2,1,0:T(8,128)S(1)}, f32[40,8,128]{2,1,0:T(8,128)S(1)}, u32[]{:S(2)}, u32[]{:S(2)}) %collective-permute-start.4) | collective-permute-done | bytes 163872 | tf_op jit(solution)/shard_map/ppermute | solution.py:740
  36.7 0.0 collective-permute-done.5.odd
  36.7 1.4 %strips.1 = (f32[56,8,128]{2,1,0:T(8,128)}, f32[56,8,128]{2,1,0:T(8,128)}, f32[2,20,24,256]{3,2,1,0:T(8,128)S(1)}) custom-call(s32[4]{0:T(128)S(1)} %pad_add_fusion.place, f32[16,16,256]{2,1,0:T(8,128)S(1)} %get-tuple-element.30.residual, f32[16,16,256]{2,1,0:T(8,128)S(1)} %get-tuple-element.25.material, f32[160,128]{1,0:T(8,128)S(1)} %get-tuple-element.31.coarse, ...), custom_call_target="tpu_custom_call" | custom-call | tf_op jit(solution)/shard_map/strips/pallas_call | solution.py:691
  38.2 0.0 collective-permute-start.6
  38.2 1.4 %collective-permute-start.7 = (f32[56,8,128]{2,1,0:T(8,128)}, f32[56,8,128]{2,1,0:T(8,128)}, u32[]{:S(2)}, u32[]{:S(2)}) collective-permute-start(f32[56,8,128]{2,1,0:T(8,128)} %get-tuple-element.36), channel_id=1, source_target_pairs={{4,8},{12,16},{20,24},{8,4},{16,12},{24,20},{5,9},{13,17},{21,25},... | collective-permute-start | bytes 688136 | tf_op jit(solution)/shard_map/ppermute | solution.py:754
  39.5 4.3 %cycle1.1 = (f32[8,8,128]{2,1,0:T(8,128)S(1)}, f32[4,59,16,128]{3,2,1,0:T(8,128)S(1)}) custom-call(s32[4]{0:T(128)S(1)} %pad_add_fusion.place, f32[32,24,128]{2,1,0:T(8,128)S(1)} %all-to-all-done.blocks), custom_call_target="tpu_custom_call" | custom-call | tf_op jit(solution)/shard_map/cycle1/pallas_call | solution.py:691
  43.8 2.3 %level1.1 = (f32[32,8,128]{2,1,0:T(8,128)}, f32[7,16,16,128]{3,2,1,0:T(8,128)S(1)}) custom-call(s32[4]{0:T(128)S(1)} %pad_add_fusion.place, f32[2,20,24,256]{3,2,1,0:T(8,128)S(1)} %get-tuple-element.34.long, f32[56,8,128]{2,1,0:T(8,128)S(1)} %collective-permute-done.6.inner, f32[56,8,128]{2,1,0:T(8,128)} %collective-permute-done.7.outer, ...), custom_call_target="tpu_custom_call" | custom-call | tf_op jit(solution)/shard_map/level1/pallas_call | solution.py:691
  46.1 0.9 %copy-done.2 = f32[7,16,16,128]{3,2,1,0:T(8,128)} copy-done((f32[7,16,16,128]{3,2,1,0:T(8,128)}, f32[7,16,16,128]{3,2,1,0:T(8,128)S(1)}, u32[]{:S(2)}) %copy-start.2) | copy-done | bytes 917528
  47.1 10.0 %all-to-all-start.1 = ((f32[32,8,128]{2,1,0:T(8,128)}), f32[32,8,128]{2,1,0:T(8,128)S(1)}, u32[]{:S(2)}, u32[]{:S(2)}) async-start(f32[32,8,128]{2,1,0:T(8,128)} %get-tuple-element.38), calls=%async_computation.1 | async-start | bytes 262144 | tf_op jit(solution)/shard_map/all_to_all | solution.py:772
  57.0 0.0 copy-start.1
  57.0 0.9 %copy-done.1 = f32[16,16,256]{2,1,0:T(8,128)S(1)} copy-done((f32[16,16,256]{2,1,0:T(8,128)S(1)}, f32[16,16,256]{2,1,0:T(8,128)}, u32[]{:S(2)}) %copy-start.1) | copy-done | bytes 262168
  58.0 5.9 %smooth.1.partial = f32[16,16,256]{2,1,0:T(8,128)S(1)} custom-call(s32[4]{0:T(128)S(1)} %pad_add_fusion.place, f32[16,16,256]{2,1,0:T(8,128)S(1)} %copy-done.1, f32[2,20,24,256]{3,2,1,0:T(8,128)S(1)} %get-tuple-element.34.long, f32[56,8,128]{2,1,0:T(8,128)S(1)} %collective-permute-done.6.inner, f32[56,8,128]{2,1,0:T(8,128)} %collective-permute-done.7.outer), custom_call_target="tpu_custom_call" | custom-call | tf_op jit(solution)/shard_map/smooth/pallas_call | solution.py:691
  63.9 1.5 %all-to-all-done.1.blocks = f32[32,8,128]{2,1,0:T(8,128)S(1)} async-done(((f32[32,8,128]{2,1,0:T(8,128)}), f32[32,8,128]{2,1,0:T(8,128)S(1)}, u32[]{:S(2)}, u32[]{:S(2)}) %all-to-all-start.1) | async-done | bytes 131104 | tf_op jit(solution)/shard_map/all_to_all | solution.py:772
  65.4 1.2 %copy-done.3 = f32[7,16,16,128]{3,2,1,0:T(8,128)S(1)} copy-done((f32[7,16,16,128]{3,2,1,0:T(8,128)S(1)}, f32[7,16,16,128]{3,2,1,0:T(8,128)}, u32[]{:S(2)}) %copy-start.3) | copy-done | bytes 917528
  66.6 3.4 %cycle2.1 = f32[16,16,256]{2,1,0:T(8,128)} custom-call(s32[4]{0:T(128)S(1)} %pad_add_fusion.place, f32[32,8,128]{2,1,0:T(8,128)S(1)} %all-to-all-done.1.blocks, f32[4,59,16,128]{3,2,1,0:T(8,128)S(1)} %get-tuple-element.39.table, f32[7,16,16,128]{3,2,1,0:T(8,128)S(1)} %copy-done.3, f32[16,16,256]{2,1,0:T(8,128)S(1)} %smooth.1.partial), custom_call_target="tpu_custom_call" | custom-call | tf_op jit(solution)/shard_map/cycle2/pallas_call | solution.py:691
  (11 shorter events, 0.0 us)
Async XLA Ops:
  0.1 1.0 %copy-start = (f32[16,16,256]{2,1,0:T(8,128)S(1)}, f32[16,16,256]{2,1,0:T(8,128)}, u32[]{:S(2)}) copy-start(f32[16,16,256]{2,1,0:T(8,128)} %potential.3) | copy-start | bytes 786436
  1.0 0.9 %copy-start.4 = (s32[16,16,256]{2,1,0:T(8,128)S(1)}, s32[16,16,256]{2,1,0:T(8,128)}, u32[]{:S(2)}) copy-start(s32[16,16,256]{2,1,0:T(8,128)} %phase.1) | copy-start | bytes 786436
  2.0 0.9 %copy-start.5 = (f32[16,16,256]{2,1,0:T(8,128)S(1)}, f32[16,16,256]{2,1,0:T(8,128)}, u32[]{:S(2)}) copy-start(f32[16,16,256]{2,1,0:T(8,128)} %source.1) | copy-start | bytes 786436
  2.9 0.7 copy-start.6
  4.8 4.5 %collective-permute-start = (f32[3,16,256]{2,1,0:T(8,128)S(1)}, f32[3,16,256]{2,1,0:T(8,128)S(1)}, u32[]{:S(2)}, u32[]{:S(2)}) collective-permute-start(f32[3,16,256]{2,1,0:T(8,128)S(1)} %get-tuple-element.26), channel_id=1, source_target_pairs={{0,4},{8,12},{16,20},{24,28},{4,0},{12,8},{20,16},{28,24},{1,5},{9... | collective-permute-start | bytes 147464 | tf_op jit(solution)/shard_map/ppermute | solution.py:731
  5.3 4.0 %collective-permute-start.1 = (f32[3,16,256]{2,1,0:T(8,128)S(1)}, f32[3,16,256]{2,1,0:T(8,128)S(1)}, u32[]{:S(2)}, u32[]{:S(2)}) collective-permute-start(f32[3,16,256]{2,1,0:T(8,128)S(1)} %get-tuple-element.27), channel_id=1, source_target_pairs={{4,8},{12,16},{20,24},{8,4},{16,12},{24,20},{5,9},{13,17},{21,25},... | collective-permute-start | bytes 147464 | tf_op jit(solution)/shard_map/ppermute | solution.py:730
  6.0 4.7 %collective-permute-start.2 = (f32[3,16,256]{2,1,0:T(8,128)S(1)}, f32[3,16,256]{2,1,0:T(8,128)S(1)}, u32[]{:S(2)}, u32[]{:S(2)}) collective-permute-start(f32[3,16,256]{2,1,0:T(8,128)S(1)} %get-tuple-element.28), channel_id=1, source_target_pairs={{0,1},{2,3},{1,0},{3,2},{4,5},{6,7},{5,4},{7,6},{8,9},{10,11},{9,8... | collective-permute-start | bytes 147464 | tf_op jit(solution)/shard_map/ppermute | solution.py:728
  8.6 2.1 %collective-permute-start.3 = (f32[3,16,256]{2,1,0:T(8,128)S(1)}, f32[3,16,256]{2,1,0:T(8,128)S(1)}, u32[]{:S(2)}, u32[]{:S(2)}) collective-permute-start(f32[3,16,256]{2,1,0:T(8,128)S(1)} %get-tuple-element.29), channel_id=1, source_target_pairs={{1,2},{2,1},{5,6},{6,5},{9,10},{10,9},{13,14},{14,13},{17,18},{18,... | collective-permute-start | bytes 147464 | tf_op jit(solution)/shard_map/ppermute | solution.py:729
  13.4 26.1 %all-to-all-start = ((f32[32,24,128]{2,1,0:T(8,128)}), f32[32,24,128]{2,1,0:T(8,128)S(1)}, u32[]{:S(2)}, u32[]{:S(2)}) async-start(f32[32,24,128]{2,1,0:T(8,128)} %payload.1), calls=%async_computation | async-start | bytes 786432 | tf_op jit(solution)/shard_map/all_to_all | solution.py:747
  24.0 12.7 %collective-permute-start.4 = (f32[40,8,128]{2,1,0:T(8,128)S(1)}, f32[40,8,128]{2,1,0:T(8,128)S(1)}, u32[]{:S(2)}, u32[]{:S(2)}) collective-permute-start(f32[40,8,128]{2,1,0:T(8,128)S(1)} %get-tuple-element.32), channel_id=1, source_target_pairs={{0,1},{2,3},{1,0},{3,2},{4,5},{6,7},{5,4},{7,6},{8,9},{10,11},{9,8... | collective-permute-start | bytes 491528 | tf_op jit(solution)/shard_map/ppermute | solution.py:740
  25.9 10.9 %collective-permute-start.5 = (f32[40,8,128]{2,1,0:T(8,128)S(1)}, f32[40,8,128]{2,1,0:T(8,128)S(1)}, u32[]{:S(2)}, u32[]{:S(2)}) collective-permute-start(f32[40,8,128]{2,1,0:T(8,128)S(1)} %get-tuple-element.33), channel_id=1, source_target_pairs={{1,2},{2,1},{5,6},{6,5},{9,10},{10,9},{13,14},{14,13},{17,18},{18,... | collective-permute-start | bytes 491528 | tf_op jit(solution)/shard_map/ppermute | solution.py:741
  38.2 5.6 %collective-permute-start.6 = (f32[56,8,128]{2,1,0:T(8,128)}, f32[56,8,128]{2,1,0:T(8,128)S(1)}, u32[]{:S(2)}, u32[]{:S(2)}) collective-permute-start(f32[56,8,128]{2,1,0:T(8,128)} %get-tuple-element.35), channel_id=1, source_target_pairs={{0,4},{8,12},{16,20},{24,28},{4,0},{12,8},{20,16},{28,24},{1,5},{9... | collective-permute-start | bytes 688136 | tf_op jit(solution)/shard_map/ppermute | solution.py:755
  38.2 5.6 %collective-permute-start.7 = (f32[56,8,128]{2,1,0:T(8,128)}, f32[56,8,128]{2,1,0:T(8,128)}, u32[]{:S(2)}, u32[]{:S(2)}) collective-permute-start(f32[56,8,128]{2,1,0:T(8,128)} %get-tuple-element.36), channel_id=1, source_target_pairs={{4,8},{12,16},{20,24},{8,4},{16,12},{24,20},{5,9},{13,17},{21,25},... | collective-permute-start | bytes 688136 | tf_op jit(solution)/shard_map/ppermute | solution.py:754
  46.1 0.9 %copy-start.2 = (f32[7,16,16,128]{3,2,1,0:T(8,128)}, f32[7,16,16,128]{3,2,1,0:T(8,128)S(1)}, u32[]{:S(2)}) copy-start(f32[7,16,16,128]{3,2,1,0:T(8,128)S(1)} %get-tuple-element.40.state) | copy-start | bytes 2752516
  47.1 18.4 %all-to-all-start.1 = ((f32[32,8,128]{2,1,0:T(8,128)}), f32[32,8,128]{2,1,0:T(8,128)S(1)}, u32[]{:S(2)}, u32[]{:S(2)}) async-start(f32[32,8,128]{2,1,0:T(8,128)} %get-tuple-element.38), calls=%async_computation.1 | async-start | bytes 262144 | tf_op jit(solution)/shard_map/all_to_all | solution.py:772
  57.0 1.0 %copy-start.1 = (f32[16,16,256]{2,1,0:T(8,128)S(1)}, f32[16,16,256]{2,1,0:T(8,128)}, u32[]{:S(2)}) copy-start(f32[16,16,256]{2,1,0:T(8,128)} %potential.3) | copy-start | bytes 786436
  65.4 1.2 %copy-start.3 = (f32[7,16,16,128]{3,2,1,0:T(8,128)S(1)}, f32[7,16,16,128]{3,2,1,0:T(8,128)}, u32[]{:S(2)}) copy-start(f32[7,16,16,128]{3,2,1,0:T(8,128)} %copy-done.2) | copy-start | bytes 2752516

commit v3 on v2

--- a/solution.py
+++ b/solution.py
@@ -55,6 +55,14 @@
 
 def upper(x, axis, stride=1):
     return pltpu.roll(x, x.shape[axis] - stride, axis)
+
+
+def split(plane, out, at):
+    for tile in range(plane.shape[0] // 8):
+        for piece in range(plane.shape[1] // LANES):
+            out[at] = plane[tile * 8 : tile * 8 + 8, piece * LANES : (piece + 1) * LANES]
+            at += 1
+    return at
 
 
 def as_float(condition):
@@ -105,13 +113,12 @@
 
 def residual_kernel(
     place, source, potential, material, inner, outer, even, odd,
-    residual, coarse, strip_even, strip_odd,
+    residual, coarse, strip_inner, strip_outer,
     wide, narrow, y_faces,
 ):
     low_x, low_y = place[0] == 1, place[1] == 1
     count, rows, depth = source.shape
     c1, r1 = count // 2, rows // 2
-    pieces = depth // LANES
 
     def ordered(flag, a, b):
         return jnp.where(flag, a, b), jnp.where(flag, b, a)
@@ -159,23 +166,23 @@
         else:
             wide[at : at + rows] = kept_left + left
             wide[c1 * rows + at : c1 * rows + at + rows] = kept_a + a
-        low = jnp.concatenate([left[:4], a[:4]], axis=0)
-        high = jnp.concatenate([left[rows - 4 :], a[rows - 4 :]], axis=0)
-        for ref, strip in ((strip_even, jnp.where(low_y, low, high)), (strip_odd, jnp.where(low_y, high, low))):
-            for piece in range(pieces):
-                ref[i * pieces + piece] = strip[:, piece * LANES : (piece + 1) * LANES]
     base = 2 * c1 * rows
     for n, both in enumerate((x_low[1] + x_low[2], x_high[1] + x_high[2], y_low[1] + y_low[2], y_high[1] + y_high[2])):
         wide[base + n * rows : base + (n + 1) * rows] = both
     narrow[...] = select(wide[...], pair_matrix(depth)) * 0.125
     half = narrow.shape[0] // 2
     coarse[...] = narrow[pl.ds(0, half, 2)] + narrow[pl.ds(1, half, 2)]
-    for k in range(c1):
-        s, m = coarse[k * r1 : (k + 1) * r1], coarse[(c1 + k) * r1 : (c1 + k + 1) * r1]
-        low = jnp.concatenate([s[:4], m[:4]], axis=0)
-        high = jnp.concatenate([s[r1 - 4 :], m[r1 - 4 :]], axis=0)
-        strip_even[count * pieces + k] = jnp.where(low_y, low, high)
-        strip_odd[count * pieces + k] = jnp.where(low_y, high, low)
+    for strip, flag in ((strip_inner, low_x), (strip_outer, jnp.logical_not(low_x))):
+        at = 0
+        for ref, planes in ((residual, 3), (material, 4)):
+            start = jnp.where(flag, 0, count - planes)
+            for k in range(planes):
+                at = split(ref[start + k], strip, at)
+        for first_row, planes in ((0, 3), (c1 * r1, 4)):
+            for k in range(planes):
+                low, high = first_row + k * r1, first_row + (c1 - planes + k) * r1
+                strip[at] = jnp.where(flag, coarse[low : low + r1], coarse[high : high + r1])
+                at += 1
 
 
 def payload_kernel(c1, r1, coarse, payload, wide, narrow):
@@ -231,73 +238,91 @@
     payload[...] = jnp.broadcast_to(block[None], payload.shape)
 
 
-def strips_kernel(place, residual, material, coarse, even, odd, inner, outer, long):
+def fine_planes(rows, depth):
+    return (rows // 8) * (depth // LANES)
+
+
+def level1_place(k, count, r1):
+    return count + 8 + k // 4, slice(k % 4 // 2 * r1, (k % 4 // 2 + 1) * r1), slice(k % 2 * LANES, (k % 2 + 1) * LANES)
+
+
+def strips_kernel(place, residual, material, coarse, inner, outer, even, odd, long):
     low_x, low_y = place[0] == 1, place[1] == 1
     count, rows, depth = residual.shape
     pieces = depth // LANES
     c1, r1 = count // 2, rows // 2
-    base = count * pieces
-
-    def sides(at):
-        a, b = even[at], odd[at]
-        return jnp.where(low_y, a, b), jnp.where(low_y, b, a)
-
-    for i in range(count):
+    both = (inner, outer)
+    empty = jnp.zeros((rows, depth), F32)
+    long[0, 0] = empty
+    long[0, count + 7] = empty
+    per = fine_planes(rows, depth)
+
+    def fetch(flag, at):
+        return jnp.where(flag, both[0][at], both[1][at])
+
+    for n, ref in enumerate((residual, material)):
+        for k in range(count):
+            long[n, 4 + k] = ref[k]
+    nothing = jnp.zeros((r1, LANES), F32)
+    for k in (0, c1 + 7):
+        plane, y, z = level1_place(k, count, r1)
+        long[0, plane, y, z] = nothing
+    for n in range(2):
+        for k in range(c1):
+            plane, y, z = level1_place(k + 4, count, r1)
+            at = (n * c1 + k) * r1
+            long[n, plane, y, z] = coarse[at : at + r1]
+    for flag, starts, starts1 in (
+        (low_x, (1, 0), (1, 0)),
+        (jnp.logical_not(low_x), (count + 4, count + 4), (c1 + 4, c1 + 4)),
+    ):
+        at = 0
+        for n, planes in enumerate((3, 4)):
+            for k in range(planes):
+                for tile in range(rows // 8):
+                    for piece in range(pieces):
+                        z = slice(piece * LANES, (piece + 1) * LANES)
+                        long[n, starts[n] + k, tile * 8 : tile * 8 + 8, z] = fetch(flag, at)
+                        at += 1
+        for n, planes in enumerate((3, 4)):
+            for k in range(planes):
+                plane, y, z = level1_place(starts1[n] + k, count, r1)
+                long[n, plane, y, z] = fetch(flag, at)
+                at += 1
+
+    def send(at, a, b):
+        last = a.shape[0] - 4
+        low = jnp.concatenate([a[:4], b[:4]], axis=0)
+        high = jnp.concatenate([a[last:], b[last:]], axis=0)
+        even[at] = jnp.where(low_y, low, high)
+        odd[at] = jnp.where(low_y, high, low)
+
+    for i in range(count + 8):
         for piece in range(pieces):
-            low, high = sides(i * pieces + piece)
             z = slice(piece * LANES, (piece + 1) * LANES)
-            long[0, i, :, z] = jnp.concatenate([low[:4], residual[i, :, z], high[:4]], axis=0)
-            long[1, i, :, z] = jnp.concatenate([low[4:], material[i, :, z], high[4:]], axis=0)
-    for k in range(c1):
-        low, high = sides(base + k)
-        s, m = coarse[k * r1 : (k + 1) * r1], coarse[(c1 + k) * r1 : (c1 + k + 1) * r1]
-        i, z = count + k // 2, slice(k % 2 * LANES, (k % 2 + 1) * LANES)
-        long[0, i, : r1 + 8, z] = jnp.concatenate([low[:4], s, high[:4]], axis=0)
-        long[1, i, : r1 + 8, z] = jnp.concatenate([low[4:], m, high[4:]], axis=0)
-
-    def pack(out, flag):
-        at = 0
-        for n, planes in ((0, 3), (1, 4)):
-            start = jnp.where(flag, 0, count - planes)
-            for k in range(planes):
-                for tile in range((rows + 8) // 8):
-                    for piece in range(pieces):
-                        out[at] = long[n, start + k, tile * 8 : tile * 8 + 8, piece * LANES : (piece + 1) * LANES]
-                        at += 1
-        for n, planes in ((0, 3), (1, 4)):
-            for k in range(planes):
-                low, high = k, c1 - planes + k
-                for tile in range((r1 + 8) // 8):
-                    y = slice(tile * 8, tile * 8 + 8)
-                    a = long[n, count + low // 2, y, low % 2 * LANES : (low % 2 + 1) * LANES]
-                    b = long[n, count + high // 2, y, high % 2 * LANES : (high % 2 + 1) * LANES]
-                    out[at] = jnp.where(flag, a, b)
-                    at += 1
-
-    pack(inner, low_x)
-    pack(outer, jnp.logical_not(low_x))
-
-
-def unpack(source, flag, out, start, planes, tiles, pieces, at):
-    for n in range(planes):
-        for tile in range(tiles):
-            for piece in range(pieces):
-                value = jnp.where(flag, source[0][at], source[1][at])
-                out[start + n, tile * 8 : tile * 8 + 8, piece * LANES : (piece + 1) * LANES] = value
-                at += 1
-    return at
-
-
-def smooth_kernel(ends, place, potential, long, inner, outer, out, mat, res, x, d, fx, fy, fz, inv):
-    low_x = place[0] == 1
+            send(i * pieces + piece, long[0, i, :, z], long[1, i, :, z])
+    for k in range(c1 + 8):
+        plane, y, z = level1_place(k, count, r1)
+        send((count + 8) * pieces + k, long[0, plane, y, z], long[1, plane, y, z])
+
+
+def extend(low_y, even, odd, at, a, b):
+    first, second = even[at], odd[at]
+    low, high = jnp.where(low_y, first, second), jnp.where(low_y, second, first)
+    return jnp.concatenate([low[:4], a, high[:4]], axis=0), jnp.concatenate([low[4:], b, high[4:]], axis=0)
+
+
+def smooth_kernel(ends, place, potential_far, long, even, odd, out, mat, res, x, d, fx, fy, fz, inv, potential, semaphore):
+    arriving = pltpu.make_async_copy(potential_far, potential, semaphore)
+    arriving.start()
+    low_y = place[1] == 1
     count, rows, depth = potential.shape
-    pieces, tiles = depth // LANES, (rows + 8) // 8
-    both = (inner, outer)
-    for flag, start_r, start_m in ((low_x, 1, 0), (jnp.logical_not(low_x), count + 4, count + 4)):
-        at = unpack(both, flag, res, start_r, 3, tiles, pieces, 0)
-        unpack(both, flag, mat, start_m, 4, tiles, pieces, at)
-    res[pl.ds(4, count)] = long[0, :count]
-    mat[pl.ds(4, count)] = long[1, :count]
+    pieces = depth // LANES
+    for i in range(count + 8):
+        for piece in range(pieces):
+            z = slice(piece * LANES, (piece + 1) * LANES)
+            at = i * pieces + piece
+            res[i, :, z], mat[i, :, z] = extend(low_y, even, odd, at, long[0, i, :, z], long[1, i, :, z])
     total, length = count + 8, rows + 8
     row, lane = iota((length, depth), 0), iota((length, depth), 1)
     outside = as_float(lane == 0) + as_float(lane == depth - 1)
@@ -327,6 +352,8 @@
     lax.fori_loop(0, (total - 2) // step, lambda n, f: weigh(1 + n * step, step, f), first)
     rho = 1.0 / SIGMA
     for turn in range(DEG - 1):
+        if turn == DEG - 2:
+            arriving.wait()
         following = 1.0 / (2.0 * SIGMA - rho)
         old, new = turn % 2, (turn + 1) % 2
         keep, gain = following * rho, 2.0 * following / DELTA
@@ -569,20 +596,15 @@
     out[...] = jnp.broadcast_to(v, (planes, 2, 2 * rows, LANES)).reshape(2 * planes, 2 * rows, LANES)
 
 
-def level1_kernel(offset, place, long, inner, outer, window1, payload, state, src, mat, flat, prolonged, wide, narrow):
-    low_x = place[0] == 1
+def level1_kernel(place, long, even, odd, window1, payload, state_far, src, mat, flat, prolonged, wide, narrow, state, semaphore):
+    low_y = place[1] == 1
     total, length, depth = src.shape
     count, rows = total - 8, length - 8
-    both = (inner, outer)
+    base = (long.shape[1] - total // 4) * (long.shape[3] // LANES)
     zero = jnp.zeros((length, depth), F32)
-    src[0] = zero
-    src[total - 1] = zero
-    for flag, start_s, start_m in ((low_x, 1, 0), (jnp.logical_not(low_x), count + 4, count + 4)):
-        at = unpack(both, flag, src, start_s, 3, length // 8, 1, offset)
-        unpack(both, flag, mat, start_m, 4, length // 8, 1, at)
-    for n, ref in enumerate((src, mat)):
-        for k in range(count):
-            ref[4 + k] = long[n, 2 * count + k // 2, :length, k % 2 * LANES : (k % 2 + 1) * LANES]
+    for k in range(total):
+        plane, y, z = level1_place(k, 2 * count, rows)
+        src[k], mat[k] = extend(low_y, even, odd, base + k, long[0, plane, y, z], long[1, plane, y, z])
     raise_window(window1, flat, prolonged)
     a = mat[...]
     lane = iota(a.shape, 2)
@@ -605,17 +627,22 @@
     e2 = DAMPING * inverse * s2
     t = KEPT * s2 + apply_off(e2, w_x, w_y, w_z)
     state[4], state[5], state[6] = c, s2, e2
+    leaving = pltpu.make_async_copy(state, state_far, semaphore)
+    leaving.start()
     own = t[4 : 4 + count, 4 : 4 + rows].reshape(count // 2, 2, rows, depth)
     wide[...] = (own[:, 0] + own[:, 1]).reshape(count // 2 * rows, depth)
     part = count // 4 * rows
     narrow[...] = (select(wide[:part], pair_matrix(depth)) + select(wide[part:], pair_matrix(depth, LANES // 2))) * 0.125
     block = narrow[pl.ds(0, part // 2, 2)] + narrow[pl.ds(1, part // 2, 2)]
     payload[...] = jnp.broadcast_to(block[None], payload.shape)
-
-
-def last_cycle_kernel(counts, bases, grid, c2, r2, place, blocks, table, state, partial, out, *scratch):
+    leaving.wait()
+
+
+def last_cycle_kernel(counts, bases, grid, c2, r2, place, blocks, table, state_far, partial, out, *scratch):
     s, e, t, pad = scratch[0:3], list(scratch[3:6]), scratch[6], scratch[7]
-    view, flat, prolonged, tall = scratch[8:12]
+    view, flat, prolonged, tall, state, semaphore = scratch[8:14]
+    arriving = pltpu.make_async_copy(state_far, state, semaphore)
+    arriving.start()
     gx, gy = grid
     half = LANES // 2
     valid = iota((c2 // 2 * r2, LANES), 1) < half
@@ -634,6 +661,7 @@
     raise_window(view, flat, prolonged)
     count, rows, depth = partial.shape
     c1, r1 = count // 2, rows // 2
+    arriving.wait()
     near = slice(3, c1 + 5)
     own = slice(4, 4 + c1)
     v = state[6, near] + prolonged[near]
@@ -664,7 +692,9 @@
 
     def held(n, x):
         nonlocal streamed
-        if x.ndim == 1 or n in apart:
+        if n in apart:
+            return pltpu.with_memory_space_constraint(x, pltpu.HBM)
+        if x.ndim == 1:
             return x
         if size_of(x.shape) <= HELD:
             return pltpu.with_memory_space_constraint(x, pltpu.VMEM)
@@ -676,23 +706,28 @@
         if isinstance(shape, jax.ShapeDtypeStruct):
             streamed += size_of(shape.shape)
             return shape
+        if far(shape):
+            return pltpu.HBM(shape[1], F32)
         if size_of(shape) <= HELD:
             return pltpu.VMEM(shape, F32)
         streamed += size_of(shape)
         return jax.ShapeDtypeStruct(shape, F32)
 
+    def far(x):
+        return isinstance(x, tuple) and x[0] == "far"
+
     def space(n, x):
-        return pl.ANY if n in apart else pltpu.SMEM if x.ndim == 1 else pltpu.VMEM
+        return pltpu.HBM if n in apart else pltpu.SMEM if x.ndim == 1 else pltpu.VMEM
 
     specs = [pl.BlockSpec(memory_space=space(n, x)) for n, x in enumerate(inputs)]
     inputs = [held(n, x) for n, x in enumerate(inputs)]
     results = [result(shape) for shape in outputs]
-    need = streamed + sum(size_of(x.shape) for x in scratch if len(x.shape) > 1) + 3 * MIB
+    need = streamed + sum(size_of(x.shape) for x in scratch if len(getattr(x, "shape", ())) > 1) + 3 * MIB
     return pl.pallas_call(
         kernel,
         out_shape=results,
         in_specs=specs,
-        out_specs=[pl.BlockSpec(memory_space=pltpu.VMEM) for _ in outputs],
+        out_specs=[pl.BlockSpec(memory_space=pltpu.HBM if far(x) else pltpu.VMEM) for x in outputs],
         scratch_shapes=list(scratch),
         compiler_params=pltpu.CompilerParams(vmem_limit_bytes=max(need, 8 * MIB)),
         name=name,
@@ -730,29 +765,28 @@
     outer = lax.ppermute(outer, "gx", swap_x[1])
     inner = lax.ppermute(inner, "gx", swap_x[0])
 
-    strip = (count * pieces + c1, 8, LANES)
+    strip = (7 * fine_planes(rows, depth) + 7, 8, LANES)
     total = 2 * c1 * rows + 4 * rows
-    residual, coarse, even, odd = call(
+    residual, coarse, inner, outer = call(
         residual_kernel, "residual", (place, source_here, potential_here, material, inner, outer, even, odd),
         (brick, (total // 2, LANES), strip, strip),
         (VM(total, depth), VM(total, LANES), VM(4, count, depth)),
     )
-    even = lax.ppermute(even, "gy", swap_y[0])
-    odd = lax.ppermute(odd, "gy", swap_y[1])
+    outer = lax.ppermute(outer, "gx", swap_x[1])
+    inner = lax.ppermute(inner, "gx", swap_x[0])
     small = c2 * r1 + 2 * r1
     (payload,) = call(
         functools.partial(payload_kernel, c1, r1), "payload", (coarse,), ((devices, c2 * r2 + 2 * r2, LANES),),
         (VM(2, small, d1), VM(small, LANES)),
     )
     blocks = lax.all_to_all(payload, ("gx", "gy"), 0, 0)
-    tiles, tiles1 = (rows + 8) // 8, (r1 + 8) // 8
-    strip = (7 * tiles * pieces + 7 * tiles1, 8, LANES)
-    inner, outer, long = call(
-        strips_kernel, "strips", (place, residual, material, coarse, even, odd),
-        (strip, strip, (2, count + c1 // 2, rows + 8, depth)),
+    strip = ((count + 8) * pieces + c1 + 8, 8, LANES)
+    even, odd, long = call(
+        strips_kernel, "strips", (place, residual, material, coarse, inner, outer),
+        (strip, strip, (2, count + 8 + (c1 + 8) // 4, rows, depth)),
     )
-    outer = lax.ppermute(outer, "gx", swap_x[1])
-    inner = lax.ppermute(inner, "gx", swap_x[0])
+    even = lax.ppermute(even, "gy", swap_y[0])
+    odd = lax.ppermute(odd, "gy", swap_y[1])
 
     counts = tuple(gx * c2 // k for k in (1, 2, 4))
     bases = (0, counts[0] + 1, counts[0] + counts[1] + 2)
@@ -765,20 +799,28 @@
     frame = (c1 + 8, r1 + 8, d1)
     flat = VM((c2 + 4) * (r2 + 4) * 2, LANES)
     payload, state = call(
-        functools.partial(level1_kernel, 7 * tiles * pieces), "level1", (place, long, inner, outer, window1),
-        ((devices, c2 // 2 * r2, LANES), (7, *frame)),
-        (VM(*frame), VM(*frame), flat, VM(*frame), VM(c1 // 2 * r1, d1), VM(c1 // 4 * r1, LANES)),
+        level1_kernel, "level1", (place, long, even, odd, window1),
+        ((devices, c2 // 2 * r2, LANES), ("far", (7, *frame))),
+        (
+            VM(*frame), VM(*frame), flat, VM(*frame), VM(c1 // 2 * r1, d1), VM(c1 // 4 * r1, LANES), VM(7, *frame),
+            pltpu.SemaphoreType.DMA,
+        ),
     )
     blocks = lax.all_to_all(payload, ("gx", "gy"), 0, 0)
     wide = (count + 8, rows + 8, depth)
     (partial,) = call(
-        functools.partial(smooth_kernel, (gx, gy)), "smooth", (place, potential, long, inner, outer), (brick,),
-        (VM(*wide), VM(*wide), VM(2, *wide), VM(*wide), VM(count + 9, rows + 8, depth), VM(*wide), VM(*wide), VM(*wide)),
+        functools.partial(smooth_kernel, (gx, gy)), "smooth", (place, potential, long, even, odd), (brick,),
+        (
+            VM(*wide), VM(*wide), VM(2, *wide), VM(*wide), VM(count + 9, rows + 8, depth), VM(*wide), VM(*wide), VM(*wide),
+            VM(*brick), pltpu.SemaphoreType.DMA,
+        ),
+        apart=(1,),
     )
     (out,) = call(
         functools.partial(last_cycle_kernel, counts, bases, (gx, gy), c2, r2), "cycle2",
         (place, blocks, table, state, partial), (jax.ShapeDtypeStruct(brick, F32),),
-        (*work, VM(*view), flat, VM(*frame), VM(pieces, count // 2 * rows, LANES)),
+        (*work, VM(*view), flat, VM(*frame), VM(pieces, count // 2 * rows, LANES), VM(7, *frame), pltpu.SemaphoreType.DMA),
+        apart=(3,),
     )
     return out
 

time: 70.5 us -> 61.9 us (0.88)
  local copies, waits for them, and re-layouts: 6.57 us -> 0 us
  waiting for transfers between devices: 13.1 us -> 10.1 us
  Pallas kernels: 21.2 us -> 22.8 us
    ppermute x2, waiting for transfers between devices: 11.6 us -> 1.39 us  [local(): even = lax.ppermute(even, 'gy', swap_y[0])]
    all_to_all x2, waiting for transfers between devices: 1.53 us -> 8.26 us  [local(): blocks = lax.all_to_all(payload, ('gx', 'gy'), 0, 0)]
    unnamed x14 -> x0, local copies, waits for them, and re-layouts: 6.57 us -> none
    pallas_call x8, Pallas kernels: 21.2 us -> 22.8 us  [call(): pl.pallas_call(kernel, out_shape=results, in_specs=specs, out_specs=[pl.B...]
    all_to_all x2, starting transfers between devices: 20.6 us -> 19.8 us  [local(): blocks = lax.all_to_all(payload, ('gx', 'gy'), 0, 0)]
    ppermute x2, starting transfers between devices: 1.31 us -> 2.02 us  [local(): odd = lax.ppermute(odd, 'gy', swap_y[1])]
  transfers between devices with their start and end apart: 10 -> 10, of which waited for: 3 -> 4; matrix products, arithmetic and copies ran while one was open for 0% -> 0% of each run, Pallas kernels for 17% -> 19%
where the time goes in v3:
time: 61.9 us; the launch traced here: 61.5 us
  starting transfers between devices  28.4 us (46%)
  Pallas kernels  22.8 us (37%)
  waiting for transfers between devices  10.1 us (16%)
    pallas_call x8, Pallas kernels, call(): pl.pallas_call(kernel, out_shape=results, in_specs=specs, out_specs=[pl.B...  22.8 us
    all_to_all x2, starting transfers between devices, local(): blocks = lax.all_to_all(payload, ('gx', 'gy'), 0, 0)  19.8 us
    all_to_all x2, waiting for transfers between devices, local(): blocks = lax.all_to_all(payload, ('gx', 'gy'), 0, 0)  8.26 us
    ppermute x2, starting transfers between devices, local(): even = lax.ppermute(even, 'gy', swap_y[0])  4.43 us
    ppermute x2, starting transfers between devices, local(): odd = lax.ppermute(odd, 'gy', swap_y[1])  2.02 us
    ppermute x2, waiting for transfers between devices, local(): even = lax.ppermute(even, 'gy', swap_y[0])  1.39 us
    ppermute x2, starting transfers between devices, local(): outer = lax.ppermute(outer, 'gx', swap_x[1])  1.31 us
  transfers between devices with their start and end apart: 10, of which 4 were waited for; matrix products, arithmetic and copies ran while one was open for 0% of the time, Pallas kernels for 19%

profile of v3, /device:TPU:0, one launch (start us, length us, event | category | flops | bytes accessed | tf_op | source)
XLA Modules:
  0.0 61.5 jit_solution(17722712374759469805)
XLA Ops:
  0.0 0.1 pad_add_fusion.place
  0.1 1.7 %faces.1 = (f32[16,16,256]{2,1,0:T(8,128)S(1)}, f32[16,16,256]{2,1,0:T(8,128)S(1)}, f32[16,16,256]{2,1,0:T(8,128)S(1)}, f32[3,16,256]{2,1,0:T(8,128)S(1)}, f32[3...) custom-call(s32[4]{0:T(128)S(1)} %pad_add_fusion.place, f32[3]{0:T(128)} %permeability.1, ...), custom_call_target="tpu_custom_call" | custom-call | tf_op jit(solution)/shard_map/faces/pallas_call | solution.py:726
  1.8 0.5 collective-permute-start
  2.3 0.7 %collective-permute-start.1 = (f32[3,16,256]{2,1,0:T(8,128)S(1)}, f32[3,16,256]{2,1,0:T(8,128)S(1)}, u32[]{:S(2)}, u32[]{:S(2)}) collective-permute-start(f32[3,16,256]{2,1,0:T(8,128)S(1)} %get-tuple-element.27), channel_id=1, source_target_pairs={{4,8},{12,16},{20,24},{8,4},{16,12},{24,20},{5,9},{13,17},{21,25},... | collective-permute-start | bytes 147464 | tf_op jit(solution)/shard_map/ppermute | solution.py:765
  2.9 2.7 %collective-permute-start.2 = (f32[3,16,256]{2,1,0:T(8,128)S(1)}, f32[3,16,256]{2,1,0:T(8,128)S(1)}, u32[]{:S(2)}, u32[]{:S(2)}) collective-permute-start(f32[3,16,256]{2,1,0:T(8,128)S(1)} %get-tuple-element.28), channel_id=1, source_target_pairs={{0,1},{2,3},{1,0},{3,2},{4,5},{6,7},{5,4},{7,6},{8,9},{10,11},{9,8... | collective-permute-start | bytes 147464 | tf_op jit(solution)/shard_map/ppermute | solution.py:763
  5.6 0.7 %collective-permute-start.3 = (f32[3,16,256]{2,1,0:T(8,128)S(1)}, f32[3,16,256]{2,1,0:T(8,128)S(1)}, u32[]{:S(2)}, u32[]{:S(2)}) collective-permute-start(f32[3,16,256]{2,1,0:T(8,128)S(1)} %get-tuple-element.29), channel_id=1, source_target_pairs={{1,2},{2,1},{5,6},{6,5},{9,10},{10,9},{13,14},{14,13},{17,18},{18,... | collective-permute-start | bytes 147464 | tf_op jit(solution)/shard_map/ppermute | solution.py:764
  6.3 0.0 collective-permute-done.inner
  6.3 0.0 collective-permute-done.1.outer
  6.3 1.4 %collective-permute-done.2.even = f32[3,16,256]{2,1,0:T(8,128)S(1)} collective-permute-done((f32[3,16,256]{2,1,0:T(8,128)S(1)}, f32[3,16,256]{2,1,0:T(8,128)S(1)}, u32[]{:S(2)}, u32[]{:S(2)}) %collective-permute-start.2) | collective-permute-done | bytes 49184 | tf_op jit(solution)/shard_map/ppermute | solution.py:763
  7.7 0.0 collective-permute-done.3.odd
  7.7 1.5 %residual.1 = (f32[16,16,256]{2,1,0:T(8,128)S(1)}, f32[160,128]{1,0:T(8,128)S(1)}, f32[35,8,128]{2,1,0:T(8,128)S(1)}, f32[35,8,128]{2,1,0:T(8,128)S(1)}) custom-call(s32[4]{0:T(128)S(1)} %pad_add_fusion.place, f32[16,16,256]{2,1,0:T(8,128)S(1)} %get-tuple-element.23.source, f32[16,16,256]{2,1,0:T(8,128)S(1)} %get-tuple-element.24.potential, ...), custom_call_target="tpu_custom_call" | custom-call | tf_op jit(solution)/shard_map/residual/pallas_call | solution.py:726
  9.2 1.2 %payload.1 = f32[32,24,128]{2,1,0:T(8,128)} custom-call(f32[160,128]{1,0:T(8,128)S(1)} %get-tuple-element.31.coarse), custom_call_target="tpu_custom_call" | custom-call | tf_op jit(solution)/shard_map/payload/pallas_call | solution.py:726
  10.4 10.6 %all-to-all-start = ((f32[32,24,128]{2,1,0:T(8,128)}), f32[32,24,128]{2,1,0:T(8,128)S(1)}, u32[]{:S(2)}, u32[]{:S(2)}) async-start(f32[32,24,128]{2,1,0:T(8,128)} %payload.1), calls=%async_computation | async-start | bytes 786432 | tf_op jit(solution)/shard_map/all_to_all | solution.py:782
  21.0 0.3 collective-permute-start.4
  21.3 0.7 %collective-permute-start.5 = (f32[35,8,128]{2,1,0:T(8,128)S(1)}, f32[35,8,128]{2,1,0:T(8,128)S(1)}, u32[]{:S(2)}, u32[]{:S(2)}) collective-permute-start(f32[35,8,128]{2,1,0:T(8,128)S(1)} %get-tuple-element.33), channel_id=1, source_target_pairs={{4,8},{12,16},{20,24},{8,4},{16,12},{24,20},{5,9},{13,17},{21,25},... | collective-permute-start | bytes 430088 | tf_op jit(solution)/shard_map/ppermute | solution.py:775
  22.0 0.4 collective-permute-done.4.inner
  22.4 0.0 collective-permute-done.5.outer
  22.4 1.4 %strips.1 = (f32[64,8,128]{2,1,0:T(8,128)}, f32[64,8,128]{2,1,0:T(8,128)}, f32[2,28,16,256]{3,2,1,0:T(8,128)S(1)}) custom-call(s32[4]{0:T(128)S(1)} %pad_add_fusion.place, f32[16,16,256]{2,1,0:T(8,128)S(1)} %get-tuple-element.30.residual, f32[16,16,256]{2,1,0:T(8,128)S(1)} %get-tuple-element.25.material, f32[160,128]{1,0:T(8,128)S(1)} %get-tuple-element.31.coarse, ...), custom_call_target="tpu_custom_call" | custom-call | tf_op jit(solution)/shard_map/strips/pallas_call | solution.py:726
  23.9 1.8 %collective-permute-start.6 = (f32[64,8,128]{2,1,0:T(8,128)}, f32[64,8,128]{2,1,0:T(8,128)S(1)}, u32[]{:S(2)}, u32[]{:S(2)}) collective-permute-start(f32[64,8,128]{2,1,0:T(8,128)} %get-tuple-element.35), channel_id=1, source_target_pairs={{0,1},{2,3},{1,0},{3,2},{4,5},{6,7},{5,4},{7,6},{8,9},{10,11},{9,8... | collective-permute-start | bytes 786440 | tf_op jit(solution)/shard_map/ppermute | solution.py:788
  25.6 1.4 %collective-permute-start.7 = (f32[64,8,128]{2,1,0:T(8,128)}, f32[64,8,128]{2,1,0:T(8,128)}, u32[]{:S(2)}, u32[]{:S(2)}) collective-permute-start(f32[64,8,128]{2,1,0:T(8,128)} %get-tuple-element.36), channel_id=1, source_target_pairs={{1,2},{2,1},{5,6},{6,5},{9,10},{10,9},{13,14},{14,13},{17,18},{18,... | collective-permute-start | bytes 786440 | tf_op jit(solution)/shard_map/ppermute | solution.py:789
  27.0 5.8 %all-to-all-done.blocks = f32[32,24,128]{2,1,0:T(8,128)S(1)} async-done(((f32[32,24,128]{2,1,0:T(8,128)}), f32[32,24,128]{2,1,0:T(8,128)S(1)}, u32[]{:S(2)}, u32[]{:S(2)}) %all-to-all-start) | async-done | bytes 393248 | tf_op jit(solution)/shard_map/all_to_all | solution.py:782
  32.8 4.3 %cycle1.1 = (f32[8,8,128]{2,1,0:T(8,128)S(1)}, f32[4,59,16,128]{3,2,1,0:T(8,128)S(1)}) custom-call(s32[4]{0:T(128)S(1)} %pad_add_fusion.place, f32[32,24,128]{2,1,0:T(8,128)S(1)} %all-to-all-done.blocks), custom_call_target="tpu_custom_call" | custom-call | tf_op jit(solution)/shard_map/cycle1/pallas_call | solution.py:726
  37.1 0.0 collective-permute-done.6.even
  37.1 0.0 collective-permute-done.7.odd
  37.1 3.4 %level1.1 = (f32[32,8,128]{2,1,0:T(8,128)}, f32[7,16,16,128]{3,2,1,0:T(8,128)}) custom-call(s32[4]{0:T(128)S(1)} %pad_add_fusion.place, f32[2,28,16,256]{3,2,1,0:T(8,128)S(1)} %get-tuple-element.34.long, f32[64,8,128]{2,1,0:T(8,128)S(1)} %collective-permute-done.6.even, f32[64,8,128]{2,1,0:T(8,128)} %collective-permute-done.7.odd, ...), custom_call_target="tpu_custom_call" | custom-call | tf_op jit(solution)/shard_map/level1/pallas_call | solution.py:726
  40.5 9.2 %all-to-all-start.1 = ((f32[32,8,128]{2,1,0:T(8,128)}), f32[32,8,128]{2,1,0:T(8,128)S(1)}, u32[]{:S(2)}, u32[]{:S(2)}) async-start(f32[32,8,128]{2,1,0:T(8,128)} %get-tuple-element.38), calls=%async_computation.1 | async-start | bytes 262144 | tf_op jit(solution)/shard_map/all_to_all | solution.py:809
  49.7 5.9 %smooth.1.partial = f32[16,16,256]{2,1,0:T(8,128)S(1)} custom-call(s32[4]{0:T(128)S(1)} %pad_add_fusion.place, f32[16,16,256]{2,1,0:T(8,128)} %potential_far.1, f32[2,28,16,256]{3,2,1,0:T(8,128)S(1)} %get-tuple-element.34.long, f32[64,8,128]{2,1,0:T(8,128)S(1)} %collective-permute-done.6.even, f32[64,8,128]{2,1,0:T(8,128)} %collective-permute-done.7.odd), custom_call_target="tpu_custom_call" | custom-call | tf_op jit(solution)/shard_map/smooth/pallas_call | solution.py:726
  55.6 2.5 %all-to-all-done.1.blocks = f32[32,8,128]{2,1,0:T(8,128)S(1)} async-done(((f32[32,8,128]{2,1,0:T(8,128)}), f32[32,8,128]{2,1,0:T(8,128)S(1)}, u32[]{:S(2)}, u32[]{:S(2)}) %all-to-all-start.1) | async-done | bytes 131104 | tf_op jit(solution)/shard_map/all_to_all | solution.py:809
  58.1 3.4 %cycle2.1 = f32[16,16,256]{2,1,0:T(8,128)} custom-call(s32[4]{0:T(128)S(1)} %pad_add_fusion.place, f32[32,8,128]{2,1,0:T(8,128)S(1)} %all-to-all-done.1.blocks, f32[4,59,16,128]{3,2,1,0:T(8,128)S(1)} %get-tuple-element.39.table, f32[7,16,16,128]{3,2,1,0:T(8,128)} %get-tuple-element.40.state_far, f32[16,16,256]{2,1,0:T(8,128)S(1)} %smooth.1.partial), custom_call_target="tpu_custom_call" | custom-call | tf_op jit(solution)/shard_map/cycle2/pallas_call | solution.py:726
Async XLA Ops:
  1.8 4.5 %collective-permute-start = (f32[3,16,256]{2,1,0:T(8,128)S(1)}, f32[3,16,256]{2,1,0:T(8,128)S(1)}, u32[]{:S(2)}, u32[]{:S(2)}) collective-permute-start(f32[3,16,256]{2,1,0:T(8,128)S(1)} %get-tuple-element.26), channel_id=1, source_target_pairs={{0,4},{8,12},{16,20},{24,28},{4,0},{12,8},{20,16},{28,24},{1,5},{9... | collective-permute-start | bytes 147464 | tf_op jit(solution)/shard_map/ppermute | solution.py:766
  2.3 4.0 %collective-permute-start.1 = (f32[3,16,256]{2,1,0:T(8,128)S(1)}, f32[3,16,256]{2,1,0:T(8,128)S(1)}, u32[]{:S(2)}, u32[]{:S(2)}) collective-permute-start(f32[3,16,256]{2,1,0:T(8,128)S(1)} %get-tuple-element.27), channel_id=1, source_target_pairs={{4,8},{12,16},{20,24},{8,4},{16,12},{24,20},{5,9},{13,17},{21,25},... | collective-permute-start | bytes 147464 | tf_op jit(solution)/shard_map/ppermute | solution.py:765
  2.9 4.7 %collective-permute-start.2 = (f32[3,16,256]{2,1,0:T(8,128)S(1)}, f32[3,16,256]{2,1,0:T(8,128)S(1)}, u32[]{:S(2)}, u32[]{:S(2)}) collective-permute-start(f32[3,16,256]{2,1,0:T(8,128)S(1)} %get-tuple-element.28), channel_id=1, source_target_pairs={{0,1},{2,3},{1,0},{3,2},{4,5},{6,7},{5,4},{7,6},{8,9},{10,11},{9,8... | collective-permute-start | bytes 147464 | tf_op jit(solution)/shard_map/ppermute | solution.py:763
  5.6 2.1 %collective-permute-start.3 = (f32[3,16,256]{2,1,0:T(8,128)S(1)}, f32[3,16,256]{2,1,0:T(8,128)S(1)}, u32[]{:S(2)}, u32[]{:S(2)}) collective-permute-start(f32[3,16,256]{2,1,0:T(8,128)S(1)} %get-tuple-element.29), channel_id=1, source_target_pairs={{1,2},{2,1},{5,6},{6,5},{9,10},{10,9},{13,14},{14,13},{17,18},{18,... | collective-permute-start | bytes 147464 | tf_op jit(solution)/shard_map/ppermute | solution.py:764
  10.4 22.4 %all-to-all-start = ((f32[32,24,128]{2,1,0:T(8,128)}), f32[32,24,128]{2,1,0:T(8,128)S(1)}, u32[]{:S(2)}, u32[]{:S(2)}) async-start(f32[32,24,128]{2,1,0:T(8,128)} %payload.1), calls=%async_computation | async-start | bytes 786432 | tf_op jit(solution)/shard_map/all_to_all | solution.py:782
  21.0 1.4 %collective-permute-start.4 = (f32[35,8,128]{2,1,0:T(8,128)S(1)}, f32[35,8,128]{2,1,0:T(8,128)S(1)}, u32[]{:S(2)}, u32[]{:S(2)}) collective-permute-start(f32[35,8,128]{2,1,0:T(8,128)S(1)} %get-tuple-element.32), channel_id=1, source_target_pairs={{0,4},{8,12},{16,20},{24,28},{4,0},{12,8},{20,16},{28,24},{1,5},{9... | collective-permute-start | bytes 430088 | tf_op jit(solution)/shard_map/ppermute | solution.py:776
  21.3 1.1 %collective-permute-start.5 = (f32[35,8,128]{2,1,0:T(8,128)S(1)}, f32[35,8,128]{2,1,0:T(8,128)S(1)}, u32[]{:S(2)}, u32[]{:S(2)}) collective-permute-start(f32[35,8,128]{2,1,0:T(8,128)S(1)} %get-tuple-element.33), channel_id=1, source_target_pairs={{4,8},{12,16},{20,24},{8,4},{16,12},{24,20},{5,9},{13,17},{21,25},... | collective-permute-start | bytes 430088 | tf_op jit(solution)/shard_map/ppermute | solution.py:775
  23.9 13.2 %collective-permute-start.6 = (f32[64,8,128]{2,1,0:T(8,128)}, f32[64,8,128]{2,1,0:T(8,128)S(1)}, u32[]{:S(2)}, u32[]{:S(2)}) collective-permute-start(f32[64,8,128]{2,1,0:T(8,128)} %get-tuple-element.35), channel_id=1, source_target_pairs={{0,1},{2,3},{1,0},{3,2},{4,5},{6,7},{5,4},{7,6},{8,9},{10,11},{9,8... | collective-permute-start | bytes 786440 | tf_op jit(solution)/shard_map/ppermute | solution.py:788
  25.6 11.5 %collective-permute-start.7 = (f32[64,8,128]{2,1,0:T(8,128)}, f32[64,8,128]{2,1,0:T(8,128)}, u32[]{:S(2)}, u32[]{:S(2)}) collective-permute-start(f32[64,8,128]{2,1,0:T(8,128)} %get-tuple-element.36), channel_id=1, source_target_pairs={{1,2},{2,1},{5,6},{6,5},{9,10},{10,9},{13,14},{14,13},{17,18},{18,... | collective-permute-start | bytes 786440 | tf_op jit(solution)/shard_map/ppermute | solution.py:789
  40.5 17.6 %all-to-all-start.1 = ((f32[32,8,128]{2,1,0:T(8,128)}), f32[32,8,128]{2,1,0:T(8,128)S(1)}, u32[]{:S(2)}, u32[]{:S(2)}) async-start(f32[32,8,128]{2,1,0:T(8,128)} %get-tuple-element.38), calls=%async_computation.1 | async-start | bytes 262144 | tf_op jit(solution)/shard_map/all_to_all | solution.py:809

commit v4 on v2

--- a/solution.py
+++ b/solution.py
@@ -63,8 +63,8 @@
 
 def faces_kernel(
     place, permeability, potential, phase, source,
-    material, pot, src, inner, outer, even, odd,
-    ids, values, semaphores,
+    material, pot, src, inner, outer, even, odd, payload,
+    ids, values, semaphores, wide, narrow, folded, narrow1, sheet,
 ):
     arriving = [
         pltpu.make_async_copy(a, b, semaphores.at[n])
@@ -80,6 +80,18 @@
     for i in range(count):
         here = ids[i]
         material[i] = jnp.where(here == 0, p0, jnp.where(here == 1, p1, p2))
+    c1, r1 = count // 2, rows // 2
+    for k in range(c1):
+        wide[k * rows : (k + 1) * rows] = material[2 * k] + material[2 * k + 1]
+    narrow[...] = select(wide[...], pair_matrix(wide.shape[1])) * 0.125
+    half = c1 * r1
+    finer = narrow[pl.ds(0, half, 2)] + narrow[pl.ds(1, half, 2)]
+    for k in range(c1 // 2):
+        folded[k * r1 : (k + 1) * r1] = finer[2 * k * r1 : (2 * k + 1) * r1] + finer[(2 * k + 1) * r1 : (2 * k + 2) * r1]
+    part = folded.shape[0] // 2
+    sheet[...] = jnp.broadcast_to(packed(folded[:part], folded[part:], narrow1)[None], sheet.shape)
+    leaving = pltpu.make_async_copy(sheet, payload, semaphores.at[4])
+    leaving.start()
     last = count - 1
     first = jnp.where(low_x, 0, last)
     second = jnp.where(low_x, 1, last - 1)
@@ -100,6 +112,7 @@
     inner[0] = pot[first]
     outer[0] = pot[last - first]
     edge(0, pot, 0, rows - 1)
+    leaving.wait()
     arriving[3].wait()
 
 
@@ -178,7 +191,7 @@
         strip_odd[count * pieces + k] = jnp.where(low_y, high, low)
 
 
-def payload_kernel(c1, r1, coarse, payload, wide, narrow):
+def payload_kernel(c1, r1, coarse, payload, wide, narrow, sheet, semaphore):
     c2 = c1 // 2
     depth = coarse.shape[1]
     s = [coarse[k * r1 : (k + 1) * r1] for k in range(c1)]
@@ -206,7 +219,7 @@
         errors.append(DAMPING * s[k] * invert(diagonal))
         tables.append((face, next_face, w_down, w_up, w_back, w_front))
         face = next_face
-    base = c2 * r1
+    base = c2 // 2 * r1
     for k in range(c1):
         e, w = errors[k], tables[k]
         t = KEPT * s[k] + w[4] * lower(e, 1) + w[5] * upper(e, 1)
@@ -215,20 +228,29 @@
             t = t + w[0] * errors[k - 1]
         if k < c1 - 1:
             t = t + w[1] * errors[k + 1]
-        at = (k // 2) * r1
+        at = k // 2 * r1
         if k % 2 == 0:
             kept = t
         else:
-            wide[0, at : at + r1] = kept + t
-            wide[1, at : at + r1] = m[k - 1] + m[k]
+            wide[at // base, at % base : at % base + r1] = kept + t
         wide[1, base + k : base + k + 1] = (w[2] * e)[:1]
         wide[1, base + r1 + k : base + r1 + k + 1] = (w[3] * e)[r1 - 1 :]
     wide[0, base : base + r1] = tables[0][0] * errors[0]
     wide[0, base + r1 : base + 2 * r1] = tables[c1 - 1][1] * errors[c1 - 1]
-    narrow[...] = (select(wide[0], pair_matrix(depth)) + select(wide[1], pair_matrix(depth, LANES // 2))) * 0.125
+    publish(wide[0], wide[1], narrow, sheet, payload, semaphore)
+
+
+def packed(low, high, narrow):
+    narrow[...] = (select(low, pair_matrix(LANES)) + select(high, pair_matrix(LANES, LANES // 2))) * 0.125
     half = narrow.shape[0] // 2
-    block = narrow[pl.ds(0, half, 2)] + narrow[pl.ds(1, half, 2)]
-    payload[...] = jnp.broadcast_to(block[None], payload.shape)
+    return narrow[pl.ds(0, half, 2)] + narrow[pl.ds(1, half, 2)]
+
+
+def publish(low, high, narrow, sheet, payload, semaphore):
+    sheet[...] = jnp.broadcast_to(packed(low, high, narrow)[None], sheet.shape)
+    leaving = pltpu.make_async_copy(sheet, payload, semaphore)
+    leaving.start()
+    leaving.wait()
 
 
 def strips_kernel(place, residual, material, coarse, even, odd, inner, outer, long):
@@ -288,7 +310,9 @@
     return at
 
 
-def smooth_kernel(ends, place, potential, long, inner, outer, out, mat, res, x, d, fx, fy, fz, inv):
+def smooth_kernel(ends, place, potential_far, long, inner, outer, out, mat, res, x, d, fx, fy, fz, inv, potential, semaphore):
+    arriving = pltpu.make_async_copy(potential_far, potential, semaphore)
+    arriving.start()
     low_x = place[0] == 1
     count, rows, depth = potential.shape
     pieces, tiles = depth // LANES, (rows + 8) // 8
@@ -327,6 +351,8 @@
     lax.fori_loop(0, (total - 2) // step, lambda n, f: weigh(1 + n * step, step, f), first)
     rho = 1.0 / SIGMA
     for turn in range(DEG - 1):
+        if turn == DEG - 2:
+            arriving.wait()
         following = 1.0 / (2.0 * SIGMA - rho)
         old, new = turn % 2, (turn + 1) % 2
         keep, gain = following * rho, 2.0 * following / DELTA
@@ -479,72 +505,84 @@
     return out + [pltpu.VMEM((c2 + 8, rows + 16, LANES), F32)]
 
 
-def first_cycle_kernel(counts, bases, grid, c2, r2, width, place, blocks, out, table, *scratch):
+def spread_blocks(blocks, out, grid, c2, r2):
+    gx, gy = grid
+    length = c2 // 2 * r2
+    low = iota((length, LANES), 1) < LANES // 2
+
+    def column(i, _):
+        for j in range(gy):
+            block = blocks[i * gy + j, :length]
+            parts = (jnp.where(low, block, 0.0), jnp.where(low, pltpu.roll(block, LANES // 2, 1), 0.0))
+            for k in range(c2):
+                n = k % (c2 // 2)
+                out[i * c2 + k + 1, j * r2 : (j + 1) * r2, :] = parts[k // (c2 // 2)][n * r2 : (n + 1) * r2]
+        return 0
+
+    lax.fori_loop(0, gx, column, 0)
+
+
+def clear_ends(refs, counts):
+    for ref, count in zip(refs, counts):
+        zero = jnp.zeros(ref.shape[1:], F32)
+        ref[0] = zero
+        ref[count + 1] = zero
+
+
+def tables_kernel(counts, bases, grid, c2, r2, width, blocks, table, *mats):
+    rows = grid[1] * r2
+    clear_ends(mats, counts)
+    spread_blocks(blocks, mats[0], grid, c2, r2)
+    for level, (count, base) in enumerate(zip(counts, bases)):
+        if level:
+
+            def coarsen(at, step):
+                shape = (step // 2, rows, LANES)
+                whole = (iota(shape, 1) % 2**level == 0) & (iota(shape, 2) % 2**level == 0)
+                mean = 0.125 * fold(mats[level - 1][pl.ds(at + 1, step)], 2 ** (level - 1))
+                mats[level][pl.ds(at // 2 + 1, step // 2)] = jnp.where(whole, mean, 0.0)
+
+            each(counts[level - 1], coarsen)
+        fill_table(mats[level], table, level, count, base, width)
+
+
+def first_cycle_kernel(counts, bases, grid, c2, r2, place, blocks, table, out, *scratch):
     s, e, t, pad = scratch[0:3], list(scratch[3:6]), scratch[6], scratch[7]
     gx, gy = grid
-    zero = jnp.zeros(t.shape[1:], F32)
-    for ref, count in zip((t, *s), (counts[0], *counts)):
-        ref[0] = zero
-        ref[count + 1] = zero
+    rows = gy * r2
     half = LANES // 2
-    rows = gy * r2
-    own = c2 * r2
+    own = c2 // 2 * r2
+    clear_ends(s, counts)
+    spread_blocks(blocks, s[0], grid, c2, r2)
     face_y = e[0]
-    edge = iota((rows, LANES), 0) % r2
-    edge = (edge == 0) | (edge == r2 - 1)
-    valid = iota((own, LANES), 1) < half
-    for n in range(counts[0] + 2):
-        face_y[n, 0:8] = jnp.zeros((8, LANES), F32)
-        face_y[n, rows - 8 : rows] = jnp.zeros((8, LANES), F32)
-
-    def column(i, _):
+    low = iota((2 * c2, LANES), 1) < half
+
+    def edges(i, _):
         for j in range(gy):
-            block = blocks[i * gy + j]
-            turned = pltpu.roll(block, half, 1)
-            values = jnp.where(valid, block[:own], 0.0)
-            materials = jnp.where(valid, turned[:own], 0.0)
-            y_faces = jnp.where(valid[: 2 * c2], turned[own:], 0.0)
+            faces = blocks[i * gy + j, own:]
+            x_faces = jnp.where(low, faces, 0.0)
+            y_faces = jnp.where(low, pltpu.roll(faces, half, 1), 0.0)
+            here = slice(j * r2, (j + 1) * r2)
+            s[0][i * c2, here, :] = s[0][i * c2, here, :] + x_faces[:r2]
+            s[0][(i + 1) * c2 + 1, here, :] = s[0][(i + 1) * c2 + 1, here, :] + x_faces[r2:]
             for k in range(c2):
                 at = i * c2 + k + 1
-                s[0][at, j * r2 : (j + 1) * r2, :] = values[k * r2 : (k + 1) * r2]
-                t[at, j * r2 : (j + 1) * r2, :] = materials[k * r2 : (k + 1) * r2]
                 if j > 0:
                     face_y[at, j * r2 - 1 : j * r2, :] = y_faces[k : k + 1]
                 if j < gy - 1:
                     face_y[at, (j + 1) * r2 : (j + 1) * r2 + 1, :] = y_faces[c2 + k : c2 + k + 1]
         return 0
 
-    lax.fori_loop(0, gx, column, 0)
-
-    def sides(i, _):
-        low = [blocks[i * gy + j, own : own + r2] for j in range(gy)]
-        high = [blocks[i * gy + j, own + r2 :] for j in range(gy)]
-        keep = iota((rows, LANES), 1) < half
-        for parts, at in ((low, i * c2), (high, (i + 1) * c2 + 1)):
-            s[0][at] = s[0][at] + jnp.where(keep, jnp.concatenate(parts, axis=0), 0.0)
-        return 0
-
-    lax.fori_loop(0, gx, sides, 0)
+    lax.fori_loop(0, gx, edges, 0)
 
     def join(at, step):
         now = pl.ds(at + 1, step)
+        row = iota((step, rows, LANES), 1)
+        edge = ((row % r2 == 0) & (row > 0)) | ((row % r2 == r2 - 1) & (row < rows - 1))
         s[0][now] = s[0][now] + jnp.where(edge, face_y[now], 0.0)
 
     each(counts[0], join)
-    s[0][0] = zero
-    s[0][counts[0] + 1] = zero
-    mats = (t, s[1], s[2])
-    for level, (count, base) in enumerate(zip(counts, bases)):
-        if level:
-
-            def coarsen(at, step):
-                shape = (step // 2, rows, LANES)
-                whole = (iota(shape, 1) % 2**level == 0) & (iota(shape, 2) % 2**level == 0)
-                mean = 0.125 * fold(mats[level - 1][pl.ds(at + 1, step)], 2 ** (level - 1))
-                mats[level][pl.ds(at // 2 + 1, step // 2)] = jnp.where(whole, mean, 0.0)
-
-            each(counts[level - 1], coarsen)
-        fill_table(mats[level], table, level, count, base, width)
+    clear_ends(s[:1], counts)
     cycle(s, e, t, table, counts, bases, place, out, c2, r2, pad)
 
 
@@ -569,7 +607,10 @@
     out[...] = jnp.broadcast_to(v, (planes, 2, 2 * rows, LANES)).reshape(2 * planes, 2 * rows, LANES)
 
 
-def level1_kernel(offset, place, long, inner, outer, window1, payload, state, src, mat, flat, prolonged, wide, narrow):
+def level1_kernel(
+    offset, place, long, inner, outer, window1, payload, state_far,
+    src, mat, flat, prolonged, fx, fy, fz, diag, inv, err, c, state, wide, narrow, sheet, semaphores,
+):
     low_x = place[0] == 1
     total, length, depth = src.shape
     count, rows = total - 8, length - 8
@@ -584,66 +625,82 @@
         for k in range(count):
             ref[4 + k] = long[n, 2 * count + k // 2, :length, k % 2 * LANES : (k % 2 + 1) * LANES]
     raise_window(window1, flat, prolonged)
-    a = mat[...]
-    lane = iota(a.shape, 2)
-    before, ahead = shifted(a)
-    down, up = lower(a, 1), upper(a, 1)
-    w_x, w_y = harmonic(a, before, 0.25), harmonic(a, down, 0.25)
-    w_z = jnp.where(lane == 0, 0.0, harmonic(a, lower(a, 2), 0.25))
-    _, w_ahead = shifted(w_x)
-    outside = as_float(lane == 0) + as_float(lane == depth - 1)
-    for b in (before, ahead, down, up):
-        outside = outside + as_float(b <= 0.0)
-    diagonal = w_x + w_ahead + w_y + upper(w_y, 1) + w_z + upper(w_z, 2) + 0.25 * a * outside
-    inverse = jnp.where(a > 0.0, invert(jnp.maximum(diagonal, 1e-4)), 0.0)
-    state[0], state[1], state[2], state[3] = w_x, w_y, w_z, inverse
-    w_x = jnp.concatenate([w_x, zero[None]], axis=0)
-    s = src[...]
-    e = DAMPING * inverse * s + prolonged[...]
-    c = KEPT * e + DAMPING * inverse * (s + apply_off(e, w_x, w_y, w_z))
-    s2 = s - diagonal * c + apply_off(c, w_x, w_y, w_z)
-    e2 = DAMPING * inverse * s2
-    t = KEPT * s2 + apply_off(e2, w_x, w_y, w_z)
-    state[4], state[5], state[6] = c, s2, e2
-    own = t[4 : 4 + count, 4 : 4 + rows].reshape(count // 2, 2, rows, depth)
-    wide[...] = (own[:, 0] + own[:, 1]).reshape(count // 2 * rows, depth)
-    part = count // 4 * rows
-    narrow[...] = (select(wide[:part], pair_matrix(depth)) + select(wide[part:], pair_matrix(depth, LANES // 2))) * 0.125
-    block = narrow[pl.ds(0, part // 2, 2)] + narrow[pl.ds(1, part // 2, 2)]
-    payload[...] = jnp.broadcast_to(block[None], payload.shape)
-
-
-def last_cycle_kernel(counts, bases, grid, c2, r2, place, blocks, table, state, partial, out, *scratch):
+    row, lane = iota((length, depth), 0), iota((length, depth), 1)
+    ends = as_float(lane == 0) + as_float(lane == depth - 1)
+    fx[1] = harmonic(mat[0], mat[1], 0.25)
+    for k in range(1, total - 1):
+        a, before, ahead = mat[k], mat[k - 1], mat[k + 1]
+        down, up = lower(a, 0), upper(a, 0)
+        f = harmonic(a, ahead, 0.25)
+        w_y = harmonic(a, down, 0.25)
+        w_z = jnp.where(lane == 0, 0.0, harmonic(a, lower(a, 1), 0.25))
+        outside = ends + as_float(before <= 0.0) + as_float(ahead <= 0.0) + as_float(down <= 0.0) + as_float(up <= 0.0)
+        diagonal = fx[k] + f + w_y + upper(w_y, 0) + w_z + upper(w_z, 1) + 0.25 * a * outside
+        inverse = jnp.where(a > 0.0, invert(jnp.maximum(diagonal, 1e-4)), 0.0)
+        fx[k + 1], fy[k], fz[k], diag[k], inv[k] = f, w_y, w_z, diagonal, inverse
+        err[k] = DAMPING * inverse * src[k] + prolonged[k]
+
+    def off(v, k):
+        here = v[k]
+        w_y, w_z = fy[k], fz[k]
+        out = fx[k] * v[k - 1] + fx[k + 1] * v[k + 1] + w_y * lower(here, 0) + upper(w_y * here, 0)
+        return here, out + w_z * lower(here, 1) + upper(w_z * here, 1)
+
+    for k in range(2, total - 2):
+        here, more = off(err, k)
+        c[k] = KEPT * here + DAMPING * inv[k] * (src[k] + more)
+    for k in range(3, total - 3):
+        here, more = off(c, k)
+        left = src[k] - diag[k] * here + more
+        src[k] = left
+        value = DAMPING * inv[k] * left
+        err[k] = value
+        state[k - 3] = value
+    base = count + 2
+    for k in range(count + 1):
+        state[base + k] = fx[k + 4]
+    base += count + 1
+    for n, ref in enumerate((fy, fz, inv, c, src)):
+        for k in range(count):
+            state[base + n * count + k] = ref[k + 4]
+    leaving = pltpu.make_async_copy(state, state_far, semaphores.at[0])
+    leaving.start()
+    for k in range(4, count + 4):
+        _, more = off(err, k)
+        t = (KEPT * src[k] + more)[4 : 4 + rows]
+        if k % 2 == 0:
+            kept = t
+        else:
+            at = (k - 5) // 2 * rows
+            wide[at : at + rows] = kept + t
+    half = wide.shape[0] // 2
+    publish(wide[:half], wide[half:], narrow, sheet, payload, semaphores.at[1])
+    leaving.wait()
+
+
+def last_cycle_kernel(counts, bases, grid, c2, r2, place, blocks, table, state_far, partial, out, *scratch):
     s, e, t, pad = scratch[0:3], list(scratch[3:6]), scratch[6], scratch[7]
-    view, flat, prolonged, tall = scratch[8:12]
-    gx, gy = grid
-    half = LANES // 2
-    valid = iota((c2 // 2 * r2, LANES), 1) < half
-
-    def column(i, _):
-        for j in range(gy):
-            block = blocks[i * gy + j]
-            parts = (jnp.where(valid, block, 0.0), jnp.where(valid, pltpu.roll(block, half, 1), 0.0))
-            for k in range(c2):
-                n = k % (c2 // 2)
-                s[0][i * c2 + k + 1, j * r2 : (j + 1) * r2, :] = parts[k // (c2 // 2)][n * r2 : (n + 1) * r2]
-        return 0
-
-    lax.fori_loop(0, gx, column, 0)
+    view, flat, prolonged, tall, coarse, state, semaphore = scratch[8:15]
+    arriving = pltpu.make_async_copy(state_far, state, semaphore)
+    arriving.start()
+    spread_blocks(blocks, s[0], grid, c2, r2)
+    clear_ends(s, counts)
     cycle(s, e, t, table, counts, bases, place, view, c2, r2, pad)
     raise_window(view, flat, prolonged)
     count, rows, depth = partial.shape
     c1, r1 = count // 2, rows // 2
-    near = slice(3, c1 + 5)
-    own = slice(4, 4 + c1)
-    v = state[6, near] + prolonged[near]
-    w_x, w_y, w_z = state[0, 4 : c1 + 5], state[1, own], state[2, own]
-    here = v[1:-1]
-    off = w_x[:-1] * v[:-2] + w_x[1:] * v[2:]
-    off = off + w_y * lower(here, 1) + upper(w_y * here, 1) + w_z * lower(here, 2) + upper(w_z * here, 2)
-    here = KEPT * here + DAMPING * state[3, own] * (state[5, own] + off)
-    coarse = (state[4, own] + here)[:, 4 : 4 + r1].reshape(c1 * r1, LANES)
-    values = select(coarse, spread_matrix(depth))
+    arriving.wait()
+    for k in range(c1 + 2):
+        prolonged[k + 3] = prolonged[k + 3] + state[k]
+    base = 2 * c1 + 3
+    for k in range(c1):
+        here = prolonged[k + 4]
+        w_y, w_z, inverse, before, left = (state[base + n * c1 + k] for n in range(5))
+        off = state[c1 + 2 + k] * prolonged[k + 3] + state[c1 + 3 + k] * prolonged[k + 5]
+        off = off + w_y * lower(here, 0) + upper(w_y * here, 0) + w_z * lower(here, 1) + upper(w_z * here, 1)
+        total = before + KEPT * here + DAMPING * inverse * (left + off)
+        coarse[k * r1 : (k + 1) * r1] = total[4 : 4 + r1]
+    values = select(coarse[...], spread_matrix(depth))
     for piece in range(depth // LANES):
         z = slice(piece * LANES, (piece + 1) * LANES)
         tall[piece, pl.ds(0, c1 * r1, 2)] = values[:, z]
@@ -659,12 +716,14 @@
     return 4 * lead * (-(-shape[-2] // 8) * 8) * (-(-shape[-1] // LANES) * LANES)
 
 
-def call(kernel, name, inputs, outputs, scratch=(), apart=()):
+def call(kernel, name, inputs, outputs, scratch=(), apart=(), cost=None):
     streamed = 0
 
     def held(n, x):
         nonlocal streamed
-        if x.ndim == 1 or n in apart:
+        if n in apart:
+            return pltpu.with_memory_space_constraint(x, pltpu.HBM)
+        if x.ndim == 1:
             return x
         if size_of(x.shape) <= HELD:
             return pltpu.with_memory_space_constraint(x, pltpu.VMEM)
@@ -676,26 +735,32 @@
         if isinstance(shape, jax.ShapeDtypeStruct):
             streamed += size_of(shape.shape)
             return shape
+        if far(shape):
+            return pltpu.HBM(shape[1], F32)
         if size_of(shape) <= HELD:
             return pltpu.VMEM(shape, F32)
         streamed += size_of(shape)
         return jax.ShapeDtypeStruct(shape, F32)
 
+    def far(x):
+        return isinstance(x, tuple) and x[0] == "far"
+
     def space(n, x):
-        return pl.ANY if n in apart else pltpu.SMEM if x.ndim == 1 else pltpu.VMEM
+        return pltpu.HBM if n in apart else pltpu.SMEM if x.ndim == 1 else pltpu.VMEM
 
     specs = [pl.BlockSpec(memory_space=space(n, x)) for n, x in enumerate(inputs)]
     inputs = [held(n, x) for n, x in enumerate(inputs)]
     results = [result(shape) for shape in outputs]
-    need = streamed + sum(size_of(x.shape) for x in scratch if len(x.shape) > 1) + 3 * MIB
+    need = streamed + sum(size_of(x.shape) for x in scratch if len(getattr(x, "shape", ())) > 1) + 3 * MIB
     return pl.pallas_call(
         kernel,
         out_shape=results,
         in_specs=specs,
-        out_specs=[pl.BlockSpec(memory_space=pltpu.VMEM) for _ in outputs],
+        out_specs=[pl.BlockSpec(memory_space=pltpu.HBM if far(x) else pltpu.VMEM) for x in outputs],
         scratch_shapes=list(scratch),
         compiler_params=pltpu.CompilerParams(vmem_limit_bytes=max(need, 8 * MIB)),
         name=name,
+        cost_estimate=None if cost is None else pl.CostEstimate(flops=cost, bytes_accessed=0, transcendentals=0),
     )(*inputs)
 
 
@@ -719,12 +784,19 @@
 
     brick = (count, rows, depth)
     face = (3, rows, depth)
-    material, potential_here, source_here, inner, outer, even, odd = call(
+    DMA = pltpu.SemaphoreType.DMA
+    sheet = (devices, c2 // 2 * r2, LANES)
+    sheet2 = (devices, c2 // 2 * r2 + 2 * r2, LANES)
+    material, potential_here, source_here, inner, outer, even, odd, materials = call(
         faces_kernel, "faces", (place, permeability, potential, phase, right_side),
-        (brick, brick, brick, face, face, (3, count, depth), (3, count, depth)),
-        (pltpu.VMEM(brick, jnp.int32), pltpu.SMEM(permeability.shape, F32), pltpu.SemaphoreType.DMA((4,))),
+        (brick, brick, brick, face, face, (3, count, depth), (3, count, depth), ("far", sheet)),
+        (
+            pltpu.VMEM(brick, jnp.int32), pltpu.SMEM(permeability.shape, F32), pltpu.SemaphoreType.DMA((5,)),
+            VM(c1 * rows, depth), VM(c1 * rows, LANES), VM(c2 * r1, LANES), VM(c2 // 2 * r1, LANES), VM(*sheet),
+        ),
         apart=(1, 2, 3, 4),
     )
+    materials = lax.all_to_all(materials, ("gx", "gy"), 0, 0)
     even = lax.ppermute(even, "gy", swap_y[0])
     odd = lax.ppermute(odd, "gy", swap_y[1])
     outer = lax.ppermute(outer, "gx", swap_x[1])
@@ -735,21 +807,21 @@
     residual, coarse, even, odd = call(
         residual_kernel, "residual", (place, source_here, potential_here, material, inner, outer, even, odd),
         (brick, (total // 2, LANES), strip, strip),
-        (VM(total, depth), VM(total, LANES), VM(4, count, depth)),
+        (VM(total, depth), VM(total, LANES), VM(4, count, depth)), cost=10**10,
     )
     even = lax.ppermute(even, "gy", swap_y[0])
     odd = lax.ppermute(odd, "gy", swap_y[1])
-    small = c2 * r1 + 2 * r1
+    small = c2 // 2 * r1 + 2 * r1
     (payload,) = call(
-        functools.partial(payload_kernel, c1, r1), "payload", (coarse,), ((devices, c2 * r2 + 2 * r2, LANES),),
-        (VM(2, small, d1), VM(small, LANES)),
+        functools.partial(payload_kernel, c1, r1), "payload", (coarse,), (("far", sheet2),),
+        (VM(2, small, d1), VM(small, LANES), VM(*sheet2), DMA),
     )
     blocks = lax.all_to_all(payload, ("gx", "gy"), 0, 0)
     tiles, tiles1 = (rows + 8) // 8, (r1 + 8) // 8
     strip = (7 * tiles * pieces + 7 * tiles1, 8, LANES)
     inner, outer, long = call(
         strips_kernel, "strips", (place, residual, material, coarse, even, odd),
-        (strip, strip, (2, count + c1 // 2, rows + 8, depth)),
+        (strip, strip, (2, count + c1 // 2, rows + 8, depth)), cost=10**11,
     )
     outer = lax.ppermute(outer, "gx", swap_x[1])
     inner = lax.ppermute(inner, "gx", swap_x[0])
@@ -758,27 +830,40 @@
     bases = (0, counts[0] + 1, counts[0] + counts[1] + 2)
     work = cycle_shapes(counts, gy * r2, c2)
     view = (c2 + 4, r2 + 4, LANES)
-    window1, table = call(
-        functools.partial(first_cycle_kernel, counts, bases, (gx, gy), c2, r2, d1 // 2), "cycle1", (place, blocks),
-        (view, (4, sum(counts) + 3, gy * r2, LANES)), work,
+    planes = [VM(n + 2, gy * r2, LANES) for n in counts]
+    (table,) = call(
+        functools.partial(tables_kernel, counts, bases, (gx, gy), c2, r2, d1 // 2), "tables", (materials,),
+        ((4, sum(counts) + 3, gy * r2, LANES),), planes,
+    )
+    (window1,) = call(
+        functools.partial(first_cycle_kernel, counts, bases, (gx, gy), c2, r2), "cycle1", (place, blocks, table), (view,), work,
     )
     frame = (c1 + 8, r1 + 8, d1)
     flat = VM((c2 + 4) * (r2 + 4) * 2, LANES)
-    payload, state = call(
-        functools.partial(level1_kernel, 7 * tiles * pieces), "level1", (place, long, inner, outer, window1),
-        ((devices, c2 // 2 * r2, LANES), (7, *frame)),
-        (VM(*frame), VM(*frame), flat, VM(*frame), VM(c1 // 2 * r1, d1), VM(c1 // 4 * r1, LANES)),
+    state = (7 * c1 + 3, r1 + 8, d1)
+    tall = VM(c1 + 9, r1 + 8, d1)
+    payload, held = call(
+        functools.partial(level1_kernel, 7 * tiles * pieces), "level1", (place, long, inner, outer, window1), (("far", sheet), ("far", state)),
+        (
+            VM(*frame), VM(*frame), flat, VM(*frame), tall, VM(*frame), VM(*frame), VM(*frame), VM(*frame), VM(*frame),
+            VM(*frame), VM(*state), VM(c1 // 2 * r1, d1), VM(c1 // 4 * r1, LANES), VM(*sheet), pltpu.SemaphoreType.DMA((2,)),
+        ),
     )
     blocks = lax.all_to_all(payload, ("gx", "gy"), 0, 0)
     wide = (count + 8, rows + 8, depth)
     (partial,) = call(
         functools.partial(smooth_kernel, (gx, gy)), "smooth", (place, potential, long, inner, outer), (brick,),
-        (VM(*wide), VM(*wide), VM(2, *wide), VM(*wide), VM(count + 9, rows + 8, depth), VM(*wide), VM(*wide), VM(*wide)),
+        (
+            VM(*wide), VM(*wide), VM(2, *wide), VM(*wide), VM(count + 9, rows + 8, depth), VM(*wide), VM(*wide), VM(*wide),
+            VM(*brick), pltpu.SemaphoreType.DMA,
+        ),
+        apart=(1,),
     )
     (out,) = call(
         functools.partial(last_cycle_kernel, counts, bases, (gx, gy), c2, r2), "cycle2",
-        (place, blocks, table, state, partial), (jax.ShapeDtypeStruct(brick, F32),),
-        (*work, VM(*view), flat, VM(*frame), VM(pieces, count // 2 * rows, LANES)),
+        (place, blocks, table, held, partial), (jax.ShapeDtypeStruct(brick, F32),),
+        (*work, VM(*view), flat, VM(*frame), VM(pieces, c1 * rows, LANES), VM(c1 * r1, LANES), VM(*state), DMA),
+        apart=(3,),
     )
     return out
 

time: 70.5 us -> 59.3 us (0.84)
  local copies, waits for them, and re-layouts: 6.57 us -> 0 us
  starting transfers between devices: 28.9 us -> 24.5 us
  waiting for transfers between devices: 13.1 us -> 10.6 us
  Pallas kernels: 21.2 us -> 23.6 us
    all_to_all x2, starting transfers between devices: 20.6 us -> 7.38 us  [local(): blocks = lax.all_to_all(payload, ('gx', 'gy'), 0, 0)]
    ppermute x2, waiting for transfers between devices: 11.6 us -> 0.01 us  [local(): even = lax.ppermute(even, 'gy', swap_y[0])]
    all_to_all x0 -> x1, starting transfers between devices: none -> 8.52 us  [local(): materials = lax.all_to_all(materials, ('gx', 'gy'), 0, 0)]
    unnamed x14 -> x0, local copies, waits for them, and re-layouts: 6.57 us -> none
    all_to_all x2, waiting for transfers between devices: 1.53 us -> 7.25 us  [local(): blocks = lax.all_to_all(payload, ('gx', 'gy'), 0, 0)]
    all_to_all x0 -> x1, waiting for transfers between devices: none -> 3.33 us  [local(): materials = lax.all_to_all(materials, ('gx', 'gy'), 0, 0)]
    pallas_call x8 -> x9, Pallas kernels: 21.2 us -> 23.6 us  [call(): pl.pallas_call(kernel, out_shape=results, in_specs=specs, out_specs=[pl.B...]
  transfers between devices with their start and end apart: 10 -> 11, of which waited for: 3 -> 3; matrix products, arithmetic and copies ran while one was open for 0% -> 0% of each run, Pallas kernels for 17% -> 26%
where the time goes in v4:
time: 59.3 us; the launch traced here: 58.9 us
  starting transfers between devices  24.5 us (41%)
  Pallas kernels  23.6 us (40%)
  waiting for transfers between devices  10.6 us (18%)
    pallas_call x9, Pallas kernels, call(): pl.pallas_call(kernel, out_shape=results, in_specs=specs, out_specs=[pl.B...  23.6 us
    all_to_all x1, starting transfers between devices, local(): materials = lax.all_to_all(materials, ('gx', 'gy'), 0, 0)  8.52 us
    all_to_all x2, starting transfers between devices, local(): blocks = lax.all_to_all(payload, ('gx', 'gy'), 0, 0)  7.38 us
    all_to_all x2, waiting for transfers between devices, local(): blocks = lax.all_to_all(payload, ('gx', 'gy'), 0, 0)  7.25 us
    ppermute x2, starting transfers between devices, local(): even = lax.ppermute(even, 'gy', swap_y[0])  4.5 us
    all_to_all x1, waiting for transfers between devices, local(): materials = lax.all_to_all(materials, ('gx', 'gy'), 0, 0)  3.33 us
    ppermute x2, starting transfers between devices, local(): outer = lax.ppermute(outer, 'gx', swap_x[1])  2 us
    ppermute x2, starting transfers between devices, local(): odd = lax.ppermute(odd, 'gy', swap_y[1])  1.31 us
  transfers between devices with their start and end apart: 11, of which 3 were waited for; matrix products, arithmetic and copies ran while one was open for 0% of the time, Pallas kernels for 26%

profile of v4, /device:TPU:0, one launch (start us, length us, event | category | flops | bytes accessed | tf_op | source)
XLA Modules:
  0.0 58.9 jit_solution(18406237647458408169)
XLA Ops:
  0.0 0.1 pad_add_fusion.place
  0.1 2.6 %faces.1 = (f32[16,16,256]{2,1,0:T(8,128)S(1)}, f32[16,16,256]{2,1,0:T(8,128)S(1)}, f32[16,16,256]{2,1,0:T(8,128)S(1)}, f32[3,16,256]{2,1,0:T(8,128)S(1)}, f32[3...) custom-call(s32[4]{0:T(128)S(1)} %pad_add_fusion.place, ...), custom_call_target="tpu_custom_call" | custom-call | tf_op jit(solution)/shard_map/faces/pallas_call | solution.py:755
  2.7 0.5 collective-permute-start
  3.2 0.7 %collective-permute-start.1 = (f32[3,16,256]{2,1,0:T(8,128)S(1)}, f32[3,16,256]{2,1,0:T(8,128)S(1)}, u32[]{:S(2)}, u32[]{:S(2)}) collective-permute-start(f32[3,16,256]{2,1,0:T(8,128)S(1)} %get-tuple-element.26), channel_id=1, source_target_pairs={{4,8},{12,16},{20,24},{8,4},{16,12},{24,20},{5,9},{13,17},{21,25},... | collective-permute-start | bytes 147464 | tf_op jit(solution)/shard_map/ppermute | solution.py:802
  3.9 2.7 %collective-permute-start.2 = (f32[3,16,256]{2,1,0:T(8,128)S(1)}, f32[3,16,256]{2,1,0:T(8,128)S(1)}, u32[]{:S(2)}, u32[]{:S(2)}) collective-permute-start(f32[3,16,256]{2,1,0:T(8,128)S(1)} %get-tuple-element.27), channel_id=1, source_target_pairs={{0,1},{2,3},{1,0},{3,2},{4,5},{6,7},{5,4},{7,6},{8,9},{10,11},{9,8... | collective-permute-start | bytes 147464 | tf_op jit(solution)/shard_map/ppermute | solution.py:800
  6.6 0.7 %collective-permute-start.3 = (f32[3,16,256]{2,1,0:T(8,128)S(1)}, f32[3,16,256]{2,1,0:T(8,128)S(1)}, u32[]{:S(2)}, u32[]{:S(2)}) collective-permute-start(f32[3,16,256]{2,1,0:T(8,128)S(1)} %get-tuple-element.28), channel_id=1, source_target_pairs={{1,2},{2,1},{5,6},{6,5},{9,10},{10,9},{13,14},{14,13},{17,18},{18,... | collective-permute-start | bytes 147464 | tf_op jit(solution)/shard_map/ppermute | solution.py:801
  7.2 8.5 %all-to-all-start.1 = ((f32[32,8,128]{2,1,0:T(8,128)}), f32[32,8,128]{2,1,0:T(8,128)S(1)}, u32[]{:S(2)}, u32[]{:S(2)}) async-start(f32[32,8,128]{2,1,0:T(8,128)} %get-tuple-element.36), calls=%async_computation.1 | async-start | bytes 262144 | tf_op jit(solution)/shard_map/all_to_all | solution.py:799
  15.7 0.0 collective-permute-done.inner
  15.8 0.0 collective-permute-done.1.outer
  15.8 0.0 collective-permute-done.2.even
  15.8 0.0 collective-permute-done.3.odd
  15.8 1.5 %residual.1 = (f32[16,16,256]{2,1,0:T(8,128)S(1)}, f32[160,128]{1,0:T(8,128)S(1)}, f32[40,8,128]{2,1,0:T(8,128)S(1)}, f32[40,8,128]{2,1,0:T(8,128)S(1)}) custom-call(s32[4]{0:T(128)S(1)} %pad_add_fusion.place, f32[16,16,256]{2,1,0:T(8,128)S(1)} %get-tuple-element.22.source, f32[16,16,256]{2,1,0:T(8,128)S(1)} %get-tuple-element.23.potential, ...), custom_call_target="tpu_custom_call" | custom-call | flops 10000000000 | tf_op jit(solution)/shard_map/residual/pallas_call | solution.py:755
  17.3 1.8 %collective-permute-start.4 = (f32[40,8,128]{2,1,0:T(8,128)S(1)}, f32[40,8,128]{2,1,0:T(8,128)S(1)}, u32[]{:S(2)}, u32[]{:S(2)}) collective-permute-start(f32[40,8,128]{2,1,0:T(8,128)S(1)} %get-tuple-element.31), channel_id=1, source_target_pairs={{0,1},{2,3},{1,0},{3,2},{4,5},{6,7},{5,4},{7,6},{8,9},{10,11},{9,8... | collective-permute-start | bytes 491528 | tf_op jit(solution)/shard_map/ppermute | solution.py:812
  19.1 0.7 %collective-permute-start.5 = (f32[40,8,128]{2,1,0:T(8,128)S(1)}, f32[40,8,128]{2,1,0:T(8,128)S(1)}, u32[]{:S(2)}, u32[]{:S(2)}) collective-permute-start(f32[40,8,128]{2,1,0:T(8,128)S(1)} %get-tuple-element.32), channel_id=1, source_target_pairs={{1,2},{2,1},{5,6},{6,5},{9,10},{10,9},{13,14},{14,13},{17,18},{18,... | collective-permute-start | bytes 491528 | tf_op jit(solution)/shard_map/ppermute | solution.py:813
  19.8 1.1 %payload.1 = f32[32,16,128]{2,1,0:T(8,128)} custom-call(f32[160,128]{1,0:T(8,128)S(1)} %get-tuple-element.30.coarse), custom_call_target="tpu_custom_call" | custom-call | tf_op jit(solution)/shard_map/payload/pallas_call | solution.py:755
  20.9 3.3 %all-to-all-done.1.blocks = f32[32,8,128]{2,1,0:T(8,128)S(1)} async-done(((f32[32,8,128]{2,1,0:T(8,128)}), f32[32,8,128]{2,1,0:T(8,128)S(1)}, u32[]{:S(2)}, u32[]{:S(2)}) %all-to-all-start.1) | async-done | bytes 131104 | tf_op jit(solution)/shard_map/all_to_all | solution.py:799
  24.3 3.1 %all-to-all-start = ((f32[32,16,128]{2,1,0:T(8,128)}), f32[32,16,128]{2,1,0:T(8,128)S(1)}, u32[]{:S(2)}, u32[]{:S(2)}) async-start(f32[32,16,128]{2,1,0:T(8,128)} %payload.1), calls=%async_computation | async-start | bytes 524288 | tf_op jit(solution)/shard_map/all_to_all | solution.py:819
  27.4 0.0 collective-permute-done.4.even
  27.4 0.0 collective-permute-done.5.odd
  27.4 1.4 %strips.1 = (f32[56,8,128]{2,1,0:T(8,128)}, f32[56,8,128]{2,1,0:T(8,128)}, f32[2,20,24,256]{3,2,1,0:T(8,128)S(1)}) custom-call(s32[4]{0:T(128)S(1)} %pad_add_fusion.place, f32[16,16,256]{2,1,0:T(8,128)S(1)} %get-tuple-element.29.residual, f32[16,16,256]{2,1,0:T(8,128)S(1)} %get-tuple-element.24.material, f32[160,128]{1,0:T(8,128)S(1)} %get-tuple-element.30.coarse, ...), custom_call_target="tpu_custom_call" | custom-call | flops 99999997952 | tf_op jit(solution)/shard_map/strips/pallas_call | solution.py:755
  28.8 0.3 collective-permute-start.6
  29.1 1.3 %collective-permute-start.7 = (f32[56,8,128]{2,1,0:T(8,128)}, f32[56,8,128]{2,1,0:T(8,128)}, u32[]{:S(2)}, u32[]{:S(2)}) collective-permute-start(f32[56,8,128]{2,1,0:T(8,128)} %get-tuple-element.35), channel_id=1, source_target_pairs={{4,8},{12,16},{20,24},{8,4},{16,12},{24,20},{5,9},{13,17},{21,25},... | collective-permute-start | bytes 688136 | tf_op jit(solution)/shard_map/ppermute | solution.py:826
  30.4 2.4 %tables.1.table = f32[4,59,16,128]{3,2,1,0:T(8,128)S(1)} custom-call(f32[32,8,128]{2,1,0:T(8,128)S(1)} %all-to-all-done.1.blocks), custom_call_target="tpu_custom_call" | custom-call | tf_op jit(solution)/shard_map/tables/pallas_call | solution.py:755
  32.9 4.8 %all-to-all-done.blocks = f32[32,16,128]{2,1,0:T(8,128)S(1)} async-done(((f32[32,16,128]{2,1,0:T(8,128)}), f32[32,16,128]{2,1,0:T(8,128)S(1)}, u32[]{:S(2)}, u32[]{:S(2)}) %all-to-all-start) | async-done | bytes 262176 | tf_op jit(solution)/shard_map/all_to_all | solution.py:819
  37.6 2.8 %cycle1.1.window1 = f32[8,8,128]{2,1,0:T(8,128)S(1)} custom-call(s32[4]{0:T(128)S(1)} %pad_add_fusion.place, f32[32,16,128]{2,1,0:T(8,128)S(1)} %all-to-all-done.blocks, f32[4,59,16,128]{3,2,1,0:T(8,128)S(1)} %tables.1.table), custom_call_target="tpu_custom_call" | custom-call | tf_op jit(solution)/shard_map/cycle1/pallas_call | solution.py:755
  40.5 0.0 collective-permute-done.6.inner
  40.5 0.0 collective-permute-done.7.outer
  40.5 2.3 %level1.1 = (f32[32,8,128]{2,1,0:T(8,128)}, f32[59,16,128]{2,1,0:T(8,128)}) custom-call(s32[4]{0:T(128)S(1)} %pad_add_fusion.place, f32[2,20,24,256]{3,2,1,0:T(8,128)S(1)} %get-tuple-element.33.long, f32[56,8,128]{2,1,0:T(8,128)S(1)} %collective-permute-done.6.inner, f32[56,8,128]{2,1,0:T(8,128)} %collective-permute-done.7.outer, f32[8,8,128]{2,1,0:T(8,128)S(1)} %cycle1.1.window1), custom_call_target="tpu_custom_call" | custom-call | tf_op jit(solution)/shard_map/level1/pallas_call | solution.py:755
  42.8 4.3 %all-to-all-start.2 = ((f32[32,8,128]{2,1,0:T(8,128)}), f32[32,8,128]{2,1,0:T(8,128)S(1)}, u32[]{:S(2)}, u32[]{:S(2)}) async-start(f32[32,8,128]{2,1,0:T(8,128)} %get-tuple-element.37), calls=%async_computation.2 | async-start | bytes 262144 | tf_op jit(solution)/shard_map/all_to_all | solution.py:852
  47.1 5.9 %smooth.1.partial = f32[16,16,256]{2,1,0:T(8,128)S(1)} custom-call(s32[4]{0:T(128)S(1)} %pad_add_fusion.place, f32[16,16,256]{2,1,0:T(8,128)} %potential_far.1, f32[2,20,24,256]{3,2,1,0:T(8,128)S(1)} %get-tuple-element.33.long, f32[56,8,128]{2,1,0:T(8,128)S(1)} %collective-permute-done.6.inner, f32[56,8,128]{2,1,0:T(8,128)} %collective-permute-done.7.outer), custom_call_target="tpu_custom_call" | custom-call | tf_op jit(solution)/shard_map/smooth/pallas_call | solution.py:755
  53.0 2.5 %all-to-all-done.2.blocks = f32[32,8,128]{2,1,0:T(8,128)S(1)} async-done(((f32[32,8,128]{2,1,0:T(8,128)}), f32[32,8,128]{2,1,0:T(8,128)S(1)}, u32[]{:S(2)}, u32[]{:S(2)}) %all-to-all-start.2) | async-done | bytes 131104 | tf_op jit(solution)/shard_map/all_to_all | solution.py:852
  55.5 3.4 %cycle2.1 = f32[16,16,256]{2,1,0:T(8,128)} custom-call(s32[4]{0:T(128)S(1)} %pad_add_fusion.place, f32[32,8,128]{2,1,0:T(8,128)S(1)} %all-to-all-done.2.blocks, f32[4,59,16,128]{3,2,1,0:T(8,128)S(1)} %tables.1.table, f32[59,16,128]{2,1,0:T(8,128)} %get-tuple-element.38.state_far, f32[16,16,256]{2,1,0:T(8,128)S(1)} %smooth.1.partial), custom_call_target="tpu_custom_call" | custom-call | tf_op jit(solution)/shard_map/cycle2/pallas_call | solution.py:755
Async XLA Ops:
  2.7 13.0 %collective-permute-start = (f32[3,16,256]{2,1,0:T(8,128)S(1)}, f32[3,16,256]{2,1,0:T(8,128)S(1)}, u32[]{:S(2)}, u32[]{:S(2)}) collective-permute-start(f32[3,16,256]{2,1,0:T(8,128)S(1)} %get-tuple-element.25), channel_id=1, source_target_pairs={{0,4},{8,12},{16,20},{24,28},{4,0},{12,8},{20,16},{28,24},{1,5},{9... | collective-permute-start | bytes 147464 | tf_op jit(solution)/shard_map/ppermute | solution.py:803
  3.2 12.5 %collective-permute-start.1 = (f32[3,16,256]{2,1,0:T(8,128)S(1)}, f32[3,16,256]{2,1,0:T(8,128)S(1)}, u32[]{:S(2)}, u32[]{:S(2)}) collective-permute-start(f32[3,16,256]{2,1,0:T(8,128)S(1)} %get-tuple-element.26), channel_id=1, source_target_pairs={{4,8},{12,16},{20,24},{8,4},{16,12},{24,20},{5,9},{13,17},{21,25},... | collective-permute-start | bytes 147464 | tf_op jit(solution)/shard_map/ppermute | solution.py:802
  3.9 11.9 %collective-permute-start.2 = (f32[3,16,256]{2,1,0:T(8,128)S(1)}, f32[3,16,256]{2,1,0:T(8,128)S(1)}, u32[]{:S(2)}, u32[]{:S(2)}) collective-permute-start(f32[3,16,256]{2,1,0:T(8,128)S(1)} %get-tuple-element.27), channel_id=1, source_target_pairs={{0,1},{2,3},{1,0},{3,2},{4,5},{6,7},{5,4},{7,6},{8,9},{10,11},{9,8... | collective-permute-start | bytes 147464 | tf_op jit(solution)/shard_map/ppermute | solution.py:800
  6.6 9.2 %collective-permute-start.3 = (f32[3,16,256]{2,1,0:T(8,128)S(1)}, f32[3,16,256]{2,1,0:T(8,128)S(1)}, u32[]{:S(2)}, u32[]{:S(2)}) collective-permute-start(f32[3,16,256]{2,1,0:T(8,128)S(1)} %get-tuple-element.28), channel_id=1, source_target_pairs={{1,2},{2,1},{5,6},{6,5},{9,10},{10,9},{13,14},{14,13},{17,18},{18,... | collective-permute-start | bytes 147464 | tf_op jit(solution)/shard_map/ppermute | solution.py:801
  7.2 17.0 %all-to-all-start.1 = ((f32[32,8,128]{2,1,0:T(8,128)}), f32[32,8,128]{2,1,0:T(8,128)S(1)}, u32[]{:S(2)}, u32[]{:S(2)}) async-start(f32[32,8,128]{2,1,0:T(8,128)} %get-tuple-element.36), calls=%async_computation.1 | async-start | bytes 262144 | tf_op jit(solution)/shard_map/all_to_all | solution.py:799
  17.3 10.1 %collective-permute-start.4 = (f32[40,8,128]{2,1,0:T(8,128)S(1)}, f32[40,8,128]{2,1,0:T(8,128)S(1)}, u32[]{:S(2)}, u32[]{:S(2)}) collective-permute-start(f32[40,8,128]{2,1,0:T(8,128)S(1)} %get-tuple-element.31), channel_id=1, source_target_pairs={{0,1},{2,3},{1,0},{3,2},{4,5},{6,7},{5,4},{7,6},{8,9},{10,11},{9,8... | collective-permute-start | bytes 491528 | tf_op jit(solution)/shard_map/ppermute | solution.py:812
  19.1 8.3 %collective-permute-start.5 = (f32[40,8,128]{2,1,0:T(8,128)S(1)}, f32[40,8,128]{2,1,0:T(8,128)S(1)}, u32[]{:S(2)}, u32[]{:S(2)}) collective-permute-start(f32[40,8,128]{2,1,0:T(8,128)S(1)} %get-tuple-element.32), channel_id=1, source_target_pairs={{1,2},{2,1},{5,6},{6,5},{9,10},{10,9},{13,14},{14,13},{17,18},{18,... | collective-permute-start | bytes 491528 | tf_op jit(solution)/shard_map/ppermute | solution.py:813
  24.3 13.4 %all-to-all-start = ((f32[32,16,128]{2,1,0:T(8,128)}), f32[32,16,128]{2,1,0:T(8,128)S(1)}, u32[]{:S(2)}, u32[]{:S(2)}) async-start(f32[32,16,128]{2,1,0:T(8,128)} %payload.1), calls=%async_computation | async-start | bytes 524288 | tf_op jit(solution)/shard_map/all_to_all | solution.py:819
  28.8 11.7 %collective-permute-start.6 = (f32[56,8,128]{2,1,0:T(8,128)}, f32[56,8,128]{2,1,0:T(8,128)S(1)}, u32[]{:S(2)}, u32[]{:S(2)}) collective-permute-start(f32[56,8,128]{2,1,0:T(8,128)} %get-tuple-element.34), channel_id=1, source_target_pairs={{0,4},{8,12},{16,20},{24,28},{4,0},{12,8},{20,16},{28,24},{1,5},{9... | collective-permute-start | bytes 688136 | tf_op jit(solution)/shard_map/ppermute | solution.py:827
  29.1 11.4 %collective-permute-start.7 = (f32[56,8,128]{2,1,0:T(8,128)}, f32[56,8,128]{2,1,0:T(8,128)}, u32[]{:S(2)}, u32[]{:S(2)}) collective-permute-start(f32[56,8,128]{2,1,0:T(8,128)} %get-tuple-element.35), channel_id=1, source_target_pairs={{4,8},{12,16},{20,24},{8,4},{16,12},{24,20},{5,9},{13,17},{21,25},... | collective-permute-start | bytes 688136 | tf_op jit(solution)/shard_map/ppermute | solution.py:826
  42.8 12.7 %all-to-all-start.2 = ((f32[32,8,128]{2,1,0:T(8,128)}), f32[32,8,128]{2,1,0:T(8,128)S(1)}, u32[]{:S(2)}, u32[]{:S(2)}) async-start(f32[32,8,128]{2,1,0:T(8,128)} %get-tuple-element.37), calls=%async_computation.2 | async-start | bytes 262144 | tf_op jit(solution)/shard_map/all_to_all | solution.py:852

commit v5 on v4

--- a/solution.py
+++ b/solution.py
@@ -19,6 +19,8 @@
 LANES = 128
 MIB = 1024 * 1024
 HELD = 4 * MIB
+SMOOTH_STEP = 4
+LEVEL1_STEP = 7
 
 
 def iota(shape, axis):
@@ -63,8 +65,8 @@
 
 def faces_kernel(
     place, permeability, potential, phase, source,
-    material, pot, src, inner, outer, even, odd, payload,
-    ids, values, semaphores, wide, narrow, folded, narrow1, sheet,
+    material, pot, src, inner, outer, even, odd,
+    ids, values, semaphores,
 ):
     arriving = [
         pltpu.make_async_copy(a, b, semaphores.at[n])
@@ -80,18 +82,6 @@
     for i in range(count):
         here = ids[i]
         material[i] = jnp.where(here == 0, p0, jnp.where(here == 1, p1, p2))
-    c1, r1 = count // 2, rows // 2
-    for k in range(c1):
-        wide[k * rows : (k + 1) * rows] = material[2 * k] + material[2 * k + 1]
-    narrow[...] = select(wide[...], pair_matrix(wide.shape[1])) * 0.125
-    half = c1 * r1
-    finer = narrow[pl.ds(0, half, 2)] + narrow[pl.ds(1, half, 2)]
-    for k in range(c1 // 2):
-        folded[k * r1 : (k + 1) * r1] = finer[2 * k * r1 : (2 * k + 1) * r1] + finer[(2 * k + 1) * r1 : (2 * k + 2) * r1]
-    part = folded.shape[0] // 2
-    sheet[...] = jnp.broadcast_to(packed(folded[:part], folded[part:], narrow1)[None], sheet.shape)
-    leaving = pltpu.make_async_copy(sheet, payload, semaphores.at[4])
-    leaving.start()
     last = count - 1
     first = jnp.where(low_x, 0, last)
     second = jnp.where(low_x, 1, last - 1)
@@ -112,14 +102,13 @@
     inner[0] = pot[first]
     outer[0] = pot[last - first]
     edge(0, pot, 0, rows - 1)
-    leaving.wait()
     arriving[3].wait()
 
 
 def residual_kernel(
     place, source, potential, material, inner, outer, even, odd,
     residual, coarse, strip_even, strip_odd,
-    wide, narrow, y_faces,
+    wide, narrow, y_faces, mat, pot,
 ):
     low_x, low_y = place[0] == 1, place[1] == 1
     count, rows, depth = source.shape
@@ -133,50 +122,56 @@
     y_low, y_high = ordered(low_y, even[...], odd[...])
     row, lane = iota((rows, depth), 0), iota((rows, depth), 1)
     first, last = row == 0, row == rows - 1
-    y_faces[0], y_faces[1] = y_low[0], y_high[0]
-    y_faces[2], y_faces[3] = y_low[1], y_high[1]
+    for n, ref in enumerate((y_low[0], y_high[0], y_low[1], y_high[1])):
+        for i in range(count):
+            y_faces[n, i] = jnp.broadcast_to(ref[i : i + 1], (8, depth))
+    mat[0], mat[count + 1] = x_low[1], x_high[1]
+    pot[0], pot[count + 1] = x_low[0], x_high[0]
+    mat[pl.ds(1, count)] = material[...]
+    pot[pl.ds(1, count)] = potential[...]
+    step = 4
     outside = as_float(lane == 0) + as_float(lane == depth - 1)
 
     def edge_count(faces):
         return as_float(faces[:1, :1] <= 0.0)
 
-    outside_y = outside + jnp.where(first, edge_count(y_low[1]), 0.0) + jnp.where(last, edge_count(y_high[1]), 0.0)
-    face = harmonic(x_low[1], material[0], 1.0)
-    for i in range(count):
-        a, v = material[i], potential[i]
-        v_before = potential[i - 1] if i else x_low[0]
-        v_ahead = potential[i + 1] if i < count - 1 else x_high[0]
-        next_face = harmonic(a, material[i + 1] if i < count - 1 else x_high[1], 1.0)
-        down = jnp.where(first, y_faces[2, i : i + 1], lower(a, 0))
+    outside = outside + jnp.where(first, edge_count(y_low[1]), 0.0) + jnp.where(last, edge_count(y_high[1]), 0.0)
+
+    def beside(ref, n, at):
+        return jnp.broadcast_to(ref[n, at : at + step, :1], (step, rows, depth))
+
+    for at in range(0, count, step):
+        here = slice(at + 1, at + 1 + step)
+        a, v = mat[here], pot[here]
+        faces = harmonic(mat[at : at + step + 1], mat[at + 1 : at + step + 2], 1.0)
+        down = jnp.where(first[None], beside(y_faces, 2, at), lower(a, 1))
         w_down = harmonic(a, down, 1.0)
-        w_top = harmonic(a[rows - 1 :], y_faces[3, i : i + 1], 1.0)
-        w_up = jnp.where(last, w_top, upper(w_down, 0))
-        w_back = jnp.where(lane == 0, 0.0, harmonic(a, lower(a, 1), 1.0))
-        w_front = upper(w_back, 1)
-        v_down = jnp.where(first, y_faces[0, i : i + 1], lower(v, 0))
-        v_up = jnp.where(last, y_faces[1, i : i + 1], upper(v, 0))
-        outer_faces = outside_y
-        if i == 0:
-            outer_faces = outer_faces + edge_count(x_low[1])
-        if i == count - 1:
-            outer_faces = outer_faces + edge_count(x_high[1])
-        diagonal = face + next_face + w_down + w_up + w_back + w_front + a * outer_faces
-        off = face * v_before + next_face * v_ahead + w_down * v_down + w_up * v_up
-        off = off + w_back * lower(v, 1) + w_front * upper(v, 1)
-        left = source[i] - diagonal * v + off
-        residual[i] = left
-        face = next_face
-        at = (i // 2) * rows
-        if i % 2 == 0:
-            kept_left, kept_a = left, a
-        else:
-            wide[at : at + rows] = kept_left + left
-            wide[c1 * rows + at : c1 * rows + at + rows] = kept_a + a
-        low = jnp.concatenate([left[:4], a[:4]], axis=0)
-        high = jnp.concatenate([left[rows - 4 :], a[rows - 4 :]], axis=0)
+        w_top = harmonic(a[:, rows - 1 :], y_faces[3, at : at + step, :1], 1.0)
+        w_up = jnp.where(last[None], jnp.broadcast_to(w_top, a.shape), upper(w_down, 1))
+        w_back = jnp.where(lane[None] == 0, 0.0, harmonic(a, lower(a, 2), 1.0))
+        w_front = upper(w_back, 2)
+        v_down = jnp.where(first[None], beside(y_faces, 0, at), lower(v, 1))
+        v_up = jnp.where(last[None], beside(y_faces, 1, at), upper(v, 1))
+        edges = jnp.broadcast_to(outside[None], a.shape)
+        if at == 0:
+            edges = edges + jnp.where(iota((step, 1, 1), 0) == 0, edge_count(x_low[1])[None], 0.0)
+        if at == count - step:
+            edges = edges + jnp.where(iota((step, 1, 1), 0) == step - 1, edge_count(x_high[1])[None], 0.0)
+        diagonal = faces[:-1] + faces[1:] + w_down + w_up + w_back + w_front + a * edges
+        off = faces[:-1] * pot[at : at + step] + faces[1:] * pot[at + 2 : at + 2 + step] + w_down * v_down + w_up * v_up
+        off = off + w_back * lower(v, 2) + w_front * upper(v, 2)
+        left = source[at : at + step] - diagonal * v + off
+        residual[at : at + step] = left
+        for n, x in enumerate((left, a)):
+            pair = x.reshape(step // 2, 2, rows, depth)
+            to = n * c1 * rows + at // 2 * rows
+            wide[to : to + step // 2 * rows] = (pair[:, 0] + pair[:, 1]).reshape(step // 2 * rows, depth)
+        low = jnp.concatenate([left[:, :4], a[:, :4]], axis=1)
+        high = jnp.concatenate([left[:, rows - 4 :], a[:, rows - 4 :]], axis=1)
         for ref, strip in ((strip_even, jnp.where(low_y, low, high)), (strip_odd, jnp.where(low_y, high, low))):
-            for piece in range(pieces):
-                ref[i * pieces + piece] = strip[:, piece * LANES : (piece + 1) * LANES]
+            for k in range(step):
+                for piece in range(pieces):
+                    ref[(at + k) * pieces + piece] = strip[k, :, piece * LANES : (piece + 1) * LANES]
     base = 2 * c1 * rows
     for n, both in enumerate((x_low[1] + x_low[2], x_high[1] + x_high[2], y_low[1] + y_low[2], y_high[1] + y_high[2])):
         wide[base + n * rows : base + (n + 1) * rows] = both
@@ -194,49 +189,48 @@
 def payload_kernel(c1, r1, coarse, payload, wide, narrow, sheet, semaphore):
     c2 = c1 // 2
     depth = coarse.shape[1]
-    s = [coarse[k * r1 : (k + 1) * r1] for k in range(c1)]
-    m = [coarse[(c1 + k) * r1 : (c1 + k + 1) * r1] for k in range(c1)]
+    shape = (c1, r1, depth)
+    s, m = coarse[: c1 * r1].reshape(shape), coarse[c1 * r1 : 2 * c1 * r1].reshape(shape)
     base = 2 * c1 * r1
-    m_xlow, m_xhigh, m_ylow, m_yhigh = (coarse[base + n * r1 : base + (n + 1) * r1] for n in range(4))
-    row, lane = iota((r1, depth), 0), iota((r1, depth), 1)
+    m_xlow, m_xhigh = coarse[base : base + r1], coarse[base + r1 : base + 2 * r1]
+    base += 2 * r1
+    m_ylow = jnp.stack([coarse[base + k : base + k + 1] for k in range(c1)])
+    m_yhigh = jnp.stack([coarse[base + r1 + k : base + r1 + k + 1] for k in range(c1)])
+    row, lane = iota(shape, 1), iota(shape, 2)
     first, last = row == 0, row == r1 - 1
-    around = [m_xlow] + m + [m_xhigh]
-    errors, tables = [], []
-    face = harmonic(around[0], around[1], 0.25)
+    around = jnp.concatenate([m_xlow[None], m, m_xhigh[None]], axis=0)
+    faces = harmonic(around[:-1], around[1:], 0.25)
+    down = jnp.where(first, jnp.broadcast_to(m_ylow, shape), lower(m, 1))
+    up = jnp.where(last, jnp.broadcast_to(m_yhigh, shape), upper(m, 1))
+    w_down = harmonic(m, down, 0.25)
+    w_up = jnp.where(last, harmonic(m, up, 0.25), upper(w_down, 1))
+    w_back = jnp.where(lane == 0, 0.0, harmonic(m, lower(m, 2), 0.25))
+    w_front = upper(w_back, 2)
+    outside = as_float(lane == 0) + as_float(lane == depth - 1)
+    for b in (down, up, around[:-2], around[2:]):
+        outside = outside + as_float(b <= 0.0)
+    diagonal = faces[:-1] + faces[1:] + w_down + w_up + w_back + w_front + 0.25 * m * outside
+    e = DAMPING * s * invert(diagonal)
+    y_low, y_high = w_down * e, w_up * e
+    t = KEPT * s + w_back * lower(e, 2) + w_front * upper(e, 2)
+    t = t + jnp.where(first, 0.0, w_down * lower(e, 1)) + jnp.where(last, 0.0, w_up * upper(e, 1))
+    nothing = jnp.zeros((1, r1, depth), F32)
+    t = t + faces[:-1] * jnp.concatenate([nothing, e[:-1]], axis=0) + faces[1:] * jnp.concatenate([e[1:], nothing], axis=0)
+    base = c2 // 2 * r1
+
+    def pairs(x):
+        x = x.reshape(c2, 2, r1, depth)
+        return (x[:, 0] + x[:, 1]).reshape(c2 * r1, depth)
+
+    t, m = pairs(t), pairs(m)
+    for n in range(2):
+        wide[n, :base] = t[n * base : (n + 1) * base]
+        wide[n, base + 2 * r1 :] = m[n * base : (n + 1) * base]
+    wide[0, base : base + r1] = faces[0] * e[0]
+    wide[0, base + r1 : base + 2 * r1] = faces[c1] * e[c1 - 1]
     for k in range(c1):
-        a = m[k]
-        down = jnp.where(first, m_ylow[k : k + 1], lower(a, 0))
-        up = jnp.where(last, m_yhigh[k : k + 1], upper(a, 0))
-        next_face = harmonic(a, around[k + 2], 0.25)
-        w_down = harmonic(a, down, 0.25)
-        w_up = jnp.where(last, harmonic(a, up, 0.25), upper(w_down, 0))
-        w_back = jnp.where(lane == 0, 0.0, harmonic(a, lower(a, 1), 0.25))
-        w_front = upper(w_back, 1)
-        outside = as_float(lane == 0) + as_float(lane == depth - 1)
-        outside = outside + as_float(down <= 0.0) + as_float(up <= 0.0)
-        outside = outside + as_float(around[k] <= 0.0) + as_float(around[k + 2] <= 0.0)
-        diagonal = face + next_face + w_down + w_up + w_back + w_front + 0.25 * a * outside
-        errors.append(DAMPING * s[k] * invert(diagonal))
-        tables.append((face, next_face, w_down, w_up, w_back, w_front))
-        face = next_face
-    base = c2 // 2 * r1
-    for k in range(c1):
-        e, w = errors[k], tables[k]
-        t = KEPT * s[k] + w[4] * lower(e, 1) + w[5] * upper(e, 1)
-        t = t + jnp.where(first, 0.0, w[2] * lower(e, 0)) + jnp.where(last, 0.0, w[3] * upper(e, 0))
-        if k > 0:
-            t = t + w[0] * errors[k - 1]
-        if k < c1 - 1:
-            t = t + w[1] * errors[k + 1]
-        at = k // 2 * r1
-        if k % 2 == 0:
-            kept = t
-        else:
-            wide[at // base, at % base : at % base + r1] = kept + t
-        wide[1, base + k : base + k + 1] = (w[2] * e)[:1]
-        wide[1, base + r1 + k : base + r1 + k + 1] = (w[3] * e)[r1 - 1 :]
-    wide[0, base : base + r1] = tables[0][0] * errors[0]
-    wide[0, base + r1 : base + 2 * r1] = tables[c1 - 1][1] * errors[c1 - 1]
+        wide[1, base + k : base + k + 1] = y_low[k, :1]
+        wide[1, base + r1 + k : base + r1 + k + 1] = y_high[k, r1 - 1 :]
     publish(wide[0], wide[1], narrow, sheet, payload, semaphore)
 
 
@@ -328,27 +322,23 @@
     outside = outside + as_float((row == 4) & (place[3] == 0)) + as_float((row == rows + 3) & (place[3] == ends[1] - 1))
     low_end, high_end = place[2] == 0, place[2] == ends[0] - 1
 
-    def weigh(at, step, previous):
-        for n in range(step):
-            i = at + n
-            a, ahead = mat[i], mat[i + 1]
-            f = harmonic(a, ahead, 1.0)
-            w_down = harmonic(a, lower(a, 0), 1.0)
-            w_back = jnp.where(lane == 0, 0.0, harmonic(a, lower(a, 1), 1.0))
-            edges = as_float((i == 4) & low_end) + as_float((i == count + 3) & high_end)
-            diagonal = previous + f + w_down + upper(w_down, 0) + w_back + upper(w_back, 1) + a * (outside + edges)
-            inverse = jnp.where(a > 0.0, invert(jnp.maximum(diagonal, 1e-3)), 0.0)
-            fx[i + 1], fy[i], fz[i], inv[i] = f, w_down, w_back, inverse
-            scaled = inverse * res[i]
-            res[i] = scaled
-            x[0, i] = scaled * (1.0 / THETA)
-            previous = f
-        return previous
-
-    first = harmonic(mat[0], mat[1], 1.0)
-    fx[1] = first
-    step = 2
-    lax.fori_loop(0, (total - 2) // step, lambda n, f: weigh(1 + n * step, step, f), first)
+    def chunks(first, last, step):
+        return [(at, min(step, last - at)) for at in range(first, last, step)]
+
+    for at, n in chunks(1, total - 1, SMOOTH_STEP):
+        here = slice(at, at + n)
+        a = mat[here]
+        faces = harmonic(mat[at - 1 : at + n], mat[at : at + n + 1], 1.0)
+        w_down = harmonic(a, lower(a, 1), 1.0)
+        w_back = jnp.where(lane[None] == 0, 0.0, harmonic(a, lower(a, 2), 1.0))
+        plane = at + iota((n, 1, 1), 0)
+        edges = outside[None] + as_float((plane == 4) & low_end) + as_float((plane == count + 3) & high_end)
+        diagonal = faces[:-1] + faces[1:] + w_down + upper(w_down, 1) + w_back + upper(w_back, 2) + a * edges
+        inverse = jnp.where(a > 0.0, invert(jnp.maximum(diagonal, 1e-3)), 0.0)
+        fx[at : at + n + 1], fy[here], fz[here], inv[here] = faces, w_down, w_back, inverse
+        scaled = inverse * res[here]
+        res[here] = scaled
+        x[0, here] = scaled * (1.0 / THETA)
     rho = 1.0 / SIGMA
     for turn in range(DEG - 1):
         if turn == DEG - 2:
@@ -356,25 +346,20 @@
         following = 1.0 / (2.0 * SIGMA - rho)
         old, new = turn % 2, (turn + 1) % 2
         keep, gain = following * rho, 2.0 * following / DELTA
-
-        def sweep(n, _):
-            for k in range(step):
-                i = 2 + turn + n * step + k
-                v = x[old, i]
-                w_down, w_back = fy[i], fz[i]
-                off = fx[i] * x[old, i - 1] + fx[i + 1] * x[old, i + 1]
-                off = off + w_down * lower(v, 0) + upper(w_down * v, 0)
-                off = off + w_back * lower(v, 1) + upper(w_back * v, 1)
-                before = v * keep if turn == 0 else d[i] * keep
-                change = before + gain * (res[i] - v + inv[i] * off)
-                if turn == DEG - 2:
-                    out[i - 4] = potential[i - 4] + (v + change)[4 : 4 + rows]
-                else:
-                    d[i] = change
-                    x[new, i] = v + change
-            return 0
-
-        lax.fori_loop(0, (total - 4 - 2 * turn) // step, sweep, 0)
+        for at, n in chunks(2 + turn, total - 2 - turn, SMOOTH_STEP):
+            here = slice(at, at + n)
+            v = x[old, here]
+            w_down, w_back = fy[here], fz[here]
+            off = fx[here] * x[old, at - 1 : at + n - 1] + fx[at + 1 : at + n + 1] * x[old, at + 1 : at + n + 1]
+            off = off + w_down * lower(v, 1) + upper(w_down * v, 1)
+            off = off + w_back * lower(v, 2) + upper(w_back * v, 2)
+            before = v * keep if turn == 0 else d[here] * keep
+            change = before + gain * (res[here] - v + inv[here] * off)
+            if turn == DEG - 2:
+                out[at - 4 : at + n - 4] = potential[at - 4 : at + n - 4] + (v + change)[:, 4 : 4 + rows]
+            else:
+                d[here] = change
+                x[new, here] = v + change
         rho = following
 
 
@@ -395,24 +380,25 @@
 def fill_table(mat, table, level, count, base, width):
     stride, scale = 2**level, 0.25 ** (level + 2)
     rows = mat.shape[1]
+    row, lane = iota((rows, LANES), 0), iota((rows, LANES), 1)
+    above, beyond = row >= stride, lane >= stride
+    outside = as_float(row == 0) + as_float(row == rows - stride) + as_float(lane == 0) + as_float(lane == width - stride)
 
     def body(at, step):
-        shape = (step, rows, LANES)
-        plane, row, lane = (iota(shape, axis) for axis in range(3))
         a, before, ahead = mat[pl.ds(at + 1, step)], mat[pl.ds(at, step)], mat[pl.ds(at + 2, step)]
         w_before, w_ahead = harmonic(a, before, scale), harmonic(a, ahead, scale)
-        w_down = jnp.where(row < stride, 0.0, harmonic(a, lower(a, 1, stride), scale))
-        w_back = jnp.where(lane < stride, 0.0, harmonic(a, lower(a, 2, stride), scale))
-        outside = as_float(row == 0) + as_float(row == rows - stride) + as_float(lane == 0) + as_float(lane == width - stride)
-        outside = outside + as_float(plane == -at) + as_float(plane == count - 1 - at)
+        w_down = jnp.where(above[None], harmonic(a, lower(a, 1, stride), scale), 0.0)
+        w_back = jnp.where(beyond[None], harmonic(a, lower(a, 2, stride), scale), 0.0)
+        plane = at + iota((step, 1, 1), 0)
+        edges = outside[None] + as_float(plane == 0) + as_float(plane == count - 1)
         diagonal = w_before + w_ahead + w_down + upper(w_down, 1, stride) + w_back + upper(w_back, 2, stride)
-        diagonal = diagonal + scale * a * outside
+        diagonal = diagonal + scale * a * edges
         table[0, pl.ds(base + at, step)] = w_before
         table[1, pl.ds(base + at, step)] = w_down
         table[2, pl.ds(base + at, step)] = w_back
         table[3, pl.ds(base + at, step)] = jnp.where(a > 0.0, invert(jnp.maximum(diagonal, 1e-4)), 0.0)
 
-    each(count, body, 4)
+    each(count, body)
     table[0, base + count] = jnp.zeros((rows, LANES), F32)
 
 
@@ -505,21 +491,29 @@
     return out + [pltpu.VMEM((c2 + 8, rows + 16, LANES), F32)]
 
 
-def spread_blocks(blocks, out, grid, c2, r2):
+def repeat(count, body):
+    if count <= 8:
+        for i in range(count):
+            body(i)
+    else:
+        lax.fori_loop(0, count, lambda i, _: body(i), None)
+
+
+def spread_blocks(blocks, outs, grid, c2, r2):
     gx, gy = grid
     length = c2 // 2 * r2
     low = iota((length, LANES), 1) < LANES // 2
 
-    def column(i, _):
+    def column(i):
         for j in range(gy):
-            block = blocks[i * gy + j, :length]
-            parts = (jnp.where(low, block, 0.0), jnp.where(low, pltpu.roll(block, LANES // 2, 1), 0.0))
-            for k in range(c2):
-                n = k % (c2 // 2)
-                out[i * c2 + k + 1, j * r2 : (j + 1) * r2, :] = parts[k // (c2 // 2)][n * r2 : (n + 1) * r2]
-        return 0
-
-    lax.fori_loop(0, gx, column, 0)
+            for start, out in outs:
+                block = blocks[i * gy + j, start : start + length]
+                parts = (jnp.where(low, block, 0.0), jnp.where(low, pltpu.roll(block, LANES // 2, 1), 0.0))
+                for k in range(c2):
+                    n = k % (c2 // 2)
+                    out[i * c2 + k + 1, j * r2 : (j + 1) * r2, :] = parts[k // (c2 // 2)][n * r2 : (n + 1) * r2]
+
+    repeat(gx, column)
 
 
 def clear_ends(refs, counts):
@@ -529,37 +523,20 @@
         ref[count + 1] = zero
 
 
-def tables_kernel(counts, bases, grid, c2, r2, width, blocks, table, *mats):
-    rows = grid[1] * r2
-    clear_ends(mats, counts)
-    spread_blocks(blocks, mats[0], grid, c2, r2)
-    for level, (count, base) in enumerate(zip(counts, bases)):
-        if level:
-
-            def coarsen(at, step):
-                shape = (step // 2, rows, LANES)
-                whole = (iota(shape, 1) % 2**level == 0) & (iota(shape, 2) % 2**level == 0)
-                mean = 0.125 * fold(mats[level - 1][pl.ds(at + 1, step)], 2 ** (level - 1))
-                mats[level][pl.ds(at // 2 + 1, step // 2)] = jnp.where(whole, mean, 0.0)
-
-            each(counts[level - 1], coarsen)
-        fill_table(mats[level], table, level, count, base, width)
-
-
-def first_cycle_kernel(counts, bases, grid, c2, r2, place, blocks, table, out, *scratch):
+def first_cycle_kernel(counts, bases, grid, c2, r2, width, place, blocks, out, table, *scratch):
     s, e, t, pad = scratch[0:3], list(scratch[3:6]), scratch[6], scratch[7]
     gx, gy = grid
     rows = gy * r2
     half = LANES // 2
     own = c2 // 2 * r2
-    clear_ends(s, counts)
-    spread_blocks(blocks, s[0], grid, c2, r2)
+    clear_ends((t, *s), (counts[0], *counts))
+    spread_blocks(blocks, ((0, s[0]), (own + 2 * r2, t)), grid, c2, r2)
     face_y = e[0]
     low = iota((2 * c2, LANES), 1) < half
 
-    def edges(i, _):
+    def edges(i):
         for j in range(gy):
-            faces = blocks[i * gy + j, own:]
+            faces = blocks[i * gy + j, own : own + 2 * r2]
             x_faces = jnp.where(low, faces, 0.0)
             y_faces = jnp.where(low, pltpu.roll(faces, half, 1), 0.0)
             here = slice(j * r2, (j + 1) * r2)
@@ -571,18 +548,28 @@
                     face_y[at, j * r2 - 1 : j * r2, :] = y_faces[k : k + 1]
                 if j < gy - 1:
                     face_y[at, (j + 1) * r2 : (j + 1) * r2 + 1, :] = y_faces[c2 + k : c2 + k + 1]
-        return 0
-
-    lax.fori_loop(0, gx, edges, 0)
+
+    repeat(gx, edges)
 
     def join(at, step):
         now = pl.ds(at + 1, step)
-        row = iota((step, rows, LANES), 1)
+        row = iota((rows, LANES), 0)
         edge = ((row % r2 == 0) & (row > 0)) | ((row % r2 == r2 - 1) & (row < rows - 1))
-        s[0][now] = s[0][now] + jnp.where(edge, face_y[now], 0.0)
+        s[0][now] = s[0][now] + jnp.where(edge[None], face_y[now], 0.0)
 
     each(counts[0], join)
     clear_ends(s[:1], counts)
+    mats = (t, s[1], s[2])
+    for level, (count, base) in enumerate(zip(counts, bases)):
+        if level:
+
+            def coarsen(at, step):
+                whole = (iota((rows, LANES), 0) % 2**level == 0) & (iota((rows, LANES), 1) % 2**level == 0)
+                mean = 0.125 * fold(mats[level - 1][pl.ds(at + 1, step)], 2 ** (level - 1))
+                mats[level][pl.ds(at // 2 + 1, step // 2)] = jnp.where(whole[None], mean, 0.0)
+
+            each(counts[level - 1], coarsen)
+        fill_table(mats[level], table, level, count, base, width)
     cycle(s, e, t, table, counts, bases, place, out, c2, r2, pad)
 
 
@@ -627,52 +614,50 @@
     raise_window(window1, flat, prolonged)
     row, lane = iota((length, depth), 0), iota((length, depth), 1)
     ends = as_float(lane == 0) + as_float(lane == depth - 1)
-    fx[1] = harmonic(mat[0], mat[1], 0.25)
-    for k in range(1, total - 1):
-        a, before, ahead = mat[k], mat[k - 1], mat[k + 1]
-        down, up = lower(a, 0), upper(a, 0)
-        f = harmonic(a, ahead, 0.25)
+    def chunks(margin):
+        first, last = margin, total - margin
+        return [(at, min(LEVEL1_STEP, last - at)) for at in range(first, last, LEVEL1_STEP)]
+
+    for at, n in chunks(1):
+        here = slice(at, at + n)
+        a, before, ahead = mat[here], mat[at - 1 : at + n - 1], mat[at + 1 : at + n + 1]
+        down, up = lower(a, 1), upper(a, 1)
+        f = harmonic(mat[at - 1 : at + n], mat[at : at + n + 1], 0.25)
         w_y = harmonic(a, down, 0.25)
-        w_z = jnp.where(lane == 0, 0.0, harmonic(a, lower(a, 1), 0.25))
-        outside = ends + as_float(before <= 0.0) + as_float(ahead <= 0.0) + as_float(down <= 0.0) + as_float(up <= 0.0)
-        diagonal = fx[k] + f + w_y + upper(w_y, 0) + w_z + upper(w_z, 1) + 0.25 * a * outside
+        w_z = jnp.where(lane[None] == 0, 0.0, harmonic(a, lower(a, 2), 0.25))
+        outside = ends[None] + as_float(before <= 0.0) + as_float(ahead <= 0.0) + as_float(down <= 0.0) + as_float(up <= 0.0)
+        diagonal = f[:-1] + f[1:] + w_y + upper(w_y, 1) + w_z + upper(w_z, 2) + 0.25 * a * outside
         inverse = jnp.where(a > 0.0, invert(jnp.maximum(diagonal, 1e-4)), 0.0)
-        fx[k + 1], fy[k], fz[k], diag[k], inv[k] = f, w_y, w_z, diagonal, inverse
-        err[k] = DAMPING * inverse * src[k] + prolonged[k]
-
-    def off(v, k):
-        here = v[k]
-        w_y, w_z = fy[k], fz[k]
-        out = fx[k] * v[k - 1] + fx[k + 1] * v[k + 1] + w_y * lower(here, 0) + upper(w_y * here, 0)
-        return here, out + w_z * lower(here, 1) + upper(w_z * here, 1)
-
-    for k in range(2, total - 2):
-        here, more = off(err, k)
-        c[k] = KEPT * here + DAMPING * inv[k] * (src[k] + more)
-    for k in range(3, total - 3):
-        here, more = off(c, k)
-        left = src[k] - diag[k] * here + more
-        src[k] = left
-        value = DAMPING * inv[k] * left
-        err[k] = value
-        state[k - 3] = value
+        fx[at : at + n + 1], fy[here], fz[here], diag[here], inv[here] = f, w_y, w_z, diagonal, inverse
+        err[here] = DAMPING * inverse * src[here] + prolonged[here]
+
+    def off(v, at, n):
+        here = slice(at, at + n)
+        mid, w_y, w_z = v[here], fy[here], fz[here]
+        out = fx[here] * v[at - 1 : at + n - 1] + fx[at + 1 : at + n + 1] * v[at + 1 : at + n + 1]
+        out = out + w_y * lower(mid, 1) + upper(w_y * mid, 1)
+        return here, mid, out + w_z * lower(mid, 2) + upper(w_z * mid, 2)
+
+    for at, n in chunks(2):
+        here, mid, more = off(err, at, n)
+        c[here] = KEPT * mid + DAMPING * inv[here] * (src[here] + more)
+    for at, n in chunks(3):
+        here, mid, more = off(c, at, n)
+        left = src[here] - diag[here] * mid + more
+        src[here] = left
+        value = DAMPING * inv[here] * left
+        err[here] = value
+        state[at - 3 : at + n - 3] = value
     base = count + 2
-    for k in range(count + 1):
-        state[base + k] = fx[k + 4]
+    state[base : base + count + 1] = fx[4 : count + 5]
     base += count + 1
     for n, ref in enumerate((fy, fz, inv, c, src)):
-        for k in range(count):
-            state[base + n * count + k] = ref[k + 4]
+        state[base + n * count : base + (n + 1) * count] = ref[4 : 4 + count]
     leaving = pltpu.make_async_copy(state, state_far, semaphores.at[0])
     leaving.start()
-    for k in range(4, count + 4):
-        _, more = off(err, k)
-        t = (KEPT * src[k] + more)[4 : 4 + rows]
-        if k % 2 == 0:
-            kept = t
-        else:
-            at = (k - 5) // 2 * rows
-            wide[at : at + rows] = kept + t
+    here, _, more = off(err, 4, count)
+    t = (KEPT * src[here] + more)[:, 4 : 4 + rows].reshape(count // 2, 2, rows, depth)
+    wide[...] = (t[:, 0] + t[:, 1]).reshape(count // 2 * rows, depth)
     half = wide.shape[0] // 2
     publish(wide[:half], wide[half:], narrow, sheet, payload, semaphores.at[1])
     leaving.wait()
@@ -680,35 +665,43 @@
 
 def last_cycle_kernel(counts, bases, grid, c2, r2, place, blocks, table, state_far, partial, out, *scratch):
     s, e, t, pad = scratch[0:3], list(scratch[3:6]), scratch[6], scratch[7]
-    view, flat, prolonged, tall, coarse, state, semaphore = scratch[8:15]
+    view, flat, prolonged, tall, coarse, state, semaphore, result, departures = scratch[8:17]
     arriving = pltpu.make_async_copy(state_far, state, semaphore)
     arriving.start()
-    spread_blocks(blocks, s[0], grid, c2, r2)
+    spread_blocks(blocks, ((0, s[0]),), grid, c2, r2)
     clear_ends(s, counts)
     cycle(s, e, t, table, counts, bases, place, view, c2, r2, pad)
     raise_window(view, flat, prolonged)
     count, rows, depth = partial.shape
     c1, r1 = count // 2, rows // 2
     arriving.wait()
-    for k in range(c1 + 2):
-        prolonged[k + 3] = prolonged[k + 3] + state[k]
+    v = prolonged[3 : c1 + 5] + state[: c1 + 2]
+    here = v[1:-1]
     base = 2 * c1 + 3
-    for k in range(c1):
-        here = prolonged[k + 4]
-        w_y, w_z, inverse, before, left = (state[base + n * c1 + k] for n in range(5))
-        off = state[c1 + 2 + k] * prolonged[k + 3] + state[c1 + 3 + k] * prolonged[k + 5]
-        off = off + w_y * lower(here, 0) + upper(w_y * here, 0) + w_z * lower(here, 1) + upper(w_z * here, 1)
-        total = before + KEPT * here + DAMPING * inverse * (left + off)
-        coarse[k * r1 : (k + 1) * r1] = total[4 : 4 + r1]
+    w_x = state[c1 + 2 : base]
+    w_y, w_z, inverse, before, left = (state[base + n * c1 : base + (n + 1) * c1] for n in range(5))
+    off = w_x[:-1] * v[:-2] + w_x[1:] * v[2:]
+    off = off + w_y * lower(here, 1) + upper(w_y * here, 1) + w_z * lower(here, 2) + upper(w_z * here, 2)
+    total = before + KEPT * here + DAMPING * inverse * (left + off)
+    coarse[...] = total[:, 4 : 4 + r1].reshape(c1 * r1, LANES)
     values = select(coarse[...], spread_matrix(depth))
     for piece in range(depth // LANES):
         z = slice(piece * LANES, (piece + 1) * LANES)
         tall[piece, pl.ds(0, c1 * r1, 2)] = values[:, z]
         tall[piece, pl.ds(1, c1 * r1, 2)] = values[:, z]
-        for k in range(c1):
+    leaving = []
+    for k in range(c1):
+        for piece in range(depth // LANES):
+            z = slice(piece * LANES, (piece + 1) * LANES)
             more = tall[piece, k * rows : (k + 1) * rows]
-            out[2 * k, :, z] = partial[2 * k, :, z] + more
-            out[2 * k + 1, :, z] = partial[2 * k + 1, :, z] + more
+            result[2 * k, :, z] = partial[2 * k, :, z] + more
+            result[2 * k + 1, :, z] = partial[2 * k + 1, :, z] + more
+        if k % 2 == 1:
+            planes = pl.ds(2 * k - 2, 4)
+            leaving.append(pltpu.make_async_copy(result.at[planes], out.at[planes], departures.at[k // 2]))
+            leaving[-1].start()
+    for copy in leaving:
+        copy.wait()
 
 
 def size_of(shape):
@@ -786,17 +779,13 @@
     face = (3, rows, depth)
     DMA = pltpu.SemaphoreType.DMA
     sheet = (devices, c2 // 2 * r2, LANES)
-    sheet2 = (devices, c2 // 2 * r2 + 2 * r2, LANES)
-    material, potential_here, source_here, inner, outer, even, odd, materials = call(
+    sheet2 = (devices, c2 * r2 + 2 * r2, LANES)
+    material, potential_here, source_here, inner, outer, even, odd = call(
         faces_kernel, "faces", (place, permeability, potential, phase, right_side),
-        (brick, brick, brick, face, face, (3, count, depth), (3, count, depth), ("far", sheet)),
-        (
-            pltpu.VMEM(brick, jnp.int32), pltpu.SMEM(permeability.shape, F32), pltpu.SemaphoreType.DMA((5,)),
-            VM(c1 * rows, depth), VM(c1 * rows, LANES), VM(c2 * r1, LANES), VM(c2 // 2 * r1, LANES), VM(*sheet),
-        ),
+        (brick, brick, brick, face, face, (3, count, depth), (3, count, depth)),
+        (pltpu.VMEM(brick, jnp.int32), pltpu.SMEM(permeability.shape, F32), pltpu.SemaphoreType.DMA((4,))),
         apart=(1, 2, 3, 4),
     )
-    materials = lax.all_to_all(materials, ("gx", "gy"), 0, 0)
     even = lax.ppermute(even, "gy", swap_y[0])
     odd = lax.ppermute(odd, "gy", swap_y[1])
     outer = lax.ppermute(outer, "gx", swap_x[1])
@@ -807,11 +796,13 @@
     residual, coarse, even, odd = call(
         residual_kernel, "residual", (place, source_here, potential_here, material, inner, outer, even, odd),
         (brick, (total // 2, LANES), strip, strip),
-        (VM(total, depth), VM(total, LANES), VM(4, count, depth)), cost=10**10,
+        (
+            VM(total, depth), VM(total, LANES), VM(4, count, 8, depth), VM(count + 2, rows, depth), VM(count + 2, rows, depth),
+        ),
     )
     even = lax.ppermute(even, "gy", swap_y[0])
     odd = lax.ppermute(odd, "gy", swap_y[1])
-    small = c2 // 2 * r1 + 2 * r1
+    small = c2 * r1 + 2 * r1
     (payload,) = call(
         functools.partial(payload_kernel, c1, r1), "payload", (coarse,), (("far", sheet2),),
         (VM(2, small, d1), VM(small, LANES), VM(*sheet2), DMA),
@@ -830,13 +821,9 @@
     bases = (0, counts[0] + 1, counts[0] + counts[1] + 2)
     work = cycle_shapes(counts, gy * r2, c2)
     view = (c2 + 4, r2 + 4, LANES)
-    planes = [VM(n + 2, gy * r2, LANES) for n in counts]
-    (table,) = call(
-        functools.partial(tables_kernel, counts, bases, (gx, gy), c2, r2, d1 // 2), "tables", (materials,),
-        ((4, sum(counts) + 3, gy * r2, LANES),), planes,
-    )
-    (window1,) = call(
-        functools.partial(first_cycle_kernel, counts, bases, (gx, gy), c2, r2), "cycle1", (place, blocks, table), (view,), work,
+    window1, table = call(
+        functools.partial(first_cycle_kernel, counts, bases, (gx, gy), c2, r2, d1 // 2), "cycle1", (place, blocks),
+        (view, (4, sum(counts) + 3, gy * r2, LANES)), work,
     )
     frame = (c1 + 8, r1 + 8, d1)
     flat = VM((c2 + 4) * (r2 + 4) * 2, LANES)
@@ -861,8 +848,11 @@
     )
     (out,) = call(
         functools.partial(last_cycle_kernel, counts, bases, (gx, gy), c2, r2), "cycle2",
-        (place, blocks, table, held, partial), (jax.ShapeDtypeStruct(brick, F32),),
-        (*work, VM(*view), flat, VM(*frame), VM(pieces, c1 * rows, LANES), VM(c1 * r1, LANES), VM(*state), DMA),
+        (place, blocks, table, held, partial), (("far", brick),),
+        (
+            *work, VM(*view), flat, VM(*frame), VM(pieces, c1 * rows, LANES), VM(c1 * r1, LANES), VM(*state), DMA,
+            VM(*brick), pltpu.SemaphoreType.DMA((c1 // 2,)),
+        ),
         apart=(3,),
     )
     return out

time: 59.3 us -> 57 us (0.961)
  Pallas kernels: 23.6 us -> 18 us
  waiting for transfers between devices: 10.6 us -> 15.1 us
  starting transfers between devices: 24.5 us -> 23.2 us
    all_to_all x1 -> x0, starting transfers between devices: 8.52 us -> none  [local(): materials = lax.all_to_all(materials, ('gx', 'gy'), 0, 0)]
    all_to_all x2, waiting for transfers between devices: 7.25 us -> 13.7 us  [local(): blocks = lax.all_to_all(payload, ('gx', 'gy'), 0, 0)]
    pallas_call x9 -> x8, Pallas kernels: 23.6 us -> 18 us  [call(): pl.pallas_call(kernel, out_shape=results, in_specs=specs, out_specs=[pl.B...]
    all_to_all x2, starting transfers between devices: 7.38 us -> 11.4 us  [local(): blocks = lax.all_to_all(payload, ('gx', 'gy'), 0, 0)]
    all_to_all x1 -> x0, waiting for transfers between devices: 3.33 us -> none  [local(): materials = lax.all_to_all(materials, ('gx', 'gy'), 0, 0)]
    ppermute x2, starting transfers between devices: 4.5 us -> 7.76 us  [local(): even = lax.ppermute(even, 'gy', swap_y[0])]
    ppermute x2, waiting for transfers between devices: 0.01 us -> 1.39 us  [local(): even = lax.ppermute(even, 'gy', swap_y[0])]
  transfers between devices with their start and end apart: 11 -> 10, of which waited for: 3 -> 3; matrix products, arithmetic and copies ran while one was open for 0% -> 0% of each run, Pallas kernels for 26% -> 16%
where the time goes in v5:
time: 57 us; the launch traced here: 56.5 us
  starting transfers between devices  23.2 us (41%)
  Pallas kernels  18 us (32%)
  waiting for transfers between devices  15.1 us (26%)
    pallas_call x8, Pallas kernels, call(): pl.pallas_call(kernel, out_shape=results, in_specs=specs, out_specs=[pl.B...  18 us
    all_to_all x2, waiting for transfers between devices, local(): blocks = lax.all_to_all(payload, ('gx', 'gy'), 0, 0)  13.7 us
    all_to_all x2, starting transfers between devices, local(): blocks = lax.all_to_all(payload, ('gx', 'gy'), 0, 0)  11.4 us
    ppermute x2, starting transfers between devices, local(): even = lax.ppermute(even, 'gy', swap_y[0])  7.76 us
    ppermute x2, starting transfers between devices, local(): outer = lax.ppermute(outer, 'gx', swap_x[1])  2 us
    ppermute x2, waiting for transfers between devices, local(): even = lax.ppermute(even, 'gy', swap_y[0])  1.39 us
    ppermute x2, starting transfers between devices, local(): odd = lax.ppermute(odd, 'gy', swap_y[1])  1.31 us
  transfers between devices with their start and end apart: 10, of which 3 were waited for; matrix products, arithmetic and copies ran while one was open for 0% of the time, Pallas kernels for 16%

profile of v5, /device:TPU:0, one launch (start us, length us, event | category | flops | bytes accessed | tf_op | source)
XLA Modules:
  0.0 56.5 jit_solution(8429880414729057715)
XLA Ops:
  0.0 0.1 pad_add_fusion.place
  0.1 1.7 %faces.1 = (f32[16,16,256]{2,1,0:T(8,128)S(1)}, f32[16,16,256]{2,1,0:T(8,128)S(1)}, f32[16,16,256]{2,1,0:T(8,128)S(1)}, f32[3,16,256]{2,1,0:T(8,128)S(1)}, f32[3...) custom-call(s32[4]{0:T(128)S(1)} %pad_add_fusion.place, f32[3]{0:T(128)} %permeability.1, ...), custom_call_target="tpu_custom_call" | custom-call | tf_op jit(solution)/shard_map/faces/pallas_call | solution.py:748
  1.8 0.5 collective-permute-start
  2.3 0.7 %collective-permute-start.1 = (f32[3,16,256]{2,1,0:T(8,128)S(1)}, f32[3,16,256]{2,1,0:T(8,128)S(1)}, u32[]{:S(2)}, u32[]{:S(2)}) collective-permute-start(f32[3,16,256]{2,1,0:T(8,128)S(1)} %get-tuple-element.27), channel_id=1, source_target_pairs={{4,8},{12,16},{20,24},{8,4},{16,12},{24,20},{5,9},{13,17},{21,25},... | collective-permute-start | bytes 147464 | tf_op jit(solution)/shard_map/ppermute | solution.py:791
  2.9 2.7 %collective-permute-start.2 = (f32[3,16,256]{2,1,0:T(8,128)S(1)}, f32[3,16,256]{2,1,0:T(8,128)S(1)}, u32[]{:S(2)}, u32[]{:S(2)}) collective-permute-start(f32[3,16,256]{2,1,0:T(8,128)S(1)} %get-tuple-element.28), channel_id=1, source_target_pairs={{0,1},{2,3},{1,0},{3,2},{4,5},{6,7},{5,4},{7,6},{8,9},{10,11},{9,8... | collective-permute-start | bytes 147464 | tf_op jit(solution)/shard_map/ppermute | solution.py:789
  5.6 0.7 %collective-permute-start.3 = (f32[3,16,256]{2,1,0:T(8,128)S(1)}, f32[3,16,256]{2,1,0:T(8,128)S(1)}, u32[]{:S(2)}, u32[]{:S(2)}) collective-permute-start(f32[3,16,256]{2,1,0:T(8,128)S(1)} %get-tuple-element.29), channel_id=1, source_target_pairs={{1,2},{2,1},{5,6},{6,5},{9,10},{10,9},{13,14},{14,13},{17,18},{18,... | collective-permute-start | bytes 147464 | tf_op jit(solution)/shard_map/ppermute | solution.py:790
  6.3 0.0 collective-permute-done.inner
  6.3 0.0 collective-permute-done.1.outer
  6.3 1.4 %collective-permute-done.2.even = f32[3,16,256]{2,1,0:T(8,128)S(1)} collective-permute-done((f32[3,16,256]{2,1,0:T(8,128)S(1)}, f32[3,16,256]{2,1,0:T(8,128)S(1)}, u32[]{:S(2)}, u32[]{:S(2)}) %collective-permute-start.2) | collective-permute-done | bytes 49184 | tf_op jit(solution)/shard_map/ppermute | solution.py:789
  7.7 0.0 collective-permute-done.3.odd
  7.7 1.6 %residual.1 = (f32[16,16,256]{2,1,0:T(8,128)S(1)}, f32[160,128]{1,0:T(8,128)S(1)}, f32[40,8,128]{2,1,0:T(8,128)S(1)}, f32[40,8,128]{2,1,0:T(8,128)S(1)}) custom-call(s32[4]{0:T(128)S(1)} %pad_add_fusion.place, f32[16,16,256]{2,1,0:T(8,128)S(1)} %get-tuple-element.23.source, f32[16,16,256]{2,1,0:T(8,128)S(1)} %get-tuple-element.24.potential, ...), custom_call_target="tpu_custom_call" | custom-call | tf_op jit(solution)/shard_map/residual/pallas_call | solution.py:748
  9.3 5.1 %collective-permute-start.4 = (f32[40,8,128]{2,1,0:T(8,128)S(1)}, f32[40,8,128]{2,1,0:T(8,128)S(1)}, u32[]{:S(2)}, u32[]{:S(2)}) collective-permute-start(f32[40,8,128]{2,1,0:T(8,128)S(1)} %get-tuple-element.32), channel_id=1, source_target_pairs={{0,1},{2,3},{1,0},{3,2},{4,5},{6,7},{5,4},{7,6},{8,9},{10,11},{9,8... | collective-permute-start | bytes 491528 | tf_op jit(solution)/shard_map/ppermute | solution.py:803
  14.4 0.7 %collective-permute-start.5 = (f32[40,8,128]{2,1,0:T(8,128)S(1)}, f32[40,8,128]{2,1,0:T(8,128)S(1)}, u32[]{:S(2)}, u32[]{:S(2)}) collective-permute-start(f32[40,8,128]{2,1,0:T(8,128)S(1)} %get-tuple-element.33), channel_id=1, source_target_pairs={{1,2},{2,1},{5,6},{6,5},{9,10},{10,9},{13,14},{14,13},{17,18},{18,... | collective-permute-start | bytes 491528 | tf_op jit(solution)/shard_map/ppermute | solution.py:804
  15.0 1.2 %payload.1 = f32[32,24,128]{2,1,0:T(8,128)} custom-call(f32[160,128]{1,0:T(8,128)S(1)} %get-tuple-element.31.coarse), custom_call_target="tpu_custom_call" | custom-call | tf_op jit(solution)/shard_map/payload/pallas_call | solution.py:748
  16.2 7.4 %all-to-all-start = ((f32[32,24,128]{2,1,0:T(8,128)}), f32[32,24,128]{2,1,0:T(8,128)S(1)}, u32[]{:S(2)}, u32[]{:S(2)}) async-start(f32[32,24,128]{2,1,0:T(8,128)} %payload.1), calls=%async_computation | async-start | bytes 786432 | tf_op jit(solution)/shard_map/all_to_all | solution.py:810
  23.7 0.0 collective-permute-done.4.even
  23.7 0.0 collective-permute-done.5.odd
  23.7 1.4 %strips.1 = (f32[56,8,128]{2,1,0:T(8,128)}, f32[56,8,128]{2,1,0:T(8,128)}, f32[2,20,24,256]{3,2,1,0:T(8,128)S(1)}) custom-call(s32[4]{0:T(128)S(1)} %pad_add_fusion.place, f32[16,16,256]{2,1,0:T(8,128)S(1)} %get-tuple-element.30.residual, f32[16,16,256]{2,1,0:T(8,128)S(1)} %get-tuple-element.25.material, f32[160,128]{1,0:T(8,128)S(1)} %get-tuple-element.31.coarse, ...), custom_call_target="tpu_custom_call" | custom-call | flops 99999997952 | tf_op jit(solution)/shard_map/strips/pallas_call | solution.py:748
  25.1 0.3 collective-permute-start.6
  25.4 1.4 %collective-permute-start.7 = (f32[56,8,128]{2,1,0:T(8,128)}, f32[56,8,128]{2,1,0:T(8,128)}, u32[]{:S(2)}, u32[]{:S(2)}) collective-permute-start(f32[56,8,128]{2,1,0:T(8,128)} %get-tuple-element.36), channel_id=1, source_target_pairs={{4,8},{12,16},{20,24},{8,4},{16,12},{24,20},{5,9},{13,17},{21,25},... | collective-permute-start | bytes 688136 | tf_op jit(solution)/shard_map/ppermute | solution.py:817
  26.7 8.8 %all-to-all-done.blocks = f32[32,24,128]{2,1,0:T(8,128)S(1)} async-done(((f32[32,24,128]{2,1,0:T(8,128)}), f32[32,24,128]{2,1,0:T(8,128)S(1)}, u32[]{:S(2)}, u32[]{:S(2)}) %all-to-all-start) | async-done | bytes 393248 | tf_op jit(solution)/shard_map/all_to_all | solution.py:810
  35.5 2.8 %cycle1.1 = (f32[8,8,128]{2,1,0:T(8,128)S(1)}, f32[4,59,16,128]{3,2,1,0:T(8,128)S(1)}) custom-call(s32[4]{0:T(128)S(1)} %pad_add_fusion.place, f32[32,24,128]{2,1,0:T(8,128)S(1)} %all-to-all-done.blocks), custom_call_target="tpu_custom_call" | custom-call | tf_op jit(solution)/shard_map/cycle1/pallas_call | solution.py:748
  38.3 0.0 collective-permute-done.6.inner
  38.3 0.0 collective-permute-done.7.outer
  38.3 2.3 %level1.1 = (f32[32,8,128]{2,1,0:T(8,128)}, f32[59,16,128]{2,1,0:T(8,128)}) custom-call(s32[4]{0:T(128)S(1)} %pad_add_fusion.place, f32[2,20,24,256]{3,2,1,0:T(8,128)S(1)} %get-tuple-element.34.long, f32[56,8,128]{2,1,0:T(8,128)S(1)} %collective-permute-done.6.inner, f32[56,8,128]{2,1,0:T(8,128)} %collective-permute-done.7.outer, ...), custom_call_target="tpu_custom_call" | custom-call | tf_op jit(solution)/shard_map/level1/pallas_call | solution.py:748
  40.6 4.0 %all-to-all-start.1 = ((f32[32,8,128]{2,1,0:T(8,128)}), f32[32,8,128]{2,1,0:T(8,128)S(1)}, u32[]{:S(2)}, u32[]{:S(2)}) async-start(f32[32,8,128]{2,1,0:T(8,128)} %get-tuple-element.38), calls=%async_computation.1 | async-start | bytes 262144 | tf_op jit(solution)/shard_map/all_to_all | solution.py:839
  44.6 3.5 %smooth.1.partial = f32[16,16,256]{2,1,0:T(8,128)S(1)} custom-call(s32[4]{0:T(128)S(1)} %pad_add_fusion.place, f32[16,16,256]{2,1,0:T(8,128)} %potential_far.1, f32[2,20,24,256]{3,2,1,0:T(8,128)S(1)} %get-tuple-element.34.long, f32[56,8,128]{2,1,0:T(8,128)S(1)} %collective-permute-done.6.inner, f32[56,8,128]{2,1,0:T(8,128)} %collective-permute-done.7.outer), custom_call_target="tpu_custom_call" | custom-call | tf_op jit(solution)/shard_map/smooth/pallas_call | solution.py:748
  48.1 4.9 %all-to-all-done.1.blocks = f32[32,8,128]{2,1,0:T(8,128)S(1)} async-done(((f32[32,8,128]{2,1,0:T(8,128)}), f32[32,8,128]{2,1,0:T(8,128)S(1)}, u32[]{:S(2)}, u32[]{:S(2)}) %all-to-all-start.1) | async-done | bytes 131104 | tf_op jit(solution)/shard_map/all_to_all | solution.py:839
  53.0 3.5 %cycle2.1 = f32[16,16,256]{2,1,0:T(8,128)} custom-call(s32[4]{0:T(128)S(1)} %pad_add_fusion.place, f32[32,8,128]{2,1,0:T(8,128)S(1)} %all-to-all-done.1.blocks, f32[4,59,16,128]{3,2,1,0:T(8,128)S(1)} %get-tuple-element.39.table, f32[59,16,128]{2,1,0:T(8,128)} %get-tuple-element.40.state_far, f32[16,16,256]{2,1,0:T(8,128)S(1)} %smooth.1.partial), custom_call_target="tpu_custom_call" | custom-call | tf_op jit(solution)/shard_map/cycle2/pallas_call | solution.py:748
Async XLA Ops:
  1.8 4.5 %collective-permute-start = (f32[3,16,256]{2,1,0:T(8,128)S(1)}, f32[3,16,256]{2,1,0:T(8,128)S(1)}, u32[]{:S(2)}, u32[]{:S(2)}) collective-permute-start(f32[3,16,256]{2,1,0:T(8,128)S(1)} %get-tuple-element.26), channel_id=1, source_target_pairs={{0,4},{8,12},{16,20},{24,28},{4,0},{12,8},{20,16},{28,24},{1,5},{9... | collective-permute-start | bytes 147464 | tf_op jit(solution)/shard_map/ppermute | solution.py:792
  2.3 4.0 %collective-permute-start.1 = (f32[3,16,256]{2,1,0:T(8,128)S(1)}, f32[3,16,256]{2,1,0:T(8,128)S(1)}, u32[]{:S(2)}, u32[]{:S(2)}) collective-permute-start(f32[3,16,256]{2,1,0:T(8,128)S(1)} %get-tuple-element.27), channel_id=1, source_target_pairs={{4,8},{12,16},{20,24},{8,4},{16,12},{24,20},{5,9},{13,17},{21,25},... | collective-permute-start | bytes 147464 | tf_op jit(solution)/shard_map/ppermute | solution.py:791
  2.9 4.7 %collective-permute-start.2 = (f32[3,16,256]{2,1,0:T(8,128)S(1)}, f32[3,16,256]{2,1,0:T(8,128)S(1)}, u32[]{:S(2)}, u32[]{:S(2)}) collective-permute-start(f32[3,16,256]{2,1,0:T(8,128)S(1)} %get-tuple-element.28), channel_id=1, source_target_pairs={{0,1},{2,3},{1,0},{3,2},{4,5},{6,7},{5,4},{7,6},{8,9},{10,11},{9,8... | collective-permute-start | bytes 147464 | tf_op jit(solution)/shard_map/ppermute | solution.py:789
  5.6 2.1 %collective-permute-start.3 = (f32[3,16,256]{2,1,0:T(8,128)S(1)}, f32[3,16,256]{2,1,0:T(8,128)S(1)}, u32[]{:S(2)}, u32[]{:S(2)}) collective-permute-start(f32[3,16,256]{2,1,0:T(8,128)S(1)} %get-tuple-element.29), channel_id=1, source_target_pairs={{1,2},{2,1},{5,6},{6,5},{9,10},{10,9},{13,14},{14,13},{17,18},{18,... | collective-permute-start | bytes 147464 | tf_op jit(solution)/shard_map/ppermute | solution.py:790
  9.3 14.4 %collective-permute-start.4 = (f32[40,8,128]{2,1,0:T(8,128)S(1)}, f32[40,8,128]{2,1,0:T(8,128)S(1)}, u32[]{:S(2)}, u32[]{:S(2)}) collective-permute-start(f32[40,8,128]{2,1,0:T(8,128)S(1)} %get-tuple-element.32), channel_id=1, source_target_pairs={{0,1},{2,3},{1,0},{3,2},{4,5},{6,7},{5,4},{7,6},{8,9},{10,11},{9,8... | collective-permute-start | bytes 491528 | tf_op jit(solution)/shard_map/ppermute | solution.py:803
  14.4 9.3 %collective-permute-start.5 = (f32[40,8,128]{2,1,0:T(8,128)S(1)}, f32[40,8,128]{2,1,0:T(8,128)S(1)}, u32[]{:S(2)}, u32[]{:S(2)}) collective-permute-start(f32[40,8,128]{2,1,0:T(8,128)S(1)} %get-tuple-element.33), channel_id=1, source_target_pairs={{1,2},{2,1},{5,6},{6,5},{9,10},{10,9},{13,14},{14,13},{17,18},{18,... | collective-permute-start | bytes 491528 | tf_op jit(solution)/shard_map/ppermute | solution.py:804
  16.2 19.2 %all-to-all-start = ((f32[32,24,128]{2,1,0:T(8,128)}), f32[32,24,128]{2,1,0:T(8,128)S(1)}, u32[]{:S(2)}, u32[]{:S(2)}) async-start(f32[32,24,128]{2,1,0:T(8,128)} %payload.1), calls=%async_computation | async-start | bytes 786432 | tf_op jit(solution)/shard_map/all_to_all | solution.py:810
  25.1 13.2 %collective-permute-start.6 = (f32[56,8,128]{2,1,0:T(8,128)}, f32[56,8,128]{2,1,0:T(8,128)S(1)}, u32[]{:S(2)}, u32[]{:S(2)}) collective-permute-start(f32[56,8,128]{2,1,0:T(8,128)} %get-tuple-element.35), channel_id=1, source_target_pairs={{0,4},{8,12},{16,20},{24,28},{4,0},{12,8},{20,16},{28,24},{1,5},{9... | collective-permute-start | bytes 688136 | tf_op jit(solution)/shard_map/ppermute | solution.py:818
  25.4 13.0 %collective-permute-start.7 = (f32[56,8,128]{2,1,0:T(8,128)}, f32[56,8,128]{2,1,0:T(8,128)}, u32[]{:S(2)}, u32[]{:S(2)}) collective-permute-start(f32[56,8,128]{2,1,0:T(8,128)} %get-tuple-element.36), channel_id=1, source_target_pairs={{4,8},{12,16},{20,24},{8,4},{16,12},{24,20},{5,9},{13,17},{21,25},... | collective-permute-start | bytes 688136 | tf_op jit(solution)/shard_map/ppermute | solution.py:817
  40.6 12.4 %all-to-all-start.1 = ((f32[32,8,128]{2,1,0:T(8,128)}), f32[32,8,128]{2,1,0:T(8,128)S(1)}, u32[]{:S(2)}, u32[]{:S(2)}) async-start(f32[32,8,128]{2,1,0:T(8,128)} %get-tuple-element.38), calls=%async_computation.1 | async-start | bytes 262144 | tf_op jit(solution)/shard_map/all_to_all | solution.py:839

commit v6 on v5

--- a/solution.py
+++ b/solution.py
@@ -247,7 +247,7 @@
     leaving.wait()
 
 
-def strips_kernel(place, residual, material, coarse, even, odd, inner, outer, long):
+def strips_kernel(place, residual, material, coarse, even, odd, inner, outer, long_far, long1, long, semaphore):
     low_x, low_y = place[0] == 1, place[1] == 1
     count, rows, depth = residual.shape
     pieces = depth // LANES
@@ -264,12 +264,13 @@
             z = slice(piece * LANES, (piece + 1) * LANES)
             long[0, i, :, z] = jnp.concatenate([low[:4], residual[i, :, z], high[:4]], axis=0)
             long[1, i, :, z] = jnp.concatenate([low[4:], material[i, :, z], high[4:]], axis=0)
+    leaving = pltpu.make_async_copy(long, long_far, semaphore)
+    leaving.start()
     for k in range(c1):
         low, high = sides(base + k)
         s, m = coarse[k * r1 : (k + 1) * r1], coarse[(c1 + k) * r1 : (c1 + k + 1) * r1]
-        i, z = count + k // 2, slice(k % 2 * LANES, (k % 2 + 1) * LANES)
-        long[0, i, : r1 + 8, z] = jnp.concatenate([low[:4], s, high[:4]], axis=0)
-        long[1, i, : r1 + 8, z] = jnp.concatenate([low[4:], m, high[4:]], axis=0)
+        long1[0, k] = jnp.concatenate([low[:4], s, high[:4]], axis=0)
+        long1[1, k] = jnp.concatenate([low[4:], m, high[4:]], axis=0)
 
     def pack(out, flag):
         at = 0
@@ -285,13 +286,12 @@
                 low, high = k, c1 - planes + k
                 for tile in range((r1 + 8) // 8):
                     y = slice(tile * 8, tile * 8 + 8)
-                    a = long[n, count + low // 2, y, low % 2 * LANES : (low % 2 + 1) * LANES]
-                    b = long[n, count + high // 2, y, high % 2 * LANES : (high % 2 + 1) * LANES]
-                    out[at] = jnp.where(flag, a, b)
+                    out[at] = jnp.where(flag, long1[n, low, y], long1[n, high, y])
                     at += 1
 
     pack(inner, low_x)
     pack(outer, jnp.logical_not(low_x))
+    leaving.wait()
 
 
 def unpack(source, flag, out, start, planes, tiles, pieces, at):
@@ -304,9 +304,18 @@
     return at
 
 
-def smooth_kernel(ends, place, potential_far, long, inner, outer, out, mat, res, x, d, fx, fy, fz, inv, potential, semaphore):
-    arriving = pltpu.make_async_copy(potential_far, potential, semaphore)
+def smooth_kernel(ends, place, potential_far, state_far, long, inner, outer, out, state, mat, res, x, d, fx, fy, fz, inv, potential, semaphores):
+    arriving = pltpu.make_async_copy(potential_far, potential, semaphores.at[0])
     arriving.start()
+    passing = pltpu.make_async_copy(state_far, state, semaphores.at[1])
+    passing.start()
+    count, rows, depth = potential.shape
+    own = pl.ds(4, count)
+    frames = [
+        pltpu.make_async_copy(long.at[n], ref.at[own], semaphores.at[2 + n]) for n, ref in enumerate((res, mat))
+    ]
+    for copy in frames:
+        copy.start()
     low_x = place[0] == 1
     count, rows, depth = potential.shape
     pieces, tiles = depth // LANES, (rows + 8) // 8
@@ -314,8 +323,8 @@
     for flag, start_r, start_m in ((low_x, 1, 0), (jnp.logical_not(low_x), count + 4, count + 4)):
         at = unpack(both, flag, res, start_r, 3, tiles, pieces, 0)
         unpack(both, flag, mat, start_m, 4, tiles, pieces, at)
-    res[pl.ds(4, count)] = long[0, :count]
-    mat[pl.ds(4, count)] = long[1, :count]
+    for copy in frames:
+        copy.wait()
     total, length = count + 8, rows + 8
     row, lane = iota((length, depth), 0), iota((length, depth), 1)
     outside = as_float(lane == 0) + as_float(lane == depth - 1)
@@ -361,6 +370,7 @@
                 d[here] = change
                 x[new, here] = v + change
         rho = following
+    passing.wait()
 
 
 def each(count, body, most=8):
@@ -494,20 +504,25 @@
 def repeat(count, body):
     if count <= 8:
         for i in range(count):
-            body(i)
-    else:
-        lax.fori_loop(0, count, lambda i, _: body(i), None)
-
-
-def spread_blocks(blocks, outs, grid, c2, r2):
+            body(i, i % 2)
+        return
+
+    def two(n, _):
+        body(2 * n, 0)
+        body(2 * n + 1, 1)
+
+    lax.fori_loop(0, count // 2, two, None)
+
+
+def spread_blocks(fetch, outs, grid, c2, r2):
     gx, gy = grid
     length = c2 // 2 * r2
     low = iota((length, LANES), 1) < LANES // 2
 
-    def column(i):
+    def column(i, parity):
         for j in range(gy):
             for start, out in outs:
-                block = blocks[i * gy + j, start : start + length]
+                block = fetch(i, parity, j, slice(start, start + length))
                 parts = (jnp.where(low, block, 0.0), jnp.where(low, pltpu.roll(block, LANES // 2, 1), 0.0))
                 for k in range(c2):
                     n = k % (c2 // 2)
@@ -523,20 +538,31 @@
         ref[count + 1] = zero
 
 
-def first_cycle_kernel(counts, bases, grid, c2, r2, width, place, blocks, out, table, *scratch):
+def pass_kernel(blocks, _, out):
+    out[...] = blocks[...]
+
+
+def first_cycle_kernel(counts, bases, grid, c2, r2, width, place, mine, theirs, out, table, *scratch):
     s, e, t, pad = scratch[0:3], list(scratch[3:6]), scratch[6], scratch[7]
     gx, gy = grid
     rows = gy * r2
     half = LANES // 2
     own = c2 // 2 * r2
     clear_ends((t, *s), (counts[0], *counts))
-    spread_blocks(blocks, ((0, s[0]), (own + 2 * r2, t)), grid, c2, r2)
+    odd = place[0] == 1
+
+    def fetch(i, parity, j, at):
+        here = i // 2 * gy + j
+        a, b = mine[here, at], theirs[here, at]
+        return jnp.where(odd, b, a) if parity == 0 else jnp.where(odd, a, b)
+
+    spread_blocks(fetch, ((0, s[0]), (own + 2 * r2, t)), grid, c2, r2)
     face_y = e[0]
     low = iota((2 * c2, LANES), 1) < half
 
-    def edges(i):
+    def edges(i, parity):
         for j in range(gy):
-            faces = blocks[i * gy + j, own : own + 2 * r2]
+            faces = fetch(i, parity, j, slice(own, own + 2 * r2))
             x_faces = jnp.where(low, faces, 0.0)
             y_faces = jnp.where(low, pltpu.roll(faces, half, 1), 0.0)
             here = slice(j * r2, (j + 1) * r2)
@@ -595,7 +621,7 @@
 
 
 def level1_kernel(
-    offset, place, long, inner, outer, window1, payload, state_far,
+    offset, place, long1, inner, outer, window1, payload, state_far,
     src, mat, flat, prolonged, fx, fy, fz, diag, inv, err, c, state, wide, narrow, sheet, semaphores,
 ):
     low_x = place[0] == 1
@@ -609,8 +635,7 @@
         at = unpack(both, flag, src, start_s, 3, length // 8, 1, offset)
         unpack(both, flag, mat, start_m, 4, length // 8, 1, at)
     for n, ref in enumerate((src, mat)):
-        for k in range(count):
-            ref[4 + k] = long[n, 2 * count + k // 2, :length, k % 2 * LANES : (k % 2 + 1) * LANES]
+        ref[pl.ds(4, count)] = long1[n]
     raise_window(window1, flat, prolonged)
     row, lane = iota((length, depth), 0), iota((length, depth), 1)
     ends = as_float(lane == 0) + as_float(lane == depth - 1)
@@ -663,18 +688,15 @@
     leaving.wait()
 
 
-def last_cycle_kernel(counts, bases, grid, c2, r2, place, blocks, table, state_far, partial, out, *scratch):
+def last_cycle_kernel(counts, bases, grid, c2, r2, place, blocks, table, state, partial, out, *scratch):
     s, e, t, pad = scratch[0:3], list(scratch[3:6]), scratch[6], scratch[7]
-    view, flat, prolonged, tall, coarse, state, semaphore, result, departures = scratch[8:17]
-    arriving = pltpu.make_async_copy(state_far, state, semaphore)
-    arriving.start()
-    spread_blocks(blocks, ((0, s[0]),), grid, c2, r2)
+    view, flat, prolonged, tall, coarse, result, departures = scratch[8:15]
+    spread_blocks(lambda i, _, j, at: blocks[i * grid[1] + j, at], ((0, s[0]),), grid, c2, r2)
     clear_ends(s, counts)
     cycle(s, e, t, table, counts, bases, place, view, c2, r2, pad)
     raise_window(view, flat, prolonged)
     count, rows, depth = partial.shape
     c1, r1 = count // 2, rows // 2
-    arriving.wait()
     v = prolonged[3 : c1 + 5] + state[: c1 + 2]
     here = v[1:-1]
     base = 2 * c1 + 3
@@ -779,7 +801,7 @@
     face = (3, rows, depth)
     DMA = pltpu.SemaphoreType.DMA
     sheet = (devices, c2 // 2 * r2, LANES)
-    sheet2 = (devices, c2 * r2 + 2 * r2, LANES)
+    sheet2 = (devices // 2, c2 * r2 + 2 * r2, LANES)
     material, potential_here, source_here, inner, outer, even, odd = call(
         faces_kernel, "faces", (place, permeability, potential, phase, right_side),
         (brick, brick, brick, face, face, (3, count, depth), (3, count, depth)),
@@ -807,22 +829,27 @@
         functools.partial(payload_kernel, c1, r1), "payload", (coarse,), (("far", sheet2),),
         (VM(2, small, d1), VM(small, LANES), VM(*sheet2), DMA),
     )
-    blocks = lax.all_to_all(payload, ("gx", "gy"), 0, 0)
+    groups = [[(2 * i + c) * gy + j for i in range(gx // 2) for j in range(gy)] for c in range(2)]
+    blocks = lax.all_to_all(payload, ("gx", "gy"), 0, 0, axis_index_groups=groups)
     tiles, tiles1 = (rows + 8) // 8, (r1 + 8) // 8
     strip = (7 * tiles * pieces + 7 * tiles1, 8, LANES)
-    inner, outer, long = call(
+    long_shape = (2, count, rows + 8, depth)
+    inner, outer, long, long1 = call(
         strips_kernel, "strips", (place, residual, material, coarse, even, odd),
-        (strip, strip, (2, count + c1 // 2, rows + 8, depth)), cost=10**11,
+        (strip, strip, ("far", long_shape), (2, c1, r1 + 8, d1)),
+        (VM(*long_shape), DMA), cost=10**11,
     )
     outer = lax.ppermute(outer, "gx", swap_x[1])
     inner = lax.ppermute(inner, "gx", swap_x[0])
 
+    (blocks,) = call(pass_kernel, "pass", (blocks, long1), (sheet2,))
+    others = lax.ppermute(blocks, "gx", swap_x[0])
     counts = tuple(gx * c2 // k for k in (1, 2, 4))
     bases = (0, counts[0] + 1, counts[0] + counts[1] + 2)
     work = cycle_shapes(counts, gy * r2, c2)
     view = (c2 + 4, r2 + 4, LANES)
     window1, table = call(
-        functools.partial(first_cycle_kernel, counts, bases, (gx, gy), c2, r2, d1 // 2), "cycle1", (place, blocks),
+        functools.partial(first_cycle_kernel, counts, bases, (gx, gy), c2, r2, d1 // 2), "cycle1", (place, blocks, others),
         (view, (4, sum(counts) + 3, gy * r2, LANES)), work,
     )
     frame = (c1 + 8, r1 + 8, d1)
@@ -830,7 +857,7 @@
     state = (7 * c1 + 3, r1 + 8, d1)
     tall = VM(c1 + 9, r1 + 8, d1)
     payload, held = call(
-        functools.partial(level1_kernel, 7 * tiles * pieces), "level1", (place, long, inner, outer, window1), (("far", sheet), ("far", state)),
+        functools.partial(level1_kernel, 7 * tiles * pieces), "level1", (place, long1, inner, outer, window1), (("far", sheet), ("far", state)),
         (
             VM(*frame), VM(*frame), flat, VM(*frame), tall, VM(*frame), VM(*frame), VM(*frame), VM(*frame), VM(*frame),
             VM(*frame), VM(*state), VM(c1 // 2 * r1, d1), VM(c1 // 4 * r1, LANES), VM(*sheet), pltpu.SemaphoreType.DMA((2,)),
@@ -838,22 +865,21 @@
     )
     blocks = lax.all_to_all(payload, ("gx", "gy"), 0, 0)
     wide = (count + 8, rows + 8, depth)
-    (partial,) = call(
-        functools.partial(smooth_kernel, (gx, gy)), "smooth", (place, potential, long, inner, outer), (brick,),
+    partial, held = call(
+        functools.partial(smooth_kernel, (gx, gy)), "smooth", (place, potential, held, long, inner, outer), (brick, state),
         (
             VM(*wide), VM(*wide), VM(2, *wide), VM(*wide), VM(count + 9, rows + 8, depth), VM(*wide), VM(*wide), VM(*wide),
-            VM(*brick), pltpu.SemaphoreType.DMA,
+            VM(*brick), pltpu.SemaphoreType.DMA((4,)),
         ),
-        apart=(1,),
+        apart=(1, 2, 3),
     )
     (out,) = call(
         functools.partial(last_cycle_kernel, counts, bases, (gx, gy), c2, r2), "cycle2",
         (place, blocks, table, held, partial), (("far", brick),),
         (
-            *work, VM(*view), flat, VM(*frame), VM(pieces, c1 * rows, LANES), VM(c1 * r1, LANES), VM(*state), DMA,
-            VM(*brick), pltpu.SemaphoreType.DMA((c1 // 2,)),
+            *work, VM(*view), flat, VM(*frame), VM(pieces, c1 * rows, LANES), VM(c1 * r1, LANES), VM(*brick),
+            pltpu.SemaphoreType.DMA((c1 // 2,)),
         ),
-        apart=(3,),
     )
     return out
 

time: 57 us -> 55.3 us (0.970)
  waiting for transfers between devices: 15.1 us -> 12.8 us
  starting transfers between devices: 23.2 us -> 24 us
    all_to_all x2 -> x1, waiting for transfers between devices: 13.7 us -> 4.16 us  [local(): blocks = lax.all_to_all(payload, ('gx', 'gy'), 0, 0)]
    all_to_all x0 -> x1, starting transfers between devices: none -> 8.42 us  [local(): lax.all_to_all(payload, ('gx', 'gy'), 0, 0, axis_index_groups=groups)]
    all_to_all x2 -> x1, starting transfers between devices: 11.4 us -> 4.48 us  [local(): blocks = lax.all_to_all(payload, ('gx', 'gy'), 0, 0)]
    all_to_all x0 -> x1, waiting for transfers between devices: none -> 5.85 us  [local(): lax.all_to_all(payload, ('gx', 'gy'), 0, 0, axis_index_groups=groups)]
    ppermute x0 -> x1, waiting for transfers between devices: none -> 1.43 us  [local(): others = lax.ppermute(blocks, 'gx', swap_x[0])]
    ppermute x2, starting transfers between devices: 2 us -> 1.33 us  [local(): outer = lax.ppermute(outer, 'gx', swap_x[1])]
    pallas_call x8 -> x9, Pallas kernels: 18 us -> 17.9 us  [call(): pl.pallas_call(kernel, out_shape=results, in_specs=specs, out_specs=[pl.B...]
  transfers between devices with their start and end apart: 10 -> 11, of which waited for: 3 -> 4; matrix products, arithmetic and copies ran while one was open for 0% -> 0% of each run, Pallas kernels for 16% -> 18%
where the time goes in v6:
time: 55.3 us; the launch traced here: 54.9 us
  starting transfers between devices  24 us (43%)
  Pallas kernels  17.9 us (32%)
  waiting for transfers between devices  12.8 us (23%)
    pallas_call x9, Pallas kernels, call(): pl.pallas_call(kernel, out_shape=results, in_specs=specs, out_specs=[pl.B...  17.9 us
    all_to_all x1, starting transfers between devices, local(): lax.all_to_all(payload, ('gx', 'gy'), 0, 0, axis_index_groups=groups)  8.42 us
    ppermute x2, starting transfers between devices, local(): even = lax.ppermute(even, 'gy', swap_y[0])  7.76 us
    all_to_all x1, waiting for transfers between devices, local(): lax.all_to_all(payload, ('gx', 'gy'), 0, 0, axis_index_groups=groups)  5.85 us
    all_to_all x1, starting transfers between devices, local(): blocks = lax.all_to_all(payload, ('gx', 'gy'), 0, 0)  4.48 us
    all_to_all x1, waiting for transfers between devices, local(): blocks = lax.all_to_all(payload, ('gx', 'gy'), 0, 0)  4.16 us
    ppermute x1, waiting for transfers between devices, local(): others = lax.ppermute(blocks, 'gx', swap_x[0])  1.43 us
    ppermute x2, waiting for transfers between devices, local(): even = lax.ppermute(even, 'gy', swap_y[0])  1.39 us
  transfers between devices with their start and end apart: 11, of which 4 were waited for; matrix products, arithmetic and copies ran while one was open for 0% of the time, Pallas kernels for 18%

profile of v6, /device:TPU:0, one launch (start us, length us, event | category | flops | bytes accessed | tf_op | source)
XLA Modules:
  0.0 54.9 jit_solution(10202566877351480022)
XLA Ops:
  0.0 0.1 pad_add_fusion.place
  0.1 1.7 %faces.1 = (f32[16,16,256]{2,1,0:T(8,128)S(1)}, f32[16,16,256]{2,1,0:T(8,128)S(1)}, f32[16,16,256]{2,1,0:T(8,128)S(1)}, f32[3,16,256]{2,1,0:T(8,128)S(1)}, f32[3...) custom-call(s32[4]{0:T(128)S(1)} %pad_add_fusion.place, f32[3]{0:T(128)} %permeability.1, ...), custom_call_target="tpu_custom_call" | custom-call | tf_op jit(solution)/shard_map/faces/pallas_call | solution.py:770
  1.8 0.5 collective-permute-start
  2.3 0.7 %collective-permute-start.1 = (f32[3,16,256]{2,1,0:T(8,128)S(1)}, f32[3,16,256]{2,1,0:T(8,128)S(1)}, u32[]{:S(2)}, u32[]{:S(2)}) collective-permute-start(f32[3,16,256]{2,1,0:T(8,128)S(1)} %get-tuple-element.30), channel_id=1, source_target_pairs={{4,8},{12,16},{20,24},{8,4},{16,12},{24,20},{5,9},{13,17},{21,25},... | collective-permute-start | bytes 147464 | tf_op jit(solution)/shard_map/ppermute | solution.py:813
  2.9 2.7 %collective-permute-start.2 = (f32[3,16,256]{2,1,0:T(8,128)S(1)}, f32[3,16,256]{2,1,0:T(8,128)S(1)}, u32[]{:S(2)}, u32[]{:S(2)}) collective-permute-start(f32[3,16,256]{2,1,0:T(8,128)S(1)} %get-tuple-element.31), channel_id=1, source_target_pairs={{0,1},{2,3},{1,0},{3,2},{4,5},{6,7},{5,4},{7,6},{8,9},{10,11},{9,8... | collective-permute-start | bytes 147464 | tf_op jit(solution)/shard_map/ppermute | solution.py:811
  5.6 0.7 %collective-permute-start.3 = (f32[3,16,256]{2,1,0:T(8,128)S(1)}, f32[3,16,256]{2,1,0:T(8,128)S(1)}, u32[]{:S(2)}, u32[]{:S(2)}) collective-permute-start(f32[3,16,256]{2,1,0:T(8,128)S(1)} %get-tuple-element.32), channel_id=1, source_target_pairs={{1,2},{2,1},{5,6},{6,5},{9,10},{10,9},{13,14},{14,13},{17,18},{18,... | collective-permute-start | bytes 147464 | tf_op jit(solution)/shard_map/ppermute | solution.py:812
  6.3 0.0 collective-permute-done.inner
  6.3 0.0 collective-permute-done.1.outer
  6.3 1.4 %collective-permute-done.2.even = f32[3,16,256]{2,1,0:T(8,128)S(1)} collective-permute-done((f32[3,16,256]{2,1,0:T(8,128)S(1)}, f32[3,16,256]{2,1,0:T(8,128)S(1)}, u32[]{:S(2)}, u32[]{:S(2)}) %collective-permute-start.2) | collective-permute-done | bytes 49184 | tf_op jit(solution)/shard_map/ppermute | solution.py:811
  7.7 0.0 collective-permute-done.3.odd
  7.7 1.6 %residual.1 = (f32[16,16,256]{2,1,0:T(8,128)S(1)}, f32[160,128]{1,0:T(8,128)S(1)}, f32[40,8,128]{2,1,0:T(8,128)S(1)}, f32[40,8,128]{2,1,0:T(8,128)S(1)}) custom-call(s32[4]{0:T(128)S(1)} %pad_add_fusion.place, f32[16,16,256]{2,1,0:T(8,128)S(1)} %get-tuple-element.26.source, f32[16,16,256]{2,1,0:T(8,128)S(1)} %get-tuple-element.27.potential, ...), custom_call_target="tpu_custom_call" | custom-call | tf_op jit(solution)/shard_map/residual/pallas_call | solution.py:770
  9.3 5.1 %collective-permute-start.4 = (f32[40,8,128]{2,1,0:T(8,128)S(1)}, f32[40,8,128]{2,1,0:T(8,128)S(1)}, u32[]{:S(2)}, u32[]{:S(2)}) collective-permute-start(f32[40,8,128]{2,1,0:T(8,128)S(1)} %get-tuple-element.35), channel_id=1, source_target_pairs={{0,1},{2,3},{1,0},{3,2},{4,5},{6,7},{5,4},{7,6},{8,9},{10,11},{9,8... | collective-permute-start | bytes 491528 | tf_op jit(solution)/shard_map/ppermute | solution.py:825
  14.4 0.7 %collective-permute-start.5 = (f32[40,8,128]{2,1,0:T(8,128)S(1)}, f32[40,8,128]{2,1,0:T(8,128)S(1)}, u32[]{:S(2)}, u32[]{:S(2)}) collective-permute-start(f32[40,8,128]{2,1,0:T(8,128)S(1)} %get-tuple-element.36), channel_id=1, source_target_pairs={{1,2},{2,1},{5,6},{6,5},{9,10},{10,9},{13,14},{14,13},{17,18},{18,... | collective-permute-start | bytes 491528 | tf_op jit(solution)/shard_map/ppermute | solution.py:826
  15.0 1.1 %payload.1 = f32[16,24,128]{2,1,0:T(8,128)} custom-call(f32[160,128]{1,0:T(8,128)S(1)} %get-tuple-element.34.coarse), custom_call_target="tpu_custom_call" | custom-call | tf_op jit(solution)/shard_map/payload/pallas_call | solution.py:770
  16.2 8.4 %all-to-all-start = ((f32[16,24,128]{2,1,0:T(8,128)}), f32[16,24,128]{2,1,0:T(8,128)S(1)}, u32[]{:S(2)}, u32[]{:S(2)}) async-start(f32[16,24,128]{2,1,0:T(8,128)} %payload.1), calls=%async_computation | async-start | bytes 393216 | tf_op jit(solution)/shard_map/all_to_all | solution.py:833
  24.6 0.0 collective-permute-done.4.even
  24.6 0.0 collective-permute-done.5.odd
  24.6 1.5 %strips.1 = (f32[56,8,128]{2,1,0:T(8,128)S(1)}, f32[56,8,128]{2,1,0:T(8,128)S(1)}, f32[2,16,24,256]{3,2,1,0:T(8,128)}, f32[2,8,16,128]{3,2,1,0:T(8,128)S(1)}) custom-call(s32[4]{0:T(128)S(1)} %pad_add_fusion.place, f32[16,16,256]{2,1,0:T(8,128)S(1)} %get-tuple-element.33.residual, f32[16,16,256]{2,1,0:T(8,128)S(1)} %get-tuple-element.28.material, ...), custom_call_target="tpu_custom_call" | custom-call | flops 99999997952 | tf_op jit(solution)/shard_map/strips/pallas_call | solution.py:770
  26.2 0.1 collective-permute-start.6
  26.2 0.7 %collective-permute-start.7 = (f32[56,8,128]{2,1,0:T(8,128)S(1)}, f32[56,8,128]{2,1,0:T(8,128)S(1)}, u32[]{:S(2)}, u32[]{:S(2)}) collective-permute-start(f32[56,8,128]{2,1,0:T(8,128)S(1)} %get-tuple-element.39), channel_id=1, source_target_pairs={{4,8},{12,16},{20,24},{8,4},{16,12},{24,20},{5,9},{13,17},{21,25},... | collective-permute-start | bytes 688136 | tf_op jit(solution)/shard_map/ppermute | solution.py:842
  26.9 5.8 %all-to-all-done.blocks = f32[16,24,128]{2,1,0:T(8,128)S(1)} async-done(((f32[16,24,128]{2,1,0:T(8,128)}), f32[16,24,128]{2,1,0:T(8,128)S(1)}, u32[]{:S(2)}, u32[]{:S(2)}) %all-to-all-start) | async-done | bytes 196640 | tf_op jit(solution)/shard_map/all_to_all | solution.py:833
  32.8 0.1 collective-permute-start.8
  32.9 1.4 %collective-permute-done.8.theirs = f32[16,24,128]{2,1,0:T(8,128)S(1)} collective-permute-done((f32[16,24,128]{2,1,0:T(8,128)S(1)}, f32[16,24,128]{2,1,0:T(8,128)S(1)}, u32[]{:S(2)}, u32[]{:S(2)}) %collective-permute-start.8) | collective-permute-done | bytes 196640 | tf_op jit(solution)/shard_map/ppermute | solution.py:846
  34.3 2.9 %cycle1.1 = (f32[8,8,128]{2,1,0:T(8,128)S(1)}, f32[4,59,16,128]{3,2,1,0:T(8,128)S(1)}) custom-call(s32[4]{0:T(128)S(1)} %pad_add_fusion.place, f32[16,24,128]{2,1,0:T(8,128)S(1)} %pass.1.mine, f32[16,24,128]{2,1,0:T(8,128)S(1)} %collective-permute-done.8.theirs), custom_call_target="tpu_custom_call" | custom-call | tf_op jit(solution)/shard_map/cycle1/pallas_call | solution.py:770
  37.2 0.0 collective-permute-done.6.inner
  37.2 0.0 collective-permute-done.7.outer
  37.2 1.9 %level1.1 = (f32[32,8,128]{2,1,0:T(8,128)}, f32[59,16,128]{2,1,0:T(8,128)}) custom-call(s32[4]{0:T(128)S(1)} %pad_add_fusion.place, f32[2,8,16,128]{3,2,1,0:T(8,128)S(1)} %get-tuple-element.37._.long1, f32[56,8,128]{2,1,0:T(8,128)S(1)} %collective-permute-done.6.inner, f32[56,8,128]{2,1,0:T(8,128)S(1)} %collective-permute-done.7.outer, ...), custom_call_target="tpu_custom_call" | custom-call | tf_op jit(solution)/shard_map/level1/pallas_call | solution.py:770
  39.1 4.5 %all-to-all-start.1 = ((f32[32,8,128]{2,1,0:T(8,128)}), f32[32,8,128]{2,1,0:T(8,128)S(1)}, u32[]{:S(2)}, u32[]{:S(2)}) async-start(f32[32,8,128]{2,1,0:T(8,128)} %get-tuple-element.41), calls=%async_computation.1 | async-start | bytes 262144 | tf_op jit(solution)/shard_map/all_to_all | solution.py:866
  43.6 4.2 %smooth.1 = (f32[16,16,256]{2,1,0:T(8,128)S(1)}, f32[59,16,128]{2,1,0:T(8,128)S(1)}) custom-call(s32[4]{0:T(128)S(1)} %pad_add_fusion.place, f32[16,16,256]{2,1,0:T(8,128)} %potential_far.1, f32[59,16,128]{2,1,0:T(8,128)} %get-tuple-element.43.state_far, f32[2,16,24,256]{3,2,1,0:T(8,128)} %get-tuple-element.44.long, ...), custom_call_target="tpu_custom_call" | custom-call | tf_op jit(solution)/shard_map/smooth/pallas_call | solution.py:770
  47.8 4.2 %all-to-all-done.1.blocks = f32[32,8,128]{2,1,0:T(8,128)S(1)} async-done(((f32[32,8,128]{2,1,0:T(8,128)}), f32[32,8,128]{2,1,0:T(8,128)S(1)}, u32[]{:S(2)}, u32[]{:S(2)}) %all-to-all-start.1) | async-done | bytes 131104 | tf_op jit(solution)/shard_map/all_to_all | solution.py:866
  52.0 2.9 %cycle2.1 = f32[16,16,256]{2,1,0:T(8,128)} custom-call(s32[4]{0:T(128)S(1)} %pad_add_fusion.place, f32[32,8,128]{2,1,0:T(8,128)S(1)} %all-to-all-done.1.blocks, f32[4,59,16,128]{3,2,1,0:T(8,128)S(1)} %get-tuple-element.42.table, f32[59,16,128]{2,1,0:T(8,128)S(1)} %get-tuple-element.45.state, f32[16,16,256]{2,1,0:T(8,128)S(1)} %get-tuple-element.46.partial), custom_call_target="tpu_custom_call" | custom-call | tf_op jit(solution)/shard_map/cycle2/pallas_call | solution.py:770
  (1 shorter events, 0.0 us)
Async XLA Ops:
  1.8 4.5 %collective-permute-start = (f32[3,16,256]{2,1,0:T(8,128)S(1)}, f32[3,16,256]{2,1,0:T(8,128)S(1)}, u32[]{:S(2)}, u32[]{:S(2)}) collective-permute-start(f32[3,16,256]{2,1,0:T(8,128)S(1)} %get-tuple-element.29), channel_id=1, source_target_pairs={{0,4},{8,12},{16,20},{24,28},{4,0},{12,8},{20,16},{28,24},{1,5},{9... | collective-permute-start | bytes 147464 | tf_op jit(solution)/shard_map/ppermute | solution.py:814
  2.3 4.0 %collective-permute-start.1 = (f32[3,16,256]{2,1,0:T(8,128)S(1)}, f32[3,16,256]{2,1,0:T(8,128)S(1)}, u32[]{:S(2)}, u32[]{:S(2)}) collective-permute-start(f32[3,16,256]{2,1,0:T(8,128)S(1)} %get-tuple-element.30), channel_id=1, source_target_pairs={{4,8},{12,16},{20,24},{8,4},{16,12},{24,20},{5,9},{13,17},{21,25},... | collective-permute-start | bytes 147464 | tf_op jit(solution)/shard_map/ppermute | solution.py:813
  2.9 4.7 %collective-permute-start.2 = (f32[3,16,256]{2,1,0:T(8,128)S(1)}, f32[3,16,256]{2,1,0:T(8,128)S(1)}, u32[]{:S(2)}, u32[]{:S(2)}) collective-permute-start(f32[3,16,256]{2,1,0:T(8,128)S(1)} %get-tuple-element.31), channel_id=1, source_target_pairs={{0,1},{2,3},{1,0},{3,2},{4,5},{6,7},{5,4},{7,6},{8,9},{10,11},{9,8... | collective-permute-start | bytes 147464 | tf_op jit(solution)/shard_map/ppermute | solution.py:811
  5.6 2.1 %collective-permute-start.3 = (f32[3,16,256]{2,1,0:T(8,128)S(1)}, f32[3,16,256]{2,1,0:T(8,128)S(1)}, u32[]{:S(2)}, u32[]{:S(2)}) collective-permute-start(f32[3,16,256]{2,1,0:T(8,128)S(1)} %get-tuple-element.32), channel_id=1, source_target_pairs={{1,2},{2,1},{5,6},{6,5},{9,10},{10,9},{13,14},{14,13},{17,18},{18,... | collective-permute-start | bytes 147464 | tf_op jit(solution)/shard_map/ppermute | solution.py:812
  9.3 15.3 %collective-permute-start.4 = (f32[40,8,128]{2,1,0:T(8,128)S(1)}, f32[40,8,128]{2,1,0:T(8,128)S(1)}, u32[]{:S(2)}, u32[]{:S(2)}) collective-permute-start(f32[40,8,128]{2,1,0:T(8,128)S(1)} %get-tuple-element.35), channel_id=1, source_target_pairs={{0,1},{2,3},{1,0},{3,2},{4,5},{6,7},{5,4},{7,6},{8,9},{10,11},{9,8... | collective-permute-start | bytes 491528 | tf_op jit(solution)/shard_map/ppermute | solution.py:825
  14.4 10.2 %collective-permute-start.5 = (f32[40,8,128]{2,1,0:T(8,128)S(1)}, f32[40,8,128]{2,1,0:T(8,128)S(1)}, u32[]{:S(2)}, u32[]{:S(2)}) collective-permute-start(f32[40,8,128]{2,1,0:T(8,128)S(1)} %get-tuple-element.36), channel_id=1, source_target_pairs={{1,2},{2,1},{5,6},{6,5},{9,10},{10,9},{13,14},{14,13},{17,18},{18,... | collective-permute-start | bytes 491528 | tf_op jit(solution)/shard_map/ppermute | solution.py:826
  16.2 16.6 %all-to-all-start = ((f32[16,24,128]{2,1,0:T(8,128)}), f32[16,24,128]{2,1,0:T(8,128)S(1)}, u32[]{:S(2)}, u32[]{:S(2)}) async-start(f32[16,24,128]{2,1,0:T(8,128)} %payload.1), calls=%async_computation | async-start | bytes 393216 | tf_op jit(solution)/shard_map/all_to_all | solution.py:833
  26.2 11.0 %collective-permute-start.6 = (f32[56,8,128]{2,1,0:T(8,128)S(1)}, f32[56,8,128]{2,1,0:T(8,128)S(1)}, u32[]{:S(2)}, u32[]{:S(2)}) collective-permute-start(f32[56,8,128]{2,1,0:T(8,128)S(1)} %get-tuple-element.38), channel_id=1, source_target_pairs={{0,4},{8,12},{16,20},{24,28},{4,0},{12,8},{20,16},{28,24},{1,5},{9... | collective-permute-start | bytes 688136 | tf_op jit(solution)/shard_map/ppermute | solution.py:843
  26.2 11.0 %collective-permute-start.7 = (f32[56,8,128]{2,1,0:T(8,128)S(1)}, f32[56,8,128]{2,1,0:T(8,128)S(1)}, u32[]{:S(2)}, u32[]{:S(2)}) collective-permute-start(f32[56,8,128]{2,1,0:T(8,128)S(1)} %get-tuple-element.39), channel_id=1, source_target_pairs={{4,8},{12,16},{20,24},{8,4},{16,12},{24,20},{5,9},{13,17},{21,25},... | collective-permute-start | bytes 688136 | tf_op jit(solution)/shard_map/ppermute | solution.py:842
  32.8 1.5 %collective-permute-start.8 = (f32[16,24,128]{2,1,0:T(8,128)S(1)}, f32[16,24,128]{2,1,0:T(8,128)S(1)}, u32[]{:S(2)}, u32[]{:S(2)}) collective-permute-start(f32[16,24,128]{2,1,0:T(8,128)S(1)} %pass.1.mine), channel_id=1, source_target_pairs={{0,4},{8,12},{16,20},{24,28},{4,0},{12,8},{20,16},{28,24},{1,5},{9... | collective-permute-start | bytes 589832 | tf_op jit(solution)/shard_map/ppermute | solution.py:846
  39.1 12.9 %all-to-all-start.1 = ((f32[32,8,128]{2,1,0:T(8,128)}), f32[32,8,128]{2,1,0:T(8,128)S(1)}, u32[]{:S(2)}, u32[]{:S(2)}) async-start(f32[32,8,128]{2,1,0:T(8,128)} %get-tuple-element.41), calls=%async_computation.1 | async-start | bytes 262144 | tf_op jit(solution)/shard_map/all_to_all | solution.py:866

commit v7 on v6

--- a/solution.py
+++ b/solution.py
@@ -106,7 +106,7 @@
 
 
 def residual_kernel(
-    place, source, potential, material, inner, outer, even, odd,
+    place, source, potential, material, outer, even, odd, inner,
     residual, coarse, strip_even, strip_odd,
     wide, narrow, y_faces, mat, pot,
 ):
@@ -304,7 +304,7 @@
     return at
 
 
-def smooth_kernel(ends, place, potential_far, state_far, long, inner, outer, out, state, mat, res, x, d, fx, fy, fz, inv, potential, semaphores):
+def smooth_kernel(ends, place, potential_far, state_far, long, outer, inner, out, state, mat, res, x, d, fx, fy, fz, inv, potential, semaphores):
     arriving = pltpu.make_async_copy(potential_far, potential, semaphores.at[0])
     arriving.start()
     passing = pltpu.make_async_copy(state_far, state, semaphores.at[1])
@@ -621,7 +621,7 @@
 
 
 def level1_kernel(
-    offset, place, long1, inner, outer, window1, payload, state_far,
+    offset, place, long1, outer, inner, window1, payload, state_far,
     src, mat, flat, prolonged, fx, fy, fz, diag, inv, err, c, state, wide, narrow, sheet, semaphores,
 ):
     low_x = place[0] == 1
@@ -691,7 +691,7 @@
 def last_cycle_kernel(counts, bases, grid, c2, r2, place, blocks, table, state, partial, out, *scratch):
     s, e, t, pad = scratch[0:3], list(scratch[3:6]), scratch[6], scratch[7]
     view, flat, prolonged, tall, coarse, result, departures = scratch[8:15]
-    spread_blocks(lambda i, _, j, at: blocks[i * grid[1] + j, at], ((0, s[0]),), grid, c2, r2)
+    spread_blocks(lambda i, _, j, at: blocks[grid[0] * grid[1] - 1 - i * grid[1] - j, at], ((0, s[0]),), grid, c2, r2)
     clear_ends(s, counts)
     cycle(s, e, t, table, counts, bases, place, view, c2, r2, pad)
     raise_window(view, flat, prolonged)
@@ -816,7 +816,7 @@
     strip = (count * pieces + c1, 8, LANES)
     total = 2 * c1 * rows + 4 * rows
     residual, coarse, even, odd = call(
-        residual_kernel, "residual", (place, source_here, potential_here, material, inner, outer, even, odd),
+        residual_kernel, "residual", (place, source_here, potential_here, material, outer, even, odd, inner),
         (brick, (total // 2, LANES), strip, strip),
         (
             VM(total, depth), VM(total, LANES), VM(4, count, 8, depth), VM(count + 2, rows, depth), VM(count + 2, rows, depth),
@@ -857,16 +857,16 @@
     state = (7 * c1 + 3, r1 + 8, d1)
     tall = VM(c1 + 9, r1 + 8, d1)
     payload, held = call(
-        functools.partial(level1_kernel, 7 * tiles * pieces), "level1", (place, long1, inner, outer, window1), (("far", sheet), ("far", state)),
+        functools.partial(level1_kernel, 7 * tiles * pieces), "level1", (place, long1, outer, inner, window1), (("far", sheet), ("far", state)),
         (
             VM(*frame), VM(*frame), flat, VM(*frame), tall, VM(*frame), VM(*frame), VM(*frame), VM(*frame), VM(*frame),
             VM(*frame), VM(*state), VM(c1 // 2 * r1, d1), VM(c1 // 4 * r1, LANES), VM(*sheet), pltpu.SemaphoreType.DMA((2,)),
         ),
     )
-    blocks = lax.all_to_all(payload, ("gx", "gy"), 0, 0)
+    blocks = lax.all_to_all(payload, ("gx", "gy"), 0, 0, axis_index_groups=[list(range(devices))[::-1]])
     wide = (count + 8, rows + 8, depth)
     partial, held = call(
-        functools.partial(smooth_kernel, (gx, gy)), "smooth", (place, potential, held, long, inner, outer), (brick, state),
+        functools.partial(smooth_kernel, (gx, gy)), "smooth", (place, potential, held, long, outer, inner), (brick, state),
         (
             VM(*wide), VM(*wide), VM(2, *wide), VM(*wide), VM(count + 9, rows + 8, depth), VM(*wide), VM(*wide), VM(*wide),
             VM(*brick), pltpu.SemaphoreType.DMA((4,)),

time: 55.3 us -> 53.3 us (0.964)
  waiting for transfers between devices: 12.8 us -> 8.97 us
  starting transfers between devices: 24 us -> 25.9 us
    ppermute x2, starting transfers between devices: 0.59 us -> 5.97 us  [local(): inner = lax.ppermute(inner, 'gx', swap_x[0])]
    all_to_all x1, waiting for transfers between devices: 5.85 us -> 3.05 us  [local(): lax.all_to_all(payload, ('gx', 'gy'), 0, 0, axis_index_groups=groups)]
    all_to_all x1, starting transfers between devices: 8.42 us -> 6.63 us  [local(): lax.all_to_all(payload, ('gx', 'gy'), 0, 0, axis_index_groups=groups)]
    ppermute x2, waiting for transfers between devices: 1.39 us -> 0.01 us  [local(): even = lax.ppermute(even, 'gy', swap_y[0])]
    all_to_all x1, starting transfers between devices: 4.48 us -> 3.31 us  [local(): lax.all_to_all(payload, ('gx', 'gy'), 0, 0, axis_index_groups=[list(range...]
    ppermute x2, waiting for transfers between devices: 0.01 us -> 0.87 us  [local(): inner = lax.ppermute(inner, 'gx', swap_x[0])]
    all_to_all x1, waiting for transfers between devices: 4.16 us -> 3.6 us  [local(): lax.all_to_all(payload, ('gx', 'gy'), 0, 0, axis_index_groups=[list(range...]
where the time goes in v7:
time: 53.3 us; the launch traced here: 53 us
  starting transfers between devices  25.9 us (49%)
  Pallas kernels  17.9 us (34%)
  waiting for transfers between devices  8.97 us (17%)
    pallas_call x9, Pallas kernels, call(): pl.pallas_call(kernel, out_shape=results, in_specs=specs, out_specs=[pl.B...  17.9 us
    ppermute x2, starting transfers between devices, local(): even = lax.ppermute(even, 'gy', swap_y[0])  7.27 us
    all_to_all x1, starting transfers between devices, local(): lax.all_to_all(payload, ('gx', 'gy'), 0, 0, axis_index_groups=groups)  6.63 us
    ppermute x2, starting transfers between devices, local(): inner = lax.ppermute(inner, 'gx', swap_x[0])  5.97 us
    all_to_all x1, waiting for transfers between devices, local(): lax.all_to_all(payload, ('gx', 'gy'), 0, 0, axis_index_groups=[list(range...  3.6 us
    all_to_all x1, starting transfers between devices, local(): lax.all_to_all(payload, ('gx', 'gy'), 0, 0, axis_index_groups=[list(range...  3.31 us
    all_to_all x1, waiting for transfers between devices, local(): lax.all_to_all(payload, ('gx', 'gy'), 0, 0, axis_index_groups=groups)  3.05 us
    ppermute x1, waiting for transfers between devices, local(): others = lax.ppermute(blocks, 'gx', swap_x[0])  1.43 us
  transfers between devices with their start and end apart: 11, of which 4 were waited for; matrix products, arithmetic and copies ran while one was open for 0% of the time, Pallas kernels for 18%

profile of v7, /device:TPU:0, one launch (start us, length us, event | category | flops | bytes accessed | tf_op | source)
XLA Modules:
  0.0 53.0 jit_solution(8821428294348834017)
XLA Ops:
  0.0 0.1 pad_add_fusion.place
  0.1 1.7 %faces.1 = (f32[16,16,256]{2,1,0:T(8,128)S(1)}, f32[16,16,256]{2,1,0:T(8,128)S(1)}, f32[16,16,256]{2,1,0:T(8,128)S(1)}, f32[3,16,256]{2,1,0:T(8,128)S(1)}, f32[3...) custom-call(s32[4]{0:T(128)S(1)} %pad_add_fusion.place, f32[3]{0:T(128)} %permeability.1, ...), custom_call_target="tpu_custom_call" | custom-call | tf_op jit(solution)/shard_map/faces/pallas_call | solution.py:770
  1.8 0.7 %collective-permute-start = (f32[3,16,256]{2,1,0:T(8,128)S(1)}, f32[3,16,256]{2,1,0:T(8,128)S(1)}, u32[]{:S(2)}, u32[]{:S(2)}) collective-permute-start(f32[3,16,256]{2,1,0:T(8,128)S(1)} %get-tuple-element.29), channel_id=1, source_target_pairs={{4,8},{12,16},{20,24},{8,4},{16,12},{24,20},{5,9},{13,17},{21,25},... | collective-permute-start | bytes 147464 | tf_op jit(solution)/shard_map/ppermute | solution.py:813
  2.4 3.1 %collective-permute-start.1 = (f32[3,16,256]{2,1,0:T(8,128)S(1)}, f32[3,16,256]{2,1,0:T(8,128)S(1)}, u32[]{:S(2)}, u32[]{:S(2)}) collective-permute-start(f32[3,16,256]{2,1,0:T(8,128)S(1)} %get-tuple-element.30), channel_id=1, source_target_pairs={{0,1},{2,3},{1,0},{3,2},{4,5},{6,7},{5,4},{7,6},{8,9},{10,11},{9,8... | collective-permute-start | bytes 147464 | tf_op jit(solution)/shard_map/ppermute | solution.py:811
  5.5 0.7 %collective-permute-start.2 = (f32[3,16,256]{2,1,0:T(8,128)S(1)}, f32[3,16,256]{2,1,0:T(8,128)S(1)}, u32[]{:S(2)}, u32[]{:S(2)}) collective-permute-start(f32[3,16,256]{2,1,0:T(8,128)S(1)} %get-tuple-element.31), channel_id=1, source_target_pairs={{1,2},{2,1},{5,6},{6,5},{9,10},{10,9},{13,14},{14,13},{17,18},{18,... | collective-permute-start | bytes 147464 | tf_op jit(solution)/shard_map/ppermute | solution.py:812
  6.2 2.6 %collective-permute-start.3 = (f32[3,16,256]{2,1,0:T(8,128)S(1)}, f32[3,16,256]{2,1,0:T(8,128)S(1)}, u32[]{:S(2)}, u32[]{:S(2)}) collective-permute-start(f32[3,16,256]{2,1,0:T(8,128)S(1)} %get-tuple-element.32), channel_id=1, source_target_pairs={{0,4},{8,12},{16,20},{24,28},{4,0},{12,8},{20,16},{28,24},{1,5},{9... | collective-permute-start | bytes 147464 | tf_op jit(solution)/shard_map/ppermute | solution.py:814
  8.8 0.0 collective-permute-done.outer
  8.8 0.0 collective-permute-done.1.even
  8.8 0.0 collective-permute-done.2.odd
  8.8 0.9 %collective-permute-done.3.inner = f32[3,16,256]{2,1,0:T(8,128)S(1)} collective-permute-done((f32[3,16,256]{2,1,0:T(8,128)S(1)}, f32[3,16,256]{2,1,0:T(8,128)S(1)}, u32[]{:S(2)}, u32[]{:S(2)}) %collective-permute-start.3) | collective-permute-done | bytes 49184 | tf_op jit(solution)/shard_map/ppermute | solution.py:814
  9.7 1.6 %residual.1 = (f32[16,16,256]{2,1,0:T(8,128)S(1)}, f32[160,128]{1,0:T(8,128)S(1)}, f32[40,8,128]{2,1,0:T(8,128)S(1)}, f32[40,8,128]{2,1,0:T(8,128)S(1)}) custom-call(s32[4]{0:T(128)S(1)} %pad_add_fusion.place, f32[16,16,256]{2,1,0:T(8,128)S(1)} %get-tuple-element.26.source, f32[16,16,256]{2,1,0:T(8,128)S(1)} %get-tuple-element.27.potential, ...), custom_call_target="tpu_custom_call" | custom-call | tf_op jit(solution)/shard_map/residual/pallas_call | solution.py:770
  11.3 4.2 %collective-permute-start.4 = (f32[40,8,128]{2,1,0:T(8,128)S(1)}, f32[40,8,128]{2,1,0:T(8,128)S(1)}, u32[]{:S(2)}, u32[]{:S(2)}) collective-permute-start(f32[40,8,128]{2,1,0:T(8,128)S(1)} %get-tuple-element.35), channel_id=1, source_target_pairs={{0,1},{2,3},{1,0},{3,2},{4,5},{6,7},{5,4},{7,6},{8,9},{10,11},{9,8... | collective-permute-start | bytes 491528 | tf_op jit(solution)/shard_map/ppermute | solution.py:825
  15.5 0.7 %collective-permute-start.5 = (f32[40,8,128]{2,1,0:T(8,128)S(1)}, f32[40,8,128]{2,1,0:T(8,128)S(1)}, u32[]{:S(2)}, u32[]{:S(2)}) collective-permute-start(f32[40,8,128]{2,1,0:T(8,128)S(1)} %get-tuple-element.36), channel_id=1, source_target_pairs={{1,2},{2,1},{5,6},{6,5},{9,10},{10,9},{13,14},{14,13},{17,18},{18,... | collective-permute-start | bytes 491528 | tf_op jit(solution)/shard_map/ppermute | solution.py:826
  16.1 1.1 %payload.1 = f32[16,24,128]{2,1,0:T(8,128)} custom-call(f32[160,128]{1,0:T(8,128)S(1)} %get-tuple-element.34.coarse), custom_call_target="tpu_custom_call" | custom-call | tf_op jit(solution)/shard_map/payload/pallas_call | solution.py:770
  17.3 6.6 %all-to-all-start = ((f32[16,24,128]{2,1,0:T(8,128)}), f32[16,24,128]{2,1,0:T(8,128)S(1)}, u32[]{:S(2)}, u32[]{:S(2)}) async-start(f32[16,24,128]{2,1,0:T(8,128)} %payload.1), calls=%async_computation | async-start | bytes 393216 | tf_op jit(solution)/shard_map/all_to_all | solution.py:833
  23.9 0.0 collective-permute-done.4.even
  23.9 0.0 collective-permute-done.5.odd
  23.9 1.5 %strips.1 = (f32[56,8,128]{2,1,0:T(8,128)S(1)}, f32[56,8,128]{2,1,0:T(8,128)S(1)}, f32[2,16,24,256]{3,2,1,0:T(8,128)}, f32[2,8,16,128]{3,2,1,0:T(8,128)S(1)}) custom-call(s32[4]{0:T(128)S(1)} %pad_add_fusion.place, f32[16,16,256]{2,1,0:T(8,128)S(1)} %get-tuple-element.33.residual, f32[16,16,256]{2,1,0:T(8,128)S(1)} %get-tuple-element.28.material, ...), custom_call_target="tpu_custom_call" | custom-call | flops 99999997952 | tf_op jit(solution)/shard_map/strips/pallas_call | solution.py:770
  25.5 0.7 %collective-permute-start.6 = (f32[56,8,128]{2,1,0:T(8,128)S(1)}, f32[56,8,128]{2,1,0:T(8,128)S(1)}, u32[]{:S(2)}, u32[]{:S(2)}) collective-permute-start(f32[56,8,128]{2,1,0:T(8,128)S(1)} %get-tuple-element.38), channel_id=1, source_target_pairs={{4,8},{12,16},{20,24},{8,4},{16,12},{24,20},{5,9},{13,17},{21,25},... | collective-permute-start | bytes 688136 | tf_op jit(solution)/shard_map/ppermute | solution.py:842
  26.2 3.3 %collective-permute-start.7 = (f32[56,8,128]{2,1,0:T(8,128)S(1)}, f32[56,8,128]{2,1,0:T(8,128)S(1)}, u32[]{:S(2)}, u32[]{:S(2)}) collective-permute-start(f32[56,8,128]{2,1,0:T(8,128)S(1)} %get-tuple-element.39), channel_id=1, source_target_pairs={{0,4},{8,12},{16,20},{24,28},{4,0},{12,8},{20,16},{28,24},{1,5},{9... | collective-permute-start | bytes 688136 | tf_op jit(solution)/shard_map/ppermute | solution.py:843
  29.5 3.0 %all-to-all-done.blocks = f32[16,24,128]{2,1,0:T(8,128)S(1)} async-done(((f32[16,24,128]{2,1,0:T(8,128)}), f32[16,24,128]{2,1,0:T(8,128)S(1)}, u32[]{:S(2)}, u32[]{:S(2)}) %all-to-all-start) | async-done | bytes 196640 | tf_op jit(solution)/shard_map/all_to_all | solution.py:833
  32.6 0.1 collective-permute-start.8
  32.6 1.4 %collective-permute-done.8.theirs = f32[16,24,128]{2,1,0:T(8,128)S(1)} collective-permute-done((f32[16,24,128]{2,1,0:T(8,128)S(1)}, f32[16,24,128]{2,1,0:T(8,128)S(1)}, u32[]{:S(2)}, u32[]{:S(2)}) %collective-permute-start.8) | collective-permute-done | bytes 196640 | tf_op jit(solution)/shard_map/ppermute | solution.py:846
  34.1 2.9 %cycle1.1 = (f32[8,8,128]{2,1,0:T(8,128)S(1)}, f32[4,59,16,128]{3,2,1,0:T(8,128)S(1)}) custom-call(s32[4]{0:T(128)S(1)} %pad_add_fusion.place, f32[16,24,128]{2,1,0:T(8,128)S(1)} %pass.1.mine, f32[16,24,128]{2,1,0:T(8,128)S(1)} %collective-permute-done.8.theirs), custom_call_target="tpu_custom_call" | custom-call | tf_op jit(solution)/shard_map/cycle1/pallas_call | solution.py:770
  37.0 0.0 collective-permute-done.6.outer
  37.0 0.0 collective-permute-done.7.inner
  37.0 1.9 %level1.1 = (f32[32,8,128]{2,1,0:T(8,128)}, f32[59,16,128]{2,1,0:T(8,128)}) custom-call(s32[4]{0:T(128)S(1)} %pad_add_fusion.place, f32[2,8,16,128]{3,2,1,0:T(8,128)S(1)} %get-tuple-element.37._.long1, f32[56,8,128]{2,1,0:T(8,128)S(1)} %collective-permute-done.6.outer, f32[56,8,128]{2,1,0:T(8,128)S(1)} %collective-permute-done.7.inner, ...), custom_call_target="tpu_custom_call" | custom-call | tf_op jit(solution)/shard_map/level1/pallas_call | solution.py:770
  38.9 3.3 %all-to-all-start.1 = ((f32[32,8,128]{2,1,0:T(8,128)}), f32[32,8,128]{2,1,0:T(8,128)S(1)}, u32[]{:S(2)}, u32[]{:S(2)}) async-start(f32[32,8,128]{2,1,0:T(8,128)} %get-tuple-element.41), calls=%async_computation.1 | async-start | bytes 262144 | tf_op jit(solution)/shard_map/all_to_all | solution.py:866
  42.2 4.2 %smooth.1 = (f32[16,16,256]{2,1,0:T(8,128)S(1)}, f32[59,16,128]{2,1,0:T(8,128)S(1)}) custom-call(s32[4]{0:T(128)S(1)} %pad_add_fusion.place, f32[16,16,256]{2,1,0:T(8,128)} %potential_far.1, f32[59,16,128]{2,1,0:T(8,128)} %get-tuple-element.43.state_far, f32[2,16,24,256]{3,2,1,0:T(8,128)} %get-tuple-element.44.long, ...), custom_call_target="tpu_custom_call" | custom-call | tf_op jit(solution)/shard_map/smooth/pallas_call | solution.py:770
  46.4 3.6 %all-to-all-done.1.blocks = f32[32,8,128]{2,1,0:T(8,128)S(1)} async-done(((f32[32,8,128]{2,1,0:T(8,128)}), f32[32,8,128]{2,1,0:T(8,128)S(1)}, u32[]{:S(2)}, u32[]{:S(2)}) %all-to-all-start.1) | async-done | bytes 131104 | tf_op jit(solution)/shard_map/all_to_all | solution.py:866
  50.1 2.9 %cycle2.1 = f32[16,16,256]{2,1,0:T(8,128)} custom-call(s32[4]{0:T(128)S(1)} %pad_add_fusion.place, f32[32,8,128]{2,1,0:T(8,128)S(1)} %all-to-all-done.1.blocks, f32[4,59,16,128]{3,2,1,0:T(8,128)S(1)} %get-tuple-element.42.table, f32[59,16,128]{2,1,0:T(8,128)S(1)} %get-tuple-element.45.state, f32[16,16,256]{2,1,0:T(8,128)S(1)} %get-tuple-element.46.partial), custom_call_target="tpu_custom_call" | custom-call | tf_op jit(solution)/shard_map/cycle2/pallas_call | solution.py:770
  (1 shorter events, 0.0 us)
Async XLA Ops:
  1.8 7.1 %collective-permute-start = (f32[3,16,256]{2,1,0:T(8,128)S(1)}, f32[3,16,256]{2,1,0:T(8,128)S(1)}, u32[]{:S(2)}, u32[]{:S(2)}) collective-permute-start(f32[3,16,256]{2,1,0:T(8,128)S(1)} %get-tuple-element.29), channel_id=1, source_target_pairs={{4,8},{12,16},{20,24},{8,4},{16,12},{24,20},{5,9},{13,17},{21,25},... | collective-permute-start | bytes 147464 | tf_op jit(solution)/shard_map/ppermute | solution.py:813
  2.4 6.4 %collective-permute-start.1 = (f32[3,16,256]{2,1,0:T(8,128)S(1)}, f32[3,16,256]{2,1,0:T(8,128)S(1)}, u32[]{:S(2)}, u32[]{:S(2)}) collective-permute-start(f32[3,16,256]{2,1,0:T(8,128)S(1)} %get-tuple-element.30), channel_id=1, source_target_pairs={{0,1},{2,3},{1,0},{3,2},{4,5},{6,7},{5,4},{7,6},{8,9},{10,11},{9,8... | collective-permute-start | bytes 147464 | tf_op jit(solution)/shard_map/ppermute | solution.py:811
  5.5 3.3 %collective-permute-start.2 = (f32[3,16,256]{2,1,0:T(8,128)S(1)}, f32[3,16,256]{2,1,0:T(8,128)S(1)}, u32[]{:S(2)}, u32[]{:S(2)}) collective-permute-start(f32[3,16,256]{2,1,0:T(8,128)S(1)} %get-tuple-element.31), channel_id=1, source_target_pairs={{1,2},{2,1},{5,6},{6,5},{9,10},{10,9},{13,14},{14,13},{17,18},{18,... | collective-permute-start | bytes 147464 | tf_op jit(solution)/shard_map/ppermute | solution.py:812
  6.2 3.5 %collective-permute-start.3 = (f32[3,16,256]{2,1,0:T(8,128)S(1)}, f32[3,16,256]{2,1,0:T(8,128)S(1)}, u32[]{:S(2)}, u32[]{:S(2)}) collective-permute-start(f32[3,16,256]{2,1,0:T(8,128)S(1)} %get-tuple-element.32), channel_id=1, source_target_pairs={{0,4},{8,12},{16,20},{24,28},{4,0},{12,8},{20,16},{28,24},{1,5},{9... | collective-permute-start | bytes 147464 | tf_op jit(solution)/shard_map/ppermute | solution.py:814
  11.3 12.6 %collective-permute-start.4 = (f32[40,8,128]{2,1,0:T(8,128)S(1)}, f32[40,8,128]{2,1,0:T(8,128)S(1)}, u32[]{:S(2)}, u32[]{:S(2)}) collective-permute-start(f32[40,8,128]{2,1,0:T(8,128)S(1)} %get-tuple-element.35), channel_id=1, source_target_pairs={{0,1},{2,3},{1,0},{3,2},{4,5},{6,7},{5,4},{7,6},{8,9},{10,11},{9,8... | collective-permute-start | bytes 491528 | tf_op jit(solution)/shard_map/ppermute | solution.py:825
  15.5 8.4 %collective-permute-start.5 = (f32[40,8,128]{2,1,0:T(8,128)S(1)}, f32[40,8,128]{2,1,0:T(8,128)S(1)}, u32[]{:S(2)}, u32[]{:S(2)}) collective-permute-start(f32[40,8,128]{2,1,0:T(8,128)S(1)} %get-tuple-element.36), channel_id=1, source_target_pairs={{1,2},{2,1},{5,6},{6,5},{9,10},{10,9},{13,14},{14,13},{17,18},{18,... | collective-permute-start | bytes 491528 | tf_op jit(solution)/shard_map/ppermute | solution.py:826
  17.3 15.3 %all-to-all-start = ((f32[16,24,128]{2,1,0:T(8,128)}), f32[16,24,128]{2,1,0:T(8,128)S(1)}, u32[]{:S(2)}, u32[]{:S(2)}) async-start(f32[16,24,128]{2,1,0:T(8,128)} %payload.1), calls=%async_computation | async-start | bytes 393216 | tf_op jit(solution)/shard_map/all_to_all | solution.py:833
  25.5 11.5 %collective-permute-start.6 = (f32[56,8,128]{2,1,0:T(8,128)S(1)}, f32[56,8,128]{2,1,0:T(8,128)S(1)}, u32[]{:S(2)}, u32[]{:S(2)}) collective-permute-start(f32[56,8,128]{2,1,0:T(8,128)S(1)} %get-tuple-element.38), channel_id=1, source_target_pairs={{4,8},{12,16},{20,24},{8,4},{16,12},{24,20},{5,9},{13,17},{21,25},... | collective-permute-start | bytes 688136 | tf_op jit(solution)/shard_map/ppermute | solution.py:842
  26.2 10.8 %collective-permute-start.7 = (f32[56,8,128]{2,1,0:T(8,128)S(1)}, f32[56,8,128]{2,1,0:T(8,128)S(1)}, u32[]{:S(2)}, u32[]{:S(2)}) collective-permute-start(f32[56,8,128]{2,1,0:T(8,128)S(1)} %get-tuple-element.39), channel_id=1, source_target_pairs={{0,4},{8,12},{16,20},{24,28},{4,0},{12,8},{20,16},{28,24},{1,5},{9... | collective-permute-start | bytes 688136 | tf_op jit(solution)/shard_map/ppermute | solution.py:843
  32.6 1.5 %collective-permute-start.8 = (f32[16,24,128]{2,1,0:T(8,128)S(1)}, f32[16,24,128]{2,1,0:T(8,128)S(1)}, u32[]{:S(2)}, u32[]{:S(2)}) collective-permute-start(f32[16,24,128]{2,1,0:T(8,128)S(1)} %pass.1.mine), channel_id=1, source_target_pairs={{0,4},{8,12},{16,20},{24,28},{4,0},{12,8},{20,16},{28,24},{1,5},{9... | collective-permute-start | bytes 589832 | tf_op jit(solution)/shard_map/ppermute | solution.py:846
  38.9 11.2 %all-to-all-start.1 = ((f32[32,8,128]{2,1,0:T(8,128)}), f32[32,8,128]{2,1,0:T(8,128)S(1)}, u32[]{:S(2)}, u32[]{:S(2)}) async-start(f32[32,8,128]{2,1,0:T(8,128)} %get-tuple-element.41), calls=%async_computation.1 | async-start | bytes 262144 | tf_op jit(solution)/shard_map/all_to_all | solution.py:866

commit v8 on v7

--- a/solution.py
+++ b/solution.py
@@ -373,6 +373,15 @@
     passing.wait()
 
 
+HALF = LANES // 2
+
+
+def seal(ref, count):
+    low = iota(ref.shape[1:], 1) < HALF
+    ref[0] = jnp.where(low, 0.0, pltpu.roll(ref[count], HALF, 1))
+    ref[count + 1] = jnp.where(low, pltpu.roll(ref[1], HALF, 1), 0.0)
+
+
 def each(count, body, most=8):
     step = min(count, most)
     if count // step <= 4:
@@ -387,12 +396,13 @@
     lax.fori_loop(0, count // step, run, 0)
 
 
-def fill_table(mat, table, level, count, base, width):
+def fill_table(mat, table, level, count, base):
     stride, scale = 2**level, 0.25 ** (level + 2)
     rows = mat.shape[1]
     row, lane = iota((rows, LANES), 0), iota((rows, LANES), 1)
-    above, beyond = row >= stride, lane >= stride
-    outside = as_float(row == 0) + as_float(row == rows - stride) + as_float(lane == 0) + as_float(lane == width - stride)
+    depth = lane % HALF
+    above, beyond = row >= stride, depth >= stride
+    outside = as_float(row == 0) + as_float(row == rows - stride) + as_float(depth == 0) + as_float(depth == HALF - stride)
 
     def body(at, step):
         a, before, ahead = mat[pl.ds(at + 1, step)], mat[pl.ds(at, step)], mat[pl.ds(at + 2, step)]
@@ -400,7 +410,8 @@
         w_down = jnp.where(above[None], harmonic(a, lower(a, 1, stride), scale), 0.0)
         w_back = jnp.where(beyond[None], harmonic(a, lower(a, 2, stride), scale), 0.0)
         plane = at + iota((step, 1, 1), 0)
-        edges = outside[None] + as_float(plane == 0) + as_float(plane == count - 1)
+        low = (lane < HALF)[None]
+        edges = outside[None] + as_float((plane == 0) & low) + as_float((plane == count - 1) & jnp.logical_not(low))
         diagonal = w_before + w_ahead + w_down + upper(w_down, 1, stride) + w_back + upper(w_back, 2, stride)
         diagonal = diagonal + scale * a * edges
         table[0, pl.ds(base + at, step)] = w_before
@@ -409,7 +420,7 @@
         table[3, pl.ds(base + at, step)] = jnp.where(a > 0.0, invert(jnp.maximum(diagonal, 1e-4)), 0.0)
 
     each(count, body)
-    table[0, base + count] = jnp.zeros((rows, LANES), F32)
+    table[0, base + count] = harmonic(mat[count], mat[count + 1], scale)
 
 
 def fold(t, stride):
@@ -435,10 +446,6 @@
 
 
 def cycle(s, e, t, table, counts, bases, place, out, c2, r2, pad):
-    zero = jnp.zeros(t.shape[1:], F32)
-    for ref, count in zip(e, counts):
-        ref[0] = zero
-        ref[count + 1] = zero
     for level, (count, base) in enumerate(zip(counts, bases)):
         s_l, e_l, stride = s[level], e[level], 2**level
 
@@ -446,6 +453,7 @@
             e_l[pl.ds(at + 1, step)] = DAMPING * s_l[pl.ds(at + 1, step)] * table[3, pl.ds(base + at, step)]
 
         each(count, start)
+        seal(e_l, count)
         if level == len(counts) - 1:
             break
 
@@ -464,41 +472,39 @@
 
         each(count, sweep)
 
-    t[0] = zero
-    t[counts[2] + 1] = zero
     now, other = e[2], t
     for _ in range(COARSE_SWEEPS - 1):
         relax(s[2], now, other, bases[2], counts[2], 4)
+        seal(other, counts[2])
         now, other = other, now
-
-    def add(at, step):
-        e[1][pl.ds(2 * at + 1, 2 * step)] = e[1][pl.ds(2 * at + 1, 2 * step)] + unfold(now[pl.ds(at + 1, step)], 2)
-
-    each(counts[2], add, 4)
-    if now is t:
-        now = e[2] = s[1]
-    relax(s[1], e[1], t, bases[1], counts[1], 2)
-
-    planes = c2 + 4
-    begin = place[2] * c2 - 2
-    inside = jnp.clip(begin, 0, counts[0] - planes)
-    coarse = jnp.clip(place[2] * c2 // 2 - 2, 0, counts[1] - planes // 2 - 2)
-    number = planes // 2 + 2
-    at = pl.ds(2 * coarse + 1, 2 * number)
-    e[0][at] = e[0][at] + unfold(t[pl.ds(coarse + 1, number)], 1)
-    v, off = off_diagonal(e[0], table, bases[0], inside, planes, 1)
-    inverse = table[3, pl.ds(bases[0] + inside, planes)]
+    for level in (1, 0):
+        coarser, e_l, stride = now, e[level], 2**level
+
+        def add(at, step):
+            here = pl.ds(2 * at + 1, 2 * step)
+            e_l[here] = e_l[here] + unfold(coarser[pl.ds(at + 1, step)], stride)
+
+        each(counts[level + 1], add, 4)
+        seal(e_l, counts[level])
+        now = s[level]
+        relax(s[level], e_l, now, bases[level], counts[level], stride)
+
+    rows = t.shape[1]
+    low = iota((rows, LANES), 1) < HALF
     pad[...] = jnp.zeros(pad.shape, F32)
-    rows = t.shape[1]
-    value = KEPT * v + DAMPING * inverse * (s[0][pl.ds(inside + 1, planes)] + off)
-    pad[pl.ds(2 + inside - begin, planes), 8 : 8 + rows, :] = value
-    for n in range(planes):
-        out[n] = pad[n + 2, pl.ds(place[3] * r2 + 6, r2 + 4), :]
+    for n in range(c2 + 4):
+        at = place[2] * c2 + n - 2
+        second = at >= counts[0]
+        inside = (at >= 0) & (at < 2 * counts[0])
+        value = now[jnp.clip(at - jnp.where(second, counts[0], 0), 0, counts[0] - 1) + 1]
+        value = jnp.where(second, pltpu.roll(value, HALF, 1), value)
+        pad[n, 8 : 8 + rows, :] = jnp.where(low & inside, value, 0.0)
+        out[n] = pad[n, pl.ds(place[3] * r2 + 6, r2 + 4), :]
 
 
 def cycle_shapes(counts, rows, c2):
     out = [pltpu.VMEM((count + 2, rows, LANES), F32) for count in (*counts, *counts, counts[0])]
-    return out + [pltpu.VMEM((c2 + 8, rows + 16, LANES), F32)]
+    return out + [pltpu.VMEM((c2 + 4, rows + 16, LANES), F32)]
 
 
 def repeat(count, body):
@@ -517,18 +523,18 @@
 def spread_blocks(fetch, outs, grid, c2, r2):
     gx, gy = grid
     length = c2 // 2 * r2
-    low = iota((length, LANES), 1) < LANES // 2
+    low = iota((length, LANES), 1) < HALF
 
     def column(i, parity):
         for j in range(gy):
             for start, out in outs:
-                block = fetch(i, parity, j, slice(start, start + length))
-                parts = (jnp.where(low, block, 0.0), jnp.where(low, pltpu.roll(block, LANES // 2, 1), 0.0))
+                a, b = (fetch(n, parity, j, slice(start, start + length)) for n in (i, i + gx // 2))
+                parts = jnp.where(low, a, pltpu.roll(b, HALF, 1)), jnp.where(low, pltpu.roll(a, HALF, 1), b)
                 for k in range(c2):
                     n = k % (c2 // 2)
                     out[i * c2 + k + 1, j * r2 : (j + 1) * r2, :] = parts[k // (c2 // 2)][n * r2 : (n + 1) * r2]
 
-    repeat(gx, column)
+    repeat(gx // 2, column)
 
 
 def clear_ends(refs, counts):
@@ -542,13 +548,12 @@
     out[...] = blocks[...]
 
 
-def first_cycle_kernel(counts, bases, grid, c2, r2, width, place, mine, theirs, out, table, *scratch):
+def first_cycle_kernel(counts, bases, grid, c2, r2, place, mine, theirs, out, table, *scratch):
     s, e, t, pad = scratch[0:3], list(scratch[3:6]), scratch[6], scratch[7]
     gx, gy = grid
     rows = gy * r2
-    half = LANES // 2
     own = c2 // 2 * r2
-    clear_ends((t, *s), (counts[0], *counts))
+    clear_ends(s[:1], counts)
     odd = place[0] == 1
 
     def fetch(i, parity, j, at):
@@ -558,13 +563,13 @@
 
     spread_blocks(fetch, ((0, s[0]), (own + 2 * r2, t)), grid, c2, r2)
     face_y = e[0]
-    low = iota((2 * c2, LANES), 1) < half
+    low = iota((2 * c2, LANES), 1) < HALF
 
     def edges(i, parity):
         for j in range(gy):
-            faces = fetch(i, parity, j, slice(own, own + 2 * r2))
-            x_faces = jnp.where(low, faces, 0.0)
-            y_faces = jnp.where(low, pltpu.roll(faces, half, 1), 0.0)
+            a, b = (fetch(n, parity, j, slice(own, own + 2 * r2)) for n in (i, i + gx // 2))
+            x_faces = jnp.where(low, a, pltpu.roll(b, HALF, 1))
+            y_faces = jnp.where(low, pltpu.roll(a, HALF, 1), b)
             here = slice(j * r2, (j + 1) * r2)
             s[0][i * c2, here, :] = s[0][i * c2, here, :] + x_faces[:r2]
             s[0][(i + 1) * c2 + 1, here, :] = s[0][(i + 1) * c2 + 1, here, :] + x_faces[r2:]
@@ -575,7 +580,11 @@
                 if j < gy - 1:
                     face_y[at, (j + 1) * r2 : (j + 1) * r2 + 1, :] = y_faces[c2 + k : c2 + k + 1]
 
-    repeat(gx, edges)
+    repeat(gx // 2, edges)
+    first, last = s[0][0], s[0][counts[0] + 1]
+    low = iota(first.shape, 1) < HALF
+    s[0][counts[0]] = s[0][counts[0]] + jnp.where(low, pltpu.roll(first, HALF, 1), 0.0)
+    s[0][1] = s[0][1] + jnp.where(low, 0.0, pltpu.roll(last, HALF, 1))
 
     def join(at, step):
         now = pl.ds(at + 1, step)
@@ -584,7 +593,6 @@
         s[0][now] = s[0][now] + jnp.where(edge[None], face_y[now], 0.0)
 
     each(counts[0], join)
-    clear_ends(s[:1], counts)
     mats = (t, s[1], s[2])
     for level, (count, base) in enumerate(zip(counts, bases)):
         if level:
@@ -595,7 +603,8 @@
                 mats[level][pl.ds(at // 2 + 1, step // 2)] = jnp.where(whole[None], mean, 0.0)
 
             each(counts[level - 1], coarsen)
-        fill_table(mats[level], table, level, count, base, width)
+        seal(mats[level], count)
+        fill_table(mats[level], table, level, count, base)
     cycle(s, e, t, table, counts, bases, place, out, c2, r2, pad)
 
 
@@ -692,7 +701,6 @@
     s, e, t, pad = scratch[0:3], list(scratch[3:6]), scratch[6], scratch[7]
     view, flat, prolonged, tall, coarse, result, departures = scratch[8:15]
     spread_blocks(lambda i, _, j, at: blocks[grid[0] * grid[1] - 1 - i * grid[1] - j, at], ((0, s[0]),), grid, c2, r2)
-    clear_ends(s, counts)
     cycle(s, e, t, table, counts, bases, place, view, c2, r2, pad)
     raise_window(view, flat, prolonged)
     count, rows, depth = partial.shape
@@ -844,12 +852,12 @@
 
     (blocks,) = call(pass_kernel, "pass", (blocks, long1), (sheet2,))
     others = lax.ppermute(blocks, "gx", swap_x[0])
-    counts = tuple(gx * c2 // k for k in (1, 2, 4))
+    counts = tuple(gx * c2 // 2 // k for k in (1, 2, 4))
     bases = (0, counts[0] + 1, counts[0] + counts[1] + 2)
     work = cycle_shapes(counts, gy * r2, c2)
     view = (c2 + 4, r2 + 4, LANES)
     window1, table = call(
-        functools.partial(first_cycle_kernel, counts, bases, (gx, gy), c2, r2, d1 // 2), "cycle1", (place, blocks, others),
+        functools.partial(first_cycle_kernel, counts, bases, (gx, gy), c2, r2), "cycle1", (place, blocks, others),
         (view, (4, sum(counts) + 3, gy * r2, LANES)), work,
     )
     frame = (c1 + 8, r1 + 8, d1)

time: 53.3 us -> 53.2 us (level)
  Pallas kernels: 17.9 us -> 17.1 us
  starting transfers between devices: 25.9 us -> 26.6 us
    pallas_call x9, Pallas kernels: 17.9 us -> 17.1 us  [call(): pl.pallas_call(kernel, out_shape=results, in_specs=specs, out_specs=[pl.B...]
    all_to_all x1, starting transfers between devices: 3.31 us -> 4.05 us  [local(): lax.all_to_all(payload, ('gx', 'gy'), 0, 0, axis_index_groups=[list(range...]
  transfers between devices with their start and end apart: 11 -> 11, of which waited for: 4 -> 4; matrix products, arithmetic and copies ran while one was open for 0% -> 0% of each run, Pallas kernels for 18% -> 17%
where the time goes in v8:
time: 53.2 us; the launch traced here: 52.9 us
  starting transfers between devices  26.6 us (50%)
  Pallas kernels  17.1 us (32%)
  waiting for transfers between devices  8.97 us (17%)
    pallas_call x9, Pallas kernels, call(): pl.pallas_call(kernel, out_shape=results, in_specs=specs, out_specs=[pl.B...  17.1 us
    ppermute x2, starting transfers between devices, local(): even = lax.ppermute(even, 'gy', swap_y[0])  7.27 us
    all_to_all x1, starting transfers between devices, local(): lax.all_to_all(payload, ('gx', 'gy'), 0, 0, axis_index_groups=groups)  6.63 us
    ppermute x2, starting transfers between devices, local(): inner = lax.ppermute(inner, 'gx', swap_x[0])  5.97 us
    all_to_all x1, starting transfers between devices, local(): lax.all_to_all(payload, ('gx', 'gy'), 0, 0, axis_index_groups=[list(range...  4.05 us
    all_to_all x1, waiting for transfers between devices, local(): lax.all_to_all(payload, ('gx', 'gy'), 0, 0, axis_index_groups=[list(range...  3.6 us
    all_to_all x1, waiting for transfers between devices, local(): lax.all_to_all(payload, ('gx', 'gy'), 0, 0, axis_index_groups=groups)  3.05 us
    ppermute x1, waiting for transfers between devices, local(): others = lax.ppermute(blocks, 'gx', swap_x[0])  1.43 us
  transfers between devices with their start and end apart: 11, of which 4 were waited for; matrix products, arithmetic and copies ran while one was open for 0% of the time, Pallas kernels for 17%

profile of v8, /device:TPU:0, one launch (start us, length us, event | category | flops | bytes accessed | tf_op | source)
XLA Modules:
  0.0 52.9 jit_solution(2119388852646232313)
XLA Ops:
  0.0 0.1 pad_add_fusion.place
  0.1 1.7 %faces.1 = (f32[16,16,256]{2,1,0:T(8,128)S(1)}, f32[16,16,256]{2,1,0:T(8,128)S(1)}, f32[16,16,256]{2,1,0:T(8,128)S(1)}, f32[3,16,256]{2,1,0:T(8,128)S(1)}, f32[3...) custom-call(s32[4]{0:T(128)S(1)} %pad_add_fusion.place, f32[3]{0:T(128)} %permeability.1, ...), custom_call_target="tpu_custom_call" | custom-call | tf_op jit(solution)/shard_map/faces/pallas_call | solution.py:778
  1.8 0.7 %collective-permute-start = (f32[3,16,256]{2,1,0:T(8,128)S(1)}, f32[3,16,256]{2,1,0:T(8,128)S(1)}, u32[]{:S(2)}, u32[]{:S(2)}) collective-permute-start(f32[3,16,256]{2,1,0:T(8,128)S(1)} %get-tuple-element.29), channel_id=1, source_target_pairs={{4,8},{12,16},{20,24},{8,4},{16,12},{24,20},{5,9},{13,17},{21,25},... | collective-permute-start | bytes 147464 | tf_op jit(solution)/shard_map/ppermute | solution.py:821
  2.4 3.1 %collective-permute-start.1 = (f32[3,16,256]{2,1,0:T(8,128)S(1)}, f32[3,16,256]{2,1,0:T(8,128)S(1)}, u32[]{:S(2)}, u32[]{:S(2)}) collective-permute-start(f32[3,16,256]{2,1,0:T(8,128)S(1)} %get-tuple-element.30), channel_id=1, source_target_pairs={{0,1},{2,3},{1,0},{3,2},{4,5},{6,7},{5,4},{7,6},{8,9},{10,11},{9,8... | collective-permute-start | bytes 147464 | tf_op jit(solution)/shard_map/ppermute | solution.py:819
  5.5 0.7 %collective-permute-start.2 = (f32[3,16,256]{2,1,0:T(8,128)S(1)}, f32[3,16,256]{2,1,0:T(8,128)S(1)}, u32[]{:S(2)}, u32[]{:S(2)}) collective-permute-start(f32[3,16,256]{2,1,0:T(8,128)S(1)} %get-tuple-element.31), channel_id=1, source_target_pairs={{1,2},{2,1},{5,6},{6,5},{9,10},{10,9},{13,14},{14,13},{17,18},{18,... | collective-permute-start | bytes 147464 | tf_op jit(solution)/shard_map/ppermute | solution.py:820
  6.2 2.6 %collective-permute-start.3 = (f32[3,16,256]{2,1,0:T(8,128)S(1)}, f32[3,16,256]{2,1,0:T(8,128)S(1)}, u32[]{:S(2)}, u32[]{:S(2)}) collective-permute-start(f32[3,16,256]{2,1,0:T(8,128)S(1)} %get-tuple-element.32), channel_id=1, source_target_pairs={{0,4},{8,12},{16,20},{24,28},{4,0},{12,8},{20,16},{28,24},{1,5},{9... | collective-permute-start | bytes 147464 | tf_op jit(solution)/shard_map/ppermute | solution.py:822
  8.8 0.0 collective-permute-done.outer
  8.8 0.0 collective-permute-done.1.even
  8.8 0.0 collective-permute-done.2.odd
  8.8 0.9 %collective-permute-done.3.inner = f32[3,16,256]{2,1,0:T(8,128)S(1)} collective-permute-done((f32[3,16,256]{2,1,0:T(8,128)S(1)}, f32[3,16,256]{2,1,0:T(8,128)S(1)}, u32[]{:S(2)}, u32[]{:S(2)}) %collective-permute-start.3) | collective-permute-done | bytes 49184 | tf_op jit(solution)/shard_map/ppermute | solution.py:822
  9.7 1.6 %residual.1 = (f32[16,16,256]{2,1,0:T(8,128)S(1)}, f32[160,128]{1,0:T(8,128)S(1)}, f32[40,8,128]{2,1,0:T(8,128)S(1)}, f32[40,8,128]{2,1,0:T(8,128)S(1)}) custom-call(s32[4]{0:T(128)S(1)} %pad_add_fusion.place, f32[16,16,256]{2,1,0:T(8,128)S(1)} %get-tuple-element.26.source, f32[16,16,256]{2,1,0:T(8,128)S(1)} %get-tuple-element.27.potential, ...), custom_call_target="tpu_custom_call" | custom-call | tf_op jit(solution)/shard_map/residual/pallas_call | solution.py:778
  11.3 4.2 %collective-permute-start.4 = (f32[40,8,128]{2,1,0:T(8,128)S(1)}, f32[40,8,128]{2,1,0:T(8,128)S(1)}, u32[]{:S(2)}, u32[]{:S(2)}) collective-permute-start(f32[40,8,128]{2,1,0:T(8,128)S(1)} %get-tuple-element.35), channel_id=1, source_target_pairs={{0,1},{2,3},{1,0},{3,2},{4,5},{6,7},{5,4},{7,6},{8,9},{10,11},{9,8... | collective-permute-start | bytes 491528 | tf_op jit(solution)/shard_map/ppermute | solution.py:833
  15.5 0.7 %collective-permute-start.5 = (f32[40,8,128]{2,1,0:T(8,128)S(1)}, f32[40,8,128]{2,1,0:T(8,128)S(1)}, u32[]{:S(2)}, u32[]{:S(2)}) collective-permute-start(f32[40,8,128]{2,1,0:T(8,128)S(1)} %get-tuple-element.36), channel_id=1, source_target_pairs={{1,2},{2,1},{5,6},{6,5},{9,10},{10,9},{13,14},{14,13},{17,18},{18,... | collective-permute-start | bytes 491528 | tf_op jit(solution)/shard_map/ppermute | solution.py:834
  16.1 1.1 %payload.1 = f32[16,24,128]{2,1,0:T(8,128)} custom-call(f32[160,128]{1,0:T(8,128)S(1)} %get-tuple-element.34.coarse), custom_call_target="tpu_custom_call" | custom-call | tf_op jit(solution)/shard_map/payload/pallas_call | solution.py:778
  17.3 6.6 %all-to-all-start = ((f32[16,24,128]{2,1,0:T(8,128)}), f32[16,24,128]{2,1,0:T(8,128)S(1)}, u32[]{:S(2)}, u32[]{:S(2)}) async-start(f32[16,24,128]{2,1,0:T(8,128)} %payload.1), calls=%async_computation | async-start | bytes 393216 | tf_op jit(solution)/shard_map/all_to_all | solution.py:841
  23.9 0.0 collective-permute-done.4.even
  23.9 0.0 collective-permute-done.5.odd
  23.9 1.5 %strips.1 = (f32[56,8,128]{2,1,0:T(8,128)S(1)}, f32[56,8,128]{2,1,0:T(8,128)S(1)}, f32[2,16,24,256]{3,2,1,0:T(8,128)}, f32[2,8,16,128]{3,2,1,0:T(8,128)S(1)}) custom-call(s32[4]{0:T(128)S(1)} %pad_add_fusion.place, f32[16,16,256]{2,1,0:T(8,128)S(1)} %get-tuple-element.33.residual, f32[16,16,256]{2,1,0:T(8,128)S(1)} %get-tuple-element.28.material, ...), custom_call_target="tpu_custom_call" | custom-call | flops 99999997952 | tf_op jit(solution)/shard_map/strips/pallas_call | solution.py:778
  25.5 0.7 %collective-permute-start.6 = (f32[56,8,128]{2,1,0:T(8,128)S(1)}, f32[56,8,128]{2,1,0:T(8,128)S(1)}, u32[]{:S(2)}, u32[]{:S(2)}) collective-permute-start(f32[56,8,128]{2,1,0:T(8,128)S(1)} %get-tuple-element.38), channel_id=1, source_target_pairs={{4,8},{12,16},{20,24},{8,4},{16,12},{24,20},{5,9},{13,17},{21,25},... | collective-permute-start | bytes 688136 | tf_op jit(solution)/shard_map/ppermute | solution.py:850
  26.2 3.3 %collective-permute-start.7 = (f32[56,8,128]{2,1,0:T(8,128)S(1)}, f32[56,8,128]{2,1,0:T(8,128)S(1)}, u32[]{:S(2)}, u32[]{:S(2)}) collective-permute-start(f32[56,8,128]{2,1,0:T(8,128)S(1)} %get-tuple-element.39), channel_id=1, source_target_pairs={{0,4},{8,12},{16,20},{24,28},{4,0},{12,8},{20,16},{28,24},{1,5},{9... | collective-permute-start | bytes 688136 | tf_op jit(solution)/shard_map/ppermute | solution.py:851
  29.5 3.0 %all-to-all-done.blocks = f32[16,24,128]{2,1,0:T(8,128)S(1)} async-done(((f32[16,24,128]{2,1,0:T(8,128)}), f32[16,24,128]{2,1,0:T(8,128)S(1)}, u32[]{:S(2)}, u32[]{:S(2)}) %all-to-all-start) | async-done | bytes 196640 | tf_op jit(solution)/shard_map/all_to_all | solution.py:841
  32.6 0.1 collective-permute-start.8
  32.6 1.4 %collective-permute-done.8.theirs = f32[16,24,128]{2,1,0:T(8,128)S(1)} collective-permute-done((f32[16,24,128]{2,1,0:T(8,128)S(1)}, f32[16,24,128]{2,1,0:T(8,128)S(1)}, u32[]{:S(2)}, u32[]{:S(2)}) %collective-permute-start.8) | collective-permute-done | bytes 196640 | tf_op jit(solution)/shard_map/ppermute | solution.py:854
  34.1 2.2 %cycle1.1 = (f32[8,8,128]{2,1,0:T(8,128)S(1)}, f32[4,31,16,128]{3,2,1,0:T(8,128)S(1)}) custom-call(s32[4]{0:T(128)S(1)} %pad_add_fusion.place, f32[16,24,128]{2,1,0:T(8,128)S(1)} %pass.1.mine, f32[16,24,128]{2,1,0:T(8,128)S(1)} %collective-permute-done.8.theirs), custom_call_target="tpu_custom_call" | custom-call | tf_op jit(solution)/shard_map/cycle1/pallas_call | solution.py:778
  36.2 0.0 collective-permute-done.6.outer
  36.2 0.0 collective-permute-done.7.inner
  36.2 1.9 %level1.1 = (f32[32,8,128]{2,1,0:T(8,128)}, f32[59,16,128]{2,1,0:T(8,128)}) custom-call(s32[4]{0:T(128)S(1)} %pad_add_fusion.place, f32[2,8,16,128]{3,2,1,0:T(8,128)S(1)} %get-tuple-element.37._.long1, f32[56,8,128]{2,1,0:T(8,128)S(1)} %collective-permute-done.6.outer, f32[56,8,128]{2,1,0:T(8,128)S(1)} %collective-permute-done.7.inner, ...), custom_call_target="tpu_custom_call" | custom-call | tf_op jit(solution)/shard_map/level1/pallas_call | solution.py:778
  38.1 4.1 %all-to-all-start.1 = ((f32[32,8,128]{2,1,0:T(8,128)}), f32[32,8,128]{2,1,0:T(8,128)S(1)}, u32[]{:S(2)}, u32[]{:S(2)}) async-start(f32[32,8,128]{2,1,0:T(8,128)} %get-tuple-element.41), calls=%async_computation.1 | async-start | bytes 262144 | tf_op jit(solution)/shard_map/all_to_all | solution.py:874
  42.2 4.2 %smooth.1 = (f32[16,16,256]{2,1,0:T(8,128)S(1)}, f32[59,16,128]{2,1,0:T(8,128)S(1)}) custom-call(s32[4]{0:T(128)S(1)} %pad_add_fusion.place, f32[16,16,256]{2,1,0:T(8,128)} %potential_far.1, f32[59,16,128]{2,1,0:T(8,128)} %get-tuple-element.43.state_far, f32[2,16,24,256]{3,2,1,0:T(8,128)} %get-tuple-element.44.long, ...), custom_call_target="tpu_custom_call" | custom-call | tf_op jit(solution)/shard_map/smooth/pallas_call | solution.py:778
  46.4 3.6 %all-to-all-done.1.blocks = f32[32,8,128]{2,1,0:T(8,128)S(1)} async-done(((f32[32,8,128]{2,1,0:T(8,128)}), f32[32,8,128]{2,1,0:T(8,128)S(1)}, u32[]{:S(2)}, u32[]{:S(2)}) %all-to-all-start.1) | async-done | bytes 131104 | tf_op jit(solution)/shard_map/all_to_all | solution.py:874
  50.1 2.8 %cycle2.1 = f32[16,16,256]{2,1,0:T(8,128)} custom-call(s32[4]{0:T(128)S(1)} %pad_add_fusion.place, f32[32,8,128]{2,1,0:T(8,128)S(1)} %all-to-all-done.1.blocks, f32[4,31,16,128]{3,2,1,0:T(8,128)S(1)} %get-tuple-element.42.table, f32[59,16,128]{2,1,0:T(8,128)S(1)} %get-tuple-element.45.state, f32[16,16,256]{2,1,0:T(8,128)S(1)} %get-tuple-element.46.partial), custom_call_target="tpu_custom_call" | custom-call | tf_op jit(solution)/shard_map/cycle2/pallas_call | solution.py:778
  (1 shorter events, 0.0 us)
Async XLA Ops:
  1.8 7.1 %collective-permute-start = (f32[3,16,256]{2,1,0:T(8,128)S(1)}, f32[3,16,256]{2,1,0:T(8,128)S(1)}, u32[]{:S(2)}, u32[]{:S(2)}) collective-permute-start(f32[3,16,256]{2,1,0:T(8,128)S(1)} %get-tuple-element.29), channel_id=1, source_target_pairs={{4,8},{12,16},{20,24},{8,4},{16,12},{24,20},{5,9},{13,17},{21,25},... | collective-permute-start | bytes 147464 | tf_op jit(solution)/shard_map/ppermute | solution.py:821
  2.4 6.4 %collective-permute-start.1 = (f32[3,16,256]{2,1,0:T(8,128)S(1)}, f32[3,16,256]{2,1,0:T(8,128)S(1)}, u32[]{:S(2)}, u32[]{:S(2)}) collective-permute-start(f32[3,16,256]{2,1,0:T(8,128)S(1)} %get-tuple-element.30), channel_id=1, source_target_pairs={{0,1},{2,3},{1,0},{3,2},{4,5},{6,7},{5,4},{7,6},{8,9},{10,11},{9,8... | collective-permute-start | bytes 147464 | tf_op jit(solution)/shard_map/ppermute | solution.py:819
  5.5 3.3 %collective-permute-start.2 = (f32[3,16,256]{2,1,0:T(8,128)S(1)}, f32[3,16,256]{2,1,0:T(8,128)S(1)}, u32[]{:S(2)}, u32[]{:S(2)}) collective-permute-start(f32[3,16,256]{2,1,0:T(8,128)S(1)} %get-tuple-element.31), channel_id=1, source_target_pairs={{1,2},{2,1},{5,6},{6,5},{9,10},{10,9},{13,14},{14,13},{17,18},{18,... | collective-permute-start | bytes 147464 | tf_op jit(solution)/shard_map/ppermute | solution.py:820
  6.2 3.5 %collective-permute-start.3 = (f32[3,16,256]{2,1,0:T(8,128)S(1)}, f32[3,16,256]{2,1,0:T(8,128)S(1)}, u32[]{:S(2)}, u32[]{:S(2)}) collective-permute-start(f32[3,16,256]{2,1,0:T(8,128)S(1)} %get-tuple-element.32), channel_id=1, source_target_pairs={{0,4},{8,12},{16,20},{24,28},{4,0},{12,8},{20,16},{28,24},{1,5},{9... | collective-permute-start | bytes 147464 | tf_op jit(solution)/shard_map/ppermute | solution.py:822
  11.3 12.6 %collective-permute-start.4 = (f32[40,8,128]{2,1,0:T(8,128)S(1)}, f32[40,8,128]{2,1,0:T(8,128)S(1)}, u32[]{:S(2)}, u32[]{:S(2)}) collective-permute-start(f32[40,8,128]{2,1,0:T(8,128)S(1)} %get-tuple-element.35), channel_id=1, source_target_pairs={{0,1},{2,3},{1,0},{3,2},{4,5},{6,7},{5,4},{7,6},{8,9},{10,11},{9,8... | collective-permute-start | bytes 491528 | tf_op jit(solution)/shard_map/ppermute | solution.py:833
  15.5 8.4 %collective-permute-start.5 = (f32[40,8,128]{2,1,0:T(8,128)S(1)}, f32[40,8,128]{2,1,0:T(8,128)S(1)}, u32[]{:S(2)}, u32[]{:S(2)}) collective-permute-start(f32[40,8,128]{2,1,0:T(8,128)S(1)} %get-tuple-element.36), channel_id=1, source_target_pairs={{1,2},{2,1},{5,6},{6,5},{9,10},{10,9},{13,14},{14,13},{17,18},{18,... | collective-permute-start | bytes 491528 | tf_op jit(solution)/shard_map/ppermute | solution.py:834
  17.3 15.3 %all-to-all-start = ((f32[16,24,128]{2,1,0:T(8,128)}), f32[16,24,128]{2,1,0:T(8,128)S(1)}, u32[]{:S(2)}, u32[]{:S(2)}) async-start(f32[16,24,128]{2,1,0:T(8,128)} %payload.1), calls=%async_computation | async-start | bytes 393216 | tf_op jit(solution)/shard_map/all_to_all | solution.py:841
  25.5 10.8 %collective-permute-start.6 = (f32[56,8,128]{2,1,0:T(8,128)S(1)}, f32[56,8,128]{2,1,0:T(8,128)S(1)}, u32[]{:S(2)}, u32[]{:S(2)}) collective-permute-start(f32[56,8,128]{2,1,0:T(8,128)S(1)} %get-tuple-element.38), channel_id=1, source_target_pairs={{4,8},{12,16},{20,24},{8,4},{16,12},{24,20},{5,9},{13,17},{21,25},... | collective-permute-start | bytes 688136 | tf_op jit(solution)/shard_map/ppermute | solution.py:850
  26.2 10.1 %collective-permute-start.7 = (f32[56,8,128]{2,1,0:T(8,128)S(1)}, f32[56,8,128]{2,1,0:T(8,128)S(1)}, u32[]{:S(2)}, u32[]{:S(2)}) collective-permute-start(f32[56,8,128]{2,1,0:T(8,128)S(1)} %get-tuple-element.39), channel_id=1, source_target_pairs={{0,4},{8,12},{16,20},{24,28},{4,0},{12,8},{20,16},{28,24},{1,5},{9... | collective-permute-start | bytes 688136 | tf_op jit(solution)/shard_map/ppermute | solution.py:851
  32.6 1.5 %collective-permute-start.8 = (f32[16,24,128]{2,1,0:T(8,128)S(1)}, f32[16,24,128]{2,1,0:T(8,128)S(1)}, u32[]{:S(2)}, u32[]{:S(2)}) collective-permute-start(f32[16,24,128]{2,1,0:T(8,128)S(1)} %pass.1.mine), channel_id=1, source_target_pairs={{0,4},{8,12},{16,20},{24,28},{4,0},{12,8},{20,16},{28,24},{1,5},{9... | collective-permute-start | bytes 589832 | tf_op jit(solution)/shard_map/ppermute | solution.py:854
  38.1 11.9 %all-to-all-start.1 = ((f32[32,8,128]{2,1,0:T(8,128)}), f32[32,8,128]{2,1,0:T(8,128)S(1)}, u32[]{:S(2)}, u32[]{:S(2)}) async-start(f32[32,8,128]{2,1,0:T(8,128)} %get-tuple-element.41), calls=%async_computation.1 | async-start | bytes 262144 | tf_op jit(solution)/shard_map/all_to_all | solution.py:874

commit v9 on v8

--- a/solution.py
+++ b/solution.py
@@ -275,15 +275,21 @@
     def pack(out, flag):
         at = 0
         for n, planes in ((0, 3), (1, 4)):
-            start = jnp.where(flag, 0, count - planes)
-            for k in range(planes):
-                for tile in range((rows + 8) // 8):
+            for away in range(1, planes + 1):
+                k = jnp.where(flag, away - 1, count - away)
+                ref = long.at[n] if away < planes else (residual, material)[n]
+                for tile in range(ref.shape[1] // 8):
                     for piece in range(pieces):
-                        out[at] = long[n, start + k, tile * 8 : tile * 8 + 8, piece * LANES : (piece + 1) * LANES]
+                        out[at] = ref[k, tile * 8 : tile * 8 + 8, piece * LANES : (piece + 1) * LANES]
                         at += 1
         for n, planes in ((0, 3), (1, 4)):
-            for k in range(planes):
-                low, high = k, c1 - planes + k
+            for away in range(1, planes + 1):
+                low, high = away - 1, c1 - away
+                if away == planes:
+                    low, high = (n * c1 + low) * r1, (n * c1 + high) * r1
+                    out[at] = jnp.where(flag, coarse[low : low + r1], coarse[high : high + r1])
+                    at += 1
+                    continue
                 for tile in range((r1 + 8) // 8):
                     y = slice(tile * 8, tile * 8 + 8)
                     out[at] = jnp.where(flag, long1[n, low, y], long1[n, high, y])
@@ -294,12 +300,23 @@
     leaving.wait()
 
 
-def unpack(source, flag, out, start, planes, tiles, pieces, at):
-    for n in range(planes):
-        for tile in range(tiles):
-            for piece in range(pieces):
-                value = jnp.where(flag, source[0][at], source[1][at])
-                out[start + n, tile * 8 : tile * 8 + 8, piece * LANES : (piece + 1) * LANES] = value
+def strip_length(rows, depth):
+    return (5 * (rows + 8) + 2 * rows) // 8 * (depth // LANES)
+
+
+def unpack(source, flag, out, base, side, planes, at):
+    rows = out.shape[1]
+    for away in range(1, planes + 1):
+        to = base + side * away
+        first = 0
+        if away == planes:
+            first = 4
+            edge = jnp.zeros((4, out.shape[2]), F32)
+            out[to, :4] = edge
+            out[to, rows - 4 :] = edge
+        for row in range(first, rows - first, 8):
+            for z in range(0, out.shape[2], LANES):
+                out[to, row : row + 8, z : z + LANES] = jnp.where(flag, source[0][at], source[1][at])
                 at += 1
     return at
 
@@ -318,11 +335,9 @@
         copy.start()
     low_x = place[0] == 1
     count, rows, depth = potential.shape
-    pieces, tiles = depth // LANES, (rows + 8) // 8
     both = (inner, outer)
-    for flag, start_r, start_m in ((low_x, 1, 0), (jnp.logical_not(low_x), count + 4, count + 4)):
-        at = unpack(both, flag, res, start_r, 3, tiles, pieces, 0)
-        unpack(both, flag, mat, start_m, 4, tiles, pieces, at)
+    for flag, base, side in ((low_x, 4, -1), (jnp.logical_not(low_x), count + 3, 1)):
+        unpack(both, flag, mat, base, side, 4, unpack(both, flag, res, base, side, 3, 0))
     for copy in frames:
         copy.wait()
     total, length = count + 8, rows + 8
@@ -640,9 +655,8 @@
     zero = jnp.zeros((length, depth), F32)
     src[0] = zero
     src[total - 1] = zero
-    for flag, start_s, start_m in ((low_x, 1, 0), (jnp.logical_not(low_x), count + 4, count + 4)):
-        at = unpack(both, flag, src, start_s, 3, length // 8, 1, offset)
-        unpack(both, flag, mat, start_m, 4, length // 8, 1, at)
+    for flag, base, side in ((low_x, 4, -1), (jnp.logical_not(low_x), count + 3, 1)):
+        unpack(both, flag, mat, base, side, 4, unpack(both, flag, src, base, side, 3, offset))
     for n, ref in enumerate((src, mat)):
         ref[pl.ds(4, count)] = long1[n]
     raise_window(window1, flat, prolonged)
@@ -839,8 +853,7 @@
     )
     groups = [[(2 * i + c) * gy + j for i in range(gx // 2) for j in range(gy)] for c in range(2)]
     blocks = lax.all_to_all(payload, ("gx", "gy"), 0, 0, axis_index_groups=groups)
-    tiles, tiles1 = (rows + 8) // 8, (r1 + 8) // 8
-    strip = (7 * tiles * pieces + 7 * tiles1, 8, LANES)
+    strip = (strip_length(rows, depth) + strip_length(r1, d1), 8, LANES)
     long_shape = (2, count, rows + 8, depth)
     inner, outer, long, long1 = call(
         strips_kernel, "strips", (place, residual, material, coarse, even, odd),
@@ -865,7 +878,7 @@
     state = (7 * c1 + 3, r1 + 8, d1)
     tall = VM(c1 + 9, r1 + 8, d1)
     payload, held = call(
-        functools.partial(level1_kernel, 7 * tiles * pieces), "level1", (place, long1, outer, inner, window1), (("far", sheet), ("far", state)),
+        functools.partial(level1_kernel, strip_length(rows, depth)), "level1", (place, long1, outer, inner, window1), (("far", sheet), ("far", state)),
         (
             VM(*frame), VM(*frame), flat, VM(*frame), tall, VM(*frame), VM(*frame), VM(*frame), VM(*frame), VM(*frame),
             VM(*frame), VM(*state), VM(c1 // 2 * r1, d1), VM(c1 // 4 * r1, LANES), VM(*sheet), pltpu.SemaphoreType.DMA((2,)),

time: 53.2 us -> 52.7 us (level)
    all_to_all x1, starting transfers between devices: 4.05 us -> 3.51 us  [local(): lax.all_to_all(payload, ('gx', 'gy'), 0, 0, axis_index_groups=[list(range...]
where the time goes in v9:
time: 52.7 us; the launch traced here: 52.3 us
  starting transfers between devices  26.1 us (50%)
  Pallas kernels  17.1 us (32%)
  waiting for transfers between devices  8.98 us (17%)
    pallas_call x9, Pallas kernels, call(): pl.pallas_call(kernel, out_shape=results, in_specs=specs, out_specs=[pl.B...  17.1 us
    ppermute x2, starting transfers between devices, local(): even = lax.ppermute(even, 'gy', swap_y[0])  7.27 us
    all_to_all x1, starting transfers between devices, local(): lax.all_to_all(payload, ('gx', 'gy'), 0, 0, axis_index_groups=groups)  6.63 us
    ppermute x2, starting transfers between devices, local(): inner = lax.ppermute(inner, 'gx', swap_x[0])  5.97 us
    all_to_all x1, waiting for transfers between devices, local(): lax.all_to_all(payload, ('gx', 'gy'), 0, 0, axis_index_groups=[list(range...  3.6 us
    all_to_all x1, starting transfers between devices, local(): lax.all_to_all(payload, ('gx', 'gy'), 0, 0, axis_index_groups=[list(range...  3.51 us
    all_to_all x1, waiting for transfers between devices, local(): lax.all_to_all(payload, ('gx', 'gy'), 0, 0, axis_index_groups=groups)  3.06 us
    ppermute x1, waiting for transfers between devices, local(): others = lax.ppermute(blocks, 'gx', swap_x[0])  1.43 us
  transfers between devices with their start and end apart: 11, of which 4 were waited for; matrix products, arithmetic and copies ran while one was open for 0% of the time, Pallas kernels for 17%

profile of v9, /device:TPU:0, one launch (start us, length us, event | category | flops | bytes accessed | tf_op | source)
XLA Modules:
  0.0 52.3 jit_solution(17175801771070677977)
XLA Ops:
  0.0 0.1 pad_add_fusion.place
  0.1 1.7 %faces.1 = (f32[16,16,256]{2,1,0:T(8,128)S(1)}, f32[16,16,256]{2,1,0:T(8,128)S(1)}, f32[16,16,256]{2,1,0:T(8,128)S(1)}, f32[3,16,256]{2,1,0:T(8,128)S(1)}, f32[3...) custom-call(s32[4]{0:T(128)S(1)} %pad_add_fusion.place, f32[3]{0:T(128)} %permeability.1, ...), custom_call_target="tpu_custom_call" | custom-call | tf_op jit(solution)/shard_map/faces/pallas_call | solution.py:792
  1.8 0.7 %collective-permute-start = (f32[3,16,256]{2,1,0:T(8,128)S(1)}, f32[3,16,256]{2,1,0:T(8,128)S(1)}, u32[]{:S(2)}, u32[]{:S(2)}) collective-permute-start(f32[3,16,256]{2,1,0:T(8,128)S(1)} %get-tuple-element.29), channel_id=1, source_target_pairs={{4,8},{12,16},{20,24},{8,4},{16,12},{24,20},{5,9},{13,17},{21,25},... | collective-permute-start | bytes 147464 | tf_op jit(solution)/shard_map/ppermute | solution.py:835
  2.4 3.1 %collective-permute-start.1 = (f32[3,16,256]{2,1,0:T(8,128)S(1)}, f32[3,16,256]{2,1,0:T(8,128)S(1)}, u32[]{:S(2)}, u32[]{:S(2)}) collective-permute-start(f32[3,16,256]{2,1,0:T(8,128)S(1)} %get-tuple-element.30), channel_id=1, source_target_pairs={{0,1},{2,3},{1,0},{3,2},{4,5},{6,7},{5,4},{7,6},{8,9},{10,11},{9,8... | collective-permute-start | bytes 147464 | tf_op jit(solution)/shard_map/ppermute | solution.py:833
  5.5 0.7 %collective-permute-start.2 = (f32[3,16,256]{2,1,0:T(8,128)S(1)}, f32[3,16,256]{2,1,0:T(8,128)S(1)}, u32[]{:S(2)}, u32[]{:S(2)}) collective-permute-start(f32[3,16,256]{2,1,0:T(8,128)S(1)} %get-tuple-element.31), channel_id=1, source_target_pairs={{1,2},{2,1},{5,6},{6,5},{9,10},{10,9},{13,14},{14,13},{17,18},{18,... | collective-permute-start | bytes 147464 | tf_op jit(solution)/shard_map/ppermute | solution.py:834
  6.2 2.6 %collective-permute-start.3 = (f32[3,16,256]{2,1,0:T(8,128)S(1)}, f32[3,16,256]{2,1,0:T(8,128)S(1)}, u32[]{:S(2)}, u32[]{:S(2)}) collective-permute-start(f32[3,16,256]{2,1,0:T(8,128)S(1)} %get-tuple-element.32), channel_id=1, source_target_pairs={{0,4},{8,12},{16,20},{24,28},{4,0},{12,8},{20,16},{28,24},{1,5},{9... | collective-permute-start | bytes 147464 | tf_op jit(solution)/shard_map/ppermute | solution.py:836
  8.8 0.0 collective-permute-done.outer
  8.8 0.0 collective-permute-done.1.even
  8.8 0.0 collective-permute-done.2.odd
  8.8 0.9 %collective-permute-done.3.inner = f32[3,16,256]{2,1,0:T(8,128)S(1)} collective-permute-done((f32[3,16,256]{2,1,0:T(8,128)S(1)}, f32[3,16,256]{2,1,0:T(8,128)S(1)}, u32[]{:S(2)}, u32[]{:S(2)}) %collective-permute-start.3) | collective-permute-done | bytes 49184 | tf_op jit(solution)/shard_map/ppermute | solution.py:836
  9.7 1.6 %residual.1 = (f32[16,16,256]{2,1,0:T(8,128)S(1)}, f32[160,128]{1,0:T(8,128)S(1)}, f32[40,8,128]{2,1,0:T(8,128)S(1)}, f32[40,8,128]{2,1,0:T(8,128)S(1)}) custom-call(s32[4]{0:T(128)S(1)} %pad_add_fusion.place, f32[16,16,256]{2,1,0:T(8,128)S(1)} %get-tuple-element.26.source, f32[16,16,256]{2,1,0:T(8,128)S(1)} %get-tuple-element.27.potential, ...), custom_call_target="tpu_custom_call" | custom-call | tf_op jit(solution)/shard_map/residual/pallas_call | solution.py:792
  11.3 4.2 %collective-permute-start.4 = (f32[40,8,128]{2,1,0:T(8,128)S(1)}, f32[40,8,128]{2,1,0:T(8,128)S(1)}, u32[]{:S(2)}, u32[]{:S(2)}) collective-permute-start(f32[40,8,128]{2,1,0:T(8,128)S(1)} %get-tuple-element.35), channel_id=1, source_target_pairs={{0,1},{2,3},{1,0},{3,2},{4,5},{6,7},{5,4},{7,6},{8,9},{10,11},{9,8... | collective-permute-start | bytes 491528 | tf_op jit(solution)/shard_map/ppermute | solution.py:847
  15.5 0.7 %collective-permute-start.5 = (f32[40,8,128]{2,1,0:T(8,128)S(1)}, f32[40,8,128]{2,1,0:T(8,128)S(1)}, u32[]{:S(2)}, u32[]{:S(2)}) collective-permute-start(f32[40,8,128]{2,1,0:T(8,128)S(1)} %get-tuple-element.36), channel_id=1, source_target_pairs={{1,2},{2,1},{5,6},{6,5},{9,10},{10,9},{13,14},{14,13},{17,18},{18,... | collective-permute-start | bytes 491528 | tf_op jit(solution)/shard_map/ppermute | solution.py:848
  16.1 1.1 %payload.1 = f32[16,24,128]{2,1,0:T(8,128)} custom-call(f32[160,128]{1,0:T(8,128)S(1)} %get-tuple-element.34.coarse), custom_call_target="tpu_custom_call" | custom-call | tf_op jit(solution)/shard_map/payload/pallas_call | solution.py:792
  17.3 6.6 %all-to-all-start = ((f32[16,24,128]{2,1,0:T(8,128)}), f32[16,24,128]{2,1,0:T(8,128)S(1)}, u32[]{:S(2)}, u32[]{:S(2)}) async-start(f32[16,24,128]{2,1,0:T(8,128)} %payload.1), calls=%async_computation | async-start | bytes 393216 | tf_op jit(solution)/shard_map/all_to_all | solution.py:855
  23.9 0.0 collective-permute-done.4.even
  23.9 0.0 collective-permute-done.5.odd
  23.9 1.5 %strips.1 = (f32[50,8,128]{2,1,0:T(8,128)S(1)}, f32[50,8,128]{2,1,0:T(8,128)S(1)}, f32[2,16,24,256]{3,2,1,0:T(8,128)}, f32[2,8,16,128]{3,2,1,0:T(8,128)S(1)}) custom-call(s32[4]{0:T(128)S(1)} %pad_add_fusion.place, f32[16,16,256]{2,1,0:T(8,128)S(1)} %get-tuple-element.33.residual, f32[16,16,256]{2,1,0:T(8,128)S(1)} %get-tuple-element.28.material, ...), custom_call_target="tpu_custom_call" | custom-call | flops 99999997952 | tf_op jit(solution)/shard_map/strips/pallas_call | solution.py:792
  25.5 0.7 %collective-permute-start.6 = (f32[50,8,128]{2,1,0:T(8,128)S(1)}, f32[50,8,128]{2,1,0:T(8,128)S(1)}, u32[]{:S(2)}, u32[]{:S(2)}) collective-permute-start(f32[50,8,128]{2,1,0:T(8,128)S(1)} %get-tuple-element.38), channel_id=1, source_target_pairs={{4,8},{12,16},{20,24},{8,4},{16,12},{24,20},{5,9},{13,17},{21,25},... | collective-permute-start | bytes 614408 | tf_op jit(solution)/shard_map/ppermute | solution.py:863
  26.1 3.3 %collective-permute-start.7 = (f32[50,8,128]{2,1,0:T(8,128)S(1)}, f32[50,8,128]{2,1,0:T(8,128)S(1)}, u32[]{:S(2)}, u32[]{:S(2)}) collective-permute-start(f32[50,8,128]{2,1,0:T(8,128)S(1)} %get-tuple-element.39), channel_id=1, source_target_pairs={{0,4},{8,12},{16,20},{24,28},{4,0},{12,8},{20,16},{28,24},{1,5},{9... | collective-permute-start | bytes 614408 | tf_op jit(solution)/shard_map/ppermute | solution.py:864
  29.5 3.1 %all-to-all-done.blocks = f32[16,24,128]{2,1,0:T(8,128)S(1)} async-done(((f32[16,24,128]{2,1,0:T(8,128)}), f32[16,24,128]{2,1,0:T(8,128)S(1)}, u32[]{:S(2)}, u32[]{:S(2)}) %all-to-all-start) | async-done | bytes 196640 | tf_op jit(solution)/shard_map/all_to_all | solution.py:855
  32.6 0.1 collective-permute-start.8
  32.6 1.4 %collective-permute-done.8.theirs = f32[16,24,128]{2,1,0:T(8,128)S(1)} collective-permute-done((f32[16,24,128]{2,1,0:T(8,128)S(1)}, f32[16,24,128]{2,1,0:T(8,128)S(1)}, u32[]{:S(2)}, u32[]{:S(2)}) %collective-permute-start.8) | collective-permute-done | bytes 196640 | tf_op jit(solution)/shard_map/ppermute | solution.py:867
  34.1 2.2 %cycle1.1 = (f32[8,8,128]{2,1,0:T(8,128)S(1)}, f32[4,31,16,128]{3,2,1,0:T(8,128)S(1)}) custom-call(s32[4]{0:T(128)S(1)} %pad_add_fusion.place, f32[16,24,128]{2,1,0:T(8,128)S(1)} %pass.1.mine, f32[16,24,128]{2,1,0:T(8,128)S(1)} %collective-permute-done.8.theirs), custom_call_target="tpu_custom_call" | custom-call | tf_op jit(solution)/shard_map/cycle1/pallas_call | solution.py:792
  36.2 0.0 collective-permute-done.6.outer
  36.2 0.0 collective-permute-done.7.inner
  36.2 1.9 %level1.1 = (f32[32,8,128]{2,1,0:T(8,128)}, f32[59,16,128]{2,1,0:T(8,128)}) custom-call(s32[4]{0:T(128)S(1)} %pad_add_fusion.place, f32[2,8,16,128]{3,2,1,0:T(8,128)S(1)} %get-tuple-element.37._.long1, f32[50,8,128]{2,1,0:T(8,128)S(1)} %collective-permute-done.6.outer, f32[50,8,128]{2,1,0:T(8,128)S(1)} %collective-permute-done.7.inner, ...), custom_call_target="tpu_custom_call" | custom-call | tf_op jit(solution)/shard_map/level1/pallas_call | solution.py:792
  38.1 3.5 %all-to-all-start.1 = ((f32[32,8,128]{2,1,0:T(8,128)}), f32[32,8,128]{2,1,0:T(8,128)S(1)}, u32[]{:S(2)}, u32[]{:S(2)}) async-start(f32[32,8,128]{2,1,0:T(8,128)} %get-tuple-element.41), calls=%async_computation.1 | async-start | bytes 262144 | tf_op jit(solution)/shard_map/all_to_all | solution.py:887
  41.7 4.2 %smooth.1 = (f32[16,16,256]{2,1,0:T(8,128)S(1)}, f32[59,16,128]{2,1,0:T(8,128)S(1)}) custom-call(s32[4]{0:T(128)S(1)} %pad_add_fusion.place, f32[16,16,256]{2,1,0:T(8,128)} %potential_far.1, f32[59,16,128]{2,1,0:T(8,128)} %get-tuple-element.43.state_far, f32[2,16,24,256]{3,2,1,0:T(8,128)} %get-tuple-element.44.long, ...), custom_call_target="tpu_custom_call" | custom-call | tf_op jit(solution)/shard_map/smooth/pallas_call | solution.py:792
  45.9 3.6 %all-to-all-done.1.blocks = f32[32,8,128]{2,1,0:T(8,128)S(1)} async-done(((f32[32,8,128]{2,1,0:T(8,128)}), f32[32,8,128]{2,1,0:T(8,128)S(1)}, u32[]{:S(2)}, u32[]{:S(2)}) %all-to-all-start.1) | async-done | bytes 131104 | tf_op jit(solution)/shard_map/all_to_all | solution.py:887
  49.5 2.8 %cycle2.1 = f32[16,16,256]{2,1,0:T(8,128)} custom-call(s32[4]{0:T(128)S(1)} %pad_add_fusion.place, f32[32,8,128]{2,1,0:T(8,128)S(1)} %all-to-all-done.1.blocks, f32[4,31,16,128]{3,2,1,0:T(8,128)S(1)} %get-tuple-element.42.table, f32[59,16,128]{2,1,0:T(8,128)S(1)} %get-tuple-element.45.state, f32[16,16,256]{2,1,0:T(8,128)S(1)} %get-tuple-element.46.partial), custom_call_target="tpu_custom_call" | custom-call | tf_op jit(solution)/shard_map/cycle2/pallas_call | solution.py:792
  (1 shorter events, 0.0 us)
Async XLA Ops:
  1.8 7.1 %collective-permute-start = (f32[3,16,256]{2,1,0:T(8,128)S(1)}, f32[3,16,256]{2,1,0:T(8,128)S(1)}, u32[]{:S(2)}, u32[]{:S(2)}) collective-permute-start(f32[3,16,256]{2,1,0:T(8,128)S(1)} %get-tuple-element.29), channel_id=1, source_target_pairs={{4,8},{12,16},{20,24},{8,4},{16,12},{24,20},{5,9},{13,17},{21,25},... | collective-permute-start | bytes 147464 | tf_op jit(solution)/shard_map/ppermute | solution.py:835
  2.4 6.4 %collective-permute-start.1 = (f32[3,16,256]{2,1,0:T(8,128)S(1)}, f32[3,16,256]{2,1,0:T(8,128)S(1)}, u32[]{:S(2)}, u32[]{:S(2)}) collective-permute-start(f32[3,16,256]{2,1,0:T(8,128)S(1)} %get-tuple-element.30), channel_id=1, source_target_pairs={{0,1},{2,3},{1,0},{3,2},{4,5},{6,7},{5,4},{7,6},{8,9},{10,11},{9,8... | collective-permute-start | bytes 147464 | tf_op jit(solution)/shard_map/ppermute | solution.py:833
  5.5 3.3 %collective-permute-start.2 = (f32[3,16,256]{2,1,0:T(8,128)S(1)}, f32[3,16,256]{2,1,0:T(8,128)S(1)}, u32[]{:S(2)}, u32[]{:S(2)}) collective-permute-start(f32[3,16,256]{2,1,0:T(8,128)S(1)} %get-tuple-element.31), channel_id=1, source_target_pairs={{1,2},{2,1},{5,6},{6,5},{9,10},{10,9},{13,14},{14,13},{17,18},{18,... | collective-permute-start | bytes 147464 | tf_op jit(solution)/shard_map/ppermute | solution.py:834
  6.2 3.5 %collective-permute-start.3 = (f32[3,16,256]{2,1,0:T(8,128)S(1)}, f32[3,16,256]{2,1,0:T(8,128)S(1)}, u32[]{:S(2)}, u32[]{:S(2)}) collective-permute-start(f32[3,16,256]{2,1,0:T(8,128)S(1)} %get-tuple-element.32), channel_id=1, source_target_pairs={{0,4},{8,12},{16,20},{24,28},{4,0},{12,8},{20,16},{28,24},{1,5},{9... | collective-permute-start | bytes 147464 | tf_op jit(solution)/shard_map/ppermute | solution.py:836
  11.3 12.6 %collective-permute-start.4 = (f32[40,8,128]{2,1,0:T(8,128)S(1)}, f32[40,8,128]{2,1,0:T(8,128)S(1)}, u32[]{:S(2)}, u32[]{:S(2)}) collective-permute-start(f32[40,8,128]{2,1,0:T(8,128)S(1)} %get-tuple-element.35), channel_id=1, source_target_pairs={{0,1},{2,3},{1,0},{3,2},{4,5},{6,7},{5,4},{7,6},{8,9},{10,11},{9,8... | collective-permute-start | bytes 491528 | tf_op jit(solution)/shard_map/ppermute | solution.py:847
  15.5 8.4 %collective-permute-start.5 = (f32[40,8,128]{2,1,0:T(8,128)S(1)}, f32[40,8,128]{2,1,0:T(8,128)S(1)}, u32[]{:S(2)}, u32[]{:S(2)}) collective-permute-start(f32[40,8,128]{2,1,0:T(8,128)S(1)} %get-tuple-element.36), channel_id=1, source_target_pairs={{1,2},{2,1},{5,6},{6,5},{9,10},{10,9},{13,14},{14,13},{17,18},{18,... | collective-permute-start | bytes 491528 | tf_op jit(solution)/shard_map/ppermute | solution.py:848
  17.3 15.3 %all-to-all-start = ((f32[16,24,128]{2,1,0:T(8,128)}), f32[16,24,128]{2,1,0:T(8,128)S(1)}, u32[]{:S(2)}, u32[]{:S(2)}) async-start(f32[16,24,128]{2,1,0:T(8,128)} %payload.1), calls=%async_computation | async-start | bytes 393216 | tf_op jit(solution)/shard_map/all_to_all | solution.py:855
  25.5 10.8 %collective-permute-start.6 = (f32[50,8,128]{2,1,0:T(8,128)S(1)}, f32[50,8,128]{2,1,0:T(8,128)S(1)}, u32[]{:S(2)}, u32[]{:S(2)}) collective-permute-start(f32[50,8,128]{2,1,0:T(8,128)S(1)} %get-tuple-element.38), channel_id=1, source_target_pairs={{4,8},{12,16},{20,24},{8,4},{16,12},{24,20},{5,9},{13,17},{21,25},... | collective-permute-start | bytes 614408 | tf_op jit(solution)/shard_map/ppermute | solution.py:863
  26.1 10.1 %collective-permute-start.7 = (f32[50,8,128]{2,1,0:T(8,128)S(1)}, f32[50,8,128]{2,1,0:T(8,128)S(1)}, u32[]{:S(2)}, u32[]{:S(2)}) collective-permute-start(f32[50,8,128]{2,1,0:T(8,128)S(1)} %get-tuple-element.39), channel_id=1, source_target_pairs={{0,4},{8,12},{16,20},{24,28},{4,0},{12,8},{20,16},{28,24},{1,5},{9... | collective-permute-start | bytes 614408 | tf_op jit(solution)/shard_map/ppermute | solution.py:864
  32.6 1.5 %collective-permute-start.8 = (f32[16,24,128]{2,1,0:T(8,128)S(1)}, f32[16,24,128]{2,1,0:T(8,128)S(1)}, u32[]{:S(2)}, u32[]{:S(2)}) collective-permute-start(f32[16,24,128]{2,1,0:T(8,128)S(1)} %pass.1.mine), channel_id=1, source_target_pairs={{0,4},{8,12},{16,20},{24,28},{4,0},{12,8},{20,16},{28,24},{1,5},{9... | collective-permute-start | bytes 589832 | tf_op jit(solution)/shard_map/ppermute | solution.py:867
  38.1 11.4 %all-to-all-start.1 = ((f32[32,8,128]{2,1,0:T(8,128)}), f32[32,8,128]{2,1,0:T(8,128)S(1)}, u32[]{:S(2)}, u32[]{:S(2)}) async-start(f32[32,8,128]{2,1,0:T(8,128)} %get-tuple-element.41), calls=%async_computation.1 | async-start | bytes 262144 | tf_op jit(solution)/shard_map/all_to_all | solution.py:887

commit v10 on v9

--- a/solution.py
+++ b/solution.py
@@ -231,7 +231,14 @@
     for k in range(c1):
         wide[1, base + k : base + k + 1] = y_low[k, :1]
         wide[1, base + r1 + k : base + r1 + k + 1] = y_high[k, r1 - 1 :]
-    publish(wide[0], wide[1], narrow, sheet, payload, semaphore)
+    block = packed(wide[0], wide[1], narrow)
+    for parity in range(2):
+        for n in range(block.shape[0] // 8):
+            value = block[8 * n + 4 * parity : 8 * n + 4 * parity + 4]
+            sheet[:, parity, :, n] = jnp.broadcast_to(value[None, None], (sheet.shape[0], sheet.shape[2], *value.shape))
+    leaving = pltpu.make_async_copy(sheet, payload, semaphore)
+    leaving.start()
+    leaving.wait()
 
 
 def packed(low, high, narrow):
@@ -571,10 +578,13 @@
     clear_ends(s[:1], counts)
     odd = place[0] == 1
 
-    def fetch(i, parity, j, at):
-        here = i // 2 * gy + j
-        a, b = mine[here, at], theirs[here, at]
-        return jnp.where(odd, b, a) if parity == 0 else jnp.where(odd, a, b)
+    def fetch(i, _, j, at):
+        here = i * gy + j
+        rows = []
+        for n in range(at.start // 8, at.stop // 8):
+            a, b = mine[here, n], theirs[here, n]
+            rows += [jnp.where(odd, b, a), jnp.where(odd, a, b)]
+        return jnp.concatenate(rows, axis=0)
 
     spread_blocks(fetch, ((0, s[0]), (own + 2 * r2, t)), grid, c2, r2)
     face_y = e[0]
@@ -823,7 +833,7 @@
     face = (3, rows, depth)
     DMA = pltpu.SemaphoreType.DMA
     sheet = (devices, c2 // 2 * r2, LANES)
-    sheet2 = (devices // 2, c2 * r2 + 2 * r2, LANES)
+    sheet2 = (gx // 2, 2, gy, (c2 * r2 + 2 * r2) // 8, 4, LANES)
     material, potential_here, source_here, inner, outer, even, odd = call(
         faces_kernel, "faces", (place, permeability, potential, phase, right_side),
         (brick, brick, brick, face, face, (3, count, depth), (3, count, depth)),
@@ -851,8 +861,7 @@
         functools.partial(payload_kernel, c1, r1), "payload", (coarse,), (("far", sheet2),),
         (VM(2, small, d1), VM(small, LANES), VM(*sheet2), DMA),
     )
-    groups = [[(2 * i + c) * gy + j for i in range(gx // 2) for j in range(gy)] for c in range(2)]
-    blocks = lax.all_to_all(payload, ("gx", "gy"), 0, 0, axis_index_groups=groups)
+    blocks = lax.all_to_all(payload.reshape(devices, *sheet2[3:]), ("gx", "gy"), 0, 0)
     strip = (strip_length(rows, depth) + strip_length(r1, d1), 8, LANES)
     long_shape = (2, count, rows + 8, depth)
     inner, outer, long, long1 = call(
@@ -863,7 +872,6 @@
     outer = lax.ppermute(outer, "gx", swap_x[1])
     inner = lax.ppermute(inner, "gx", swap_x[0])
 
-    (blocks,) = call(pass_kernel, "pass", (blocks, long1), (sheet2,))
     others = lax.ppermute(blocks, "gx", swap_x[0])
     counts = tuple(gx * c2 // 2 // k for k in (1, 2, 4))
     bases = (0, counts[0] + 1, counts[0] + counts[1] + 2)

time: 52.7 us -> 52.2 us (level)
  starting transfers between devices: 26.1 us -> 24.8 us
  waiting for transfers between devices: 8.98 us -> 9.84 us
    all_to_all x1, starting transfers between devices: 6.63 us -> 5.61 us  [local(): lax.all_to_all(payload.reshape(devices, *sheet2[3:]), ('gx', 'gy'), 0, 0)]
    all_to_all x1, waiting for transfers between devices: 3.06 us -> 3.92 us  [local(): lax.all_to_all(payload.reshape(devices, *sheet2[3:]), ('gx', 'gy'), 0, 0)]
    pallas_call x9 -> x8, Pallas kernels: 17.1 us -> 17.1 us  [call(): pl.pallas_call(kernel, out_shape=results, in_specs=specs, out_specs=[pl.B...]
where the time goes in v10:
time: 52.2 us; the launch traced here: 51.9 us
  starting transfers between devices  24.8 us (48%)
  Pallas kernels  17.1 us (33%)
  waiting for transfers between devices  9.84 us (19%)
    pallas_call x8, Pallas kernels, call(): pl.pallas_call(kernel, out_shape=results, in_specs=specs, out_specs=[pl.B...  17.1 us
    ppermute x2, starting transfers between devices, local(): even = lax.ppermute(even, 'gy', swap_y[0])  7.27 us
    ppermute x2, starting transfers between devices, local(): inner = lax.ppermute(inner, 'gx', swap_x[0])  5.82 us
    all_to_all x1, starting transfers between devices, local(): lax.all_to_all(payload.reshape(devices, *sheet2[3:]), ('gx', 'gy'), 0, 0)  5.61 us
    all_to_all x1, waiting for transfers between devices, local(): lax.all_to_all(payload.reshape(devices, *sheet2[3:]), ('gx', 'gy'), 0, 0)  3.92 us
    all_to_all x1, waiting for transfers between devices, local(): lax.all_to_all(payload, ('gx', 'gy'), 0, 0, axis_index_groups=[list(range...  3.6 us
    all_to_all x1, starting transfers between devices, local(): lax.all_to_all(payload, ('gx', 'gy'), 0, 0, axis_index_groups=[list(range...  3.41 us
    ppermute x1, waiting for transfers between devices, local(): others = lax.ppermute(blocks, 'gx', swap_x[0])  1.44 us
  transfers between devices with their start and end apart: 11, of which 4 were waited for; matrix products, arithmetic and copies ran while one was open for 0% of the time, Pallas kernels for 17%

profile of v10, /device:TPU:0, one launch (start us, length us, event | category | flops | bytes accessed | tf_op | source)
XLA Modules:
  0.0 51.9 jit_solution(4490416567661123630)
XLA Ops:
  0.0 0.1 pad_add_fusion.place
  0.1 1.7 %faces.1 = (f32[16,16,256]{2,1,0:T(8,128)S(1)}, f32[16,16,256]{2,1,0:T(8,128)S(1)}, f32[16,16,256]{2,1,0:T(8,128)S(1)}, f32[3,16,256]{2,1,0:T(8,128)S(1)}, f32[3...) custom-call(s32[4]{0:T(128)S(1)} %pad_add_fusion.place, f32[3]{0:T(128)} %permeability.1, ...), custom_call_target="tpu_custom_call" | custom-call | tf_op jit(solution)/shard_map/faces/pallas_call | solution.py:802
  1.8 0.7 %collective-permute-start = (f32[3,16,256]{2,1,0:T(8,128)S(1)}, f32[3,16,256]{2,1,0:T(8,128)S(1)}, u32[]{:S(2)}, u32[]{:S(2)}) collective-permute-start(f32[3,16,256]{2,1,0:T(8,128)S(1)} %get-tuple-element.29), channel_id=1, source_target_pairs={{4,8},{12,16},{20,24},{8,4},{16,12},{24,20},{5,9},{13,17},{21,25},... | collective-permute-start | bytes 147464 | tf_op jit(solution)/shard_map/ppermute | solution.py:845
  2.4 3.1 %collective-permute-start.1 = (f32[3,16,256]{2,1,0:T(8,128)S(1)}, f32[3,16,256]{2,1,0:T(8,128)S(1)}, u32[]{:S(2)}, u32[]{:S(2)}) collective-permute-start(f32[3,16,256]{2,1,0:T(8,128)S(1)} %get-tuple-element.30), channel_id=1, source_target_pairs={{0,1},{2,3},{1,0},{3,2},{4,5},{6,7},{5,4},{7,6},{8,9},{10,11},{9,8... | collective-permute-start | bytes 147464 | tf_op jit(solution)/shard_map/ppermute | solution.py:843
  5.5 0.7 %collective-permute-start.2 = (f32[3,16,256]{2,1,0:T(8,128)S(1)}, f32[3,16,256]{2,1,0:T(8,128)S(1)}, u32[]{:S(2)}, u32[]{:S(2)}) collective-permute-start(f32[3,16,256]{2,1,0:T(8,128)S(1)} %get-tuple-element.31), channel_id=1, source_target_pairs={{1,2},{2,1},{5,6},{6,5},{9,10},{10,9},{13,14},{14,13},{17,18},{18,... | collective-permute-start | bytes 147464 | tf_op jit(solution)/shard_map/ppermute | solution.py:844
  6.2 2.6 %collective-permute-start.3 = (f32[3,16,256]{2,1,0:T(8,128)S(1)}, f32[3,16,256]{2,1,0:T(8,128)S(1)}, u32[]{:S(2)}, u32[]{:S(2)}) collective-permute-start(f32[3,16,256]{2,1,0:T(8,128)S(1)} %get-tuple-element.32), channel_id=1, source_target_pairs={{0,4},{8,12},{16,20},{24,28},{4,0},{12,8},{20,16},{28,24},{1,5},{9... | collective-permute-start | bytes 147464 | tf_op jit(solution)/shard_map/ppermute | solution.py:846
  8.8 0.0 collective-permute-done.outer
  8.8 0.0 collective-permute-done.1.even
  8.8 0.0 collective-permute-done.2.odd
  8.8 0.9 %collective-permute-done.3.inner = f32[3,16,256]{2,1,0:T(8,128)S(1)} collective-permute-done((f32[3,16,256]{2,1,0:T(8,128)S(1)}, f32[3,16,256]{2,1,0:T(8,128)S(1)}, u32[]{:S(2)}, u32[]{:S(2)}) %collective-permute-start.3) | collective-permute-done | bytes 49184 | tf_op jit(solution)/shard_map/ppermute | solution.py:846
  9.7 1.6 %residual.1 = (f32[16,16,256]{2,1,0:T(8,128)S(1)}, f32[160,128]{1,0:T(8,128)S(1)}, f32[40,8,128]{2,1,0:T(8,128)S(1)}, f32[40,8,128]{2,1,0:T(8,128)S(1)}) custom-call(s32[4]{0:T(128)S(1)} %pad_add_fusion.place, f32[16,16,256]{2,1,0:T(8,128)S(1)} %get-tuple-element.26.source, f32[16,16,256]{2,1,0:T(8,128)S(1)} %get-tuple-element.27.potential, ...), custom_call_target="tpu_custom_call" | custom-call | tf_op jit(solution)/shard_map/residual/pallas_call | solution.py:802
  11.3 4.2 %collective-permute-start.4 = (f32[40,8,128]{2,1,0:T(8,128)S(1)}, f32[40,8,128]{2,1,0:T(8,128)S(1)}, u32[]{:S(2)}, u32[]{:S(2)}) collective-permute-start(f32[40,8,128]{2,1,0:T(8,128)S(1)} %get-tuple-element.35), channel_id=1, source_target_pairs={{0,1},{2,3},{1,0},{3,2},{4,5},{6,7},{5,4},{7,6},{8,9},{10,11},{9,8... | collective-permute-start | bytes 491528 | tf_op jit(solution)/shard_map/ppermute | solution.py:857
  15.5 0.7 %collective-permute-start.5 = (f32[40,8,128]{2,1,0:T(8,128)S(1)}, f32[40,8,128]{2,1,0:T(8,128)S(1)}, u32[]{:S(2)}, u32[]{:S(2)}) collective-permute-start(f32[40,8,128]{2,1,0:T(8,128)S(1)} %get-tuple-element.36), channel_id=1, source_target_pairs={{1,2},{2,1},{5,6},{6,5},{9,10},{10,9},{13,14},{14,13},{17,18},{18,... | collective-permute-start | bytes 491528 | tf_op jit(solution)/shard_map/ppermute | solution.py:858
  16.1 1.1 %payload.1 = f32[4,2,4,3,4,128]{5,4,3,2,1,0:T(4,128)} custom-call(f32[160,128]{1,0:T(8,128)S(1)} %get-tuple-element.34.coarse), custom_call_target="tpu_custom_call" | custom-call | tf_op jit(solution)/shard_map/payload/pallas_call | solution.py:802
  17.3 5.6 %all-to-all-start = ((f32[32,3,4,128]{3,2,1,0:T(4,128)}), f32[32,3,4,128]{3,2,1,0:T(4,128)S(1)}, u32[]{:S(2)}, u32[]{:S(2)}) async-start(f32[32,3,4,128]{3,2,1,0:T(4,128)} %bitcast.5), calls=%async_computation | async-start | bytes 393216 | tf_op jit(solution)/shard_map/all_to_all | solution.py:864
  22.9 0.0 collective-permute-done.4.even
  22.9 0.0 collective-permute-done.5.odd
  22.9 1.5 %strips.1 = (f32[50,8,128]{2,1,0:T(8,128)S(1)}, f32[50,8,128]{2,1,0:T(8,128)S(1)}, f32[2,16,24,256]{3,2,1,0:T(8,128)}, f32[2,8,16,128]{3,2,1,0:T(8,128)S(1)}) custom-call(s32[4]{0:T(128)S(1)} %pad_add_fusion.place, f32[16,16,256]{2,1,0:T(8,128)S(1)} %get-tuple-element.33.residual, f32[16,16,256]{2,1,0:T(8,128)S(1)} %get-tuple-element.28.material, ...), custom_call_target="tpu_custom_call" | custom-call | flops 99999997952 | tf_op jit(solution)/shard_map/strips/pallas_call | solution.py:802
  24.4 0.7 %collective-permute-start.6 = (f32[50,8,128]{2,1,0:T(8,128)S(1)}, f32[50,8,128]{2,1,0:T(8,128)S(1)}, u32[]{:S(2)}, u32[]{:S(2)}) collective-permute-start(f32[50,8,128]{2,1,0:T(8,128)S(1)} %get-tuple-element.38), channel_id=1, source_target_pairs={{4,8},{12,16},{20,24},{8,4},{16,12},{24,20},{5,9},{13,17},{21,25},... | collective-permute-start | bytes 614408 | tf_op jit(solution)/shard_map/ppermute | solution.py:872
  25.1 3.2 %collective-permute-start.7 = (f32[50,8,128]{2,1,0:T(8,128)S(1)}, f32[50,8,128]{2,1,0:T(8,128)S(1)}, u32[]{:S(2)}, u32[]{:S(2)}) collective-permute-start(f32[50,8,128]{2,1,0:T(8,128)S(1)} %get-tuple-element.39), channel_id=1, source_target_pairs={{0,4},{8,12},{16,20},{24,28},{4,0},{12,8},{20,16},{28,24},{1,5},{9... | collective-permute-start | bytes 614408 | tf_op jit(solution)/shard_map/ppermute | solution.py:873
  28.3 3.9 %all-to-all-done.mine = f32[32,3,4,128]{3,2,1,0:T(4,128)S(1)} async-done(((f32[32,3,4,128]{3,2,1,0:T(4,128)}), f32[32,3,4,128]{3,2,1,0:T(4,128)S(1)}, u32[]{:S(2)}, u32[]{:S(2)}) %all-to-all-start) | async-done | bytes 196640 | tf_op jit(solution)/shard_map/all_to_all | solution.py:864
  32.2 0.0 collective-permute-start.8
  32.2 1.4 %collective-permute-done.8.theirs = f32[32,3,4,128]{3,2,1,0:T(4,128)S(1)} collective-permute-done((f32[32,3,4,128]{3,2,1,0:T(4,128)S(1)}, f32[32,3,4,128]{3,2,1,0:T(4,128)S(1)}, u32[]{:S(2)}, u32[]{:S(2)}) %collective-permute-start.8) | collective-permute-done | bytes 196640 | tf_op jit(solution)/shard_map/ppermute | solution.py:875
  33.7 2.2 %cycle1.1 = (f32[8,8,128]{2,1,0:T(8,128)S(1)}, f32[4,31,16,128]{3,2,1,0:T(8,128)S(1)}) custom-call(s32[4]{0:T(128)S(1)} %pad_add_fusion.place, f32[32,3,4,128]{3,2,1,0:T(4,128)S(1)} %all-to-all-done.mine, f32[32,3,4,128]{3,2,1,0:T(4,128)S(1)} %collective-permute-done.8.theirs), custom_call_target="tpu_custom_call" | custom-call | tf_op jit(solution)/shard_map/cycle1/pallas_call | solution.py:802
  35.8 0.0 collective-permute-done.6.outer
  35.8 0.0 collective-permute-done.7.inner
  35.8 1.9 %level1.1 = (f32[32,8,128]{2,1,0:T(8,128)}, f32[59,16,128]{2,1,0:T(8,128)}) custom-call(s32[4]{0:T(128)S(1)} %pad_add_fusion.place, f32[2,8,16,128]{3,2,1,0:T(8,128)S(1)} %get-tuple-element.37.long1, f32[50,8,128]{2,1,0:T(8,128)S(1)} %collective-permute-done.6.outer, f32[50,8,128]{2,1,0:T(8,128)S(1)} %collective-permute-done.7.inner, ...), custom_call_target="tpu_custom_call" | custom-call | tf_op jit(solution)/shard_map/level1/pallas_call | solution.py:802
  37.8 3.4 %all-to-all-start.1 = ((f32[32,8,128]{2,1,0:T(8,128)}), f32[32,8,128]{2,1,0:T(8,128)S(1)}, u32[]{:S(2)}, u32[]{:S(2)}) async-start(f32[32,8,128]{2,1,0:T(8,128)} %get-tuple-element.41), calls=%async_computation.1 | async-start | bytes 262144 | tf_op jit(solution)/shard_map/all_to_all | solution.py:895
  41.2 4.2 %smooth.1 = (f32[16,16,256]{2,1,0:T(8,128)S(1)}, f32[59,16,128]{2,1,0:T(8,128)S(1)}) custom-call(s32[4]{0:T(128)S(1)} %pad_add_fusion.place, f32[16,16,256]{2,1,0:T(8,128)} %potential_far.1, f32[59,16,128]{2,1,0:T(8,128)} %get-tuple-element.43.state_far, f32[2,16,24,256]{3,2,1,0:T(8,128)} %get-tuple-element.44.long, ...), custom_call_target="tpu_custom_call" | custom-call | tf_op jit(solution)/shard_map/smooth/pallas_call | solution.py:802
  45.4 3.6 %all-to-all-done.1.blocks = f32[32,8,128]{2,1,0:T(8,128)S(1)} async-done(((f32[32,8,128]{2,1,0:T(8,128)}), f32[32,8,128]{2,1,0:T(8,128)S(1)}, u32[]{:S(2)}, u32[]{:S(2)}) %all-to-all-start.1) | async-done | bytes 131104 | tf_op jit(solution)/shard_map/all_to_all | solution.py:895
  49.0 2.8 %cycle2.1 = f32[16,16,256]{2,1,0:T(8,128)} custom-call(s32[4]{0:T(128)S(1)} %pad_add_fusion.place, f32[32,8,128]{2,1,0:T(8,128)S(1)} %all-to-all-done.1.blocks, f32[4,31,16,128]{3,2,1,0:T(8,128)S(1)} %get-tuple-element.42.table, f32[59,16,128]{2,1,0:T(8,128)S(1)} %get-tuple-element.45.state, f32[16,16,256]{2,1,0:T(8,128)S(1)} %get-tuple-element.46.partial), custom_call_target="tpu_custom_call" | custom-call | tf_op jit(solution)/shard_map/cycle2/pallas_call | solution.py:802
Async XLA Ops:
  1.8 7.1 %collective-permute-start = (f32[3,16,256]{2,1,0:T(8,128)S(1)}, f32[3,16,256]{2,1,0:T(8,128)S(1)}, u32[]{:S(2)}, u32[]{:S(2)}) collective-permute-start(f32[3,16,256]{2,1,0:T(8,128)S(1)} %get-tuple-element.29), channel_id=1, source_target_pairs={{4,8},{12,16},{20,24},{8,4},{16,12},{24,20},{5,9},{13,17},{21,25},... | collective-permute-start | bytes 147464 | tf_op jit(solution)/shard_map/ppermute | solution.py:845
  2.4 6.4 %collective-permute-start.1 = (f32[3,16,256]{2,1,0:T(8,128)S(1)}, f32[3,16,256]{2,1,0:T(8,128)S(1)}, u32[]{:S(2)}, u32[]{:S(2)}) collective-permute-start(f32[3,16,256]{2,1,0:T(8,128)S(1)} %get-tuple-element.30), channel_id=1, source_target_pairs={{0,1},{2,3},{1,0},{3,2},{4,5},{6,7},{5,4},{7,6},{8,9},{10,11},{9,8... | collective-permute-start | bytes 147464 | tf_op jit(solution)/shard_map/ppermute | solution.py:843
  5.5 3.3 %collective-permute-start.2 = (f32[3,16,256]{2,1,0:T(8,128)S(1)}, f32[3,16,256]{2,1,0:T(8,128)S(1)}, u32[]{:S(2)}, u32[]{:S(2)}) collective-permute-start(f32[3,16,256]{2,1,0:T(8,128)S(1)} %get-tuple-element.31), channel_id=1, source_target_pairs={{1,2},{2,1},{5,6},{6,5},{9,10},{10,9},{13,14},{14,13},{17,18},{18,... | collective-permute-start | bytes 147464 | tf_op jit(solution)/shard_map/ppermute | solution.py:844
  6.2 3.5 %collective-permute-start.3 = (f32[3,16,256]{2,1,0:T(8,128)S(1)}, f32[3,16,256]{2,1,0:T(8,128)S(1)}, u32[]{:S(2)}, u32[]{:S(2)}) collective-permute-start(f32[3,16,256]{2,1,0:T(8,128)S(1)} %get-tuple-element.32), channel_id=1, source_target_pairs={{0,4},{8,12},{16,20},{24,28},{4,0},{12,8},{20,16},{28,24},{1,5},{9... | collective-permute-start | bytes 147464 | tf_op jit(solution)/shard_map/ppermute | solution.py:846
  11.3 11.6 %collective-permute-start.4 = (f32[40,8,128]{2,1,0:T(8,128)S(1)}, f32[40,8,128]{2,1,0:T(8,128)S(1)}, u32[]{:S(2)}, u32[]{:S(2)}) collective-permute-start(f32[40,8,128]{2,1,0:T(8,128)S(1)} %get-tuple-element.35), channel_id=1, source_target_pairs={{0,1},{2,3},{1,0},{3,2},{4,5},{6,7},{5,4},{7,6},{8,9},{10,11},{9,8... | collective-permute-start | bytes 491528 | tf_op jit(solution)/shard_map/ppermute | solution.py:857
  15.5 7.4 %collective-permute-start.5 = (f32[40,8,128]{2,1,0:T(8,128)S(1)}, f32[40,8,128]{2,1,0:T(8,128)S(1)}, u32[]{:S(2)}, u32[]{:S(2)}) collective-permute-start(f32[40,8,128]{2,1,0:T(8,128)S(1)} %get-tuple-element.36), channel_id=1, source_target_pairs={{1,2},{2,1},{5,6},{6,5},{9,10},{10,9},{13,14},{14,13},{17,18},{18,... | collective-permute-start | bytes 491528 | tf_op jit(solution)/shard_map/ppermute | solution.py:858
  17.3 15.0 %all-to-all-start = ((f32[32,3,4,128]{3,2,1,0:T(4,128)}), f32[32,3,4,128]{3,2,1,0:T(4,128)S(1)}, u32[]{:S(2)}, u32[]{:S(2)}) async-start(f32[32,3,4,128]{3,2,1,0:T(4,128)} %bitcast.5), calls=%async_computation | async-start | bytes 393216 | tf_op jit(solution)/shard_map/all_to_all | solution.py:864
  24.4 11.4 %collective-permute-start.6 = (f32[50,8,128]{2,1,0:T(8,128)S(1)}, f32[50,8,128]{2,1,0:T(8,128)S(1)}, u32[]{:S(2)}, u32[]{:S(2)}) collective-permute-start(f32[50,8,128]{2,1,0:T(8,128)S(1)} %get-tuple-element.38), channel_id=1, source_target_pairs={{4,8},{12,16},{20,24},{8,4},{16,12},{24,20},{5,9},{13,17},{21,25},... | collective-permute-start | bytes 614408 | tf_op jit(solution)/shard_map/ppermute | solution.py:872
  25.1 10.7 %collective-permute-start.7 = (f32[50,8,128]{2,1,0:T(8,128)S(1)}, f32[50,8,128]{2,1,0:T(8,128)S(1)}, u32[]{:S(2)}, u32[]{:S(2)}) collective-permute-start(f32[50,8,128]{2,1,0:T(8,128)S(1)} %get-tuple-element.39), channel_id=1, source_target_pairs={{0,4},{8,12},{16,20},{24,28},{4,0},{12,8},{20,16},{28,24},{1,5},{9... | collective-permute-start | bytes 614408 | tf_op jit(solution)/shard_map/ppermute | solution.py:873
  32.2 1.4 %collective-permute-start.8 = (f32[32,3,4,128]{3,2,1,0:T(4,128)S(1)}, f32[32,3,4,128]{3,2,1,0:T(4,128)S(1)}, u32[]{:S(2)}, u32[]{:S(2)}) collective-permute-start(f32[32,3,4,128]{3,2,1,0:T(4,128)S(1)} %all-to-all-done.mine), channel_id=1, source_target_pairs={{0,4},{8,12},{16,20},{24,28},{4,0},{12,8},{20,16},{28,24},{1,5},{9... | collective-permute-start | bytes 589832 | tf_op jit(solution)/shard_map/ppermute | solution.py:875
  37.8 11.3 %all-to-all-start.1 = ((f32[32,8,128]{2,1,0:T(8,128)}), f32[32,8,128]{2,1,0:T(8,128)S(1)}, u32[]{:S(2)}, u32[]{:S(2)}) async-start(f32[32,8,128]{2,1,0:T(8,128)} %get-tuple-element.41), calls=%async_computation.1 | async-start | bytes 262144 | tf_op jit(solution)/shard_map/all_to_all | solution.py:895

commit v11 on v10

--- a/solution.py
+++ b/solution.py
@@ -254,7 +254,7 @@
     leaving.wait()
 
 
-def strips_kernel(place, residual, material, coarse, even, odd, inner, outer, long_far, long1, long, semaphore):
+def strips_kernel(place, residual, material, coarse, even, odd, inner, outer, long, long1):
     low_x, low_y = place[0] == 1, place[1] == 1
     count, rows, depth = residual.shape
     pieces = depth // LANES
@@ -271,8 +271,6 @@
             z = slice(piece * LANES, (piece + 1) * LANES)
             long[0, i, :, z] = jnp.concatenate([low[:4], residual[i, :, z], high[:4]], axis=0)
             long[1, i, :, z] = jnp.concatenate([low[4:], material[i, :, z], high[4:]], axis=0)
-    leaving = pltpu.make_async_copy(long, long_far, semaphore)
-    leaving.start()
     for k in range(c1):
         low, high = sides(base + k)
         s, m = coarse[k * r1 : (k + 1) * r1], coarse[(c1 + k) * r1 : (c1 + k + 1) * r1]
@@ -304,7 +302,6 @@
 
     pack(inner, low_x)
     pack(outer, jnp.logical_not(low_x))
-    leaving.wait()
 
 
 def strip_length(rows, depth):
@@ -328,25 +325,17 @@
     return at
 
 
-def smooth_kernel(ends, place, potential_far, state_far, long, outer, inner, out, state, mat, res, x, d, fx, fy, fz, inv, potential, semaphores):
+def smooth_kernel(ends, place, potential_far, long, outer, inner, out, mat, res, x, d, fx, fy, fz, inv, potential, semaphores):
     arriving = pltpu.make_async_copy(potential_far, potential, semaphores.at[0])
     arriving.start()
-    passing = pltpu.make_async_copy(state_far, state, semaphores.at[1])
-    passing.start()
     count, rows, depth = potential.shape
-    own = pl.ds(4, count)
-    frames = [
-        pltpu.make_async_copy(long.at[n], ref.at[own], semaphores.at[2 + n]) for n, ref in enumerate((res, mat))
-    ]
-    for copy in frames:
-        copy.start()
+    res[pl.ds(4, count)] = long[0]
+    mat[pl.ds(4, count)] = long[1]
     low_x = place[0] == 1
     count, rows, depth = potential.shape
     both = (inner, outer)
     for flag, base, side in ((low_x, 4, -1), (jnp.logical_not(low_x), count + 3, 1)):
         unpack(both, flag, mat, base, side, 4, unpack(both, flag, res, base, side, 3, 0))
-    for copy in frames:
-        copy.wait()
     total, length = count + 8, rows + 8
     row, lane = iota((length, depth), 0), iota((length, depth), 1)
     outside = as_float(lane == 0) + as_float(lane == depth - 1)
@@ -392,7 +381,6 @@
                 d[here] = change
                 x[new, here] = v + change
         rho = following
-    passing.wait()
 
 
 HALF = LANES // 2
@@ -655,8 +643,8 @@
 
 
 def level1_kernel(
-    offset, place, long1, outer, inner, window1, payload, state_far,
-    src, mat, flat, prolonged, fx, fy, fz, diag, inv, err, c, state, wide, narrow, sheet, semaphores,
+    offset, place, long1, outer, inner, window1, payload, state,
+    src, mat, flat, prolonged, fx, fy, fz, diag, inv, err, c, wide, narrow, sheet, semaphore,
 ):
     low_x = place[0] == 1
     total, length, depth = src.shape
@@ -711,14 +699,11 @@
     base += count + 1
     for n, ref in enumerate((fy, fz, inv, c, src)):
         state[base + n * count : base + (n + 1) * count] = ref[4 : 4 + count]
-    leaving = pltpu.make_async_copy(state, state_far, semaphores.at[0])
-    leaving.start()
     here, _, more = off(err, 4, count)
     t = (KEPT * src[here] + more)[:, 4 : 4 + rows].reshape(count // 2, 2, rows, depth)
     wide[...] = (t[:, 0] + t[:, 1]).reshape(count // 2 * rows, depth)
     half = wide.shape[0] // 2
-    publish(wide[:half], wide[half:], narrow, sheet, payload, semaphores.at[1])
-    leaving.wait()
+    publish(wide[:half], wide[half:], narrow, sheet, payload, semaphore)
 
 
 def last_cycle_kernel(counts, bases, grid, c2, r2, place, blocks, table, state, partial, out, *scratch):
@@ -866,8 +851,7 @@
     long_shape = (2, count, rows + 8, depth)
     inner, outer, long, long1 = call(
         strips_kernel, "strips", (place, residual, material, coarse, even, odd),
-        (strip, strip, ("far", long_shape), (2, c1, r1 + 8, d1)),
-        (VM(*long_shape), DMA), cost=10**11,
+        (strip, strip, long_shape, (2, c1, r1 + 8, d1)), cost=10**11,
     )
     outer = lax.ppermute(outer, "gx", swap_x[1])
     inner = lax.ppermute(inner, "gx", swap_x[0])
@@ -886,21 +870,21 @@
     state = (7 * c1 + 3, r1 + 8, d1)
     tall = VM(c1 + 9, r1 + 8, d1)
     payload, held = call(
-        functools.partial(level1_kernel, strip_length(rows, depth)), "level1", (place, long1, outer, inner, window1), (("far", sheet), ("far", state)),
+        functools.partial(level1_kernel, strip_length(rows, depth)), "level1", (place, long1, outer, inner, window1), (("far", sheet), state),
         (
             VM(*frame), VM(*frame), flat, VM(*frame), tall, VM(*frame), VM(*frame), VM(*frame), VM(*frame), VM(*frame),
-            VM(*frame), VM(*state), VM(c1 // 2 * r1, d1), VM(c1 // 4 * r1, LANES), VM(*sheet), pltpu.SemaphoreType.DMA((2,)),
+            VM(*frame), VM(c1 // 2 * r1, d1), VM(c1 // 4 * r1, LANES), VM(*sheet), DMA,
         ),
     )
     blocks = lax.all_to_all(payload, ("gx", "gy"), 0, 0, axis_index_groups=[list(range(devices))[::-1]])
     wide = (count + 8, rows + 8, depth)
-    partial, held = call(
-        functools.partial(smooth_kernel, (gx, gy)), "smooth", (place, potential, held, long, outer, inner), (brick, state),
+    (partial,) = call(
+        functools.partial(smooth_kernel, (gx, gy)), "smooth", (place, potential, long, outer, inner), (brick,),
         (
             VM(*wide), VM(*wide), VM(2, *wide), VM(*wide), VM(count + 9, rows + 8, depth), VM(*wide), VM(*wide), VM(*wide),
-            VM(*brick), pltpu.SemaphoreType.DMA((4,)),
+            VM(*brick), pltpu.SemaphoreType.DMA((1,)),
         ),
-        apart=(1, 2, 3),
+        apart=(1,),
     )
     (out,) = call(
         functools.partial(last_cycle_kernel, counts, bases, (gx, gy), c2, r2), "cycle2",

time: 52.2 us -> 51.4 us (0.985)
  Pallas kernels: 17.1 us -> 14.9 us
  waiting for transfers between devices: 9.84 us -> 12 us
  starting transfers between devices: 24.8 us -> 24 us
    pallas_call x8, Pallas kernels: 17.1 us -> 14.9 us  [call(): pl.pallas_call(kernel, out_shape=results, in_specs=specs, out_specs=[pl.B...]
    all_to_all x1, waiting for transfers between devices: 3.6 us -> 4.88 us  [local(): lax.all_to_all(payload, ('gx', 'gy'), 0, 0, axis_index_groups=[list(range...]
    all_to_all x1, waiting for transfers between devices: 3.92 us -> 4.79 us  [local(): lax.all_to_all(payload.reshape(devices, *sheet2[3:]), ('gx', 'gy'), 0, 0)]
    all_to_all x1, starting transfers between devices: 3.41 us -> 2.67 us  [local(): lax.all_to_all(payload, ('gx', 'gy'), 0, 0, axis_index_groups=[list(range...]
  transfers between devices with their start and end apart: 11 -> 11, of which waited for: 4 -> 4; matrix products, arithmetic and copies ran while one was open for 0% -> 0% of each run, Pallas kernels for 17% -> 13%
where the time goes in v11:
time: 51.4 us; the launch traced here: 51.1 us
  starting transfers between devices  24 us (47%)
  Pallas kernels  14.9 us (29%)
  waiting for transfers between devices  12 us (23%)
    pallas_call x8, Pallas kernels, call(): pl.pallas_call(kernel, out_shape=results, in_specs=specs, out_specs=[pl.B...  14.9 us
    ppermute x2, starting transfers between devices, local(): even = lax.ppermute(even, 'gy', swap_y[0])  7.27 us
    ppermute x2, starting transfers between devices, local(): inner = lax.ppermute(inner, 'gx', swap_x[0])  5.82 us
    all_to_all x1, starting transfers between devices, local(): lax.all_to_all(payload.reshape(devices, *sheet2[3:]), ('gx', 'gy'), 0, 0)  5.61 us
    all_to_all x1, waiting for transfers between devices, local(): lax.all_to_all(payload, ('gx', 'gy'), 0, 0, axis_index_groups=[list(range...  4.88 us
    all_to_all x1, waiting for transfers between devices, local(): lax.all_to_all(payload.reshape(devices, *sheet2[3:]), ('gx', 'gy'), 0, 0)  4.79 us
    all_to_all x1, starting transfers between devices, local(): lax.all_to_all(payload, ('gx', 'gy'), 0, 0, axis_index_groups=[list(range...  2.67 us
    ppermute x1, waiting for transfers between devices, local(): others = lax.ppermute(blocks, 'gx', swap_x[0])  1.44 us
  transfers between devices with their start and end apart: 11, of which 4 were waited for; matrix products, arithmetic and copies ran while one was open for 0% of the time, Pallas kernels for 13%

profile of v11, /device:TPU:0, one launch (start us, length us, event | category | flops | bytes accessed | tf_op | source)
XLA Modules:
  0.0 51.1 jit_solution(16832820896991874324)
XLA Ops:
  0.0 0.1 pad_add_fusion.place
  0.1 1.7 %faces.1 = (f32[16,16,256]{2,1,0:T(8,128)S(1)}, f32[16,16,256]{2,1,0:T(8,128)S(1)}, f32[16,16,256]{2,1,0:T(8,128)S(1)}, f32[3,16,256]{2,1,0:T(8,128)S(1)}, f32[3...) custom-call(s32[4]{0:T(128)S(1)} %pad_add_fusion.place, f32[3]{0:T(128)} %permeability.1, ...), custom_call_target="tpu_custom_call" | custom-call | tf_op jit(solution)/shard_map/faces/pallas_call | solution.py:787
  1.8 0.7 %collective-permute-start = (f32[3,16,256]{2,1,0:T(8,128)S(1)}, f32[3,16,256]{2,1,0:T(8,128)S(1)}, u32[]{:S(2)}, u32[]{:S(2)}) collective-permute-start(f32[3,16,256]{2,1,0:T(8,128)S(1)} %get-tuple-element.27), channel_id=1, source_target_pairs={{4,8},{12,16},{20,24},{8,4},{16,12},{24,20},{5,9},{13,17},{21,25},... | collective-permute-start | bytes 147464 | tf_op jit(solution)/shard_map/ppermute | solution.py:830
  2.4 3.1 %collective-permute-start.1 = (f32[3,16,256]{2,1,0:T(8,128)S(1)}, f32[3,16,256]{2,1,0:T(8,128)S(1)}, u32[]{:S(2)}, u32[]{:S(2)}) collective-permute-start(f32[3,16,256]{2,1,0:T(8,128)S(1)} %get-tuple-element.28), channel_id=1, source_target_pairs={{0,1},{2,3},{1,0},{3,2},{4,5},{6,7},{5,4},{7,6},{8,9},{10,11},{9,8... | collective-permute-start | bytes 147464 | tf_op jit(solution)/shard_map/ppermute | solution.py:828
  5.5 0.7 %collective-permute-start.2 = (f32[3,16,256]{2,1,0:T(8,128)S(1)}, f32[3,16,256]{2,1,0:T(8,128)S(1)}, u32[]{:S(2)}, u32[]{:S(2)}) collective-permute-start(f32[3,16,256]{2,1,0:T(8,128)S(1)} %get-tuple-element.29), channel_id=1, source_target_pairs={{1,2},{2,1},{5,6},{6,5},{9,10},{10,9},{13,14},{14,13},{17,18},{18,... | collective-permute-start | bytes 147464 | tf_op jit(solution)/shard_map/ppermute | solution.py:829
  6.2 2.6 %collective-permute-start.3 = (f32[3,16,256]{2,1,0:T(8,128)S(1)}, f32[3,16,256]{2,1,0:T(8,128)S(1)}, u32[]{:S(2)}, u32[]{:S(2)}) collective-permute-start(f32[3,16,256]{2,1,0:T(8,128)S(1)} %get-tuple-element.30), channel_id=1, source_target_pairs={{0,4},{8,12},{16,20},{24,28},{4,0},{12,8},{20,16},{28,24},{1,5},{9... | collective-permute-start | bytes 147464 | tf_op jit(solution)/shard_map/ppermute | solution.py:831
  8.8 0.0 collective-permute-done.outer
  8.8 0.0 collective-permute-done.1.even
  8.8 0.0 collective-permute-done.2.odd
  8.8 0.9 %collective-permute-done.3.inner = f32[3,16,256]{2,1,0:T(8,128)S(1)} collective-permute-done((f32[3,16,256]{2,1,0:T(8,128)S(1)}, f32[3,16,256]{2,1,0:T(8,128)S(1)}, u32[]{:S(2)}, u32[]{:S(2)}) %collective-permute-start.3) | collective-permute-done | bytes 49184 | tf_op jit(solution)/shard_map/ppermute | solution.py:831
  9.7 1.6 %residual.1 = (f32[16,16,256]{2,1,0:T(8,128)S(1)}, f32[160,128]{1,0:T(8,128)S(1)}, f32[40,8,128]{2,1,0:T(8,128)S(1)}, f32[40,8,128]{2,1,0:T(8,128)S(1)}) custom-call(s32[4]{0:T(128)S(1)} %pad_add_fusion.place, f32[16,16,256]{2,1,0:T(8,128)S(1)} %get-tuple-element.24.source, f32[16,16,256]{2,1,0:T(8,128)S(1)} %get-tuple-element.25.potential, ...), custom_call_target="tpu_custom_call" | custom-call | tf_op jit(solution)/shard_map/residual/pallas_call | solution.py:787
  11.3 4.2 %collective-permute-start.4 = (f32[40,8,128]{2,1,0:T(8,128)S(1)}, f32[40,8,128]{2,1,0:T(8,128)S(1)}, u32[]{:S(2)}, u32[]{:S(2)}) collective-permute-start(f32[40,8,128]{2,1,0:T(8,128)S(1)} %get-tuple-element.33), channel_id=1, source_target_pairs={{0,1},{2,3},{1,0},{3,2},{4,5},{6,7},{5,4},{7,6},{8,9},{10,11},{9,8... | collective-permute-start | bytes 491528 | tf_op jit(solution)/shard_map/ppermute | solution.py:842
  15.5 0.7 %collective-permute-start.5 = (f32[40,8,128]{2,1,0:T(8,128)S(1)}, f32[40,8,128]{2,1,0:T(8,128)S(1)}, u32[]{:S(2)}, u32[]{:S(2)}) collective-permute-start(f32[40,8,128]{2,1,0:T(8,128)S(1)} %get-tuple-element.34), channel_id=1, source_target_pairs={{1,2},{2,1},{5,6},{6,5},{9,10},{10,9},{13,14},{14,13},{17,18},{18,... | collective-permute-start | bytes 491528 | tf_op jit(solution)/shard_map/ppermute | solution.py:843
  16.1 1.1 %payload.1 = f32[4,2,4,3,4,128]{5,4,3,2,1,0:T(4,128)} custom-call(f32[160,128]{1,0:T(8,128)S(1)} %get-tuple-element.32.coarse), custom_call_target="tpu_custom_call" | custom-call | tf_op jit(solution)/shard_map/payload/pallas_call | solution.py:787
  17.3 5.6 %all-to-all-start = ((f32[32,3,4,128]{3,2,1,0:T(4,128)}), f32[32,3,4,128]{3,2,1,0:T(4,128)S(1)}, u32[]{:S(2)}, u32[]{:S(2)}) async-start(f32[32,3,4,128]{3,2,1,0:T(4,128)} %bitcast.5), calls=%async_computation | async-start | bytes 393216 | tf_op jit(solution)/shard_map/all_to_all | solution.py:849
  22.9 0.0 collective-permute-done.4.even
  22.9 0.0 collective-permute-done.5.odd
  22.9 0.7 %strips.1 = (f32[50,8,128]{2,1,0:T(8,128)S(1)}, f32[50,8,128]{2,1,0:T(8,128)S(1)}, f32[2,16,24,256]{3,2,1,0:T(8,128)S(1)}, f32[2,8,16,128]{3,2,1,0:T(8,128)S(1)}) custom-call(s32[4]{0:T(128)S(1)} %pad_add_fusion.place, f32[16,16,256]{2,1,0:T(8,128)S(1)} %get-tuple-element.31.residual, f32[16,16,256]{2,1,0:T(8,128)S(1)} %get-tuple-element.26.material, ...), custom_call_target="tpu_custom_call" | custom-call | flops 99999997952 | tf_op jit(solution)/shard_map/strips/pallas_call | solution.py:787
  23.5 0.7 %collective-permute-start.6 = (f32[50,8,128]{2,1,0:T(8,128)S(1)}, f32[50,8,128]{2,1,0:T(8,128)S(1)}, u32[]{:S(2)}, u32[]{:S(2)}) collective-permute-start(f32[50,8,128]{2,1,0:T(8,128)S(1)} %get-tuple-element.36), channel_id=1, source_target_pairs={{4,8},{12,16},{20,24},{8,4},{16,12},{24,20},{5,9},{13,17},{21,25},... | collective-permute-start | bytes 614408 | tf_op jit(solution)/shard_map/ppermute | solution.py:856
  24.2 3.2 %collective-permute-start.7 = (f32[50,8,128]{2,1,0:T(8,128)S(1)}, f32[50,8,128]{2,1,0:T(8,128)S(1)}, u32[]{:S(2)}, u32[]{:S(2)}) collective-permute-start(f32[50,8,128]{2,1,0:T(8,128)S(1)} %get-tuple-element.37), channel_id=1, source_target_pairs={{0,4},{8,12},{16,20},{24,28},{4,0},{12,8},{20,16},{28,24},{1,5},{9... | collective-permute-start | bytes 614408 | tf_op jit(solution)/shard_map/ppermute | solution.py:857
  27.4 4.8 %all-to-all-done.mine = f32[32,3,4,128]{3,2,1,0:T(4,128)S(1)} async-done(((f32[32,3,4,128]{3,2,1,0:T(4,128)}), f32[32,3,4,128]{3,2,1,0:T(4,128)S(1)}, u32[]{:S(2)}, u32[]{:S(2)}) %all-to-all-start) | async-done | bytes 196640 | tf_op jit(solution)/shard_map/all_to_all | solution.py:849
  32.2 0.0 collective-permute-start.8
  32.2 1.4 %collective-permute-done.8.theirs = f32[32,3,4,128]{3,2,1,0:T(4,128)S(1)} collective-permute-done((f32[32,3,4,128]{3,2,1,0:T(4,128)S(1)}, f32[32,3,4,128]{3,2,1,0:T(4,128)S(1)}, u32[]{:S(2)}, u32[]{:S(2)}) %collective-permute-start.8) | collective-permute-done | bytes 196640 | tf_op jit(solution)/shard_map/ppermute | solution.py:859
  33.7 2.2 %cycle1.1 = (f32[8,8,128]{2,1,0:T(8,128)S(1)}, f32[4,31,16,128]{3,2,1,0:T(8,128)S(1)}) custom-call(s32[4]{0:T(128)S(1)} %pad_add_fusion.place, f32[32,3,4,128]{3,2,1,0:T(4,128)S(1)} %all-to-all-done.mine, f32[32,3,4,128]{3,2,1,0:T(4,128)S(1)} %collective-permute-done.8.theirs), custom_call_target="tpu_custom_call" | custom-call | tf_op jit(solution)/shard_map/cycle1/pallas_call | solution.py:787
  35.8 0.0 collective-permute-done.6.outer
  35.8 0.0 collective-permute-done.7.inner
  35.8 1.9 %level1.1 = (f32[32,8,128]{2,1,0:T(8,128)}, f32[59,16,128]{2,1,0:T(8,128)S(1)}) custom-call(s32[4]{0:T(128)S(1)} %pad_add_fusion.place, f32[2,8,16,128]{3,2,1,0:T(8,128)S(1)} %get-tuple-element.35.long1, f32[50,8,128]{2,1,0:T(8,128)S(1)} %collective-permute-done.6.outer, f32[50,8,128]{2,1,0:T(8,128)S(1)} %collective-permute-done.7.inner, ...), custom_call_target="tpu_custom_call" | custom-call | tf_op jit(solution)/shard_map/level1/pallas_call | solution.py:787
  37.7 2.7 %all-to-all-start.1 = ((f32[32,8,128]{2,1,0:T(8,128)}), f32[32,8,128]{2,1,0:T(8,128)S(1)}, u32[]{:S(2)}, u32[]{:S(2)}) async-start(f32[32,8,128]{2,1,0:T(8,128)} %get-tuple-element.39), calls=%async_computation.1 | async-start | bytes 262144 | tf_op jit(solution)/shard_map/all_to_all | solution.py:879
  40.4 3.0 %smooth.1.partial = f32[16,16,256]{2,1,0:T(8,128)S(1)} custom-call(s32[4]{0:T(128)S(1)} %pad_add_fusion.place, f32[16,16,256]{2,1,0:T(8,128)} %potential_far.1, f32[2,16,24,256]{3,2,1,0:T(8,128)S(1)} %get-tuple-element.42.long, f32[50,8,128]{2,1,0:T(8,128)S(1)} %collective-permute-done.6.outer, f32[50,8,128]{2,1,0:T(8,128)S(1)} %collective-permute-done.7.inner), custom_call_target="tpu_custom_call" | custom-call | tf_op jit(solution)/shard_map/smooth/pallas_call | solution.py:787
  43.4 4.9 %all-to-all-done.1.blocks = f32[32,8,128]{2,1,0:T(8,128)S(1)} async-done(((f32[32,8,128]{2,1,0:T(8,128)}), f32[32,8,128]{2,1,0:T(8,128)S(1)}, u32[]{:S(2)}, u32[]{:S(2)}) %all-to-all-start.1) | async-done | bytes 131104 | tf_op jit(solution)/shard_map/all_to_all | solution.py:879
  48.3 2.8 %cycle2.1 = f32[16,16,256]{2,1,0:T(8,128)} custom-call(s32[4]{0:T(128)S(1)} %pad_add_fusion.place, f32[32,8,128]{2,1,0:T(8,128)S(1)} %all-to-all-done.1.blocks, f32[4,31,16,128]{3,2,1,0:T(8,128)S(1)} %get-tuple-element.40.table, f32[59,16,128]{2,1,0:T(8,128)S(1)} %get-tuple-element.41.state, f32[16,16,256]{2,1,0:T(8,128)S(1)} %smooth.1.partial), custom_call_target="tpu_custom_call" | custom-call | tf_op jit(solution)/shard_map/cycle2/pallas_call | solution.py:787
Async XLA Ops:
  1.8 7.1 %collective-permute-start = (f32[3,16,256]{2,1,0:T(8,128)S(1)}, f32[3,16,256]{2,1,0:T(8,128)S(1)}, u32[]{:S(2)}, u32[]{:S(2)}) collective-permute-start(f32[3,16,256]{2,1,0:T(8,128)S(1)} %get-tuple-element.27), channel_id=1, source_target_pairs={{4,8},{12,16},{20,24},{8,4},{16,12},{24,20},{5,9},{13,17},{21,25},... | collective-permute-start | bytes 147464 | tf_op jit(solution)/shard_map/ppermute | solution.py:830
  2.4 6.4 %collective-permute-start.1 = (f32[3,16,256]{2,1,0:T(8,128)S(1)}, f32[3,16,256]{2,1,0:T(8,128)S(1)}, u32[]{:S(2)}, u32[]{:S(2)}) collective-permute-start(f32[3,16,256]{2,1,0:T(8,128)S(1)} %get-tuple-element.28), channel_id=1, source_target_pairs={{0,1},{2,3},{1,0},{3,2},{4,5},{6,7},{5,4},{7,6},{8,9},{10,11},{9,8... | collective-permute-start | bytes 147464 | tf_op jit(solution)/shard_map/ppermute | solution.py:828
  5.5 3.3 %collective-permute-start.2 = (f32[3,16,256]{2,1,0:T(8,128)S(1)}, f32[3,16,256]{2,1,0:T(8,128)S(1)}, u32[]{:S(2)}, u32[]{:S(2)}) collective-permute-start(f32[3,16,256]{2,1,0:T(8,128)S(1)} %get-tuple-element.29), channel_id=1, source_target_pairs={{1,2},{2,1},{5,6},{6,5},{9,10},{10,9},{13,14},{14,13},{17,18},{18,... | collective-permute-start | bytes 147464 | tf_op jit(solution)/shard_map/ppermute | solution.py:829
  6.2 3.5 %collective-permute-start.3 = (f32[3,16,256]{2,1,0:T(8,128)S(1)}, f32[3,16,256]{2,1,0:T(8,128)S(1)}, u32[]{:S(2)}, u32[]{:S(2)}) collective-permute-start(f32[3,16,256]{2,1,0:T(8,128)S(1)} %get-tuple-element.30), channel_id=1, source_target_pairs={{0,4},{8,12},{16,20},{24,28},{4,0},{12,8},{20,16},{28,24},{1,5},{9... | collective-permute-start | bytes 147464 | tf_op jit(solution)/shard_map/ppermute | solution.py:831
  11.3 11.6 %collective-permute-start.4 = (f32[40,8,128]{2,1,0:T(8,128)S(1)}, f32[40,8,128]{2,1,0:T(8,128)S(1)}, u32[]{:S(2)}, u32[]{:S(2)}) collective-permute-start(f32[40,8,128]{2,1,0:T(8,128)S(1)} %get-tuple-element.33), channel_id=1, source_target_pairs={{0,1},{2,3},{1,0},{3,2},{4,5},{6,7},{5,4},{7,6},{8,9},{10,11},{9,8... | collective-permute-start | bytes 491528 | tf_op jit(solution)/shard_map/ppermute | solution.py:842
  15.5 7.4 %collective-permute-start.5 = (f32[40,8,128]{2,1,0:T(8,128)S(1)}, f32[40,8,128]{2,1,0:T(8,128)S(1)}, u32[]{:S(2)}, u32[]{:S(2)}) collective-permute-start(f32[40,8,128]{2,1,0:T(8,128)S(1)} %get-tuple-element.34), channel_id=1, source_target_pairs={{1,2},{2,1},{5,6},{6,5},{9,10},{10,9},{13,14},{14,13},{17,18},{18,... | collective-permute-start | bytes 491528 | tf_op jit(solution)/shard_map/ppermute | solution.py:843
  17.3 15.0 %all-to-all-start = ((f32[32,3,4,128]{3,2,1,0:T(4,128)}), f32[32,3,4,128]{3,2,1,0:T(4,128)S(1)}, u32[]{:S(2)}, u32[]{:S(2)}) async-start(f32[32,3,4,128]{3,2,1,0:T(4,128)} %bitcast.5), calls=%async_computation | async-start | bytes 393216 | tf_op jit(solution)/shard_map/all_to_all | solution.py:849
  23.5 12.3 %collective-permute-start.6 = (f32[50,8,128]{2,1,0:T(8,128)S(1)}, f32[50,8,128]{2,1,0:T(8,128)S(1)}, u32[]{:S(2)}, u32[]{:S(2)}) collective-permute-start(f32[50,8,128]{2,1,0:T(8,128)S(1)} %get-tuple-element.36), channel_id=1, source_target_pairs={{4,8},{12,16},{20,24},{8,4},{16,12},{24,20},{5,9},{13,17},{21,25},... | collective-permute-start | bytes 614408 | tf_op jit(solution)/shard_map/ppermute | solution.py:856
  24.2 11.6 %collective-permute-start.7 = (f32[50,8,128]{2,1,0:T(8,128)S(1)}, f32[50,8,128]{2,1,0:T(8,128)S(1)}, u32[]{:S(2)}, u32[]{:S(2)}) collective-permute-start(f32[50,8,128]{2,1,0:T(8,128)S(1)} %get-tuple-element.37), channel_id=1, source_target_pairs={{0,4},{8,12},{16,20},{24,28},{4,0},{12,8},{20,16},{28,24},{1,5},{9... | collective-permute-start | bytes 614408 | tf_op jit(solution)/shard_map/ppermute | solution.py:857
  32.2 1.4 %collective-permute-start.8 = (f32[32,3,4,128]{3,2,1,0:T(4,128)S(1)}, f32[32,3,4,128]{3,2,1,0:T(4,128)S(1)}, u32[]{:S(2)}, u32[]{:S(2)}) collective-permute-start(f32[32,3,4,128]{3,2,1,0:T(4,128)S(1)} %all-to-all-done.mine), channel_id=1, source_target_pairs={{0,4},{8,12},{16,20},{24,28},{4,0},{12,8},{20,16},{28,24},{1,5},{9... | collective-permute-start | bytes 589832 | tf_op jit(solution)/shard_map/ppermute | solution.py:859
  37.7 10.5 %all-to-all-start.1 = ((f32[32,8,128]{2,1,0:T(8,128)}), f32[32,8,128]{2,1,0:T(8,128)S(1)}, u32[]{:S(2)}, u32[]{:S(2)}) async-start(f32[32,8,128]{2,1,0:T(8,128)} %get-tuple-element.39), calls=%async_computation.1 | async-start | bytes 262144 | tf_op jit(solution)/shard_map/all_to_all | solution.py:879
